TPU v7x, 32 devices: a whole 2x2x4 slice. The times are simulated.
32 devices in a mesh: wide: 8 (over z, y), narrow: 4 (over x, core).
Axes of the slice: x: 2, y: 2, z: 4, core: 2. Of those that a mesh axis runs over, the one named last changes fastest.
Arguments:
- tokens: bfloat16 [16384, 768], P(('wide', 'narrow')), may hold values from -6 to 6
- memory: bfloat16 [16384, 768], P(('wide', 'narrow')), may hold values from -6 to 6
- cotangent: bfloat16 [16384, 768], P(('wide', 'narrow')), may hold values from -6 to 6
- dec_segments: int32 [32, 512], P(('wide', 'narrow')), may hold values from 0 to 15, never falling along the last dimension, each value on 1 to 256 neighbouring positions
- enc_segments: int32 [32, 512], P(('wide', 'narrow')), may hold values from 0 to 15, never falling along the last dimension, each value on 1 to 256 neighbouring positions
- dec_valid: int32 [32, 512], P(('wide', 'narrow')), may hold values 0 or 1
- attn_weights: bfloat16 [8, 768, 768], P(None, ('wide', 'narrow')), may hold values from -0.3125 to 0.3125
- w_in: bfloat16 [768, 3072], P(('wide', 'narrow')), may hold values from -0.21875 to 0.21875
- w_out: bfloat16 [3072, 768], P(('wide', 'narrow')), may hold values from -0.109375 to 0.109375
- norm_gains: bfloat16 [3, 768], P(None, ('wide', 'narrow')), may hold values from 0.5 to 1.5
- rel_table: bfloat16 [32, 12], replicated, may hold values from -4 to 4
- row_main: float32 [9, 768], P(None, ('wide', 'narrow')), may hold values from 1 to 1000
- row_out: float32 [3072], P(('wide', 'narrow')), may hold values from 1 to 1000
- col_main: float32 [9, 768], replicated, may hold values from 1 to 1000
- col_in: float32 [3072], replicated, may hold values from 1 to 1000
Outputs:
- layer_out: bfloat16 [16384, 768], P(('wide', 'narrow'))
- grad_tokens: float32 [16384, 768], P(('wide', 'narrow'))
- grad_memory: float32 [16384, 768], P(('wide', 'narrow'))
- grad_attn: float32 [8, 768, 768], P(None, ('wide', 'narrow'))
- grad_in: float32 [768, 3072], P(('wide', 'narrow'))
- grad_out: float32 [3072, 768], P(('wide', 'narrow'))
- grad_gains: float32 [3, 768], P(None, ('wide', 'narrow'))
- grad_table: float32 [32, 12], replicated
- new_row_main: float32 [9, 768], P(None, ('wide', 'narrow'))
- new_row_out: float32 [3072], P(('wide', 'narrow'))
- new_col_main: float32 [9, 768], replicated
- new_col_in: float32 [3072], replicated
Inputs may be any that keep to these rules, and one draw needn't show every extreme that they name: `dec_segments`: in each row the ids never fall, every id 0 to 15 appears, and a document has 1 to 256 positions. `enc_segments`: in each row the ids never fall, every id 0 to 15 appears, and a document has 1 to 256 positions.
All inputs are finite; a program needn't handle non-finite values. No bound on the sum of `dec_valid` on one device may be relied on, other than what follows from the above.
Results may differ from a plain program's by a relative error of at most 0.018.
The roundings to bfloat16 on the way count: a program that leaves them out, or rounds other values in their place, can miss the bound.
Values may be sent and summed in bfloat16 or wider, within the bound.
No kernel may reach another device: no remote copies, remote signals or barrier semaphores. Data moves between devices by JAX's collectives and lax.ppermute only.
A program may use at most 256 MiB of HBM per device.

v0:
```python
import math

import jax
import jax.numpy as jnp
from jax import lax
from jax.sharding import PartitionSpec as P

D = 768
HEADS = 12
HEAD = 64
FF = 3072
BUCKETS = 32
MAXDIST = 128
BLOCK = 512


EPSILON = 1e-06
DECAY = 0.8
NEGATIVE = -1e30


def thresholds():
    exact_count = BUCKETS // 2
    limits = list(range(1, exact_count + 1))
    for bucket_level in range(exact_count + 1, BUCKETS):
        limits.append(
            int(
                math.ceil(
                    exact_count
                    * (MAXDIST / exact_count) ** ((bucket_level - exact_count) / exact_count)
                )
            )
        )
    return limits


def bucket_table(distance, number_type):
    level_count = jnp.zeros(distance.shape, jnp.int32)
    for threshold in thresholds():
        level_count = level_count + (distance >= threshold).astype(jnp.int32)
    return (level_count[..., None] == jnp.arange(BUCKETS, dtype=jnp.int32)).astype(number_type)


def rms_norm(hidden, gain_row):
    return (
        hidden * lax.rsqrt(jnp.mean(hidden * hidden, axis=-1, keepdims=True) + EPSILON) * gain_row
    )


def smooth(values):
    return jax.nn.gelu(values, approximate=True)


def project(left_side, right_side):
    return jnp.dot(left_side, right_side, preferred_element_type=jnp.float32)


def project_back(gradient, right_side):
    return lax.dot_general(
        gradient, right_side, (((1,), (1,)), ((), ())), preferred_element_type=jnp.float32
    )


def weight_grad(left_side, gradient):
    return lax.dot_general(
        left_side, gradient, (((0,), (0,)), ((), ())), preferred_element_type=jnp.float32
    )


def split_heads(matrix):
    return matrix.reshape(matrix.shape[0], HEADS, HEAD)


def join_heads(tensor):
    return tensor.reshape(tensor.shape[0], HEADS * HEAD)


def self_mask(first_row, segment, key_valid):
    row_index = first_row + jnp.arange(BLOCK, dtype=jnp.int32)
    col_index = jnp.arange(segment.shape[0], dtype=jnp.int32)
    distance = row_index[:, None] - col_index[None, :]
    allowed = (
        (segment[:, None] == segment[None, :])
        & (distance >= 0)
        & ((key_valid[None, :] > 0) | (distance == 0))
    )
    return (allowed, bucket_table(distance, jnp.bfloat16))


def cross_mask(segment, mem_segment):
    return (segment[:, None] == mem_segment[None, :], None)


def block_scores(query_block, key_heads, bias_table, allowed, buckets):
    scores = jnp.einsum(
        "qhd,khd->hqk", query_block, key_heads, preferred_element_type=jnp.float32
    ) * HEAD ** (-0.5)
    if buckets is not None:
        scores = scores + jnp.einsum(
            "qkb,bh->hqk", buckets, bias_table, preferred_element_type=jnp.float32
        )
    return jnp.where(allowed[None], scores, NEGATIVE)


def attend_forward(query_heads, key_heads, value_heads, make_mask, bias_table):
    allowed, buckets = make_mask(0)
    scores = block_scores(query_heads, key_heads, bias_table, allowed, buckets)
    largest = jnp.max(scores, axis=-1, keepdims=True)
    weights = jnp.exp(scores - largest)
    totals = jnp.sum(weights, axis=-1, keepdims=True)
    weights_low = (weights / totals).astype(jnp.bfloat16)
    results = jnp.einsum(
        "hqk,khd->qhd", weights_low, value_heads, preferred_element_type=jnp.float32
    )
    log_totals = [largest + jnp.log(totals)]
    return (results, log_totals)


def attend_backward(
    query_heads, key_heads, value_heads, make_mask, bias_table, log_totals, grad_heads
):
    table_grad = jnp.zeros((BUCKETS, HEADS), jnp.float32)
    allowed, buckets = make_mask(0)
    scores = block_scores(query_heads, key_heads, bias_table, allowed, buckets)
    weights = jnp.exp(scores - log_totals[0])
    grad_weights = jnp.einsum(
        "qhd,khd->hqk", grad_heads, value_heads, preferred_element_type=jnp.float32
    )
    centre = jnp.sum(weights * grad_weights, axis=-1, keepdims=True)
    grad_scores = (weights * (grad_weights - centre)).astype(jnp.bfloat16)
    query_grads = jnp.einsum(
        "hqk,khd->qhd", grad_scores, key_heads, preferred_element_type=jnp.float32
    ) * HEAD ** (-0.5)
    key_grad = jnp.einsum(
        "hqk,qhd->khd", grad_scores, query_heads, preferred_element_type=jnp.float32
    ) * HEAD ** (-0.5)
    value_grad = jnp.einsum(
        "hqk,qhd->khd", weights.astype(jnp.bfloat16), grad_heads, preferred_element_type=jnp.float32
    )
    if buckets is not None:
        table_grad = jnp.einsum(
            "qkb,hqk->bh", buckets, grad_scores, preferred_element_type=jnp.float32
        )
    return (query_grads, key_grad, value_grad, table_grad)


def collect(attn_part, in_part, out_part, gain_part):
    return (
        lax.all_gather(attn_part, ("wide", "narrow"), axis=1, tiled=True),
        lax.all_gather(in_part, ("wide", "narrow"), axis=0, tiled=True),
        lax.all_gather(out_part, ("wide", "narrow"), axis=0, tiled=True),
        lax.all_gather(gain_part, ("wide", "narrow"), axis=1, tiled=True),
    )


def spread(attn_grad, in_grad, out_grad, gain_grad):
    return (
        lax.psum_scatter(attn_grad, ("wide", "narrow"), scatter_dimension=1, tiled=True),
        lax.psum_scatter(in_grad, ("wide", "narrow"), scatter_dimension=0, tiled=True),
        lax.psum_scatter(out_grad, ("wide", "narrow"), scatter_dimension=0, tiled=True),
        lax.psum_scatter(gain_grad, ("wide", "narrow"), scatter_dimension=1, tiled=True),
    )


def on_device(
    tokens,
    memory,
    cotangent,
    dec_segments,
    enc_segments,
    dec_valid,
    attn_weights,
    w_in,
    w_out,
    norm_gains,
    rel_table,
    row_main,
    row_out,
    col_main,
    col_in,
):
    attn_full, in_full, out_full, gain_full = collect(attn_weights, w_in, w_out, norm_gains)
    segment = dec_segments[0]
    mem_segment = enc_segments[0]
    key_valid = dec_valid[0]

    def self_masks(first_row):
        return self_mask(first_row, segment, key_valid)

    def cross_masks(first_row):
        return cross_mask(segment, mem_segment)

    residual = tokens.astype(jnp.float32)
    normed_first, norm_back_first = jax.vjp(rms_norm, residual, gain_full[0].astype(jnp.float32))
    first_low = normed_first.astype(jnp.bfloat16)
    query_heads = split_heads(project(first_low, attn_full[0]).astype(jnp.bfloat16))
    key_heads = split_heads(project(first_low, attn_full[1]).astype(jnp.bfloat16))
    value_heads = split_heads(project(first_low, attn_full[2]).astype(jnp.bfloat16))
    mixed, self_logs = attend_forward(query_heads, key_heads, value_heads, self_masks, rel_table)
    mixed_low = join_heads(mixed).astype(jnp.bfloat16)
    middle = residual + project(mixed_low, attn_full[3])
    normed_second, norm_back_second = jax.vjp(rms_norm, middle, gain_full[1].astype(jnp.float32))
    second_low = normed_second.astype(jnp.bfloat16)
    cross_query = split_heads(project(second_low, attn_full[4]).astype(jnp.bfloat16))
    memory_keys = split_heads(project(memory, attn_full[5]).astype(jnp.bfloat16))
    memory_values = split_heads(project(memory, attn_full[6]).astype(jnp.bfloat16))
    crossed, cross_logs = attend_forward(
        cross_query, memory_keys, memory_values, cross_masks, rel_table
    )
    crossed_low = join_heads(crossed).astype(jnp.bfloat16)
    upper = middle + project(crossed_low, attn_full[7])
    normed_third, norm_back_third = jax.vjp(rms_norm, upper, gain_full[2].astype(jnp.float32))
    third_low = normed_third.astype(jnp.bfloat16)
    inner = project(third_low, in_full)
    activated, smooth_back = jax.vjp(smooth, inner)
    active_low = activated.astype(jnp.bfloat16)
    layer_out = (upper + project(active_low, out_full)).astype(jnp.bfloat16)
    attn_full, in_full, out_full, gain_full = collect(attn_weights, w_in, w_out, norm_gains)
    grad_upper = cotangent.astype(jnp.float32)
    grad_ffn_branch = grad_upper.astype(jnp.bfloat16)
    grad_w_out = weight_grad(active_low, grad_ffn_branch)
    (grad_inner,) = smooth_back(project_back(grad_ffn_branch, out_full))
    grad_inner_low = grad_inner.astype(jnp.bfloat16)
    grad_w_in = weight_grad(third_low, grad_inner_low)
    grad_from_third, grad_gain_third = norm_back_third(project_back(grad_inner_low, in_full))
    grad_upper = grad_upper + grad_from_third
    grad_cross_branch = grad_upper.astype(jnp.bfloat16)
    grad_cross_out = weight_grad(crossed_low, grad_cross_branch)
    grad_crossed = split_heads(project_back(grad_cross_branch, attn_full[7]).astype(jnp.bfloat16))
    cross_query_grad, memory_key_grad, memory_value_grad, unused_table = attend_backward(
        cross_query, memory_keys, memory_values, cross_masks, rel_table, cross_logs, grad_crossed
    )
    cross_query_low = join_heads(cross_query_grad).astype(jnp.bfloat16)
    memory_key_low = join_heads(memory_key_grad).astype(jnp.bfloat16)
    memory_value_low = join_heads(memory_value_grad).astype(jnp.bfloat16)
    grad_cross_query = weight_grad(second_low, cross_query_low)
    grad_cross_key = weight_grad(memory, memory_key_low)
    grad_cross_value = weight_grad(memory, memory_value_low)
    grad_memory = project_back(memory_key_low, attn_full[5]) + project_back(
        memory_value_low, attn_full[6]
    )
    grad_from_second, grad_gain_second = norm_back_second(
        project_back(cross_query_low, attn_full[4])
    )
    grad_middle = grad_upper + grad_from_second
    grad_self_branch = grad_middle.astype(jnp.bfloat16)
    grad_self_out = weight_grad(mixed_low, grad_self_branch)
    grad_mixed = split_heads(project_back(grad_self_branch, attn_full[3]).astype(jnp.bfloat16))
    query_grad, key_grad, value_grad, table_grad = attend_backward(
        query_heads, key_heads, value_heads, self_masks, rel_table, self_logs, grad_mixed
    )
    query_low = join_heads(query_grad).astype(jnp.bfloat16)
    key_low = join_heads(key_grad).astype(jnp.bfloat16)
    value_low = join_heads(value_grad).astype(jnp.bfloat16)
    grad_self_query = weight_grad(first_low, query_low)
    grad_self_key = weight_grad(first_low, key_low)
    grad_self_value = weight_grad(first_low, value_low)
    grad_first = (
        project_back(query_low, attn_full[0])
        + project_back(key_low, attn_full[1])
        + project_back(value_low, attn_full[2])
    )
    grad_from_first, grad_gain_first = norm_back_first(grad_first)
    grad_tokens = grad_middle + grad_from_first
    attn_local = jnp.stack(
        [
            grad_self_query,
            grad_self_key,
            grad_self_value,
            grad_self_out,
            grad_cross_query,
            grad_cross_key,
            grad_cross_value,
            grad_cross_out,
        ]
    )
    gain_local = jnp.stack([grad_gain_first, grad_gain_second, grad_gain_third])
    grad_attn, grad_in, grad_out, grad_gains = spread(attn_local, grad_w_in, grad_w_out, gain_local)
    square_attn = grad_attn * grad_attn
    square_in = grad_in * grad_in
    square_out = grad_out * grad_out
    row_means = jnp.concatenate(
        [jnp.mean(square_attn, axis=2), jnp.mean(square_in, axis=1)[None]], axis=0
    )
    new_row_main = DECAY * row_main + (1.0 - DECAY) * row_means
    new_row_out = DECAY * row_out + (1.0 - DECAY) * jnp.mean(square_out, axis=1)
    column_main = jnp.concatenate(
        [jnp.sum(square_attn, axis=1), jnp.sum(square_out, axis=0)[None]], axis=0
    )
    column_in = jnp.sum(square_in, axis=0)
    column_main, column_in, grad_table = lax.psum(
        (column_main, column_in, table_grad), ("wide", "narrow")
    )
    col_means = jnp.concatenate([column_main[:8] / D, column_main[8:] / FF], axis=0)
    new_col_main = DECAY * col_main + (1.0 - DECAY) * col_means
    new_col_in = DECAY * col_in + (1.0 - DECAY) * (column_in / D)
    return (
        layer_out,
        grad_tokens,
        grad_memory,
        grad_attn,
        grad_in,
        grad_out,
        grad_gains,
        grad_table,
        new_row_main,
        new_row_out,
        new_col_main,
        new_col_in,
    )


def solution(mesh):
    placed = (
        P(("wide", "narrow"), None),
        P(("wide", "narrow"), None),
        P(("wide", "narrow"), None),
        P(("wide", "narrow"), None),
        P(("wide", "narrow"), None),
        P(("wide", "narrow"), None),
        P(None, ("wide", "narrow"), None),
        P(("wide", "narrow"), None),
        P(("wide", "narrow"), None),
        P(None, ("wide", "narrow")),
        P(),
        P(None, ("wide", "narrow")),
        P(("wide", "narrow")),
        P(),
        P(),
    )
    return jax.shard_map(
        on_device,
        mesh=mesh,
        in_specs=placed,
        out_specs=(
            P(("wide", "narrow"), None),
            P(("wide", "narrow"), None),
            P(("wide", "narrow"), None),
            P(None, ("wide", "narrow"), None),
            P(("wide", "narrow"), None),
            P(("wide", "narrow"), None),
            P(None, ("wide", "narrow")),
            P(),
            P(None, ("wide", "narrow")),
            P(("wide", "narrow")),
            P(),
            P(),
        ),
        check_vma=False,
    )
```

profile of v0, /device:TPU:0, one launch (start us, length us, event | category | flops | bytes accessed | tf_op | source)
XLA Modules:
  0.0 785.0 jit_solution(14176448015330795165)
XLA Ops:
  13.0 43.5 %all-gather = bf16[32,24,3]{1,2,0:T(4,128)(2,1)S(1)} all-gather(bf16[1,24,3]{1,2,0:T(4,128)(2,1)} %bitcast.206), channel_id=1, replica_groups=mesh['wide'=8,'narrow'=4] {'wide','narrow'}, dimensions={0}, use_global_device_ids=true | all-gather | bytes 4752 | tf_op jit(solution)/shard_map/all_gather | solution.py:152
  56.7 9.3 %fusion.1 = f32[512,512,12]{0,2,1:T(8,128)} fusion(s32[512,512]{0,1:T(8,128)S(1)} %convert_add_fusion.1, bf16[32,12]{0,1:T(8,128)(2,1)} %param.25), kind=kOutput, calls=%fused_computation.2 | convolution fusion | flops 209715200 | bytes 13632256 | tf_op jit(solution)/shard_map/qkb,bh->hqk/dot_general | solution.py:99
  67.1 10.1 %all-gather.9.cloned.1.call-done = bf16[3072,768]{1,0:T(8,128)(2,1)} async-done(((bf16[96,768]{1,0:T(8,128)(2,1)}), bf16[3072,768]{1,0:T(8,128)(2,1)}) %all-gather.9.cloned.1.call-update) | async-done | bytes 4718608 | tf_op jit(solution)/shard_map/all_gather | solution.py:151
  77.2 6.9 fusion.113
  84.1 77.0 %all-gather.5.cloned.1.call-done = bf16[8,768,768]{2,1,0:T(8,128)(2,1)} async-done(((bf16[8,24,768]{2,1,0:T(8,128)(2,1)}), bf16[8,768,768]{2,1,0:T(8,128)(2,1)}) %all-gather.5.cloned.1.call-update) | async-done | bytes 9437200 | tf_op jit(solution)/shard_map/all_gather | solution.py:149
  166.7 2.4 convolution_convert_fusion.7
  170.3 3.0 convolution_convert_fusion.2
  174.6 3.2 convolution_convert_fusion.4
  177.9 2.3 copy.84
  180.1 14.5 %fusion.112 = (f32[12,512]{1,0:T(8,128)S(1)}, f32[12,512,512]{1,2,0:T(8,128)S(1)}) fusion(f32[512,512,12]{0,2,1:T(8,128)} %fusion.1, bf16[512,12,64]{0,2,1:T(8,128)(2,1)} %bitcast.177, bf16[512,12,64]{0,2,1:T(8,128)(2,1)S(1)} %bitcast.171, pred[512,512]{0,1:T(8,128)(4,1)} %get-tuple-element.32), kind=kOutput, calls=%fused_computation.194 | convolution fusion | flops 415229952 | bytes 27025408 | tf_op jit(solution)/shard_map/qhd,khd->hqk/dot_general | solution.py:95
  196.5 2.7 copy-done.1
  199.2 2.7 fusion.42
  201.9 2.5 multiply_reduce_fusion.7
  205.6 3.1 convolution_convert_fusion.3
  212.2 2.6 fusion.6
  216.8 3.6 fusion.41
  220.4 2.5 multiply_reduce_fusion.6
  222.9 3.3 all-gather.7.cloned.1.call-done
  226.2 11.5 %fusion.16 = (bf16[512,3072]{1,0:T(8,128)(2,1)}, f32[512,3072]{1,0:T(8,128)S(1)}) fusion(f32[512,3072]{1,0:T(8,128)} %fusion.113, bf16[768,3072]{1,0:T(8,128)(2,1)} %all-gather.7.cloned.1.call-done, f32[512,768]{1,0:T(8,128)S(1)} %get-tuple-element.40, f32[768]{0:T(1024)S(1)} %get-tuple-element.24, f32[512]{0:T(512)S(1)} %fusion.98), kind=kOutput, calls=%fused_computation.31 | convolution fusion | flops 2448556032 | bytes 22025216 | tf_op jit(solution)/shard_map/dot_general | solution.py:55
  237.8 2.6 copy-done.57
  240.3 5.6 fusion.105
  246.0 7.9 %multiply_reduce_fusion.2 = (f32[768]{0:T(1024)}, f32[512]{0:T(512)S(1)}, f32[512,768]{1,0:T(8,128)}) fusion(f32[512,768]{1,0:T(8,128)S(1)} %get-tuple-element.40, f32[512]{0:T(512)S(1)} %fusion.98, f32[768]{0:T(1024)S(1)} %get-tuple-element.24, bf16[512,3072]{1,0:T(8,128)(2,1)} %get-tuple-element.41, bf16[768,3072]{1,0:T(8,128)(2,1)} %all-gather.7.cloned.1.call-done), kind=kOutput, calls=%fused_computation.65 | convolution fusion | flops 2418277120 | bytes 11020288 | tf_op jit(solution)/shard_map/dot_general | solution.py:59
  253.9 5.3 fusion.103
  263.1 3.0 convolution_convert_fusion.1
  266.1 2.4 copy.88
  269.3 14.5 %multiply_reduce_fusion.1 = (f32[12,512]{1,0:T(8,128)S(1)}, f32[12,512,512]{1,2,0:T(8,128)}) fusion(f32[12,512]{1,0:T(8,128)S(1)} %log_add_fusion.1, f32[12,512,512]{1,2,0:T(8,128)} %copy-done.2, pred[512,512]{0,1:T(8,128)(4,1)S(1)} %get-tuple-element.31, bf16[512,12,64]{0,2,1:T(8,128)(2,1)} %bitcast.189, bf16[512,12,64]{0,2,1:T(8,128)(2,1)} %bitcast.187), kind=kOutput, calls=%fused_computation.11 | convolution fusion | flops 418375680 | bytes 27049984 | tf_op jit(solution)/shard_map/qhd,khd->hqk/dot_general | solution.py:126
  283.8 7.5 multiply_convert_fusion.1
  294.0 2.7 multiply_reduce_fusion.3
  298.3 3.0 convolution_convert_fusion
  301.3 2.3 copy.90
  303.7 12.3 %multiply_reduce_fusion = (f32[12,512]{1,0:T(8,128)S(1)}, f32[12,512,512]{1,2,0:T(8,128)}) fusion(f32[12,512,512]{1,2,0:T(8,128)} %copy-done.1, f32[12,512]{1,0:T(8,128)S(1)} %log_add_fusion, bf16[512,12,64]{0,2,1:T(8,128)(2,1)} %bitcast.175, bf16[512,12,64]{0,2,1:T(8,128)(2,1)} %bitcast.185), kind=kOutput, calls=%fused_computation.8 | convolution fusion | flops 412084224 | bytes 26787840 | tf_op jit(solution)/shard_map/qhd,khd->hqk/dot_general | solution.py:126
  316.0 7.3 multiply_convert_fusion
  326.0 2.4 bitcast_dynamic-update-slice_fusion.7
  330.4 2.4 bitcast_dynamic-update-slice_fusion.6
  334.9 2.4 bitcast_dynamic-update-slice_fusion.5
  337.3 4.2 bitcast_dynamic-update-slice_fusion.4
  341.5 2.3 bitcast_dynamic-update-slice_fusion.3
  349.0 3.3 fusion.35
  358.4 2.3 fusion.83
  360.8 2.4 fusion.82
  363.2 2.6 fusion.29
  365.9 2.3 fusion.85
  368.2 3.4 convolution_add_fusion
  373.3 7.8 fusion.43
  381.2 5.0 add_convert_fusion
  387.3 135.0 %reduce-scatter.7.cloned.1.call-done = f32[24,3072]{1,0:T(8,128)} async-done(((f32[768,3072]{1,0:T(8,128)}), f32[24,3072]{1,0:T(8,128)}) %reduce-scatter.7.cloned.1.call-update) | async-done | bytes 294928 | tf_op jit(solution)/shard_map/reduce_scatter | solution.py:159
  524.0 209.5 %reduce-scatter.5.cloned.1.call-done = f32[8,24,768]{2,1,0:T(8,128)} async-done(((f32[8,768,768]{2,1,0:T(8,128)}), f32[8,24,768]{2,1,0:T(8,128)}) %reduce-scatter.5.cloned.1.call-update) | async-done | bytes 589840 | tf_op jit(solution)/shard_map/reduce_scatter | solution.py:158
  734.7 40.4 %all-reduce.1 = (f32[3,768]{1,0:T(4,128)S(1)}, f32[32,12]{0,1:T(8,128)}, f32[9,768]{1,0:T(8,128)S(1)}, f32[3072]{0:T(1024)S(1)}) all-reduce(f32[3,768]{1,0:T(4,128)S(1)} %pad_maximum_fusion.1, f32[32,12]{0,1:T(8,128)S(1)} %fusion.43, f32[9,768]{1,0:T(8,128)S(1)} %pad_maximum_fusion, ...), channel_id=5, replica_groups=mesh['wide'=8,'narrow'=4] {'wide','narrow'}, use_global_device_ids=true, to_apply=%region_18.19.clone | all-reduce | flops 12672 | bytes 101376
  (221 shorter events, 58.6 us)
Async XLA Ops:
  7.2 163.1 %copy-start = (bf16[512,768]{1,0:T(8,128)(2,1)S(1)}, bf16[512,768]{1,0:T(8,128)(2,1)}, u32[]{:S(2)}) copy-start(bf16[512,768]{1,0:T(8,128)(2,1)} %param.16) | copy-start | bytes 2359300
  7.2 70.0 %all-gather.9.cloned.1.call-start = ((), (), s32[]{:S(2)}) async-start(), calls=%async_computation.5 | async-start | bytes 4866048 | tf_op jit(solution)/shard_map/all_gather | solution.py:151
  7.9 153.1 %all-gather.5.cloned.1.call-start = ((), (), s32[]{:S(2)}) async-start(), calls=%async_computation.3 | async-start | bytes 9732096 | tf_op jit(solution)/shard_map/all_gather | solution.py:149
  8.7 217.5 %all-gather.7.cloned.1.call-start = ((), (), s32[]{:S(2)}) async-start(), calls=%async_computation.4 | async-start | bytes 4866048 | tf_op jit(solution)/shard_map/all_gather | solution.py:150
  9.4 376.8 %reduce-scatter.9.cloned.1.call-start = ((), (), s32[]{:S(2)}) async-start(), calls=%async_computation.8 | async-start | bytes 9732096 | tf_op jit(solution)/shard_map/reduce_scatter | solution.py:160
  10.3 55.7 %copy-start.26 = (s32[512,512]{0,1:T(8,128)}, s32[512,512]{0,1:T(8,128)S(1)}, u32[]{:S(2)}) copy-start(s32[512,512]{0,1:T(8,128)S(1)} %convert_add_fusion.1) | copy-start | bytes 3145732
  56.6 9.4 %copy-start.50 = (s32[1,512]{1,0:T(1,128)S(1)}, s32[1,512]{1,0:T(1,128)}, u32[]{:S(2)}) copy-start(s32[1,512]{1,0:T(1,128)} %param.18) | copy-start | bytes 6148
  56.6 9.4 %copy-start.55 = (s32[1,512]{1,0:T(1,128)S(1)}, s32[1,512]{1,0:T(1,128)}, u32[]{:S(2)}) copy-start(s32[1,512]{1,0:T(1,128)} %param.19) | copy-start | bytes 6148
  56.6 20.6 %copy-start.43 = (bf16[512,768]{1,0:T(8,128)(2,1)S(1)}, bf16[512,768]{1,0:T(8,128)(2,1)}, u32[]{:S(2)}) copy-start(bf16[512,768]{1,0:T(8,128)(2,1)} %param.17) | copy-start | bytes 2359300
  67.1 93.9 %copy-start.5 = (bf16[512,768]{1,0:T(8,128)(2,1)S(1)}, bf16[512,768]{1,0:T(8,128)(2,1)}, u32[]{:S(2)}) copy-start(bf16[512,768]{1,0:T(8,128)(2,1)} %param.15) | copy-start | bytes 2359300
  166.7 13.4 %copy-start.16 = (bf16[512,768]{0,1:T(8,128)(2,1)}, bf16[512,768]{0,1:T(8,128)(2,1)S(1)}, u32[]{:S(2)}) copy-start(bf16[512,768]{0,1:T(8,128)(2,1)S(1)} %copy.81) | copy-start | bytes 2359300
  174.6 35.5 %copy-start.18 = (bf16[512,768]{0,1:T(8,128)(2,1)}, bf16[512,768]{0,1:T(8,128)(2,1)S(1)}, u32[]{:S(2)}) copy-start(bf16[512,768]{0,1:T(8,128)(2,1)S(1)} %copy.86) | copy-start | bytes 2359300
  204.4 7.8 copy-start.51
  214.8 5.6 copy-start.45
  226.2 14.1 %copy-start.44 = (bf16[512,768]{1,0:T(8,128)(2,1)S(1)}, bf16[512,768]{1,0:T(8,128)(2,1)}, u32[]{:S(2)}) copy-start(bf16[512,768]{1,0:T(8,128)(2,1)} %param.17) | copy-start | bytes 2359300
  246.0 276.3 %reduce-scatter.7.cloned.1.call-start = ((), (), s32[]{:S(2)}) async-start(), calls=%async_computation.7 | async-start | bytes 9732096 | tf_op jit(solution)/shard_map/reduce_scatter | solution.py:159
  246.0 7.9 %copy-start.35 = (bf16[512,3072]{1,0:T(8,128)(2,1)S(1)}, bf16[512,3072]{1,0:T(8,128)(2,1)}, u32[]{:S(2)}) copy-start(bf16[512,3072]{1,0:T(8,128)(2,1)} %get-tuple-element.41) | copy-start | bytes 9437188
  259.2 474.2 %reduce-scatter.5.cloned.1.call-start = ((), (), s32[]{:S(2)}) async-start(), calls=%async_computation.6 | async-start | bytes 19464192 | tf_op jit(solution)/shard_map/reduce_scatter | solution.py:158
  269.3 14.5 %slice-start.3 = ((s8[12582912]{0:T(1024)(128)(4,1)}), s8[4194304]{0:T(1024)(128)(4,1)S(1)}, s32[]{:S(2)}) async-start(s8[12582912]{0:T(1024)(128)(4,1)} %bitcast.163), calls=%async_computation.12 | async-start | bytes 8388608
  269.3 14.5 %slice-start.4 = ((s8[12582912]{0:T(1024)(128)(4,1)}), s8[4194304]{0:T(1024)(128)(4,1)S(1)}, s32[]{:S(2)}) async-start(s8[12582912]{0:T(1024)(128)(4,1)} %bitcast.163), calls=%async_computation.13 | async-start | bytes 8388608
  269.3 14.5 %slice-start.5 = ((s8[12582912]{0:T(1024)(128)(4,1)}), s8[4194304]{0:T(1024)(128)(4,1)S(1)}, s32[]{:S(2)}) async-start(s8[12582912]{0:T(1024)(128)(4,1)} %bitcast.163), calls=%async_computation.14 | async-start | bytes 8388608
  283.8 7.5 copy-start.19
  303.7 12.3 %slice-start = ((s8[12582912]{0:T(1024)(128)(4,1)}), s8[4194304]{0:T(1024)(128)(4,1)S(1)}, s32[]{:S(2)}) async-start(s8[12582912]{0:T(1024)(128)(4,1)} %bitcast.161), calls=%async_computation.9 | async-start | bytes 8388608
  303.7 12.3 %slice-start.1 = ((s8[12582912]{0:T(1024)(128)(4,1)}), s8[4194304]{0:T(1024)(128)(4,1)S(1)}, s32[]{:S(2)}) async-start(s8[12582912]{0:T(1024)(128)(4,1)} %bitcast.161), calls=%async_computation.10 | async-start | bytes 8388608
  303.7 12.3 %slice-start.2 = ((s8[12582912]{0:T(1024)(128)(4,1)}), s8[4194304]{0:T(1024)(128)(4,1)S(1)}, s32[]{:S(2)}) async-start(s8[12582912]{0:T(1024)(128)(4,1)} %bitcast.161), calls=%async_computation.11 | async-start | bytes 8388608
  316.0 7.4 copy-start.17
  330.4 13.4 %slice-start.11 = ((s8[6291456]{0:T(1024)(128)(4,1)}), s8[4194304]{0:T(1024)(128)(4,1)S(1)}, s32[]{:S(2)}) async-start(s8[6291456]{0:T(1024)(128)(4,1)} %bitcast.169), calls=%async_computation.20 | async-start | bytes 8388608
  332.8 11.0 %slice-start.12 = ((s8[6291456]{0:T(1024)(128)(4,1)}), s8[2097152]{0:T(1024)(128)(4,1)S(1)}, s32[]{:S(2)}) async-start(s8[6291456]{0:T(1024)(128)(4,1)} %bitcast.169), calls=%async_computation.21 | async-start | bytes 4194304
  334.8 9.0 %copy-start.24 = (bf16[12,64,512]{2,1,0:T(8,128)(2,1)}, bf16[12,64,512]{2,1,0:T(8,128)(2,1)S(1)}, u32[]{:S(2)}) copy-start(bf16[12,64,512]{2,1,0:T(8,128)(2,1)S(1)} %fusion.38) | copy-start | bytes 2359300
  334.8 6.6 copy-start.9
  334.9 6.6 copy-start.29
  334.9 8.9 %copy-start.23 = (bf16[512,768]{0,1:T(8,128)(2,1)S(1)}, bf16[512,768]{0,1:T(8,128)(2,1)}, u32[]{:S(2)}) copy-start(bf16[512,768]{0,1:T(8,128)(2,1)} %copy-done.22) | copy-start | bytes 2359300
  334.9 14.1 %slice-start.6 = ((s8[12582912]{0:T(1024)(128)(4,1)}), s8[4194304]{0:T(1024)(128)(4,1)S(1)}, s32[]{:S(2)}) async-start(s8[12582912]{0:T(1024)(128)(4,1)} %bitcast.165), calls=%async_computation.15 | async-start | bytes 8388608
  337.3 11.7 %slice-start.7 = ((s8[12582912]{0:T(1024)(128)(4,1)}), s8[4194304]{0:T(1024)(128)(4,1)S(1)}, s32[]{:S(2)}) async-start(s8[12582912]{0:T(1024)(128)(4,1)} %bitcast.165), calls=%async_computation.16 | async-start | bytes 8388608
  349.0 6.5 copy-start.15
  349.0 6.5 copy-start.34
  357.7 5.5 copy-start.25
  365.8 5.8 copy-start.12
  365.9 7.3 slice-start.9
  365.9 7.3 copy-start.27
  371.6 9.5 %slice-start.13 = ((s8[4718592]{0:T(1024)(128)(4,1)}), s8[4194304]{0:T(1024)(128)(4,1)S(1)}, s32[]{:S(2)}) async-start(s8[4718592]{0:T(1024)(128)(4,1)} %bitcast.207), calls=%async_computation.22 | async-start | bytes 8388608
  371.6 9.5 %slice-start.15 = ((s8[6291456]{0:T(1024)(128)(4,1)}), s8[4194304]{0:T(1024)(128)(4,1)S(1)}, s32[]{:S(2)}) async-start(s8[6291456]{0:T(1024)(128)(4,1)} %bitcast.209), calls=%async_computation.24 | async-start | bytes 8388608
  373.2 7.9 %slice-start.14 = ((s8[4718592]{0:T(1024)(128)(4,1)}), s8[524288]{0:T(1024)(128)(4,1)S(1)}, s32[]{:S(2)}) async-start(s8[4718592]{0:T(1024)(128)(4,1)} %bitcast.207), calls=%async_computation.23 | async-start | bytes 1048576
  373.2 7.9 %slice-start.16 = ((s8[6291456]{0:T(1024)(128)(4,1)}), s8[2097152]{0:T(1024)(128)(4,1)S(1)}, s32[]{:S(2)}) async-start(s8[6291456]{0:T(1024)(128)(4,1)} %bitcast.209), calls=%async_computation.25 | async-start | bytes 4194304
  381.2 142.3 %copy-start.56 = (f32[96]{0:T(128)S(1)}, f32[96]{0:T(128)}, u32[]{:S(2)}) copy-start(f32[96]{0:T(128)} %param.27) | copy-start | bytes 1156
  381.2 394.6 %copy-start.49 = (f32[3072]{0:T(1024)S(1)}, f32[3072]{0:T(1024)}, u32[]{:S(2)}) copy-start(f32[3072]{0:T(1024)} %param.29) | copy-start | bytes 36868
  381.2 395.2 %copy-start.53 = (f32[9,24]{1,0:T(8,128)S(1)}, f32[9,24]{1,0:T(8,128)}, u32[]{:S(2)}) copy-start(f32[9,24]{1,0:T(8,128)} %param.26) | copy-start | bytes 2596
  381.2 395.8 %copy-start.46 = (f32[9,768]{1,0:T(8,128)S(1)}, f32[9,768]{1,0:T(8,128)}, u32[]{:S(2)}) copy-start(f32[9,768]{1,0:T(8,128)} %param.28) | copy-start | bytes 82948
  (33 other events, 109.8 us)
Sparse Core Ops, SparseCore 0:
  10.9 66.2 all-gather.8
  80.1 80.8 all-gather.4
  164.0 62.2 all-gather.6
  246.1 134.2 reduce-scatter.8
  387.8 134.5 reduce-scatter.6
  529.1 204.2 reduce-scatter.4
where the time goes:
time: 794 us; the launch traced here: 785 us
  waiting for transfers between devices  437 us (55%)
  matrix products  184 us (23%)
  blocking collectives  83.9 us (11%)
  other arithmetic  34.1 us (4%)
  local copies, waits for them, and re-layouts  30 us (4%)
  between operations  15.6 us (2%)
    reduce_scatter x1, waiting for transfers between devices, spread(): lax.psum_scatter(attn_grad, ('wide', 'narrow'), scatter_dimension=1, tile...  210 us
    reduce_scatter x1, waiting for transfers between devices, spread(): lax.psum_scatter(in_grad, ('wide', 'narrow'), scatter_dimension=0, tiled=...  135 us
    all_gather x1, waiting for transfers between devices, collect(): lax.all_gather(attn_part, ('wide', 'narrow'), axis=1, tiled=True)  77 us
    all_gather x1, blocking collectives, collect(): lax.all_gather(gain_part, ('wide', 'narrow'), axis=1, tiled=True)  43.5 us
    unnamed x1, blocking collectives  40.4 us
    dot_general x10, matrix products, project(): return jnp.dot(left_side, right_side, preferred_element_type=jnp.float32)  37.4 us
    dot_general x10, matrix products, project_back(): lax.dot_general(gradient, right_side, (((1,), (1,)), ((), ())), preferred...  36.6 us
    dot_general x10, matrix products, weight_grad(): lax.dot_general(left_side, gradient, (((0,), (0,)), ((), ())), preferred_...  31.3 us
  transfers between devices with their start and end apart: 6, of which 5 were waited for; matrix products, arithmetic and copies ran while one was open for 27% of the time, Pallas kernels for 0%

commit v1 on v0

--- a/solution.py
+++ b/solution.py
@@ -144,22 +144,127 @@
     return (query_grads, key_grad, value_grad, table_grad)
 
 
-def collect(attn_part, in_part, out_part, gain_part):
-    return (
-        lax.all_gather(attn_part, ("wide", "narrow"), axis=1, tiled=True),
-        lax.all_gather(in_part, ("wide", "narrow"), axis=0, tiled=True),
-        lax.all_gather(out_part, ("wide", "narrow"), axis=0, tiled=True),
-        lax.all_gather(gain_part, ("wide", "narrow"), axis=1, tiled=True),
-    )
-
-
-def spread(attn_grad, in_grad, out_grad, gain_grad):
-    return (
-        lax.psum_scatter(attn_grad, ("wide", "narrow"), scatter_dimension=1, tiled=True),
-        lax.psum_scatter(in_grad, ("wide", "narrow"), scatter_dimension=0, tiled=True),
-        lax.psum_scatter(out_grad, ("wide", "narrow"), scatter_dimension=0, tiled=True),
-        lax.psum_scatter(gain_grad, ("wide", "narrow"), scatter_dimension=1, tiled=True),
-    )
+AXES = ("wide", "narrow")
+
+
+class Cube:
+    def __init__(self):
+        self.count = lax.axis_size("wide") * lax.axis_size("narrow")
+        self.bits = self.count.bit_length() - 1
+        self.me = lax.axis_index("wide") * lax.axis_size("narrow") + lax.axis_index("narrow")
+        high = list(range(self.bits - 1, 1, -1))
+        self.plan_a = high + [1]
+        self.plan_b = [1] + high
+
+    def bit(self, which):
+        return (self.me >> which) & 1
+
+    def swap(self, value, which):
+        pairs = [(i, i ^ (1 << which)) for i in range(self.count)]
+        return lax.ppermute(value, AXES, pairs)
+
+    def place(self, mine, theirs, which, axis, joined):
+        join = jnp.concatenate if joined else jnp.stack
+        return jnp.where(
+            self.bit(which) == 0, join([mine, theirs], axis), join([theirs, mine], axis)
+        )
+
+    def gather(self, value, plan):
+        held = []
+        for which in plan:
+            axis = sum(other > which for other in held)
+            value = self.place(value, self.swap(value, which), which, axis, False)
+            held.append(which)
+        return value.reshape((-1,) + value.shape[len(plan) :])
+
+    def scatter(self, value, plan):
+        value = value.reshape((2,) * (self.bits - 1) + value.shape[1:])
+        held = sorted(plan, reverse=True)
+        for which in reversed(plan):
+            axis = held.index(which)
+            mine = self.bit(which)
+            send = lax.dynamic_index_in_dim(value, 1 - mine, axis, False).astype(jnp.bfloat16)
+            keep = lax.dynamic_index_in_dim(value, mine, axis, False)
+            value = keep + self.swap(send, which).astype(jnp.float32)
+            held.remove(which)
+        return value
+
+    def half(self, value, whose):
+        size = value.shape[-1] // 2
+        return lax.dynamic_slice_in_dim(value, whose * size, size, value.ndim - 1)
+
+    def total(self, value):
+        for which in range(self.bits):
+            value = value + self.swap(value, which)
+        return value
+
+
+def gather_weights(cube, attn, w_in, w_out, gains):
+    rows = attn.shape[1]
+    wide_in = w_in.shape[1] // 2
+    core = cube.bit(0)
+
+    def packed(whose):
+        attn_half = cube.half(attn, whose).reshape(-1, D // 2)
+        in_half = cube.half(w_in, whose).reshape(-1, D // 2)
+        out_half = cube.half(w_out, whose)
+        gain_rows = jnp.pad(gains, ((0, 5), (0, D // 2 - gains.shape[1])))
+        return attn_half, in_half, out_half, gain_rows
+
+    mine = packed(core)
+    sizes = [part.shape[0] for part in mine]
+    theirs = cube.swap(jnp.concatenate(packed(1 - core), axis=0), 0)
+    starts = [sum(sizes[:k]) for k in range(5)]
+    theirs = [theirs[starts[k] : starts[k + 1]] for k in range(4)]
+    attn_pair = cube.place(
+        mine[0].reshape(8, rows, D // 2), theirs[0].reshape(8, rows, D // 2), 0, 1, True
+    )
+    in_pair = cube.place(
+        mine[1].reshape(rows, wide_in), theirs[1].reshape(rows, wide_in), 0, 0, True
+    )
+    out_pair = cube.place(mine[2], theirs[2], 0, 0, True)
+    gain_pair = cube.place(mine[3], theirs[3], 0, 0, True)
+
+    def whole(value):
+        return cube.place(value, cube.swap(value, 0), 0, value.ndim - 1, True)
+
+    def attn_chunk(first, last, plan, extra):
+        chunk = attn_pair[first:last].reshape(-1, D // 2)
+        chunk = chunk if extra is None else jnp.concatenate([chunk, extra], axis=0)
+        gathered = cube.gather(chunk, plan)
+        full = whole(gathered)
+        size = (last - first) * rows * 2
+        weights = full[:, :size].reshape(-1, last - first, rows * 2, D)
+        return [weights[:, k].reshape(D, D) for k in range(last - first)], gathered[:, size:]
+
+    first_two, gain_rows = attn_chunk(0, 2, cube.plan_a, gain_pair)
+    next_two, _ = attn_chunk(2, 4, cube.plan_b, None)
+    last_four, _ = attn_chunk(4, 8, cube.plan_a, None)
+    in_full = whole(cube.gather(in_pair, cube.plan_b)).reshape(D, -1)
+    out_full = whole(cube.gather(out_pair, cube.plan_a)).reshape(-1, D)
+    gain_full = gain_rows.reshape(-1, 8, D // 2)[:, :3, : gains.shape[1]]
+    gain_full = gain_full.transpose(1, 0, 2).reshape(3, D)
+    return first_two + next_two + last_four, in_full, out_full, gain_full
+
+
+def pair_grads(cube, products, plan):
+    core = cube.bit(0)
+    chips = cube.count // 2
+    sent = [weight_grad(left, cube.half(right, 1 - core)) for left, right in products]
+    kept = [weight_grad(left, cube.half(right, core)) for left, right in products]
+    columns = kept[0].shape[1]
+
+    def stacked(parts):
+        return jnp.concatenate(
+            [part.reshape(chips, part.shape[0] // chips, columns) for part in parts], axis=1
+        )
+
+    value = stacked(kept) + cube.swap(stacked(sent).astype(jnp.bfloat16), 0).astype(jnp.float32)
+    value = cube.scatter(value, plan)
+    value = value.reshape(len(products), 2, -1, columns)
+    mine = lax.dynamic_index_in_dim(value, core, 1, False)
+    theirs = cube.swap(lax.dynamic_index_in_dim(value, 1 - core, 1, False), 0)
+    return cube.place(mine, theirs, 0, 2, True)
 
 
 def on_device(
@@ -179,7 +284,10 @@
     col_main,
     col_in,
 ):
-    attn_full, in_full, out_full, gain_full = collect(attn_weights, w_in, w_out, norm_gains)
+    cube = Cube()
+    attn_full, in_full, out_full, gain_full = gather_weights(
+        cube, attn_weights, w_in, w_out, norm_gains
+    )
     segment = dec_segments[0]
     mem_segment = enc_segments[0]
     key_valid = dec_valid[0]
@@ -215,17 +323,15 @@
     activated, smooth_back = jax.vjp(smooth, inner)
     active_low = activated.astype(jnp.bfloat16)
     layer_out = (upper + project(active_low, out_full)).astype(jnp.bfloat16)
-    attn_full, in_full, out_full, gain_full = collect(attn_weights, w_in, w_out, norm_gains)
     grad_upper = cotangent.astype(jnp.float32)
     grad_ffn_branch = grad_upper.astype(jnp.bfloat16)
-    grad_w_out = weight_grad(active_low, grad_ffn_branch)
+    grad_out = pair_grads(cube, [(active_low, grad_ffn_branch)], cube.plan_a)[0]
     (grad_inner,) = smooth_back(project_back(grad_ffn_branch, out_full))
     grad_inner_low = grad_inner.astype(jnp.bfloat16)
-    grad_w_in = weight_grad(third_low, grad_inner_low)
+    grad_in = pair_grads(cube, [(third_low, grad_inner_low)], cube.plan_b)[0]
     grad_from_third, grad_gain_third = norm_back_third(project_back(grad_inner_low, in_full))
     grad_upper = grad_upper + grad_from_third
     grad_cross_branch = grad_upper.astype(jnp.bfloat16)
-    grad_cross_out = weight_grad(crossed_low, grad_cross_branch)
     grad_crossed = split_heads(project_back(grad_cross_branch, attn_full[7]).astype(jnp.bfloat16))
     cross_query_grad, memory_key_grad, memory_value_grad, unused_table = attend_backward(
         cross_query, memory_keys, memory_values, cross_masks, rel_table, cross_logs, grad_crossed
@@ -233,9 +339,16 @@
     cross_query_low = join_heads(cross_query_grad).astype(jnp.bfloat16)
     memory_key_low = join_heads(memory_key_grad).astype(jnp.bfloat16)
     memory_value_low = join_heads(memory_value_grad).astype(jnp.bfloat16)
-    grad_cross_query = weight_grad(second_low, cross_query_low)
-    grad_cross_key = weight_grad(memory, memory_key_low)
-    grad_cross_value = weight_grad(memory, memory_value_low)
+    cross_grads = pair_grads(
+        cube,
+        [
+            (second_low, cross_query_low),
+            (memory, memory_key_low),
+            (memory, memory_value_low),
+            (crossed_low, grad_cross_branch),
+        ],
+        cube.plan_a,
+    )
     grad_memory = project_back(memory_key_low, attn_full[5]) + project_back(
         memory_value_low, attn_full[6]
     )
@@ -244,7 +357,6 @@
     )
     grad_middle = grad_upper + grad_from_second
     grad_self_branch = grad_middle.astype(jnp.bfloat16)
-    grad_self_out = weight_grad(mixed_low, grad_self_branch)
     grad_mixed = split_heads(project_back(grad_self_branch, attn_full[3]).astype(jnp.bfloat16))
     query_grad, key_grad, value_grad, table_grad = attend_backward(
         query_heads, key_heads, value_heads, self_masks, rel_table, self_logs, grad_mixed
@@ -252,9 +364,10 @@
     query_low = join_heads(query_grad).astype(jnp.bfloat16)
     key_low = join_heads(key_grad).astype(jnp.bfloat16)
     value_low = join_heads(value_grad).astype(jnp.bfloat16)
-    grad_self_query = weight_grad(first_low, query_low)
-    grad_self_key = weight_grad(first_low, key_low)
-    grad_self_value = weight_grad(first_low, value_low)
+    late_grads = pair_grads(
+        cube, [(first_low, value_low), (mixed_low, grad_self_branch)], cube.plan_b
+    )
+    self_grads = pair_grads(cube, [(first_low, query_low), (first_low, key_low)], cube.plan_a)
     grad_first = (
         project_back(query_low, attn_full[0])
         + project_back(key_low, attn_full[1])
@@ -262,20 +375,8 @@
     )
     grad_from_first, grad_gain_first = norm_back_first(grad_first)
     grad_tokens = grad_middle + grad_from_first
-    attn_local = jnp.stack(
-        [
-            grad_self_query,
-            grad_self_key,
-            grad_self_value,
-            grad_self_out,
-            grad_cross_query,
-            grad_cross_key,
-            grad_cross_value,
-            grad_cross_out,
-        ]
-    )
     gain_local = jnp.stack([grad_gain_first, grad_gain_second, grad_gain_third])
-    grad_attn, grad_in, grad_out, grad_gains = spread(attn_local, grad_w_in, grad_w_out, gain_local)
+    grad_attn = jnp.concatenate([self_grads, late_grads, cross_grads], axis=0)
     square_attn = grad_attn * grad_attn
     square_in = grad_in * grad_in
     square_out = grad_out * grad_out
@@ -288,8 +389,11 @@
         [jnp.sum(square_attn, axis=1), jnp.sum(square_out, axis=0)[None]], axis=0
     )
     column_in = jnp.sum(square_in, axis=0)
-    column_main, column_in, grad_table = lax.psum(
-        (column_main, column_in, table_grad), ("wide", "narrow")
+    column_main, column_in, grad_table, gain_sums = lax.psum(
+        (column_main, column_in, table_grad, gain_local), AXES
+    )
+    grad_gains = lax.dynamic_slice_in_dim(
+        gain_sums, cube.me * norm_gains.shape[1], norm_gains.shape[1], 1
     )
     col_means = jnp.concatenate([column_main[:8] / D, column_main[8:] / FF], axis=0)
     new_col_main = DECAY * col_main + (1.0 - DECAY) * col_means

time: 794 us -> 603 us (0.76)
  waiting for transfers between devices: 437 us -> 181 us
  starting transfers between devices: 0.7 us -> 57.6 us
  other arithmetic: 34.1 us -> 79.1 us
  blocking collectives: 83.9 us -> 39.7 us
  local copies, waits for them, and re-layouts: 30 us -> 48.3 us
  between operations: 15.6 us -> 2.83 us
    reduce_scatter x3 -> x0, waiting for transfers between devices: 344 us -> none  [the longest x1 210 us: spread(): lax.psum_scatter(attn_grad, ('wide', 'narrow'), scatter_dimension=1, tile...]
    ppermute x0 -> x56, waiting for transfers between devices: none -> 181 us  [swap(): return lax.ppermute(value, AXES, pairs)]
    all_gather x3 -> x0, waiting for transfers between devices: 90.4 us -> none  [the longest x1 77 us: collect(): lax.all_gather(attn_part, ('wide', 'narrow'), axis=1, tiled=True)]
    ppermute x0 -> x56, starting transfers between devices: none -> 57.6 us  [swap(): return lax.ppermute(value, AXES, pairs)]
    all_gather x1 -> x0, blocking collectives: 43.5 us -> none  [collect(): lax.all_gather(gain_part, ('wide', 'narrow'), axis=1, tiled=True)]
    unnamed x1 -> x0, blocking collectives: 40.4 us -> none
    psum x0 -> x1, blocking collectives: none -> 39.7 us  [on_device(): lax.psum((column_main, column_in, table_grad, gain_local), AXES)]
    select_n x0 -> x47, other arithmetic: none -> 29 us  [place(): jnp.where(self.bit(which) == 0, join([mine, theirs], axis), join([theirs,...]
  transfers between devices with their start and end apart: 6 -> 56, of which waited for: 5 -> 21; matrix products, arithmetic and copies ran while one was open for 27% -> 26% of each run, Pallas kernels for 0% -> 0%
where the time goes in v1:
time: 603 us; the launch traced here: 592 us
  matrix products  183 us (30%)
  waiting for transfers between devices  181 us (30%)
  other arithmetic  79.1 us (13%)
  starting transfers between devices  57.6 us (10%)
  local copies, waits for them, and re-layouts  48.3 us (8%)
  blocking collectives  39.7 us (7%)
    ppermute x56, waiting for transfers between devices, swap(): return lax.ppermute(value, AXES, pairs)  181 us
    ppermute x56, starting transfers between devices, swap(): return lax.ppermute(value, AXES, pairs)  57.6 us
    psum x1, blocking collectives, on_device(): lax.psum((column_main, column_in, table_grad, gain_local), AXES)  39.7 us
    dot_general x20, matrix products, weight_grad(): lax.dot_general(left_side, gradient, (((0,), (0,)), ((), ())), preferred_...  36.4 us
    dot_general x10, matrix products, project_back(): lax.dot_general(gradient, right_side, (((1,), (1,)), ((), ())), preferred...  33.8 us
    dot_general x10, matrix products, project(): return jnp.dot(left_side, right_side, preferred_element_type=jnp.float32)  30.5 us
    select_n x47, other arithmetic, place(): jnp.where(self.bit(which) == 0, join([mine, theirs], axis), join([theirs,...  29 us
    dot_general x2, matrix products, block_scores(): jnp.einsum('qhd,khd->hqk', query_block, key_heads, preferred_element_type...  17.2 us
  transfers between devices with their start and end apart: 56, of which 21 were waited for; matrix products, arithmetic and copies ran while one was open for 26% of the time, Pallas kernels for 0%

profile of v1, /device:TPU:0, one launch (start us, length us, event | category | flops | bytes accessed | tf_op | source)
XLA Modules:
  0.0 591.8 jit_solution(9508735828426083129)
XLA Ops:
  6.8 8.5 %fusion.1 = f32[512,512,12]{0,2,1:T(8,128)} fusion(s32[512,512]{0,1:T(8,128)S(1)} %convert_add_fusion.3, bf16[32,12]{0,1:T(8,128)(2,1)S(1)} %copy-done.82), kind=kOutput, calls=%fused_computation.2 | convolution fusion | flops 209715200 | bytes 13632256 | tf_op jit(solution)/shard_map/qkb,bh->hqk/dot_general | solution.py:99
  25.1 3.0 collective-permute-start.1
  28.4 17.3 %collective-permute-done.1 = bf16[112,384]{1,0:T(8,128)(2,1)S(1)} collective-permute-done((bf16[112,384]{1,0:T(8,128)(2,1)S(1)}, bf16[112,384]{1,0:T(8,128)(2,1)S(1)}, u32[]{:S(2)}, u32[]{:S(2)}) %collective-permute-start.1) | collective-permute-done | bytes 86048 | tf_op jit(solution)/shard_map/ppermute | solution.py:164
  52.1 7.3 %collective-permute-done.2 = bf16[2,112,384]{2,1,0:T(8,128)(2,1)S(1)} collective-permute-done((bf16[2,112,384]{2,1,0:T(8,128)(2,1)S(1)}, bf16[2,112,384]{2,1,0:T(8,128)(2,1)S(1)}, u32[]{:S(2)}, u32[]{:S(2)}) %collective-permute-start.2) | collective-permute-done | bytes 172064 | tf_op jit(solution)/shard_map/ppermute | solution.py:164
  61.2 10.9 %collective-permute-done.22 = bf16[2,192,384]{2,1,0:T(8,128)(2,1)S(1)} collective-permute-done((bf16[2,192,384]{2,1,0:T(8,128)(2,1)S(1)}, bf16[2,192,384]{2,1,0:T(8,128)(2,1)S(1)}, u32[]{:S(2)}, u32[]{:S(2)}) %collective-permute-start.22) | collective-permute-done | bytes 294944 | tf_op jit(solution)/shard_map/ppermute | solution.py:164
  75.3 3.1 collective-permute-done.7
  81.2 20.1 %collective-permute-done.13 = bf16[2,2,192,384]{3,2,0,1:T(8,128)(2,1)S(1)} collective-permute-done((bf16[2,2,192,384]{3,2,0,1:T(8,128)(2,1)S(1)}, bf16[2,2,192,384]{3,2,0,1:T(8,128)(2,1)S(1)}, u32[]{:S(2)}, u32[]{:S(2)}) %collective-permute-start.13) | collective-permute-done | bytes 589856 | tf_op jit(solution)/shard_map/ppermute | solution.py:164
  111.4 2.6 collective-permute-done.8
  117.6 14.3 %collective-permute-done.14 = bf16[2,2,2,192,384]{4,3,0,1,2:T(8,128)(2,1)} collective-permute-done((bf16[2,2,2,192,384]{4,3,0,1,2:T(8,128)(2,1)}, bf16[2,2,2,192,384]{4,3,0,1,2:T(8,128)(2,1)}, u32[]{:S(2)}, u32[]{:S(2)}) %collective-permute-start.14) | collective-permute-done | bytes 1179680 | tf_op jit(solution)/shard_map/ppermute | solution.py:164
  131.8 2.9 maximum_select_fusion.4
  136.4 12.9 %collective-permute-done.24 = bf16[2,2,2,192,384]{4,3,0,1,2:T(8,128)(2,1)} collective-permute-done((bf16[2,2,2,192,384]{4,3,0,1,2:T(8,128)(2,1)}, bf16[2,2,2,192,384]{4,3,0,1,2:T(8,128)(2,1)}, u32[]{:S(2)}, u32[]{:S(2)}) %collective-permute-start.24) | collective-permute-done | bytes 1179680 | tf_op jit(solution)/shard_map/ppermute | solution.py:164
  153.0 3.4 maximum_select_fusion.5
  156.9 3.2 maximum_select_fusion.3
  173.7 3.3 convolution_convert_fusion.7
  178.4 15.1 %fusion.195 = (f32[12,512]{1,0:T(8,128)S(1)}, f32[12,512,512]{1,2,0:T(8,128)S(1)}) fusion(f32[512,512,12]{0,2,1:T(8,128)} %fusion.1, bf16[512,12,64]{0,2,1:T(8,128)(2,1)S(1)} %bitcast.429, bf16[512,12,64]{0,2,1:T(8,128)(2,1)S(1)} %bitcast.420, pred[512,512]{0,1:T(8,128)(4,1)} %get-tuple-element.77), kind=kOutput, calls=%fused_computation.401 | convolution fusion | flops 415229952 | bytes 27025408 | tf_op jit(solution)/shard_map/qhd,khd->hqk/dot_general | solution.py:95
  195.4 2.7 copy-done.1
  202.9 4.9 maximum_select_fusion
  221.5 3.8 fusion.48
  226.5 9.8 %multiply_convert_fusion.2 = (bf16[512,3072]{1,0:T(8,128)(2,1)}, f32[512,3072]{1,0:T(8,128)S(1)}) fusion(bf16[512,768]{1,0:T(8,128)(2,1)S(1)} %multiply_convert_fusion.7, bf16[768,1536]{1,0:T(8,128)(2,1)} %bitcast.87, bf16[768,1536]{1,0:T(8,128)(2,1)} %bitcast.85, pred[]{:T(512)S(6)} %eq.52), kind=kOutput, calls=%fused_computation.41 | convolution fusion | flops 2451308544 | bytes 14942209 | tf_op jit(solution)/shard_map/dot_general | solution.py:55
  236.3 10.2 %fusion.16 = bf16[512,3072]{1,0:T(8,128)(2,1)S(1)} fusion(f32[512,3072]{1,0:T(8,128)S(1)} %get-tuple-element.87, bf16[512,768]{1,0:T(8,128)(2,1)S(1)} %copy-done.27, bf16[3072,384]{1,0:T(8,128)(2,1)} %bitcast.102, bf16[3072,384]{1,0:T(8,128)(2,1)} %bitcast.100, pred[]{:T(512)S(6)} %eq.52), kind=kOutput, calls=%fused_computation.31 | convolution fusion | flops 2468610048 | bytes 14942209 | tf_op jit(solution)/shard_map/dot_general | solution.py:59
  246.6 8.0 %multiply_reduce_fusion.2 = (f32[768]{0:T(1024)S(1)}, f32[512]{0:T(512)S(1)}, f32[512,768]{1,0:T(8,128)S(1)}) fusion(f32[512,768]{1,0:T(8,128)S(1)} %get-tuple-element.85, f32[512]{0:T(512)S(1)} %fusion.168, f32[768]{0:T(1024)S(1)} %reshape.2373, bf16[512,3072]{1,0:T(8,128)(2,1)S(1)} %fusion.16, bf16[768,1536]{1,0:T(8,128)(2,1)} %bitcast.87, ...), kind=kOutput, calls=%fused_computation.86 | convolution fusion | flops 2439510784 | bytes 11020289 | tf_op jit(solution)/shard_map/dot_general | solution.py:59
  262.7 8.0 %fusion.42 = bf16[12,64,512]{2,1,0:T(8,128)(2,1)S(1)} fusion(bf16[512,12,64]{0,2,1:T(8,128)(2,1)} %bitcast.467, f32[12,512]{1,0:T(8,128)S(1)} %log_add_fusion.1, f32[12,512,512]{1,2,0:T(8,128)} %copy-done.2, pred[512,512]{0,1:T(8,128)(4,1)S(1)} %get-tuple-element.76), kind=kOutput, calls=%fused_computation.115 | convolution fusion | flops 415629312 | bytes 14442496 | tf_op jit(solution)/shard_map/hqk,qhd->khd/dot_general | solution.py:137
  275.5 2.9 convolution_convert_fusion.1
  278.3 3.6 fusion.40
  282.0 8.0 %add_convert_fusion = bf16[512,768]{1,0:T(8,128)(2,1)} fusion(f32[512,768]{1,0:T(8,128)S(1)} %get-tuple-element.85, bf16[512,3072]{1,0:T(8,128)(2,1)S(1)} %copy-done.46, bf16[3072,384]{1,0:T(8,128)(2,1)} %bitcast.102, bf16[3072,384]{1,0:T(8,128)(2,1)} %bitcast.100, pred[]{:T(512)S(6)} %eq.52), kind=kOutput, calls=%fused_computation.98 | convolution fusion | flops 2437939200 | bytes 10223617 | tf_op jit(solution)/shard_map/dot_general | solution.py:55
  290.0 3.3 convolution_convert_fusion
  293.3 4.0 fusion.108
  297.3 6.8 %multiply_reduce_fusion.1 = (f32[12,512]{1,0:T(8,128)S(1)}, f32[12,512,512]{1,2,0:T(8,128)}) fusion(f32[12,512]{1,0:T(8,128)S(1)} %log_add_fusion.1, f32[12,512,512]{1,2,0:T(8,128)S(1)} %bitcast.407, pred[512,512]{0,1:T(8,128)(4,1)S(1)} %get-tuple-element.76, bf16[512,12,64]{0,2,1:T(8,128)(2,1)S(1)} %bitcast.468, bf16[512,12,64]{0,2,1:T(8,128)(2,1)S(1)} %bitcast.536), kind=kOutput, calls=%fused_computation.11 | convolution fusion | flops 418375680 | bytes 27049984 | tf_op jit(solution)/shard_map/qhd,khd->hqk/dot_general | solution.py:126
  304.2 7.3 %multiply_convert_fusion.1 = bf16[12,512,512]{1,2,0:T(8,128)(2,1)S(1)} fusion(f32[12,512,512]{1,2,0:T(8,128)} %get-tuple-element.90, f32[12,512]{1,0:T(8,128)S(1)} %get-tuple-element.89, f32[12,512]{1,0:T(8,128)S(1)} %log_add_fusion.1, f32[12,512,512]{1,2,0:T(8,128)S(1)} %bitcast.407, pred[512,512]{0,1:T(8,128)(4,1)S(1)} %get-tuple-element.76), kind=kLoop, calls=%fused_computation.10 | loop fusion | flops 18874368 | bytes 31768576 | tf_op jit(solution)/shard_map/convert_element_type | solution.py:130
  329.5 6.6 %fusion.45 = bf16[12,64,512]{2,1,0:T(8,128)(2,1)S(1)} fusion(bf16[512,12,64]{0,2,1:T(8,128)(2,1)S(1)} %bitcast.427, f32[12,512,512]{1,2,0:T(8,128)} %copy-done.1, f32[12,512]{1,0:T(8,128)S(1)} %log_add_fusion), kind=kOutput, calls=%fused_computation.116 | convolution fusion | flops 409337856 | bytes 14180352 | tf_op jit(solution)/shard_map/hqk,qhd->khd/dot_general | solution.py:137
  339.5 10.3 %multiply_reduce_fusion = (f32[12,512]{1,0:T(8,128)S(1)}, f32[12,512,512]{1,2,0:T(8,128)}) fusion(f32[12,512,512]{1,2,0:T(8,128)} %copy-done.1, f32[12,512]{1,0:T(8,128)S(1)} %log_add_fusion, bf16[512,12,64]{0,2,1:T(8,128)(2,1)S(1)} %bitcast.428, bf16[512,12,64]{0,2,1:T(8,128)(2,1)S(1)} %bitcast.466), kind=kOutput, calls=%fused_computation.8 | convolution fusion | flops 412084224 | bytes 26787840 | tf_op jit(solution)/shard_map/qhd,khd->hqk/dot_general | solution.py:126
  350.8 7.2 %multiply_convert_fusion = bf16[12,512,512]{1,2,0:T(8,128)(2,1)S(1)} fusion(f32[12,512,512]{1,2,0:T(8,128)} %get-tuple-element.93, f32[12,512,512]{1,2,0:T(8,128)S(1)} %bitcast.405, f32[12,512]{1,0:T(8,128)S(1)} %get-tuple-element.92, f32[12,512]{1,0:T(8,128)S(1)} %log_add_fusion), kind=kLoop, calls=%fused_computation.7 | loop fusion | flops 12582912 | bytes 31506432 | tf_op jit(solution)/shard_map/convert_element_type | solution.py:130
  373.6 3.7 convolution_add_fusion
  382.6 3.3 pad_maximum_fusion.2
  390.7 2.8 copy.136
  393.4 2.7 copy.135
  397.4 12.3 %fusion.55 = f32[32,12]{0,1:T(8,128)S(1)} fusion(bf16[12,512,512]{1,2,0:T(8,128)(2,1)} %copy-done.3, s32[512,512]{0,1:T(8,128)S(1)} %copy-done.19), kind=kOutput, calls=%fused_computation.154 | convolution fusion | flops 209715200 | bytes 7341568 | tf_op jit(solution)/shard_map/qkb,hqk->bh/dot_general | solution.py:141
  414.8 12.4 %collective-permute-done.33 = bf16[2,2,2,96,384]{4,3,2,1,0:T(8,128)(2,1)S(1)} collective-permute-done((bf16[2,2,2,96,384]{4,3,2,1,0:T(8,128)(2,1)S(1)}, bf16[2,2,2,96,384]{4,3,2,1,0:T(8,128)(2,1)S(1)}, u32[]{:S(2)}, u32[]{:S(2)}) %collective-permute-start.33) | collective-permute-done | bytes 589856 | tf_op jit(solution)/shard_map/ppermute | solution.py:164
  430.3 5.7 collective-permute-done.34
  436.1 4.5 collective-permute-start.35
  442.5 4.4 collective-permute-done.35
  465.1 20.2 %collective-permute-done.51 = bf16[2,2,2,192,384]{4,3,2,1,0:T(8,128)(2,1)S(1)} collective-permute-done((bf16[2,2,2,192,384]{4,3,2,1,0:T(8,128)(2,1)S(1)}, bf16[2,2,2,192,384]{4,3,2,1,0:T(8,128)(2,1)S(1)}, u32[]{:S(2)}, u32[]{:S(2)}) %collective-permute-start.51) | collective-permute-done | bytes 1179680 | tf_op jit(solution)/shard_map/ppermute | solution.py:164
  490.6 19.5 %collective-permute-done.39 = bf16[2,2,2,192,384]{4,3,2,1,0:T(8,128)(2,1)S(1)} collective-permute-done((bf16[2,2,2,192,384]{4,3,2,1,0:T(8,128)(2,1)S(1)}, bf16[2,2,2,192,384]{4,3,2,1,0:T(8,128)(2,1)S(1)}, u32[]{:S(2)}, u32[]{:S(2)}) %collective-permute-start.39) | collective-permute-done | bytes 1179680 | tf_op jit(solution)/shard_map/ppermute | solution.py:164
  512.8 2.9 collective-permute-start.47
  515.7 9.7 %collective-permute-done.40 = bf16[2,2,192,384]{3,2,1,0:T(8,128)(2,1)S(1)} collective-permute-done((bf16[2,2,192,384]{3,2,1,0:T(8,128)(2,1)S(1)}, bf16[2,2,192,384]{3,2,1,0:T(8,128)(2,1)S(1)}, u32[]{:S(2)}, u32[]{:S(2)}) %collective-permute-start.40) | collective-permute-done | bytes 589856 | tf_op jit(solution)/shard_map/ppermute | solution.py:164
  530.8 6.3 %collective-permute-done.41 = bf16[2,192,384]{2,1,0:T(8,128)(2,1)S(1)} collective-permute-done((bf16[2,192,384]{2,1,0:T(8,128)(2,1)S(1)}, bf16[2,192,384]{2,1,0:T(8,128)(2,1)S(1)}, u32[]{:S(2)}, u32[]{:S(2)}) %collective-permute-start.41) | collective-permute-done | bytes 294944 | tf_op jit(solution)/shard_map/ppermute | solution.py:164
  539.3 6.7 %collective-permute-done.42 = bf16[192,384]{1,0:T(8,128)(2,1)S(1)} collective-permute-done((bf16[192,384]{1,0:T(8,128)(2,1)S(1)}, bf16[192,384]{1,0:T(8,128)(2,1)S(1)}, u32[]{:S(2)}, u32[]{:S(2)}) %collective-permute-start.42) | collective-permute-done | bytes 147488 | tf_op jit(solution)/shard_map/ppermute | solution.py:164
  548.9 39.7 %all-reduce.1 = (f32[3,768]{1,0:T(4,128)S(1)}, f32[32,12]{0,1:T(8,128)}, f32[9,768]{1,0:T(8,128)S(1)}, f32[3072]{0:T(1024)S(1)}) all-reduce(f32[3,768]{1,0:T(4,128)S(1)} %pad_maximum_fusion.17, f32[32,12]{0,1:T(8,128)S(1)} %fusion.55, f32[9,768]{1,0:T(8,128)S(1)} %pad_maximum_fusion.16, ...), channel_id=1, replica_groups=mesh['wide'=8,'narrow'=4] {'wide','narrow'}, use_global_device_ids=true, to_apply=%region_15.16 | all-reduce | flops 12672 | bytes 101376 | tf_op jit(solution)/shard_map/psum | solution.py:392
  (503 shorter events, 197.1 us)
Async XLA Ops:
  5.2 11.2 %collective-permute-start = (bf16[392,384]{1,0:T(8,128)(2,1)}, bf16[392,384]{1,0:T(8,128)(2,1)}, u32[]{:S(2)}, u32[]{:S(2)}) collective-permute-start(bf16[392,384]{1,0:T(8,128)(2,1)} %pad_maximum_fusion.14), channel_id=1, source_target_pairs={{0,1},{1,0},{2,3},{3,2},{4,5},{5,4},{6,7},{7,6},{8,9},{9,8},{10,11... | collective-permute-start | bytes 903176 | tf_op jit(solution)/shard_map/ppermute | solution.py:164
  19.3 8.9 %collective-permute-start.5 = (bf16[96,384]{1,0:T(8,128)(2,1)S(1)}, bf16[96,384]{1,0:T(8,128)(2,1)S(1)}, u32[]{:S(2)}, u32[]{:S(2)}) collective-permute-start(bf16[96,384]{1,0:T(8,128)(2,1)S(1)} %bitcast.531), channel_id=1, source_target_pairs={{0,2},{1,3},{2,0},{3,1},{4,6},{5,7},{6,4},{7,5},{8,10},{9,11},{10,... | collective-permute-start | bytes 221192 | tf_op jit(solution)/shard_map/ppermute | solution.py:164
  21.8 24.4 %collective-permute-start.11 = (bf16[192,384]{1,0:T(8,128)(2,1)S(1)}, bf16[192,384]{1,0:T(8,128)(2,1)S(1)}, u32[]{:S(2)}, u32[]{:S(2)}) collective-permute-start(bf16[192,384]{1,0:T(8,128)(2,1)S(1)} %bitcast.491), channel_id=1, source_target_pairs={{0,16},{1,17},{2,18},{3,19},{4,20},{5,21},{6,22},{7,23},{8,24},{9,... | collective-permute-start | bytes 442376 | tf_op jit(solution)/shard_map/ppermute | solution.py:164
  24.4 21.5 %collective-permute-start.16 = (bf16[48,1536]{1,0:T(8,128)(2,1)S(1)}, bf16[48,1536]{1,0:T(8,128)(2,1)S(1)}, u32[]{:S(2)}, u32[]{:S(2)}) collective-permute-start(bf16[48,1536]{1,0:T(8,128)(2,1)S(1)} %maximum_select_fusion.43), channel_id=1, source_target_pairs={{0,2},{1,3},{2,0},{3,1},{4,6},{5,7},{6,4},{7,5},{8,10},{9,11},{10,... | collective-permute-start | bytes 442376 | tf_op jit(solution)/shard_map/ppermute | solution.py:164
  25.0 21.0 %collective-permute-start.21 = (bf16[192,384]{1,0:T(8,128)(2,1)S(1)}, bf16[192,384]{1,0:T(8,128)(2,1)S(1)}, u32[]{:S(2)}, u32[]{:S(2)}) collective-permute-start(bf16[192,384]{1,0:T(8,128)(2,1)S(1)} %maximum_select_fusion.45), channel_id=1, source_target_pairs={{0,16},{1,17},{2,18},{3,19},{4,20},{5,21},{6,22},{7,23},{8,24},{9,... | collective-permute-start | bytes 442376 | tf_op jit(solution)/shard_map/ppermute | solution.py:164
  25.1 20.5 %collective-permute-start.1 = (bf16[112,384]{1,0:T(8,128)(2,1)S(1)}, bf16[112,384]{1,0:T(8,128)(2,1)S(1)}, u32[]{:S(2)}, u32[]{:S(2)}) collective-permute-start(bf16[112,384]{1,0:T(8,128)(2,1)S(1)} %get-tuple-element.72), channel_id=1, source_target_pairs={{0,16},{1,17},{2,18},{3,19},{4,20},{5,21},{6,22},{7,23},{8,24},{9,... | collective-permute-start | bytes 258056 | tf_op jit(solution)/shard_map/ppermute | solution.py:164
  28.2 23.6 %collective-permute-start.6 = (bf16[2,96,384]{2,1,0:T(8,128)(2,1)S(1)}, bf16[2,96,384]{2,1,0:T(8,128)(2,1)S(1)}, u32[]{:S(2)}, u32[]{:S(2)}) collective-permute-start(bf16[2,96,384]{2,1,0:T(8,128)(2,1)S(1)} %maximum_select_fusion.41), channel_id=1, source_target_pairs={{0,16},{1,17},{2,18},{3,19},{4,20},{5,21},{6,22},{7,23},{8,24},{9,... | collective-permute-start | bytes 442376 | tf_op jit(solution)/shard_map/ppermute | solution.py:164
  45.7 13.7 %collective-permute-start.2 = (bf16[2,112,384]{2,1,0:T(8,128)(2,1)S(1)}, bf16[2,112,384]{2,1,0:T(8,128)(2,1)S(1)}, u32[]{:S(2)}, u32[]{:S(2)}) collective-permute-start(bf16[2,112,384]{2,1,0:T(8,128)(2,1)S(1)} %maximum_select_fusion.39), channel_id=1, source_target_pairs={{0,8},{1,9},{2,10},{3,11},{4,12},{5,13},{6,14},{7,15},{8,0},{9,1},... | collective-permute-start | bytes 516104 | tf_op jit(solution)/shard_map/ppermute | solution.py:164
  46.2 27.7 %collective-permute-start.12 = (bf16[2,192,384]{2,1,0:T(8,128)(2,1)S(1)}, bf16[2,192,384]{2,1,0:T(8,128)(2,1)S(1)}, u32[]{:S(2)}, u32[]{:S(2)}) collective-permute-start(bf16[2,192,384]{2,1,0:T(8,128)(2,1)S(1)} %maximum_select_fusion.30), channel_id=1, source_target_pairs={{0,8},{1,9},{2,10},{3,11},{4,12},{5,13},{6,14},{7,15},{8,0},{9,1},... | collective-permute-start | bytes 884744 | tf_op jit(solution)/shard_map/ppermute | solution.py:164
  48.3 25.9 %collective-permute-start.17 = (bf16[2,48,1536]{2,1,0:T(8,128)(2,1)S(1)}, bf16[2,48,1536]{2,1,0:T(8,128)(2,1)S(1)}, u32[]{:S(2)}, u32[]{:S(2)}) collective-permute-start(bf16[2,48,1536]{2,1,0:T(8,128)(2,1)S(1)} %maximum_select_fusion.32), channel_id=1, source_target_pairs={{0,16},{1,17},{2,18},{3,19},{4,20},{5,21},{6,22},{7,23},{8,24},{9,... | collective-permute-start | bytes 884744 | tf_op jit(solution)/shard_map/ppermute | solution.py:164
  49.8 22.3 %collective-permute-start.22 = (bf16[2,192,384]{2,1,0:T(8,128)(2,1)S(1)}, bf16[2,192,384]{2,1,0:T(8,128)(2,1)S(1)}, u32[]{:S(2)}, u32[]{:S(2)}) collective-permute-start(bf16[2,192,384]{2,1,0:T(8,128)(2,1)S(1)} %maximum_select_fusion.34), channel_id=1, source_target_pairs={{0,8},{1,9},{2,10},{3,11},{4,12},{5,13},{6,14},{7,15},{8,0},{9,1},... | collective-permute-start | bytes 884744 | tf_op jit(solution)/shard_map/ppermute | solution.py:164
  51.9 26.5 %collective-permute-start.7 = (bf16[2,2,96,384]{3,2,1,0:T(8,128)(2,1)S(1)}, bf16[2,2,96,384]{3,2,1,0:T(8,128)(2,1)S(1)}, u32[]{:S(2)}, u32[]{:S(2)}) collective-permute-start(bf16[2,2,96,384]{3,2,1,0:T(8,128)(2,1)S(1)} %maximum_select_fusion.29), channel_id=1, source_target_pairs={{0,8},{1,9},{2,10},{3,11},{4,12},{5,13},{6,14},{7,15},{8,0},{9,1},... | collective-permute-start | bytes 884744 | tf_op jit(solution)/shard_map/ppermute | solution.py:164
  59.5 20.8 %collective-permute-start.3 = (bf16[2,2,112,384]{3,2,1,0:T(8,128)(2,1)S(1)}, bf16[2,2,112,384]{3,2,1,0:T(8,128)(2,1)S(1)}, u32[]{:S(2)}, u32[]{:S(2)}) collective-permute-start(bf16[2,2,112,384]{3,2,1,0:T(8,128)(2,1)S(1)} %maximum_select_fusion.26), channel_id=1, source_target_pairs={{0,4},{1,5},{2,6},{3,7},{4,0},{5,1},{6,2},{7,3},{8,12},{9,13},{10,... | collective-permute-start | bytes 1032200 | tf_op jit(solution)/shard_map/ppermute | solution.py:164
  72.4 33.5 %collective-permute-start.23 = (bf16[2,2,192,384]{3,2,0,1:T(8,128)(2,1)S(1)}, bf16[2,2,192,384]{3,2,0,1:T(8,128)(2,1)S(1)}, u32[]{:S(2)}, u32[]{:S(2)}) collective-permute-start(bf16[2,2,192,384]{3,2,0,1:T(8,128)(2,1)S(1)} %maximum_select_fusion.25), channel_id=1, source_target_pairs={{0,4},{1,5},{2,6},{3,7},{4,0},{5,1},{6,2},{7,3},{8,12},{9,13},{10,... | collective-permute-start | bytes 1769480 | tf_op jit(solution)/shard_map/ppermute | solution.py:164
  74.3 28.5 %collective-permute-start.18 = (bf16[2,2,48,1536]{3,2,1,0:T(8,128)(2,1)S(1)}, bf16[2,2,48,1536]{3,2,1,0:T(8,128)(2,1)S(1)}, u32[]{:S(2)}, u32[]{:S(2)}) collective-permute-start(bf16[2,2,48,1536]{3,2,1,0:T(8,128)(2,1)S(1)} %maximum_select_fusion.23), channel_id=1, source_target_pairs={{0,8},{1,9},{2,10},{3,11},{4,12},{5,13},{6,14},{7,15},{8,0},{9,1},... | collective-permute-start | bytes 1769480 | tf_op jit(solution)/shard_map/ppermute | solution.py:164
  74.6 26.7 %collective-permute-start.13 = (bf16[2,2,192,384]{3,2,0,1:T(8,128)(2,1)S(1)}, bf16[2,2,192,384]{3,2,0,1:T(8,128)(2,1)S(1)}, u32[]{:S(2)}, u32[]{:S(2)}) collective-permute-start(bf16[2,2,192,384]{3,2,0,1:T(8,128)(2,1)S(1)} %maximum_select_fusion.21), channel_id=1, source_target_pairs={{0,4},{1,5},{2,6},{3,7},{4,0},{5,1},{6,2},{7,3},{8,12},{9,13},{10,... | collective-permute-start | bytes 1769480 | tf_op jit(solution)/shard_map/ppermute | solution.py:164
  78.5 35.5 %collective-permute-start.8 = (bf16[2,2,2,96,384]{4,3,2,1,0:T(8,128)(2,1)S(1)}, bf16[2,2,2,96,384]{4,3,2,1,0:T(8,128)(2,1)S(1)}, u32[]{:S(2)}, u32[]{:S(2)}) collective-permute-start(bf16[2,2,2,96,384]{4,3,2,1,0:T(8,128)(2,1)S(1)} %maximum_select_fusion.19), channel_id=1, source_target_pairs={{0,4},{1,5},{2,6},{3,7},{4,0},{5,1},{6,2},{7,3},{8,12},{9,13},{10,... | collective-permute-start | bytes 1769480 | tf_op jit(solution)/shard_map/ppermute | solution.py:164
  80.4 36.1 %collective-permute-start.4 = (bf16[2,2,2,112,384]{4,3,2,1,0:T(8,128)(2,1)S(1)}, bf16[2,2,2,112,384]{4,3,2,1,0:T(8,128)(2,1)S(1)}, u32[]{:S(2)}, u32[]{:S(2)}) collective-permute-start(bf16[2,2,2,112,384]{4,3,2,1,0:T(8,128)(2,1)S(1)} %maximum_select_fusion.18), channel_id=1, source_target_pairs={{0,2},{1,3},{2,0},{3,1},{4,6},{5,7},{6,4},{7,5},{8,10},{9,11},{10,... | collective-permute-start | bytes 2064392 | tf_op jit(solution)/shard_map/ppermute | solution.py:164
  102.6 29.2 %collective-permute-start.14 = (bf16[2,2,2,192,384]{4,3,0,1,2:T(8,128)(2,1)}, bf16[2,2,2,192,384]{4,3,0,1,2:T(8,128)(2,1)}, u32[]{:S(2)}, u32[]{:S(2)}) collective-permute-start(bf16[2,2,2,192,384]{4,3,0,1,2:T(8,128)(2,1)} %maximum_select_fusion.10), channel_id=1, source_target_pairs={{0,2},{1,3},{2,0},{3,1},{4,6},{5,7},{6,4},{7,5},{8,10},{9,11},{10,... | collective-permute-start | bytes 3538952 | tf_op jit(solution)/shard_map/ppermute | solution.py:164
  104.0 49.0 %collective-permute-start.19 = (bf16[2,2,2,48,1536]{4,3,2,1,0:T(8,128)(2,1)}, bf16[2,2,2,48,1536]{4,3,2,1,0:T(8,128)(2,1)}, u32[]{:S(2)}, u32[]{:S(2)}) collective-permute-start(bf16[2,2,2,48,1536]{4,3,2,1,0:T(8,128)(2,1)} %maximum_select_fusion.11), channel_id=1, source_target_pairs={{0,4},{1,5},{2,6},{3,7},{4,0},{5,1},{6,2},{7,3},{8,12},{9,13},{10,... | collective-permute-start | bytes 3538952 | tf_op jit(solution)/shard_map/ppermute | solution.py:164
  107.2 42.1 %collective-permute-start.24 = (bf16[2,2,2,192,384]{4,3,0,1,2:T(8,128)(2,1)}, bf16[2,2,2,192,384]{4,3,0,1,2:T(8,128)(2,1)}, u32[]{:S(2)}, u32[]{:S(2)}) collective-permute-start(bf16[2,2,2,192,384]{4,3,0,1,2:T(8,128)(2,1)} %maximum_select_fusion.13), channel_id=1, source_target_pairs={{0,2},{1,3},{2,0},{3,1},{4,6},{5,7},{6,4},{7,5},{8,10},{9,11},{10,... | collective-permute-start | bytes 3538952 | tf_op jit(solution)/shard_map/ppermute | solution.py:164
  115.2 41.7 %collective-permute-start.9 = (bf16[16,96,384]{2,1,0:T(8,128)(2,1)}, bf16[16,96,384]{2,1,0:T(8,128)(2,1)}, u32[]{:S(2)}, u32[]{:S(2)}) collective-permute-start(bf16[16,96,384]{2,1,0:T(8,128)(2,1)} %bitcast.30), channel_id=1, source_target_pairs={{0,1},{1,0},{2,3},{3,2},{4,5},{5,4},{6,7},{7,6},{8,9},{9,8},{10,11... | collective-permute-start | bytes 3538952 | tf_op jit(solution)/shard_map/ppermute | solution.py:164
  116.7 49.7 %collective-permute-start.10 = (bf16[16,112,384]{2,1,0:T(8,128)(2,1)S(1)}, bf16[16,112,384]{2,1,0:T(8,128)(2,1)}, u32[]{:S(2)}, u32[]{:S(2)}) collective-permute-start(bf16[16,112,384]{2,1,0:T(8,128)(2,1)S(1)} %bitcast.440), channel_id=1, source_target_pairs={{0,1},{1,0},{2,3},{3,2},{4,5},{5,4},{6,7},{7,6},{8,9},{9,8},{10,11... | collective-permute-start | bytes 4128776 | tf_op jit(solution)/shard_map/ppermute | solution.py:164
  156.4 70.1 %collective-permute-start.20 = (bf16[16,48,1536]{2,1,0:T(8,128)(2,1)}, bf16[16,48,1536]{2,1,0:T(8,128)(2,1)}, u32[]{:S(2)}, u32[]{:S(2)}) collective-permute-start(bf16[16,48,1536]{2,1,0:T(8,128)(2,1)} %bitcast.86), channel_id=1, source_target_pairs={{0,1},{1,0},{2,3},{3,2},{4,5},{5,4},{6,7},{7,6},{8,9},{9,8},{10,11... | collective-permute-start | bytes 7077896 | tf_op jit(solution)/shard_map/ppermute | solution.py:164
  156.4 79.9 %collective-permute-start.25 = (bf16[16,192,384]{2,1,0:T(8,128)(2,1)}, bf16[16,192,384]{2,1,0:T(8,128)(2,1)}, u32[]{:S(2)}, u32[]{:S(2)}) collective-permute-start(bf16[16,192,384]{2,1,0:T(8,128)(2,1)} %bitcast.101), channel_id=1, source_target_pairs={{0,1},{1,0},{2,3},{3,2},{4,5},{5,4},{6,7},{7,6},{8,9},{9,8},{10,11... | collective-permute-start | bytes 7077896 | tf_op jit(solution)/shard_map/ppermute | solution.py:164
  156.9 45.1 %collective-permute-start.15 = (bf16[16,192,384]{2,1,0:T(8,128)(2,1)}, bf16[16,192,384]{2,1,0:T(8,128)(2,1)}, u32[]{:S(2)}, u32[]{:S(2)}) collective-permute-start(bf16[16,192,384]{2,1,0:T(8,128)(2,1)} %bitcast.60), channel_id=1, source_target_pairs={{0,1},{1,0},{2,3},{3,2},{4,5},{5,4},{6,7},{7,6},{8,9},{9,8},{10,11... | collective-permute-start | bytes 7077896 | tf_op jit(solution)/shard_map/ppermute | solution.py:164
  373.0 80.8 %collective-permute-start.50 = (bf16[16,192,384]{2,1,0:T(8,128)(2,1)}, bf16[16,192,384]{2,1,0:T(8,128)(2,1)}, u32[]{:S(2)}, u32[]{:S(2)}) collective-permute-start(bf16[16,192,384]{2,1,0:T(8,128)(2,1)} %bitcast.567), channel_id=1, source_target_pairs={{0,1},{1,0},{2,3},{3,2},{4,5},{5,4},{6,7},{7,6},{8,9},{9,8},{10,11... | collective-permute-start | bytes 7077896 | tf_op jit(solution)/shard_map/ppermute | solution.py:164
  373.5 84.5 %collective-permute-start.44 = (bf16[16,48,1536]{2,1,0:T(8,128)(2,1)}, bf16[16,48,1536]{2,1,0:T(8,128)(2,1)}, u32[]{:S(2)}, u32[]{:S(2)}) collective-permute-start(bf16[16,48,1536]{2,1,0:T(8,128)(2,1)} %bitcast.566), channel_id=1, source_target_pairs={{0,1},{1,0},{2,3},{3,2},{4,5},{5,4},{6,7},{7,6},{8,9},{9,8},{10,11... | collective-permute-start | bytes 7077896 | tf_op jit(solution)/shard_map/ppermute | solution.py:164
  382.1 27.6 %collective-permute-start.32 = (bf16[16,96,384]{2,1,0:T(8,128)(2,1)}, bf16[16,96,384]{2,1,0:T(8,128)(2,1)}, u32[]{:S(2)}, u32[]{:S(2)}) collective-permute-start(bf16[16,96,384]{2,1,0:T(8,128)(2,1)} %pad_maximum_fusion.6), channel_id=1, source_target_pairs={{0,1},{1,0},{2,3},{3,2},{4,5},{5,4},{6,7},{7,6},{8,9},{9,8},{10,11... | collective-permute-start | bytes 3538952 | tf_op jit(solution)/shard_map/ppermute | solution.py:164
  385.9 76.5 %collective-permute-start.38 = (bf16[16,192,384]{2,1,0:T(8,128)(2,1)}, bf16[16,192,384]{2,1,0:T(8,128)(2,1)}, u32[]{:S(2)}, u32[]{:S(2)}) collective-permute-start(bf16[16,192,384]{2,1,0:T(8,128)(2,1)} %pad_maximum_fusion.2), channel_id=1, source_target_pairs={{0,1},{1,0},{2,3},{3,2},{4,5},{5,4},{6,7},{7,6},{8,9},{9,8},{10,11... | collective-permute-start | bytes 7077896 | tf_op jit(solution)/shard_map/ppermute | solution.py:164
  396.1 16.9 %collective-permute-start.26 = (bf16[16,96,384]{2,1,0:T(8,128)(2,1)}, bf16[16,96,384]{2,1,0:T(8,128)(2,1)S(1)}, u32[]{:S(2)}, u32[]{:S(2)}) collective-permute-start(bf16[16,96,384]{2,1,0:T(8,128)(2,1)} %pad_maximum_fusion.5), channel_id=1, source_target_pairs={{0,1},{1,0},{2,3},{3,2},{4,5},{5,4},{6,7},{7,6},{8,9},{9,8},{10,11... | collective-permute-start | bytes 3538952 | tf_op jit(solution)/shard_map/ppermute | solution.py:164
  411.4 15.7 %collective-permute-start.33 = (bf16[2,2,2,96,384]{4,3,2,1,0:T(8,128)(2,1)S(1)}, bf16[2,2,2,96,384]{4,3,2,1,0:T(8,128)(2,1)S(1)}, u32[]{:S(2)}, u32[]{:S(2)}) collective-permute-start(bf16[2,2,2,96,384]{4,3,2,1,0:T(8,128)(2,1)S(1)} %fusion.97), channel_id=1, source_target_pairs={{0,4},{1,5},{2,6},{3,7},{4,0},{5,1},{6,2},{7,3},{8,12},{9,13},{10,... | collective-permute-start | bytes 1769480 | tf_op jit(solution)/shard_map/ppermute | solution.py:164
  413.4 15.5 %collective-permute-start.27 = (bf16[2,2,2,96,384]{4,3,2,1,0:T(8,128)(2,1)S(1)}, bf16[2,2,2,96,384]{4,3,2,1,0:T(8,128)(2,1)S(1)}, u32[]{:S(2)}, u32[]{:S(2)}) collective-permute-start(bf16[2,2,2,96,384]{4,3,2,1,0:T(8,128)(2,1)S(1)} %fusion.96), channel_id=1, source_target_pairs={{0,2},{1,3},{2,0},{3,1},{4,6},{5,7},{6,4},{7,5},{8,10},{9,11},{10,... | collective-permute-start | bytes 1769480 | tf_op jit(solution)/shard_map/ppermute | solution.py:164
  429.0 11.6 %collective-permute-start.28 = (bf16[2,2,96,384]{3,2,1,0:T(8,128)(2,1)S(1)}, bf16[2,2,96,384]{3,2,1,0:T(8,128)(2,1)S(1)}, u32[]{:S(2)}, u32[]{:S(2)}) collective-permute-start(bf16[2,2,96,384]{3,2,1,0:T(8,128)(2,1)S(1)} %fusion.130), channel_id=1, source_target_pairs={{0,4},{1,5},{2,6},{3,7},{4,0},{5,1},{6,2},{7,3},{8,12},{9,13},{10,... | collective-permute-start | bytes 884744 | tf_op jit(solution)/shard_map/ppermute | solution.py:164
  436.1 10.8 %collective-permute-start.35 = (bf16[2,96,384]{2,1,0:T(8,128)(2,1)S(1)}, bf16[2,96,384]{2,1,0:T(8,128)(2,1)S(1)}, u32[]{:S(2)}, u32[]{:S(2)}) collective-permute-start(bf16[2,96,384]{2,1,0:T(8,128)(2,1)S(1)} %fusion.137), channel_id=1, source_target_pairs={{0,16},{1,17},{2,18},{3,19},{4,20},{5,21},{6,22},{7,23},{8,24},{9,... | collective-permute-start | bytes 442376 | tf_op jit(solution)/shard_map/ppermute | solution.py:164
  451.4 13.6 %collective-permute-start.37 = (f32[2,24,384]{2,1,0:T(8,128)S(1)}, f32[2,24,384]{2,1,0:T(8,128)S(1)}, u32[]{:S(2)}, u32[]{:S(2)}) collective-permute-start(f32[2,24,384]{2,1,0:T(8,128)S(1)} %get-tuple-element.65), channel_id=1, source_target_pairs={{0,1},{1,0},{2,3},{3,2},{4,5},{5,4},{6,7},{7,6},{8,9},{9,8},{10,11... | collective-permute-start | bytes 221192 | tf_op jit(solution)/shard_map/ppermute | solution.py:164
  453.7 11.3 %collective-permute-start.31 = (f32[2,24,384]{2,1,0:T(8,128)S(1)}, f32[2,24,384]{2,1,0:T(8,128)S(1)}, u32[]{:S(2)}, u32[]{:S(2)}) collective-permute-start(f32[2,24,384]{2,1,0:T(8,128)S(1)} %get-tuple-element.63), channel_id=1, source_target_pairs={{0,1},{1,0},{2,3},{3,2},{4,5},{5,4},{6,7},{7,6},{8,9},{9,8},{10,11... | collective-permute-start | bytes 221192 | tf_op jit(solution)/shard_map/ppermute | solution.py:164
  456.5 28.8 %collective-permute-start.51 = (bf16[2,2,2,192,384]{4,3,2,1,0:T(8,128)(2,1)S(1)}, bf16[2,2,2,192,384]{4,3,2,1,0:T(8,128)(2,1)S(1)}, u32[]{:S(2)}, u32[]{:S(2)}) collective-permute-start(bf16[2,2,2,192,384]{4,3,2,1,0:T(8,128)(2,1)S(1)} %fusion.54), channel_id=1, source_target_pairs={{0,2},{1,3},{2,0},{3,1},{4,6},{5,7},{6,4},{7,5},{8,10},{9,11},{10,... | collective-permute-start | bytes 3538952 | tf_op jit(solution)/shard_map/ppermute | solution.py:164
  460.8 28.9 %collective-permute-start.45 = (bf16[2,2,2,48,1536]{4,3,2,1,0:T(8,128)(2,1)S(1)}, bf16[2,2,2,48,1536]{4,3,2,1,0:T(8,128)(2,1)S(1)}, u32[]{:S(2)}, u32[]{:S(2)}) collective-permute-start(bf16[2,2,2,48,1536]{4,3,2,1,0:T(8,128)(2,1)S(1)} %fusion.53), channel_id=1, source_target_pairs={{0,4},{1,5},{2,6},{3,7},{4,0},{5,1},{6,2},{7,3},{8,12},{9,13},{10,... | collective-permute-start | bytes 3538952 | tf_op jit(solution)/shard_map/ppermute | solution.py:164
  464.4 45.7 %collective-permute-start.39 = (bf16[2,2,2,192,384]{4,3,2,1,0:T(8,128)(2,1)S(1)}, bf16[2,2,2,192,384]{4,3,2,1,0:T(8,128)(2,1)S(1)}, u32[]{:S(2)}, u32[]{:S(2)}) collective-permute-start(bf16[2,2,2,192,384]{4,3,2,1,0:T(8,128)(2,1)S(1)} %fusion.52), channel_id=1, source_target_pairs={{0,2},{1,3},{2,0},{3,1},{4,6},{5,7},{6,4},{7,5},{8,10},{9,11},{10,... | collective-permute-start | bytes 3538952 | tf_op jit(solution)/shard_map/ppermute | solution.py:164
  485.6 26.4 %collective-permute-start.52 = (bf16[2,2,192,384]{3,2,1,0:T(8,128)(2,1)S(1)}, bf16[2,2,192,384]{3,2,1,0:T(8,128)(2,1)S(1)}, u32[]{:S(2)}, u32[]{:S(2)}) collective-permute-start(bf16[2,2,192,384]{3,2,1,0:T(8,128)(2,1)S(1)} %fusion.100), channel_id=1, source_target_pairs={{0,4},{1,5},{2,6},{3,7},{4,0},{5,1},{6,2},{7,3},{8,12},{9,13},{10,... | collective-permute-start | bytes 1769480 | tf_op jit(solution)/shard_map/ppermute | solution.py:164
  490.1 22.5 %collective-permute-start.46 = (bf16[2,2,48,1536]{3,2,1,0:T(8,128)(2,1)S(1)}, bf16[2,2,48,1536]{3,2,1,0:T(8,128)(2,1)S(1)}, u32[]{:S(2)}, u32[]{:S(2)}) collective-permute-start(bf16[2,2,48,1536]{3,2,1,0:T(8,128)(2,1)S(1)} %fusion.99), channel_id=1, source_target_pairs={{0,8},{1,9},{2,10},{3,11},{4,12},{5,13},{6,14},{7,15},{8,0},{9,1},... | collective-permute-start | bytes 1769480 | tf_op jit(solution)/shard_map/ppermute | solution.py:164
  510.4 15.0 %collective-permute-start.40 = (bf16[2,2,192,384]{3,2,1,0:T(8,128)(2,1)S(1)}, bf16[2,2,192,384]{3,2,1,0:T(8,128)(2,1)S(1)}, u32[]{:S(2)}, u32[]{:S(2)}) collective-permute-start(bf16[2,2,192,384]{3,2,1,0:T(8,128)(2,1)S(1)} %fusion.98), channel_id=1, source_target_pairs={{0,4},{1,5},{2,6},{3,7},{4,0},{5,1},{6,2},{7,3},{8,12},{9,13},{10,... | collective-permute-start | bytes 1769480 | tf_op jit(solution)/shard_map/ppermute | solution.py:164
  512.2 14.2 %collective-permute-start.53 = (bf16[2,192,384]{2,1,0:T(8,128)(2,1)S(1)}, bf16[2,192,384]{2,1,0:T(8,128)(2,1)S(1)}, u32[]{:S(2)}, u32[]{:S(2)}) collective-permute-start(bf16[2,192,384]{2,1,0:T(8,128)(2,1)S(1)} %fusion.134), channel_id=1, source_target_pairs={{0,8},{1,9},{2,10},{3,11},{4,12},{5,13},{6,14},{7,15},{8,0},{9,1},... | collective-permute-start | bytes 884744 | tf_op jit(solution)/shard_map/ppermute | solution.py:164
  512.8 16.3 %collective-permute-start.47 = (bf16[2,48,1536]{2,1,0:T(8,128)(2,1)S(1)}, bf16[2,48,1536]{2,1,0:T(8,128)(2,1)S(1)}, u32[]{:S(2)}, u32[]{:S(2)}) collective-permute-start(bf16[2,48,1536]{2,1,0:T(8,128)(2,1)S(1)} %fusion.133), channel_id=1, source_target_pairs={{0,16},{1,17},{2,18},{3,19},{4,20},{5,21},{6,22},{7,23},{8,24},{9,... | collective-permute-start | bytes 884744 | tf_op jit(solution)/shard_map/ppermute | solution.py:164
  525.6 11.4 %collective-permute-start.41 = (bf16[2,192,384]{2,1,0:T(8,128)(2,1)S(1)}, bf16[2,192,384]{2,1,0:T(8,128)(2,1)S(1)}, u32[]{:S(2)}, u32[]{:S(2)}) collective-permute-start(bf16[2,192,384]{2,1,0:T(8,128)(2,1)S(1)} %fusion.132), channel_id=1, source_target_pairs={{0,8},{1,9},{2,10},{3,11},{4,12},{5,13},{6,14},{7,15},{8,0},{9,1},... | collective-permute-start | bytes 884744 | tf_op jit(solution)/shard_map/ppermute | solution.py:164
  526.5 12.0 %collective-permute-start.54 = (bf16[192,384]{1,0:T(8,128)(2,1)S(1)}, bf16[192,384]{1,0:T(8,128)(2,1)S(1)}, u32[]{:S(2)}, u32[]{:S(2)}) collective-permute-start(bf16[192,384]{1,0:T(8,128)(2,1)S(1)} %fusion.140), channel_id=1, source_target_pairs={{0,16},{1,17},{2,18},{3,19},{4,20},{5,21},{6,22},{7,23},{8,24},{9,... | collective-permute-start | bytes 442376 | tf_op jit(solution)/shard_map/ppermute | solution.py:164
  529.2 9.5 %collective-permute-start.48 = (bf16[48,1536]{1,0:T(8,128)(2,1)S(1)}, bf16[48,1536]{1,0:T(8,128)(2,1)S(1)}, u32[]{:S(2)}, u32[]{:S(2)}) collective-permute-start(bf16[48,1536]{1,0:T(8,128)(2,1)S(1)} %fusion.139), channel_id=1, source_target_pairs={{0,2},{1,3},{2,0},{3,1},{4,6},{5,7},{6,4},{7,5},{8,10},{9,11},{10,... | collective-permute-start | bytes 442376 | tf_op jit(solution)/shard_map/ppermute | solution.py:164
  (104 other events, 1208.5 us)

commit v2 on v0

v2 whole, which is shorter than its diff:
```python
import functools
import math

import jax
import jax.numpy as jnp
from jax import lax
from jax.experimental import pallas as pl
from jax.experimental.pallas import tpu as pltpu
from jax.sharding import PartitionSpec as P

D = 768
HEADS = 12
HEAD = 64
FF = 3072
BUCKETS = 32
MAXDIST = 128


EPSILON = 1e-06
DECAY = 0.8
NEGATIVE = -1e30


def thresholds():
    exact_count = BUCKETS // 2
    limits = list(range(1, exact_count + 1))
    for bucket_level in range(exact_count + 1, BUCKETS):
        limits.append(
            int(
                math.ceil(
                    exact_count
                    * (MAXDIST / exact_count) ** ((bucket_level - exact_count) / exact_count)
                )
            )
        )
    return limits


def bucket_table(distance, number_type):
    level_count = jnp.zeros(distance.shape, jnp.int32)
    for threshold in thresholds():
        level_count = level_count + (distance >= threshold).astype(jnp.int32)
    return (level_count[..., None] == jnp.arange(BUCKETS, dtype=jnp.int32)).astype(number_type)


def rms_norm(hidden, gain_row):
    return (
        hidden * lax.rsqrt(jnp.mean(hidden * hidden, axis=-1, keepdims=True) + EPSILON) * gain_row
    )


def project(left_side, right_side):
    return jnp.dot(left_side, right_side, preferred_element_type=jnp.float32)


def project_back(gradient, right_side):
    return lax.dot_general(
        gradient, right_side, (((1,), (1,)), ((), ())), preferred_element_type=jnp.float32
    )


def weight_grad(left_side, gradient):
    return lax.dot_general(
        left_side, gradient, (((0,), (0,)), ((), ())), preferred_element_type=jnp.float32
    )


LANES = 128
GROUP = LANES // HEAD
CUT = 256
VMEM_BYTES = 56 * 1024 * 1024
COST = pl.CostEstimate(flops=1000, bytes_accessed=1000, transcendentals=0)

NT = (((1,), (1,)), ((), ()))
TN = (((0,), (0,)), ((), ()))


def dot(left, right, dims=(((1,), (0,)), ((), ()))):
    return lax.dot_general(left, right, dims, preferred_element_type=jnp.float32)


def spans(rows, causal):
    return [(at, at + CUT if causal else rows) for at in range(0, rows, CUT)]


def lane_mask(head):
    lanes = lax.broadcasted_iota(jnp.int32, (1, LANES), 1)
    return ((lanes // HEAD) == head).astype(jnp.float32)


def only_head(block, head, scale):
    return (block.astype(jnp.float32) * (lane_mask(head) * scale)).astype(jnp.bfloat16)


def near_bias(line_ref, head):
    line = jnp.broadcast_to(line_ref[0, head : head + 1], (LANES, 2 * LANES))
    return pltpu.roll(line, 0, 1, stride=1, stride_axis=0)


def add_bias(scores, bias, at):
    columns = []
    for first in range(0, CUT, LANES):
        rows = []
        for key in range(0, scores.shape[0], LANES):
            apart = at + first - key
            block = scores[key : key + LANES, first : first + LANES]
            if apart >= 2 * LANES:
                block = block + bias[:1, 2 * LANES - 1 :]
            elif apart >= 0:
                block = block + bias[:, apart : apart + LANES]
            rows.append(block)
        columns.append(jnp.concatenate(rows, axis=0))
    return jnp.concatenate(columns, axis=1)


def attend_kernel(causal, q_ref, k_ref, v_ref, mask_ref, line_ref, probs_ref, out_ref):
    rows = q_ref.shape[0]
    biases = [near_bias(line_ref, head) for head in range(GROUP)] if causal else None
    for at, depth in spans(rows, causal):
        keys, values = k_ref[:depth], v_ref[:depth]
        total = jnp.zeros((CUT, LANES), jnp.float32)
        for head in range(GROUP):
            query = only_head(q_ref[at : at + CUT], head, HEAD**-0.5)
            scores = dot(keys, query, NT)
            if causal:
                scores = add_bias(scores, biases[head], at)
            scores = scores + mask_ref[:depth, at : at + CUT]
            weights = jnp.exp(scores - jnp.max(scores, axis=0, keepdims=True))
            weights = weights * (1.0 / jnp.sum(weights, axis=0, keepdims=True))
            low = weights.astype(jnp.bfloat16)
            probs_ref[head, :depth, at : at + CUT] = low
            total = total + dot(low, values, TN) * lane_mask(head)
        out_ref[at : at + CUT] = total.astype(jnp.bfloat16)


def diagonal_sums(block):
    width = block.shape[1]
    slabs = [block[at : at + 8] for at in range(0, block.shape[0], 8)]
    total = slabs[0]
    for at, slab in enumerate(slabs[1:], 1):
        total = total + pltpu.roll(slab, width - 8 * at, 1)
    row = lax.broadcasted_iota(jnp.int32, total.shape, 0)
    for step in (1, 2, 4):
        total = jnp.where((row & step) != 0, pltpu.roll(total, width - step, 1), total)
    return jnp.sum(total, axis=0, keepdims=True)


def attend_back_kernel(causal, q_ref, k_ref, v_ref, g_ref, probs_ref, *rest):
    if causal:
        dq_ref, dk_ref, dv_ref, sums_ref, dk_sum, dv_sum = rest
    else:
        dq_ref, dk_ref, dv_ref, dk_sum, dv_sum = rest
    rows = q_ref.shape[0]
    dk_sum[...] = jnp.zeros_like(dk_sum)
    dv_sum[...] = jnp.zeros_like(dv_sum)
    near = [[], []]
    far = [[], []]
    for at, depth in spans(rows, causal):
        dq = jnp.zeros((CUT, LANES), jnp.float32)
        for head in range(GROUP):
            grad = only_head(g_ref[at : at + CUT], head, 1.0)
            query = only_head(q_ref[at : at + CUT], head, HEAD**-0.5)
            keys = only_head(k_ref[:depth], head, HEAD**-0.5)
            low = probs_ref[head, :depth, at : at + CUT]
            probs = low.astype(jnp.float32)
            scaled = probs * dot(v_ref[:depth], grad, NT)
            centre = jnp.sum(scaled, axis=0, keepdims=True)
            grad_scores = (scaled - probs * centre).astype(jnp.bfloat16)
            dv_sum[:depth] += dot(low, grad)
            dk_sum[:depth] += dot(grad_scores, query)
            dq = dq + dot(grad_scores, keys, TN)
            if causal:
                parts = grad_scores.astype(jnp.float32)
                for first in range(0, CUT, LANES):
                    own = at + first
                    column = parts[:, first : first + LANES]
                    if own:
                        before = column[own - LANES : own]
                    else:
                        before = jnp.zeros((LANES, LANES), jnp.float32)
                    near[head].append((column[own : own + LANES], before))
                    if own > LANES:
                        far[head].append(jnp.sum(column[: own - LANES], axis=0, keepdims=True))
        dq_ref[at : at + CUT] = dq.astype(jnp.bfloat16)
    dk_ref[...] = dk_sum[...].astype(jnp.bfloat16)
    dv_ref[...] = dv_sum[...].astype(jnp.bfloat16)
    if causal:
        lines = []
        for head in range(GROUP):
            own = sum(pair[0] for pair in near[head][1:]) + near[head][0][0]
            before = sum(pair[1] for pair in near[head][1:]) + near[head][0][1]
            lines.append(diagonal_sums(jnp.concatenate([own, before], axis=1)))
        for head in range(GROUP):
            line = sum(far[head][1:]) + far[head][0]
            lines.append(jnp.concatenate([line, jnp.zeros_like(line)], axis=1))
        lines.append(jnp.zeros((8 - len(lines), 2 * LANES), jnp.float32))
        sums_ref[0] = jnp.concatenate(lines, axis=0)


def head_spec(rows):
    return pl.BlockSpec((rows, LANES), lambda pair: (0, pair))


def probs_spec(rows):
    return pl.BlockSpec((GROUP, rows, rows), lambda pair: (pair, 0, 0))


def attend_forward(query, keys, values, mask, lines, causal):
    rows = query.shape[0]
    return pl.pallas_call(
        functools.partial(attend_kernel, causal),
        grid=(HEADS // GROUP,),
        in_specs=[head_spec(rows)] * 3
        + [
            pl.BlockSpec((rows, rows), lambda pair: (0, 0)),
            pl.BlockSpec((1, 8, 2 * LANES), lambda pair: (pair, 0, 0)),
        ],
        out_specs=[probs_spec(rows), head_spec(rows)],
        out_shape=[
            jax.ShapeDtypeStruct((HEADS, rows, rows), jnp.bfloat16),
            jax.ShapeDtypeStruct(query.shape, jnp.bfloat16),
        ],
        compiler_params=pltpu.CompilerParams(vmem_limit_bytes=VMEM_BYTES),
        cost_estimate=COST,
        name="attend",
    )(query, keys, values, mask, lines)


def attend_backward(query, keys, values, grad, probs, causal):
    rows = query.shape[0]
    out_specs = [head_spec(rows)] * 3
    out_shape = [jax.ShapeDtypeStruct(query.shape, jnp.bfloat16)] * 3
    if causal:
        out_specs.append(pl.BlockSpec((1, 8, 2 * LANES), lambda pair: (pair, 0, 0)))
        out_shape.append(jax.ShapeDtypeStruct((HEADS // GROUP, 8, 2 * LANES), jnp.float32))
    return pl.pallas_call(
        functools.partial(attend_back_kernel, causal),
        grid=(HEADS // GROUP,),
        in_specs=[head_spec(rows)] * 4 + [probs_spec(rows)],
        out_specs=out_specs,
        out_shape=out_shape,
        scratch_shapes=[pltpu.VMEM((rows, LANES), jnp.float32)] * 2,
        compiler_params=pltpu.CompilerParams(vmem_limit_bytes=VMEM_BYTES),
        cost_estimate=COST,
        name="attend_back",
    )(query, keys, values, grad, probs)


def self_mask(segment, key_valid):
    rows = segment.shape[0]
    index = jnp.arange(rows, dtype=jnp.int32)
    distance = index[None, :] - index[:, None]
    allowed = (
        (segment[:, None] == segment[None, :])
        & (distance >= 0)
        & ((key_valid[:, None] > 0) | (distance == 0))
    )
    return jnp.where(allowed, 0.0, NEGATIVE).astype(jnp.float32)


def cross_mask(segment, mem_segment):
    allowed = mem_segment[:, None] == segment[None, :]
    return jnp.where(allowed, 0.0, NEGATIVE).astype(jnp.float32)


def bias_lines(table):
    places = bucket_table(jnp.arange(2 * LANES, dtype=jnp.int32), jnp.float32)
    lines = jnp.einsum(
        "nb,bh->hn", places, table.astype(jnp.float32), precision=lax.Precision.HIGHEST
    )
    lines = lines.reshape(HEADS // GROUP, GROUP, 2 * LANES)
    return jnp.pad(lines, ((0, 0), (0, 8 - GROUP), (0, 0)))


def table_sums(sums):
    near = sums[:, :GROUP].reshape(HEADS, 2 * LANES)
    far = jnp.sum(sums[:, GROUP : 2 * GROUP], axis=-1).reshape(HEADS)
    places = bucket_table(jnp.arange(2 * LANES, dtype=jnp.int32), jnp.float32)
    grad = jnp.einsum("nb,hn->bh", places, near, precision=lax.Precision.HIGHEST)
    return grad.at[BUCKETS - 1].add(far)


GELU_SCALE = math.sqrt(2.0 / math.pi)
GELU_CUBE = 0.044715
BLOCK = 768
CUTS = FF // (2 * BLOCK)


def ffn_kernel(
    core_ref, third_ref, upper_ref, cot_ref, in_ref, other_in_ref, out_ref, other_out_ref,
    layer_ref, gthird_ref, gin_ref, other_gin_ref, gout_ref, other_gout_ref,
    total, third_turned, out_block, gout_block,
):
    step = pl.program_id(0)
    half = D // 2
    mine = pl.ds(pl.multiple_of(core_ref[0] * half, half), half)
    other = pl.ds(pl.multiple_of((1 - core_ref[0]) * half, half), half)

    @pl.when(step == 0)
    def _():
        total[...] = upper_ref[...]
        gthird_ref[...] = jnp.zeros_like(gthird_ref)
        third_turned[...] = third_ref[...].T

    out_block[:, mine] = out_ref[...]
    out_block[:, other] = other_out_ref[...]

    def block(weight_ref, grad_ref):
        inner = dot(third_ref[...], weight_ref[...])
        square = inner * inner
        slope = jnp.tanh(inner * (GELU_SCALE + (GELU_SCALE * GELU_CUBE) * square))
        half_up = 0.5 + 0.5 * slope
        active = (inner * half_up).astype(jnp.bfloat16)
        total[...] += dot(active, out_block[...])
        grad_active = dot(cot_ref[...], out_block[...], NT)
        bend = (0.5 * inner) * (1.0 - slope * slope)
        bend = bend * (GELU_SCALE + (3.0 * GELU_SCALE * GELU_CUBE) * square)
        grad_inner = (grad_active * (half_up + bend)).astype(jnp.bfloat16)
        gthird_ref[...] += dot(grad_inner, weight_ref[...], NT)
        grad_ref[...] = dot(third_turned[...], grad_inner).astype(jnp.bfloat16)
        gout_block[...] = dot(active, cot_ref[...], TN).astype(jnp.bfloat16)

    @pl.when(step < CUTS)
    def _():
        block(other_in_ref, other_gin_ref)

    @pl.when(step >= CUTS)
    def _():
        block(in_ref, gin_ref)

    gout_ref[...] = gout_block[:, mine]
    other_gout_ref[...] = gout_block[:, other]

    @pl.when(step == 2 * CUTS - 1)
    def _():
        layer_ref[...] = total[...].astype(jnp.bfloat16)


def ffn(core, third, upper, cotangent, w_in, other_in, w_out, other_out):
    rows = third.shape[0]
    half = D // 2

    def place(step, core_ref):
        return ((1 - core_ref[0]) * CUTS + step) % (2 * CUTS)

    whole = pl.BlockSpec((rows, D), lambda step, core_ref: (0, 0))
    late = pl.BlockSpec((D, BLOCK), lambda step, core_ref: (0, jnp.maximum(step - CUTS, 0)))
    early = pl.BlockSpec((D, BLOCK), lambda step, core_ref: (0, jnp.minimum(step, CUTS - 1)))
    lines = pl.BlockSpec((BLOCK, half), lambda step, core_ref: (place(step, core_ref), 0))
    return pl.pallas_call(
        ffn_kernel,
        grid_spec=pltpu.PrefetchScalarGridSpec(
            num_scalar_prefetch=1,
            grid=(2 * CUTS,),
            in_specs=[whole, whole, whole, late, early, lines, lines],
            out_specs=[whole, whole, late, early, lines, lines],
            scratch_shapes=[
                pltpu.VMEM((rows, D), jnp.float32),
                pltpu.VMEM((D, rows), jnp.bfloat16),
                pltpu.VMEM((BLOCK, D), jnp.bfloat16),
                pltpu.VMEM((BLOCK, D), jnp.bfloat16),
            ],
        ),
        out_shape=[
            jax.ShapeDtypeStruct((rows, D), jnp.bfloat16),
            jax.ShapeDtypeStruct((rows, D), jnp.float32),
            jax.ShapeDtypeStruct((D, FF // 2), jnp.bfloat16),
            jax.ShapeDtypeStruct((D, FF // 2), jnp.bfloat16),
            jax.ShapeDtypeStruct((FF, half), jnp.bfloat16),
            jax.ShapeDtypeStruct((FF, half), jnp.bfloat16),
        ],
        compiler_params=pltpu.CompilerParams(vmem_limit_bytes=VMEM_BYTES),
        cost_estimate=COST,
        name="ffn",
    )(core[None], third, upper, cotangent, w_in, other_in, w_out, other_out)


AXES = ("wide", "narrow")


def after(value, *others):
    return lax.optimization_barrier((value,) + others)[0]


class Cube:
    def __init__(self):
        self.count = lax.axis_size("wide") * lax.axis_size("narrow")
        self.bits = self.count.bit_length() - 1
        self.me = lax.axis_index("wide") * lax.axis_size("narrow") + lax.axis_index("narrow")
        high = list(range(self.bits - 1, 1, -1))
        self.plan_a = high + [1]
        self.plan_b = [1] + high

    def bit(self, which):
        return (self.me >> which) & 1

    def swap(self, value, flip):
        return lax.ppermute(value, AXES, [(i, i ^ flip) for i in range(self.count)])

    def place(self, mine, theirs, which, axis, joined):
        join = jnp.concatenate if joined else jnp.stack
        return jnp.where(
            self.bit(which) == 0, join([mine, theirs], axis), join([theirs, mine], axis)
        )

    def send_step(self, value, plan, step):
        return self.swap(value, 1 << plan[step])

    def place_step(self, value, theirs, plan, step):
        axis = sum(other > plan[step] for other in plan[:step])
        return self.place(value, theirs, plan[step], axis, False)

    def half(self, value, whose):
        size = value.shape[-1] // 2
        return lax.dynamic_slice_in_dim(value, whose * size, size, value.ndim - 1)

    def total(self, value):
        for low in [0] + list(range(1, self.bits, 2)):
            top = 1 if low == 0 else min(2, self.bits - low)
            flips = [flip << low for flip in range(1, 1 << top)]
            value = value + sum(self.swap(value, flip) for flip in flips)
        return value


class Gather:
    def __init__(self, cube, value, plan):
        self.cube, self.value, self.plan, self.steps = cube, value, plan, 0

    def send(self, *behind):
        self.value = after(self.value, *behind)
        self.theirs = self.cube.send_step(self.value, self.plan, self.steps)

    def take(self, *behind):
        value = after(self.value, *behind) if behind else self.value
        self.value = self.cube.place_step(value, self.theirs, self.plan, self.steps)
        self.steps += 1
        return self.value


def pair_weights(cube, w_in, w_out):
    rows = w_in.shape[0]
    core = cube.bit(0)
    count = FF // D
    in_rows = jnp.stack([w_in[:, k * D // 2 : (k + 1) * D // 2] for k in range(2 * count)])

    def packed(whose):
        in_half = lax.dynamic_slice_in_dim(in_rows, whose * count, count, 0)
        return [in_half, cube.half(w_out, whose)]

    mine = packed(core)
    sent = [part.reshape(-1, D // 2) for part in packed(1 - core)]
    other = cube.swap(jnp.concatenate(sent, axis=0), 1)
    size = count * rows
    theirs = [other[:size].reshape(mine[0].shape), other[size:]]
    in_pair, out_pair = [
        cube.place(ours, others, 0, ours.ndim - 2, True) for ours, others in zip(mine, theirs)
    ]
    return jnp.concatenate([in_pair[k] for k in range(count)], axis=1), out_pair


def both_halves(cube, value):
    value = value.reshape((-1,) + value.shape[-2:])
    return value, cube.swap(value, 1)


def whole_weights(cube, parts, first, count):
    rows = D // cube.count
    full = cube.place(parts[0], parts[1], 0, 1, False)
    return [
        full[:, :, first + k * rows : first + (k + 1) * rows].reshape(D, D) for k in range(count)
    ]


class Sums:
    def __init__(self, cube, plan, sent, kept):
        self.cube, self.plan, self.steps = cube, plan, 0
        self.kept, self.theirs = kept, cube.swap(sent, 1)

    def take(self, *behind):
        kept = after(self.kept, *behind) if behind else self.kept
        value = kept.astype(jnp.float32) + self.theirs.astype(jnp.float32)
        if self.steps == 0:
            shape = (value.shape[0],) + (2,) * len(self.plan) + (-1, value.shape[-1])
            value = value.reshape(shape)
        self.value = value

    def send(self, *behind):
        which = self.plan[-1 - self.steps]
        axis = 1 + sum(other > which for other in self.plan[: len(self.plan) - self.steps])
        mine = self.cube.bit(which)
        sent = lax.dynamic_index_in_dim(self.value, 1 - mine, axis, False).astype(jnp.bfloat16)
        sent = after(sent, *behind)
        self.kept = lax.dynamic_index_in_dim(self.value, mine, axis, False)
        self.theirs = self.cube.swap(sent, 1 << which)
        self.steps += 1
        return sent

    def going(self):
        return self.steps < len(self.plan)


def product_sums(cube, plan, pairs):
    grads = jnp.stack([weight_grad(left, right).astype(jnp.bfloat16) for left, right in pairs])
    grads = grads.reshape(len(pairs), cube.count // 2, 2, -1, D)
    core = cube.bit(0)
    sent = lax.dynamic_index_in_dim(grads, 1 - core, 2, False)
    kept = lax.dynamic_index_in_dim(grads, core, 2, False)
    return Sums(cube, plan, sent, kept)


def half_swap(cube, value):
    value = value.reshape(2, -1, value.shape[-1])
    core = cube.bit(0)
    mine = lax.dynamic_index_in_dim(value, core, 0, False)
    return mine, cube.swap(lax.dynamic_index_in_dim(value, 1 - core, 0, False), 1)


def on_device(
    tokens,
    memory,
    cotangent,
    dec_segments,
    enc_segments,
    dec_valid,
    attn_weights,
    w_in,
    w_out,
    norm_gains,
    rel_table,
    row_main,
    row_out,
    col_main,
    col_in,
):
    cube = Cube()
    core = cube.bit(0)
    rows = attn_weights.shape[1]
    gain_rows = jnp.pad(norm_gains, ((0, 5), (0, D - norm_gains.shape[1])))
    one = Gather(
        cube,
        jnp.concatenate([attn_weights[:2].reshape(-1, D), gain_rows], axis=0),
        cube.plan_a,
    )
    two = Gather(cube, attn_weights[2:4].reshape(-1, D), cube.plan_b)
    one.send()
    two.send()
    in_pair, out_pair = pair_weights(cube, w_in, w_out)
    three = Gather(cube, attn_weights[4:].reshape(-1, D), cube.plan_a)
    inner_half = Gather(cube, in_pair, cube.plan_b)
    outer_half = Gather(cube, out_pair, cube.plan_a)
    last = len(cube.plan_a) - 1
    for step in range(last):
        one.take()
        two.take()
        one.send()
        two.send()
        if step > 0:
            three.take()
        three.send(one.value, two.value)
        if step > 1:
            inner_half.take()
            outer_half.take()
        if step > 0:
            inner_half.send(three.value)
            outer_half.send(three.value)
    one.take()
    two.take()
    first_halves = both_halves(cube, one.value)
    second_halves = both_halves(cube, two.value)
    three.take()
    three.send(one.value, two.value)
    inner_half.take()
    outer_half.take()
    inner_half.send(three.value)
    outer_half.send(three.value)
    attn_full = whole_weights(cube, first_halves, 0, 2)
    attn_full = attn_full + whole_weights(cube, second_halves, 0, 2)
    gain_full = cube.place(
        first_halves[0][:, 2 * rows :], first_halves[1][:, 2 * rows :], 0, 1, False
    )[:, :, :3, : norm_gains.shape[1]]
    gain_full = gain_full.transpose(2, 0, 1, 3).reshape(3, D)
    segment = dec_segments[0]
    see_self = self_mask(segment, dec_valid[0])
    see_cross = cross_mask(segment, enc_segments[0])
    lines = bias_lines(rel_table)

    residual = tokens.astype(jnp.float32)
    normed_first, norm_back_first = jax.vjp(rms_norm, residual, gain_full[0].astype(jnp.float32))
    first_low = normed_first.astype(jnp.bfloat16)
    query = project(first_low, attn_full[0]).astype(jnp.bfloat16)
    keys = project(first_low, attn_full[1]).astype(jnp.bfloat16)
    values = project(first_low, attn_full[2]).astype(jnp.bfloat16)
    inner_half.take(query, keys, values)
    outer_half.take(query, keys, values)
    query = after(query, inner_half.value, outer_half.value)
    inner_half.send()
    outer_half.send()
    self_probs, mixed_low = attend_forward(query, keys, values, see_self, lines, True)
    three.take(mixed_low)
    attn_full = attn_full + whole_weights(cube, both_halves(cube, three.value), 0, 4)
    middle = residual + project(mixed_low, attn_full[3])
    normed_second, norm_back_second = jax.vjp(rms_norm, middle, gain_full[1].astype(jnp.float32))
    second_low = normed_second.astype(jnp.bfloat16)
    cross_query = project(second_low, attn_full[4]).astype(jnp.bfloat16)
    memory_keys = project(memory, attn_full[5]).astype(jnp.bfloat16)
    memory_values = project(memory, attn_full[6]).astype(jnp.bfloat16)
    inner_half.take(cross_query)
    outer_half.take(cross_query)
    cross_query = after(cross_query, inner_half.value, outer_half.value)
    own_in, other_in = both_halves(cube, inner_half.value)
    own_out, other_out = both_halves(cube, outer_half.value)
    cross_probs, crossed_low = attend_forward(
        cross_query, memory_keys, memory_values, see_cross, lines, False
    )
    upper = middle + project(crossed_low, attn_full[7])
    normed_third, norm_back_third = jax.vjp(rms_norm, upper, gain_full[2].astype(jnp.float32))
    third_low = normed_third.astype(jnp.bfloat16)
    layer_out, grad_third, grad_in, other_grad_in, grad_out, other_grad_out = ffn(
        core,
        third_low,
        upper,
        cotangent,
        own_in.reshape(D, -1),
        other_in.reshape(D, -1),
        own_out.reshape(FF, -1),
        other_out.reshape(FF, -1),
    )
    in_sums = Sums(cube, cube.plan_b, other_grad_in[None], grad_in[None])
    out_sums = Sums(cube, cube.plan_a, other_grad_out[None], grad_out[None])
    grad_from_third, grad_gain_third = norm_back_third(grad_third)
    grad_upper = cotangent.astype(jnp.float32) + grad_from_third
    grad_cross_branch = grad_upper.astype(jnp.bfloat16)
    grad_crossed = project_back(grad_cross_branch, attn_full[7]).astype(jnp.bfloat16)
    in_sums.take(grad_crossed)
    out_sums.take(grad_crossed)
    grad_crossed = after(grad_crossed, in_sums.send(), out_sums.send())
    cross_query_low, memory_key_low, memory_value_low = attend_backward(
        cross_query, memory_keys, memory_values, grad_crossed, cross_probs, False
    )
    cross_sums = product_sums(
        cube,
        cube.plan_a,
        [
            (second_low, cross_query_low),
            (memory, memory_key_low),
            (memory, memory_value_low),
            (crossed_low, grad_cross_branch),
        ],
    )
    grad_from_second, grad_gain_second = norm_back_second(
        project_back(cross_query_low, attn_full[4])
    )
    grad_middle = grad_upper + grad_from_second
    grad_self_branch = grad_middle.astype(jnp.bfloat16)
    grad_mixed = project_back(grad_self_branch, attn_full[3]).astype(jnp.bfloat16)
    sums = [cross_sums, in_sums, out_sums]
    for each in sums:
        each.take(grad_mixed)
    grad_mixed = after(grad_mixed, *[each.send() for each in sums])
    query_low, key_low, value_low, score_sums = attend_backward(
        query, keys, values, grad_mixed, self_probs, True
    )
    for each in sums[1:]:
        each.take(query_low)
    query_low, key_low, value_low = lax.optimization_barrier(
        (query_low, key_low, value_low) + tuple(each.send() for each in sums[1:])
    )[:3]
    late_sums = product_sums(
        cube, cube.plan_b, [(first_low, value_low), (mixed_low, grad_self_branch)]
    )
    early_sums = product_sums(cube, cube.plan_a, [(first_low, query_low), (first_low, key_low)])
    memory_key_low, memory_value_low = lax.optimization_barrier(
        (memory_key_low, memory_value_low, late_sums.kept, early_sums.kept)
    )[:2]
    grad_memory = project_back(memory_key_low, attn_full[5]) + project_back(
        memory_value_low, attn_full[6]
    )
    sums = [late_sums, early_sums, cross_sums, in_sums, out_sums]
    for each in sums:
        each.take(grad_memory)
    started = [each.send() for each in sums if each.going()]
    query_low, key_low, value_low = lax.optimization_barrier(
        (query_low, key_low, value_low, *started)
    )[:3]
    grad_first = (
        project_back(query_low, attn_full[0])
        + project_back(key_low, attn_full[1])
        + project_back(value_low, attn_full[2])
    )
    grad_from_first, grad_gain_first = norm_back_first(grad_first)
    grad_tokens = grad_middle + grad_from_first
    table_grad = table_sums(score_sums)
    gain_local = jnp.stack([grad_gain_first, grad_gain_second, grad_gain_third])
    behind = (grad_tokens,)
    while any(each.going() for each in sums):
        moving = [each for each in sums if each.going()]
        for each in moving:
            each.take(*behind)
            each.send()
        behind = ()
    for each in sums:
        each.take(*behind)
    grad_in, grad_out = [
        cube.place(*half_swap(cube, each.value), 0, 1, True) for each in sums[3:]
    ]
    grad_attn = jnp.concatenate(
        [each.value.reshape(-1, rows, D) for each in (early_sums, late_sums, cross_sums)], axis=0
    )
    square_attn = grad_attn * grad_attn
    square_in = grad_in * grad_in
    square_out = grad_out * grad_out
    row_means = jnp.concatenate(
        [jnp.mean(square_attn, axis=2), jnp.mean(square_in, axis=1)[None]], axis=0
    )
    new_row_main = DECAY * row_main + (1.0 - DECAY) * row_means
    new_row_out = DECAY * row_out + (1.0 - DECAY) * jnp.mean(square_out, axis=1)
    column_main = jnp.concatenate(
        [jnp.sum(square_attn, axis=1), jnp.sum(square_out, axis=0)[None]], axis=0
    )
    column_in = jnp.sum(square_in, axis=0)
    parts = [column_main, column_in, table_grad, gain_local]
    sizes = [part.size for part in parts]
    width = D // 2
    lines = -(-sum(sizes) // (8 * width)) * 8
    flat = jnp.concatenate([part.reshape(-1, width) for part in parts], axis=0)
    flat = cube.total(jnp.pad(flat, ((0, lines - flat.shape[0]), (0, 0))))
    sums, at = [], 0
    for part, size in zip(parts, sizes):
        sums.append(flat[at : at + size // width].reshape(part.shape))
        at += size // width
    column_main, column_in, grad_table, gain_sums = sums
    grad_gains = lax.dynamic_slice_in_dim(
        gain_sums, cube.me * norm_gains.shape[1], norm_gains.shape[1], 1
    )
    col_means = jnp.concatenate([column_main[:8] / D, column_main[8:] / FF], axis=0)
    new_col_main = DECAY * col_main + (1.0 - DECAY) * col_means
    new_col_in = DECAY * col_in + (1.0 - DECAY) * (column_in / D)
    return (
        layer_out,
        grad_tokens,
        grad_memory,
        grad_attn,
        grad_in,
        grad_out,
        grad_gains,
        grad_table,
        new_row_main,
        new_row_out,
        new_col_main,
        new_col_in,
    )


def solution(mesh):
    placed = (
        P(("wide", "narrow"), None),
        P(("wide", "narrow"), None),
        P(("wide", "narrow"), None),
        P(("wide", "narrow"), None),
        P(("wide", "narrow"), None),
        P(("wide", "narrow"), None),
        P(None, ("wide", "narrow"), None),
        P(("wide", "narrow"), None),
        P(("wide", "narrow"), None),
        P(None, ("wide", "narrow")),
        P(),
        P(None, ("wide", "narrow")),
        P(("wide", "narrow")),
        P(),
        P(),
    )
    return jax.shard_map(
        on_device,
        mesh=mesh,
        in_specs=placed,
        out_specs=(
            P(("wide", "narrow"), None),
            P(("wide", "narrow"), None),
            P(("wide", "narrow"), None),
            P(None, ("wide", "narrow"), None),
            P(("wide", "narrow"), None),
            P(("wide", "narrow"), None),
            P(None, ("wide", "narrow")),
            P(),
            P(None, ("wide", "narrow")),
            P(("wide", "narrow")),
            P(),
            P(),
        ),
        check_vma=False,
    )
```

time: 794 us -> 403 us (0.51)
  waiting for transfers between devices: 437 us -> 95.9 us
  matrix products: 184 us -> 33.5 us
  blocking collectives: 83.9 us -> 0 us
  Pallas kernels: 0 us -> 71.9 us
  starting transfers between devices: 0.7 us -> 58.1 us
  other arithmetic: 34.1 us -> 71.9 us
  local copies, waits for them, and re-layouts: 30 us -> 62.4 us
  between operations: 15.6 us -> 2.59 us
    reduce_scatter x3 -> x0, waiting for transfers between devices: 344 us -> none  [the longest x1 210 us: spread(): lax.psum_scatter(attn_grad, ('wide', 'narrow'), scatter_dimension=1, tile...]
    ppermute x0 -> x60, waiting for transfers between devices: none -> 95.9 us  [swap(): return lax.ppermute(value, AXES, [(i, i ^ flip) for i in range(self.count)])]
    all_gather x3 -> x0, waiting for transfers between devices: 90.4 us -> none  [the longest x1 77 us: collect(): lax.all_gather(attn_part, ('wide', 'narrow'), axis=1, tiled=True)]
    dot_general x14 -> x2, matrix products: 78.5 us -> 1.78 us  [the longest x1 0.95 us: table_sums(): jnp.einsum('nb,hn->bh', places, near, precision=lax.Precision.HIGHEST)]
    pallas_call x0 -> x5, Pallas kernels: none -> 71.9 us  [the longest x1 24.4 us: ffn(): pl.pallas_call(ffn_kernel, grid_spec=pltpu.PrefetchScalarGridSpec(num_sca...]
    ppermute x0 -> x60, starting transfers between devices: none -> 58.1 us  [swap(): return lax.ppermute(value, AXES, [(i, i ^ flip) for i in range(self.count)])]
    all_gather x1 -> x0, blocking collectives: 43.5 us -> none  [collect(): lax.all_gather(gain_part, ('wide', 'narrow'), axis=1, tiled=True)]
    unnamed x1 -> x0, blocking collectives: 40.4 us -> none
  transfers between devices with their start and end apart: 6 -> 60, of which waited for: 5 -> 24; matrix products, arithmetic and copies ran while one was open for 27% -> 35% of each run, Pallas kernels for 0% -> 12%
where the time goes in v2:
time: 403 us; the launch traced here: 396 us
  waiting for transfers between devices  95.9 us (24%)
  other arithmetic  71.9 us (18%)
  Pallas kernels  71.9 us (18%)
  local copies, waits for them, and re-layouts  62.4 us (15%)
  starting transfers between devices  58.1 us (14%)
  matrix products  33.5 us (8%)
    ppermute x60, waiting for transfers between devices, swap(): return lax.ppermute(value, AXES, [(i, i ^ flip) for i in range(self.count)])  95.9 us
    ppermute x60, starting transfers between devices, swap(): return lax.ppermute(value, AXES, [(i, i ^ flip) for i in range(self.count)])  58.1 us
    select_n x25, other arithmetic, place(): jnp.where(self.bit(which) == 0, join([mine, theirs], axis), join([theirs,...  30.6 us
    unnamed x191, local copies, waits for them, and re-layouts  24.6 us
    pallas_call x1, Pallas kernels, ffn(): pl.pallas_call(ffn_kernel, grid_spec=pltpu.PrefetchScalarGridSpec(num_sca...  24.4 us
    pallas_call x2, Pallas kernels, attend_forward(): pl.pallas_call(functools.partial(attend_kernel, causal), grid=(HEADS // G...  23.8 us
    pallas_call x2, Pallas kernels, attend_backward(): pl.pallas_call(functools.partial(attend_back_kernel, causal), grid=(HEADS...  23.7 us
    add x25, other arithmetic, take(): value = kept.astype(jnp.float32) + self.theirs.astype(jnp.float32)  20.7 us
  transfers between devices with their start and end apart: 60, of which 24 were waited for; matrix products, arithmetic and copies ran while one was open for 35% of the time, Pallas kernels for 12%

profile of v2, /device:TPU:0, one launch (start us, length us, event | category | flops | bytes accessed | tf_op | source)
XLA Modules:
  0.0 396.4 jit_solution(6103322877200794759)
XLA Ops:
  1.7 3.0 collective-permute-start.6
  5.4 2.6 collective-permute-start
  20.0 2.6 collective-permute-start.7
  22.7 6.1 %collective-permute-done.8 = bf16[2,48,768]{2,1,0:T(8,128)(2,1)S(1)} collective-permute-done((bf16[2,48,768]{2,1,0:T(8,128)(2,1)S(1)}, bf16[2,48,768]{2,1,0:T(8,128)(2,1)S(1)}, u32[]{:S(2)}, u32[]{:S(2)}) %collective-permute-start.8) | collective-permute-done | bytes 147488 | tf_op jit(solution)/shard_map/ppermute | solution.py:398
  30.5 4.3 %collective-permute-done.7 = bf16[96,768]{1,0:T(8,128)(2,1)S(1)} collective-permute-done((bf16[96,768]{1,0:T(8,128)(2,1)S(1)}, bf16[96,768]{1,0:T(8,128)(2,1)S(1)}, u32[]{:S(2)}, u32[]{:S(2)}) %collective-permute-start.7) | collective-permute-done | bytes 147488 | tf_op jit(solution)/shard_map/ppermute | solution.py:398
  35.4 3.2 collective-permute-done.11
  41.1 3.1 collective-permute-start.17
  44.3 4.5 %collective-permute-done.17 = bf16[192,384]{1,0:T(8,128)(2,1)S(1)} collective-permute-done((bf16[192,384]{1,0:T(8,128)(2,1)S(1)}, bf16[192,384]{1,0:T(8,128)(2,1)S(1)}, u32[]{:S(2)}, u32[]{:S(2)}) %collective-permute-start.17) | collective-permute-done | bytes 147488 | tf_op jit(solution)/shard_map/ppermute | solution.py:398
  48.8 3.6 collective-permute-done.14
  56.3 3.7 collective-permute-start.12
  63.4 8.1 %collective-permute-done.18 = bf16[2,192,384]{2,1,0:T(8,128)(2,1)} collective-permute-done((bf16[2,192,384]{2,1,0:T(8,128)(2,1)S(1)}, bf16[2,192,384]{2,1,0:T(8,128)(2,1)}, u32[]{:S(2)}, u32[]{:S(2)}) %collective-permute-start.18) | collective-permute-done | bytes 294944 | tf_op jit(solution)/shard_map/ppermute | solution.py:398
  71.5 2.0 maximum_select_fusion.15
  74.9 3.1 maximum_select_fusion.7
  82.3 3.0 maximum_select_fusion.2
  89.8 2.3 maximum_select_fusion.1
  99.3 2.9 maximum_select_fusion.10
  102.2 2.4 maximum_select_fusion.9
  104.6 10.9 %attend.2 = (bf16[12,512,512]{2,1,0:T(8,128)(2,1)}, bf16[512,768]{1,0:T(8,128)(2,1)}) custom-call(bf16[512,768]{1,0:T(8,128)(2,1)} %convolution_convert_fusion.15.q_ref, bf16[512,768]{1,0:T(8,128)(2,1)} %convolution_convert_fusion.14.k_ref, bf16[512,768]{1,0:T(8,128)(2,1)} %convolution_convert_fusion.13.v_ref, f32[512,512]{1,0:T(8,128)} %get-tuple-element.225.mask_ref, ...), custom_call_target="tpu_custom_call" | custom-call | flops 1000 | bytes 1000 | tf_op jit(solution)/shard_map/attend/pallas_call | solution.py:210
  115.6 3.0 maximum_select_fusion.3
  120.4 1.9 multiply_reduce_fusion.5
  124.4 3.3 maximum_select_fusion
  127.7 2.0 fusion.129
  131.5 1.7 convolution_convert_fusion.12.q_ref
  133.2 14.3 %collective-permute-done.24 = bf16[2,2,2,192,384]{4,3,2,1,0:T(8,128)(2,1)} collective-permute-done((bf16[2,2,2,192,384]{4,3,2,1,0:T(8,128)(2,1)}, bf16[2,2,2,192,384]{4,3,2,1,0:T(8,128)(2,1)}, u32[]{:S(2)}, u32[]{:S(2)}) %collective-permute-start.24) | collective-permute-done | bytes 1179680 | tf_op jit(solution)/shard_map/ppermute | solution.py:398
  147.5 2.8 maximum_select_fusion.5
  151.1 1.8 maximum_select_fusion.4
  158.1 12.9 %attend.3 = (bf16[12,512,512]{2,1,0:T(8,128)(2,1)}, bf16[512,768]{1,0:T(8,128)(2,1)}) custom-call(bf16[512,768]{1,0:T(8,128)(2,1)} %convolution_convert_fusion.12.q_ref, bf16[512,768]{1,0:T(8,128)(2,1)} %fusion.9.k_ref, bf16[512,768]{1,0:T(8,128)(2,1)} %fusion.10.v_ref, f32[512,512]{1,0:T(8,128)} %get-tuple-element.224.mask_ref, f32[6,8,256]{2,1,0:T(8,128)} %pad.15.line_ref), custom_call_target="tpu_custom_call" | custom-call | flops 1000 | bytes 1000 | tf_op jit(solution)/shard_map/attend/pallas_call | solution.py:210
  175.4 24.4 %ffn.1 = (bf16[512,768]{1,0:T(8,128)(2,1)}, f32[512,768]{1,0:T(8,128)}, bf16[768,1536]{1,0:T(8,128)(2,1)}, bf16[768,1536]{1,0:T(8,128)(2,1)}, bf16[3072,384]{1,0:T(8,128)(2,1)}, /*index=5*/bf16[3072,384]{1,0:T(8,128)(2,1)}) custom-call(s32[1]{0:T(128)} %bitcast.core_ref, bf16[512,768]{1,0:T(8,128)(2,1)} %multiply_convert_fusion.third_ref, ...), custom_call_target="tpu_custom_call" | custom-call | flops 1000 | bytes 1000 | tf_op jit(solution)/shard_map/ffn/pallas_call | solution.py:350
  200.5 2.5 multiply_reduce_fusion
  208.5 2.1 convert_add_fusion.1
  213.5 2.1 copy-done.4
  219.3 12.7 %attend_back.2 = (bf16[512,768]{1,0:T(8,128)(2,1)}, bf16[512,768]{1,0:T(8,128)(2,1)}, bf16[512,768]{1,0:T(8,128)(2,1)}) custom-call(bf16[512,768]{1,0:T(8,128)(2,1)} %convolution_convert_fusion.12.q_ref, bf16[512,768]{1,0:T(8,128)(2,1)} %fusion.9.k_ref, bf16[512,768]{1,0:T(8,128)(2,1)} %fusion.10.v_ref, bf16[512,768]{1,0:T(8,128)(2,1)} %convolution_convert_fusion.11.g_ref, ...), custom_call_target="tpu_custom_call" | custom-call | flops 1000 | bytes 1000 | tf_op jit(solution)/shard_map/attend_back/pallas_call | solution.py:236
  232.0 2.6 multiply_reduce_fusion.1
  257.1 11.1 %attend_back.3 = (bf16[512,768]{1,0:T(8,128)(2,1)}, bf16[512,768]{1,0:T(8,128)(2,1)}, bf16[512,768]{1,0:T(8,128)(2,1)}, f32[6,8,256]{2,1,0:T(8,128)}) custom-call(bf16[512,768]{1,0:T(8,128)(2,1)} %convolution_convert_fusion.15.q_ref, bf16[512,768]{1,0:T(8,128)(2,1)} %convolution_convert_fusion.14.k_ref, bf16[512,768]{1,0:T(8,128)(2,1)} %convolution_convert_fusion.13.v_ref, ...), custom_call_target="tpu_custom_call" | custom-call | flops 1000 | bytes 1000 | tf_op jit(solution)/shard_map/attend_back/pallas_call | solution.py:236
  275.9 2.7 collective-permute-start.36
  287.0 2.0 convolution_add_fusion
  296.9 6.8 %collective-permute-done.51 = bf16[1,192,384]{2,1,0:T(8,128)(2,1)S(1)} collective-permute-done((bf16[1,192,384]{2,1,0:T(8,128)(2,1)S(1)}, bf16[1,192,384]{2,1,0:T(8,128)(2,1)S(1)}, u32[]{:S(2)}, u32[]{:S(2)}) %collective-permute-start.51) | collective-permute-done | bytes 147488 | tf_op jit(solution)/shard_map/ppermute | solution.py:398
  309.0 2.3 convert_add_fusion.4
  329.2 6.5 %collective-permute-done.38 = bf16[2,2,2,2,24,768]{5,4,0,1,2,3:T(8,128)(2,1)} collective-permute-done((bf16[2,2,2,2,24,768]{5,4,0,1,2,3:T(8,128)(2,1)}, bf16[2,2,2,2,24,768]{5,4,0,1,2,3:T(8,128)(2,1)}, u32[]{:S(2)}, u32[]{:S(2)}) %collective-permute-start.38) | collective-permute-done | bytes 589856 | tf_op jit(solution)/shard_map/ppermute | solution.py:398
  339.2 11.3 %collective-permute-done.46 = bf16[4,2,2,24,768]{4,3,2,1,0:T(8,128)(2,1)} collective-permute-done((bf16[4,2,2,24,768]{4,3,2,1,0:T(8,128)(2,1)}, bf16[4,2,2,24,768]{4,3,2,1,0:T(8,128)(2,1)}, u32[]{:S(2)}, u32[]{:S(2)}) %collective-permute-start.46) | collective-permute-done | bytes 589856 | tf_op jit(solution)/shard_map/ppermute | solution.py:398
  351.8 3.6 collective-permute-done.39
  355.7 2.1 collective-permute-start.44
  357.9 5.4 %collective-permute-done.47 = bf16[4,2,24,768]{3,2,1,0:T(8,128)(2,1)S(1)} collective-permute-done((bf16[4,2,24,768]{3,2,1,0:T(8,128)(2,1)S(1)}, bf16[4,2,24,768]{3,2,1,0:T(8,128)(2,1)S(1)}, u32[]{:S(2)}, u32[]{:S(2)}) %collective-permute-start.47) | collective-permute-done | bytes 294944 | tf_op jit(solution)/shard_map/ppermute | solution.py:398
  366.5 4.7 %collective-permute-done.44 = bf16[2,2,24,768]{3,2,0,1:T(8,128)(2,1)S(1)} collective-permute-done((bf16[2,2,24,768]{3,2,0,1:T(8,128)(2,1)S(1)}, bf16[2,2,24,768]{3,2,0,1:T(8,128)(2,1)S(1)}, u32[]{:S(2)}, u32[]{:S(2)}) %collective-permute-start.44) | collective-permute-done | bytes 147488 | tf_op jit(solution)/shard_map/ppermute | solution.py:398
  379.9 1.8 collective-permute-start.56
  385.1 2.2 collective-permute-start.58
  387.3 2.2 collective-permute-start.59
  390.9 2.4 collective-permute-done.59
  (470 shorter events, 165.3 us)
Async XLA Ops:
  1.7 16.2 %collective-permute-start.6 = (bf16[48,768]{1,0:T(8,128)(2,1)S(1)}, bf16[48,768]{1,0:T(8,128)(2,1)S(1)}, u32[]{:S(2)}, u32[]{:S(2)}) collective-permute-start(bf16[48,768]{1,0:T(8,128)(2,1)S(1)} %bitcast.343), channel_id=1, source_target_pairs={{0,2},{1,3},{2,0},{3,1},{4,6},{5,7},{6,4},{7,5},{8,10},{9,11},{10,... | collective-permute-start | bytes 221192 | tf_op jit(solution)/shard_map/ppermute | solution.py:398
  5.4 13.0 %collective-permute-start = (bf16[56,768]{1,0:T(8,128)(2,1)S(1)}, bf16[56,768]{1,0:T(8,128)(2,1)S(1)}, u32[]{:S(2)}, u32[]{:S(2)}) collective-permute-start(bf16[56,768]{1,0:T(8,128)(2,1)S(1)} %fusion.49), channel_id=1, source_target_pairs={{0,16},{1,17},{2,18},{3,19},{4,20},{5,21},{6,22},{7,23},{8,24},{9,... | collective-permute-start | bytes 258056 | tf_op jit(solution)/shard_map/ppermute | solution.py:398
  14.9 7.7 %collective-permute-start.5 = (bf16[192,384]{1,0:T(8,128)(2,1)S(1)}, bf16[192,384]{1,0:T(8,128)(2,1)S(1)}, u32[]{:S(2)}, u32[]{:S(2)}) collective-permute-start(bf16[192,384]{1,0:T(8,128)(2,1)S(1)} %pad_maximum_fusion.2), channel_id=1, source_target_pairs={{0,1},{1,0},{2,3},{3,2},{4,5},{5,4},{6,7},{7,6},{8,9},{9,8},{10,11... | collective-permute-start | bytes 442376 | tf_op jit(solution)/shard_map/ppermute | solution.py:398
  18.0 10.8 %collective-permute-start.8 = (bf16[2,48,768]{2,1,0:T(8,128)(2,1)S(1)}, bf16[2,48,768]{2,1,0:T(8,128)(2,1)S(1)}, u32[]{:S(2)}, u32[]{:S(2)}) collective-permute-start(bf16[2,48,768]{2,1,0:T(8,128)(2,1)S(1)} %maximum_select_fusion.25), channel_id=1, source_target_pairs={{0,16},{1,17},{2,18},{3,19},{4,20},{5,21},{6,22},{7,23},{8,24},{9,... | collective-permute-start | bytes 442376 | tf_op jit(solution)/shard_map/ppermute | solution.py:398
  18.4 10.5 %collective-permute-start.1 = (bf16[2,56,768]{2,1,0:T(8,128)(2,1)S(1)}, bf16[2,56,768]{2,1,0:T(8,128)(2,1)S(1)}, u32[]{:S(2)}, u32[]{:S(2)}) collective-permute-start(bf16[2,56,768]{2,1,0:T(8,128)(2,1)S(1)} %maximum_select_fusion.23), channel_id=1, source_target_pairs={{0,8},{1,9},{2,10},{3,11},{4,12},{5,13},{6,14},{7,15},{8,0},{9,1},... | collective-permute-start | bytes 516104 | tf_op jit(solution)/shard_map/ppermute | solution.py:398
  20.0 14.8 %collective-permute-start.7 = (bf16[96,768]{1,0:T(8,128)(2,1)S(1)}, bf16[96,768]{1,0:T(8,128)(2,1)S(1)}, u32[]{:S(2)}, u32[]{:S(2)}) collective-permute-start(bf16[96,768]{1,0:T(8,128)(2,1)S(1)} %bitcast.333), channel_id=1, source_target_pairs={{0,16},{1,17},{2,18},{3,19},{4,20},{5,21},{6,22},{7,23},{8,24},{9,... | collective-permute-start | bytes 442376 | tf_op jit(solution)/shard_map/ppermute | solution.py:398
  28.8 9.8 %collective-permute-start.11 = (bf16[2,2,48,768]{3,2,1,0:T(8,128)(2,1)S(1)}, bf16[2,2,48,768]{3,2,1,0:T(8,128)(2,1)S(1)}, u32[]{:S(2)}, u32[]{:S(2)}) collective-permute-start(bf16[2,2,48,768]{3,2,1,0:T(8,128)(2,1)S(1)} %maximum_select_fusion.18), channel_id=1, source_target_pairs={{0,8},{1,9},{2,10},{3,11},{4,12},{5,13},{6,14},{7,15},{8,0},{9,1},... | collective-permute-start | bytes 884744 | tf_op jit(solution)/shard_map/ppermute | solution.py:398
  28.9 11.3 %collective-permute-start.2 = (bf16[2,2,56,768]{3,2,1,0:T(8,128)(2,1)S(1)}, bf16[2,2,56,768]{3,2,1,0:T(8,128)(2,1)S(1)}, u32[]{:S(2)}, u32[]{:S(2)}) collective-permute-start(bf16[2,2,56,768]{3,2,1,0:T(8,128)(2,1)S(1)} %maximum_select_fusion.16), channel_id=1, source_target_pairs={{0,4},{1,5},{2,6},{3,7},{4,0},{5,1},{6,2},{7,3},{8,12},{9,13},{10,... | collective-permute-start | bytes 1032200 | tf_op jit(solution)/shard_map/ppermute | solution.py:398
  34.8 9.4 %collective-permute-start.9 = (bf16[48,1536]{1,0:T(8,128)(2,1)S(1)}, bf16[48,1536]{1,0:T(8,128)(2,1)S(1)}, u32[]{:S(2)}, u32[]{:S(2)}) collective-permute-start(bf16[48,1536]{1,0:T(8,128)(2,1)S(1)} %pad_maximum_fusion.3), channel_id=1, source_target_pairs={{0,2},{1,3},{2,0},{3,1},{4,6},{5,7},{6,4},{7,5},{8,10},{9,11},{10,... | collective-permute-start | bytes 442376 | tf_op jit(solution)/shard_map/ppermute | solution.py:398
  38.7 13.7 %collective-permute-start.14 = (bf16[2,2,2,48,768]{4,3,2,1,0:T(8,128)(2,1)S(1)}, bf16[2,2,2,48,768]{4,3,2,1,0:T(8,128)(2,1)S(1)}, u32[]{:S(2)}, u32[]{:S(2)}) collective-permute-start(bf16[2,2,2,48,768]{4,3,2,1,0:T(8,128)(2,1)S(1)} %maximum_select_fusion.13), channel_id=1, source_target_pairs={{0,4},{1,5},{2,6},{3,7},{4,0},{5,1},{6,2},{7,3},{8,12},{9,13},{10,... | collective-permute-start | bytes 1769480 | tf_op jit(solution)/shard_map/ppermute | solution.py:398
  40.3 19.7 %collective-permute-start.3 = (bf16[2,2,2,56,768]{4,3,2,1,0:T(8,128)(2,1)S(1)}, bf16[2,2,2,56,768]{4,3,2,1,0:T(8,128)(2,1)S(1)}, u32[]{:S(2)}, u32[]{:S(2)}) collective-permute-start(bf16[2,2,2,56,768]{4,3,2,1,0:T(8,128)(2,1)S(1)} %maximum_select_fusion.11), channel_id=1, source_target_pairs={{0,2},{1,3},{2,0},{3,1},{4,6},{5,7},{6,4},{7,5},{8,10},{9,11},{10,... | collective-permute-start | bytes 2064392 | tf_op jit(solution)/shard_map/ppermute | solution.py:398
  41.0 12.6 %collective-permute-start.10 = (bf16[2,96,768]{2,1,0:T(8,128)(2,1)S(1)}, bf16[2,96,768]{2,1,0:T(8,128)(2,1)S(1)}, u32[]{:S(2)}, u32[]{:S(2)}) collective-permute-start(bf16[2,96,768]{2,1,0:T(8,128)(2,1)S(1)} %maximum_select_fusion.17), channel_id=1, source_target_pairs={{0,8},{1,9},{2,10},{3,11},{4,12},{5,13},{6,14},{7,15},{8,0},{9,1},... | collective-permute-start | bytes 884744 | tf_op jit(solution)/shard_map/ppermute | solution.py:398
  53.5 28.7 %collective-permute-start.15 = (bf16[16,48,768]{2,1,0:T(8,128)(2,1)}, bf16[16,48,768]{2,1,0:T(8,128)(2,1)}, u32[]{:S(2)}, u32[]{:S(2)}) collective-permute-start(bf16[16,48,768]{2,1,0:T(8,128)(2,1)} %bitcast.53), channel_id=1, source_target_pairs={{0,1},{1,0},{2,3},{3,2},{4,5},{5,4},{6,7},{7,6},{8,9},{9,8},{10,11... | collective-permute-start | bytes 3538952 | tf_op jit(solution)/shard_map/ppermute | solution.py:398
  54.4 20.5 %collective-permute-start.13 = (bf16[2,2,96,768]{3,2,1,0:T(8,128)(2,1)}, bf16[2,2,96,768]{3,2,1,0:T(8,128)(2,1)}, u32[]{:S(2)}, u32[]{:S(2)}) collective-permute-start(bf16[2,2,96,768]{3,2,1,0:T(8,128)(2,1)} %maximum_select_fusion.12), channel_id=1, source_target_pairs={{0,4},{1,5},{2,6},{3,7},{4,0},{5,1},{6,2},{7,3},{8,12},{9,13},{10,... | collective-permute-start | bytes 1769480 | tf_op jit(solution)/shard_map/ppermute | solution.py:398
  55.9 15.6 %collective-permute-start.18 = (bf16[2,192,384]{2,1,0:T(8,128)(2,1)S(1)}, bf16[2,192,384]{2,1,0:T(8,128)(2,1)}, u32[]{:S(2)}, u32[]{:S(2)}) collective-permute-start(bf16[2,192,384]{2,1,0:T(8,128)(2,1)S(1)} %maximum_select_fusion.20), channel_id=1, source_target_pairs={{0,8},{1,9},{2,10},{3,11},{4,12},{5,13},{6,14},{7,15},{8,0},{9,1},... | collective-permute-start | bytes 884744 | tf_op jit(solution)/shard_map/ppermute | solution.py:398
  56.3 17.2 %collective-permute-start.12 = (bf16[2,48,1536]{2,1,0:T(8,128)(2,1)S(1)}, bf16[2,48,1536]{2,1,0:T(8,128)(2,1)}, u32[]{:S(2)}, u32[]{:S(2)}) collective-permute-start(bf16[2,48,1536]{2,1,0:T(8,128)(2,1)S(1)} %maximum_select_fusion.19), channel_id=1, source_target_pairs={{0,16},{1,17},{2,18},{3,19},{4,20},{5,21},{6,22},{7,23},{8,24},{9,... | collective-permute-start | bytes 884744 | tf_op jit(solution)/shard_map/ppermute | solution.py:398
  61.5 26.1 %collective-permute-start.4 = (bf16[16,56,768]{2,0,1:T(8,128)(2,1)}, bf16[16,56,768]{2,0,1:T(8,128)(2,1)}, u32[]{:S(2)}, u32[]{:S(2)}) collective-permute-start(bf16[16,56,768]{2,0,1:T(8,128)(2,1)} %copy.63), channel_id=1, source_target_pairs={{0,1},{1,0},{2,3},{3,2},{4,5},{5,4},{6,7},{7,6},{8,9},{9,8},{10,11... | collective-permute-start | bytes 4128776 | tf_op jit(solution)/shard_map/ppermute | solution.py:398
  78.0 37.6 %collective-permute-start.20 = (bf16[2,2,2,96,768]{4,3,2,1,0:T(8,128)(2,1)}, bf16[2,2,2,96,768]{4,3,2,1,0:T(8,128)(2,1)}, u32[]{:S(2)}, u32[]{:S(2)}) collective-permute-start(bf16[2,2,2,96,768]{4,3,2,1,0:T(8,128)(2,1)} %maximum_select_fusion.7), channel_id=1, source_target_pairs={{0,2},{1,3},{2,0},{3,1},{4,6},{5,7},{6,4},{7,5},{8,10},{9,11},{10,... | collective-permute-start | bytes 3538952 | tf_op jit(solution)/shard_map/ppermute | solution.py:398
  78.5 20.8 %collective-permute-start.19 = (bf16[2,2,192,384]{3,2,1,0:T(8,128)(2,1)}, bf16[2,2,192,384]{3,2,1,0:T(8,128)(2,1)}, u32[]{:S(2)}, u32[]{:S(2)}) collective-permute-start(bf16[2,2,192,384]{3,2,1,0:T(8,128)(2,1)} %maximum_select_fusion.15), channel_id=1, source_target_pairs={{0,4},{1,5},{2,6},{3,7},{4,0},{5,1},{6,2},{7,3},{8,12},{9,13},{10,... | collective-permute-start | bytes 1769480 | tf_op jit(solution)/shard_map/ppermute | solution.py:398
  80.0 22.2 %collective-permute-start.16 = (bf16[2,2,48,1536]{3,2,1,0:T(8,128)(2,1)S(1)}, bf16[2,2,48,1536]{3,2,1,0:T(8,128)(2,1)}, u32[]{:S(2)}, u32[]{:S(2)}) collective-permute-start(bf16[2,2,48,1536]{3,2,1,0:T(8,128)(2,1)S(1)} %maximum_select_fusion.14), channel_id=1, source_target_pairs={{0,8},{1,9},{2,10},{3,11},{4,12},{5,13},{6,14},{7,15},{8,0},{9,1},... | collective-permute-start | bytes 1769480 | tf_op jit(solution)/shard_map/ppermute | solution.py:398
  118.8 28.7 %collective-permute-start.24 = (bf16[2,2,2,192,384]{4,3,2,1,0:T(8,128)(2,1)}, bf16[2,2,2,192,384]{4,3,2,1,0:T(8,128)(2,1)}, u32[]{:S(2)}, u32[]{:S(2)}) collective-permute-start(bf16[2,2,2,192,384]{4,3,2,1,0:T(8,128)(2,1)} %maximum_select_fusion.10), channel_id=1, source_target_pairs={{0,2},{1,3},{2,0},{3,1},{4,6},{5,7},{6,4},{7,5},{8,10},{9,11},{10,... | collective-permute-start | bytes 3538952 | tf_op jit(solution)/shard_map/ppermute | solution.py:398
  123.0 28.1 %collective-permute-start.22 = (bf16[2,2,2,48,1536]{4,3,2,1,0:T(8,128)(2,1)}, bf16[2,2,2,48,1536]{4,3,2,1,0:T(8,128)(2,1)S(1)}, u32[]{:S(2)}, u32[]{:S(2)}) collective-permute-start(bf16[2,2,2,48,1536]{4,3,2,1,0:T(8,128)(2,1)} %maximum_select_fusion.9), channel_id=1, source_target_pairs={{0,4},{1,5},{2,6},{3,7},{4,0},{5,1},{6,2},{7,3},{8,12},{9,13},{10,... | collective-permute-start | bytes 3538952 | tf_op jit(solution)/shard_map/ppermute | solution.py:398
  150.4 24.9 %collective-permute-start.25 = (bf16[16,192,384]{2,1,0:T(8,128)(2,1)S(1)}, bf16[16,192,384]{2,1,0:T(8,128)(2,1)}, u32[]{:S(2)}, u32[]{:S(2)}) collective-permute-start(bf16[16,192,384]{2,1,0:T(8,128)(2,1)S(1)} %bitcast.284), channel_id=1, source_target_pairs={{0,1},{1,0},{2,3},{3,2},{4,5},{5,4},{6,7},{7,6},{8,9},{9,8},{10,11... | collective-permute-start | bytes 7077896 | tf_op jit(solution)/shard_map/ppermute | solution.py:398
  152.9 22.4 %collective-permute-start.23 = (bf16[16,48,1536]{2,1,0:T(8,128)(2,1)}, bf16[16,48,1536]{2,1,0:T(8,128)(2,1)}, u32[]{:S(2)}, u32[]{:S(2)}) collective-permute-start(bf16[16,48,1536]{2,1,0:T(8,128)(2,1)} %bitcast.82), channel_id=1, source_target_pairs={{0,1},{1,0},{2,3},{3,2},{4,5},{5,4},{6,7},{7,6},{8,9},{9,8},{10,11... | collective-permute-start | bytes 7077896 | tf_op jit(solution)/shard_map/ppermute | solution.py:398
  199.8 7.9 %collective-permute-start.27 = (bf16[1,3072,384]{2,1,0:T(8,128)(2,1)}, bf16[1,3072,384]{2,1,0:T(8,128)(2,1)}, u32[]{:S(2)}, u32[]{:S(2)}) collective-permute-start(bf16[1,3072,384]{2,1,0:T(8,128)(2,1)} %bitcast.358), channel_id=1, source_target_pairs={{0,1},{1,0},{2,3},{3,2},{4,5},{5,4},{6,7},{7,6},{8,9},{9,8},{10,11... | collective-permute-start | bytes 7077896 | tf_op jit(solution)/shard_map/ppermute | solution.py:398
  200.4 11.5 %collective-permute-start.26 = (bf16[1,768,1536]{2,1,0:T(8,128)(2,1)}, bf16[1,768,1536]{2,1,0:T(8,128)(2,1)S(1)}, u32[]{:S(2)}, u32[]{:S(2)}) collective-permute-start(bf16[1,768,1536]{2,1,0:T(8,128)(2,1)} %bitcast.357), channel_id=1, source_target_pairs={{0,1},{1,0},{2,3},{3,2},{4,5},{5,4},{6,7},{7,6},{8,9},{9,8},{10,11... | collective-permute-start | bytes 7077896 | tf_op jit(solution)/shard_map/ppermute | solution.py:398
  216.7 28.7 %collective-permute-start.30 = (bf16[1,2,2,2,192,384]{5,4,3,2,1,0:T(8,128)(2,1)}, bf16[1,2,2,2,192,384]{5,4,3,2,1,0:T(8,128)(2,1)}, u32[]{:S(2)}, u32[]{:S(2)}) collective-permute-start(bf16[1,2,2,2,192,384]{5,4,3,2,1,0:T(8,128)(2,1)} %fusion.12), channel_id=1, source_target_pairs={{0,2},{1,3},{2,0},{3,1},{4,6},{5,7},{6,4},{7,5},{8,10},{9,11},{10,... | collective-permute-start | bytes 3538952 | tf_op jit(solution)/shard_map/ppermute | solution.py:398
  217.8 29.3 %collective-permute-start.29 = (bf16[1,2,2,2,48,1536]{5,4,3,2,1,0:T(8,128)(2,1)}, bf16[1,2,2,2,48,1536]{5,4,3,2,1,0:T(8,128)(2,1)}, u32[]{:S(2)}, u32[]{:S(2)}) collective-permute-start(bf16[1,2,2,2,48,1536]{5,4,3,2,1,0:T(8,128)(2,1)} %fusion.11), channel_id=1, source_target_pairs={{0,4},{1,5},{2,6},{3,7},{4,0},{5,1},{6,2},{7,3},{8,12},{9,13},{10,... | collective-permute-start | bytes 3538952 | tf_op jit(solution)/shard_map/ppermute | solution.py:398
  243.5 11.0 %collective-permute-start.28 = (bf16[4,16,24,768]{3,2,1,0:T(8,128)(2,1)S(1)}, bf16[4,16,24,768]{3,2,1,0:T(8,128)(2,1)S(1)}, u32[]{:S(2)}, u32[]{:S(2)}) collective-permute-start(bf16[4,16,24,768]{3,2,1,0:T(8,128)(2,1)S(1)} %get-tuple-element.190), channel_id=1, source_target_pairs={{0,1},{1,0},{2,3},{3,2},{4,5},{5,4},{6,7},{7,6},{8,9},{9,8},{10,11... | collective-permute-start | bytes 7077896 | tf_op jit(solution)/shard_map/ppermute | solution.py:398
  249.7 18.5 %collective-permute-start.32 = (bf16[1,2,2,192,384]{4,3,2,1,0:T(8,128)(2,1)S(1)}, bf16[1,2,2,192,384]{4,3,2,1,0:T(8,128)(2,1)}, u32[]{:S(2)}, u32[]{:S(2)}) collective-permute-start(bf16[1,2,2,192,384]{4,3,2,1,0:T(8,128)(2,1)S(1)} %fusion.29), channel_id=1, source_target_pairs={{0,4},{1,5},{2,6},{3,7},{4,0},{5,1},{6,2},{7,3},{8,12},{9,13},{10,... | collective-permute-start | bytes 1769480 | tf_op jit(solution)/shard_map/ppermute | solution.py:398
  251.1 22.0 %collective-permute-start.31 = (bf16[1,2,2,48,1536]{4,3,2,1,0:T(8,128)(2,1)}, bf16[1,2,2,48,1536]{4,3,2,1,0:T(8,128)(2,1)}, u32[]{:S(2)}, u32[]{:S(2)}) collective-permute-start(bf16[1,2,2,48,1536]{4,3,2,1,0:T(8,128)(2,1)} %fusion.28), channel_id=1, source_target_pairs={{0,8},{1,9},{2,10},{3,11},{4,12},{5,13},{6,14},{7,15},{8,0},{9,1},... | collective-permute-start | bytes 1769480 | tf_op jit(solution)/shard_map/ppermute | solution.py:398
  256.3 52.8 %collective-permute-start.35 = (bf16[4,2,2,2,24,768]{5,4,3,2,1,0:T(8,128)(2,1)}, bf16[4,2,2,2,24,768]{5,4,3,2,1,0:T(8,128)(2,1)}, u32[]{:S(2)}, u32[]{:S(2)}) collective-permute-start(bf16[4,2,2,2,24,768]{5,4,3,2,1,0:T(8,128)(2,1)} %fusion.13), channel_id=1, source_target_pairs={{0,2},{1,3},{2,0},{3,1},{4,6},{5,7},{6,4},{7,5},{8,10},{9,11},{10,... | collective-permute-start | bytes 3538952 | tf_op jit(solution)/shard_map/ppermute | solution.py:398
  275.1 18.1 %collective-permute-start.37 = (bf16[1,2,192,384]{3,2,1,0:T(8,128)(2,1)}, bf16[1,2,192,384]{3,2,1,0:T(8,128)(2,1)}, u32[]{:S(2)}, u32[]{:S(2)}) collective-permute-start(bf16[1,2,192,384]{3,2,1,0:T(8,128)(2,1)} %fusion.38), channel_id=1, source_target_pairs={{0,8},{1,9},{2,10},{3,11},{4,12},{5,13},{6,14},{7,15},{8,0},{9,1},... | collective-permute-start | bytes 884744 | tf_op jit(solution)/shard_map/ppermute | solution.py:398
  275.9 18.7 %collective-permute-start.36 = (bf16[1,2,48,1536]{3,2,1,0:T(8,128)(2,1)}, bf16[1,2,48,1536]{3,2,1,0:T(8,128)(2,1)}, u32[]{:S(2)}, u32[]{:S(2)}) collective-permute-start(bf16[1,2,48,1536]{3,2,1,0:T(8,128)(2,1)} %fusion.37), channel_id=1, source_target_pairs={{0,16},{1,17},{2,18},{3,19},{4,20},{5,21},{6,22},{7,23},{8,24},{9,... | collective-permute-start | bytes 884744 | tf_op jit(solution)/shard_map/ppermute | solution.py:398
  289.1 27.5 %collective-permute-start.34 = (bf16[2,16,24,768]{3,2,1,0:T(8,128)(2,1)}, bf16[2,16,24,768]{3,2,1,0:T(8,128)(2,1)}, u32[]{:S(2)}, u32[]{:S(2)}) collective-permute-start(bf16[2,16,24,768]{3,2,1,0:T(8,128)(2,1)} %get-tuple-element.197), channel_id=1, source_target_pairs={{0,1},{1,0},{2,3},{3,2},{4,5},{5,4},{6,7},{7,6},{8,9},{9,8},{10,11... | collective-permute-start | bytes 3538952 | tf_op jit(solution)/shard_map/ppermute | solution.py:398
  289.1 23.1 %collective-permute-start.33 = (bf16[2,16,24,768]{3,2,1,0:T(8,128)(2,1)}, bf16[2,16,24,768]{3,2,1,0:T(8,128)(2,1)}, u32[]{:S(2)}, u32[]{:S(2)}) collective-permute-start(bf16[2,16,24,768]{3,2,1,0:T(8,128)(2,1)} %get-tuple-element.200), channel_id=1, source_target_pairs={{0,1},{1,0},{2,3},{3,2},{4,5},{5,4},{6,7},{7,6},{8,9},{9,8},{10,11... | collective-permute-start | bytes 3538952 | tf_op jit(solution)/shard_map/ppermute | solution.py:398
  294.3 9.4 %collective-permute-start.51 = (bf16[1,192,384]{2,1,0:T(8,128)(2,1)S(1)}, bf16[1,192,384]{2,1,0:T(8,128)(2,1)S(1)}, u32[]{:S(2)}, u32[]{:S(2)}) collective-permute-start(bf16[1,192,384]{2,1,0:T(8,128)(2,1)S(1)} %fusion.44), channel_id=1, source_target_pairs={{0,16},{1,17},{2,18},{3,19},{4,20},{5,21},{6,22},{7,23},{8,24},{9,... | collective-permute-start | bytes 442376 | tf_op jit(solution)/shard_map/ppermute | solution.py:398
  295.7 8.2 %collective-permute-start.49 = (bf16[1,48,1536]{2,1,0:T(8,128)(2,1)S(1)}, bf16[1,48,1536]{2,1,0:T(8,128)(2,1)S(1)}, u32[]{:S(2)}, u32[]{:S(2)}) collective-permute-start(bf16[1,48,1536]{2,1,0:T(8,128)(2,1)S(1)} %fusion.43), channel_id=1, source_target_pairs={{0,2},{1,3},{2,0},{3,1},{4,6},{5,7},{6,4},{7,5},{8,10},{9,11},{10,... | collective-permute-start | bytes 442376 | tf_op jit(solution)/shard_map/ppermute | solution.py:398
  320.2 15.6 %collective-permute-start.38 = (bf16[2,2,2,2,24,768]{5,4,0,1,2,3:T(8,128)(2,1)}, bf16[2,2,2,2,24,768]{5,4,0,1,2,3:T(8,128)(2,1)}, u32[]{:S(2)}, u32[]{:S(2)}) collective-permute-start(bf16[2,2,2,2,24,768]{5,4,0,1,2,3:T(8,128)(2,1)} %fusion.32), channel_id=1, source_target_pairs={{0,2},{1,3},{2,0},{3,1},{4,6},{5,7},{6,4},{7,5},{8,10},{9,11},{10,... | collective-permute-start | bytes 1769480 | tf_op jit(solution)/shard_map/ppermute | solution.py:398
  321.3 16.5 %collective-permute-start.42 = (bf16[2,2,2,2,24,768]{5,4,0,3,1,2:T(8,128)(2,1)}, bf16[2,2,2,2,24,768]{5,4,0,3,1,2:T(8,128)(2,1)}, u32[]{:S(2)}, u32[]{:S(2)}) collective-permute-start(bf16[2,2,2,2,24,768]{5,4,0,3,1,2:T(8,128)(2,1)} %fusion.31), channel_id=1, source_target_pairs={{0,4},{1,5},{2,6},{3,7},{4,0},{5,1},{6,2},{7,3},{8,12},{9,13},{10,... | collective-permute-start | bytes 1769480 | tf_op jit(solution)/shard_map/ppermute | solution.py:398
  321.9 28.6 %collective-permute-start.46 = (bf16[4,2,2,24,768]{4,3,2,1,0:T(8,128)(2,1)}, bf16[4,2,2,24,768]{4,3,2,1,0:T(8,128)(2,1)}, u32[]{:S(2)}, u32[]{:S(2)}) collective-permute-start(bf16[4,2,2,24,768]{4,3,2,1,0:T(8,128)(2,1)} %fusion.30), channel_id=1, source_target_pairs={{0,4},{1,5},{2,6},{3,7},{4,0},{5,1},{6,2},{7,3},{8,12},{9,13},{10,... | collective-permute-start | bytes 1769480 | tf_op jit(solution)/shard_map/ppermute | solution.py:398
  337.0 18.5 %collective-permute-start.39 = (bf16[2,2,2,24,768]{4,3,0,1,2:T(8,128)(2,1)S(1)}, bf16[2,2,2,24,768]{4,3,0,1,2:T(8,128)(2,1)S(1)}, u32[]{:S(2)}, u32[]{:S(2)}) collective-permute-start(bf16[2,2,2,24,768]{4,3,0,1,2:T(8,128)(2,1)S(1)} %fusion.39), channel_id=1, source_target_pairs={{0,4},{1,5},{2,6},{3,7},{4,0},{5,1},{6,2},{7,3},{8,12},{9,13},{10,... | collective-permute-start | bytes 884744 | tf_op jit(solution)/shard_map/ppermute | solution.py:398
  339.1 16.5 %collective-permute-start.43 = (bf16[2,2,2,24,768]{4,3,0,2,1:T(8,128)(2,1)S(1)}, bf16[2,2,2,24,768]{4,3,0,2,1:T(8,128)(2,1)S(1)}, u32[]{:S(2)}, u32[]{:S(2)}) collective-permute-start(bf16[2,2,2,24,768]{4,3,0,2,1:T(8,128)(2,1)S(1)} %fusion.40), channel_id=1, source_target_pairs={{0,8},{1,9},{2,10},{3,11},{4,12},{5,13},{6,14},{7,15},{8,0},{9,1},... | collective-permute-start | bytes 884744 | tf_op jit(solution)/shard_map/ppermute | solution.py:398
  351.7 11.6 %collective-permute-start.47 = (bf16[4,2,24,768]{3,2,1,0:T(8,128)(2,1)S(1)}, bf16[4,2,24,768]{3,2,1,0:T(8,128)(2,1)S(1)}, u32[]{:S(2)}, u32[]{:S(2)}) collective-permute-start(bf16[4,2,24,768]{3,2,1,0:T(8,128)(2,1)S(1)} %fusion.41), channel_id=1, source_target_pairs={{0,8},{1,9},{2,10},{3,11},{4,12},{5,13},{6,14},{7,15},{8,0},{9,1},... | collective-permute-start | bytes 884744 | tf_op jit(solution)/shard_map/ppermute | solution.py:398
  355.6 9.5 %collective-permute-start.40 = (bf16[2,2,24,768]{3,2,0,1:T(8,128)(2,1)S(1)}, bf16[2,2,24,768]{3,2,0,1:T(8,128)(2,1)S(1)}, u32[]{:S(2)}, u32[]{:S(2)}) collective-permute-start(bf16[2,2,24,768]{3,2,0,1:T(8,128)(2,1)S(1)} %fusion.45), channel_id=1, source_target_pairs={{0,8},{1,9},{2,10},{3,11},{4,12},{5,13},{6,14},{7,15},{8,0},{9,1},... | collective-permute-start | bytes 442376 | tf_op jit(solution)/shard_map/ppermute | solution.py:398
  355.7 15.5 %collective-permute-start.44 = (bf16[2,2,24,768]{3,2,0,1:T(8,128)(2,1)S(1)}, bf16[2,2,24,768]{3,2,0,1:T(8,128)(2,1)S(1)}, u32[]{:S(2)}, u32[]{:S(2)}) collective-permute-start(bf16[2,2,24,768]{3,2,0,1:T(8,128)(2,1)S(1)} %fusion.46), channel_id=1, source_target_pairs={{0,16},{1,17},{2,18},{3,19},{4,20},{5,21},{6,22},{7,23},{8,24},{9,... | collective-permute-start | bytes 442376 | tf_op jit(solution)/shard_map/ppermute | solution.py:398
  363.4 9.8 %collective-permute-start.48 = (bf16[4,24,768]{2,1,0:T(8,128)(2,1)S(1)}, bf16[4,24,768]{2,1,0:T(8,128)(2,1)S(1)}, u32[]{:S(2)}, u32[]{:S(2)}) collective-permute-start(bf16[4,24,768]{2,1,0:T(8,128)(2,1)S(1)} %fusion.47), channel_id=1, source_target_pairs={{0,16},{1,17},{2,18},{3,19},{4,20},{5,21},{6,22},{7,23},{8,24},{9,... | collective-permute-start | bytes 442376 | tf_op jit(solution)/shard_map/ppermute | solution.py:398
  365.2 8.9 %collective-permute-start.41 = (bf16[2,24,768]{2,1,0:T(8,128)(2,1)S(1)}, bf16[2,24,768]{2,1,0:T(8,128)(2,1)S(1)}, u32[]{:S(2)}, u32[]{:S(2)}) collective-permute-start(bf16[2,24,768]{2,1,0:T(8,128)(2,1)S(1)} %fusion.50), channel_id=1, source_target_pairs={{0,16},{1,17},{2,18},{3,19},{4,20},{5,21},{6,22},{7,23},{8,24},{9,... | collective-permute-start | bytes 221192 | tf_op jit(solution)/shard_map/ppermute | solution.py:398
  (103 other events, 679.3 us)

commit v3 on v2

--- a/solution.py
+++ b/solution.py
@@ -43,22 +43,6 @@
     return (level_count[..., None] == jnp.arange(BUCKETS, dtype=jnp.int32)).astype(number_type)
 
 
-def rms_norm(hidden, gain_row):
-    return (
-        hidden * lax.rsqrt(jnp.mean(hidden * hidden, axis=-1, keepdims=True) + EPSILON) * gain_row
-    )
-
-
-def project(left_side, right_side):
-    return jnp.dot(left_side, right_side, preferred_element_type=jnp.float32)
-
-
-def project_back(gradient, right_side):
-    return lax.dot_general(
-        gradient, right_side, (((1,), (1,)), ((), ())), preferred_element_type=jnp.float32
-    )
-
-
 def weight_grad(left_side, gradient):
     return lax.dot_general(
         left_side, gradient, (((0,), (0,)), ((), ())), preferred_element_type=jnp.float32
@@ -69,7 +53,6 @@
 GROUP = LANES // HEAD
 CUT = 256
 VMEM_BYTES = 56 * 1024 * 1024
-COST = pl.CostEstimate(flops=1000, bytes_accessed=1000, transcendentals=0)
 
 NT = (((1,), (1,)), ((), ()))
 TN = (((0,), (0,)), ((), ()))
@@ -113,14 +96,15 @@
     return jnp.concatenate(columns, axis=1)
 
 
-def attend_kernel(causal, q_ref, k_ref, v_ref, mask_ref, line_ref, probs_ref, out_ref):
+def attend_pair(causal, pair, q_ref, k_ref, v_ref, mask_ref, line_ref, probs_ref, out_ref):
     rows = q_ref.shape[0]
+    lanes = pl.ds(pl.multiple_of(pair * LANES, LANES), LANES)
     biases = [near_bias(line_ref, head) for head in range(GROUP)] if causal else None
     for at, depth in spans(rows, causal):
-        keys, values = k_ref[:depth], v_ref[:depth]
+        keys, values = k_ref[:depth, lanes], v_ref[:depth, lanes]
         total = jnp.zeros((CUT, LANES), jnp.float32)
         for head in range(GROUP):
-            query = only_head(q_ref[at : at + CUT], head, HEAD**-0.5)
+            query = only_head(q_ref[at : at + CUT, lanes], head, HEAD**-0.5)
             scores = dot(keys, query, NT)
             if causal:
                 scores = add_bias(scores, biases[head], at)
@@ -130,7 +114,7 @@
             low = weights.astype(jnp.bfloat16)
             probs_ref[head, :depth, at : at + CUT] = low
             total = total + dot(low, values, TN) * lane_mask(head)
-        out_ref[at : at + CUT] = total.astype(jnp.bfloat16)
+        out_ref[at : at + CUT, lanes] = total.astype(jnp.bfloat16)
 
 
 def diagonal_sums(block):
@@ -145,12 +129,12 @@
     return jnp.sum(total, axis=0, keepdims=True)
 
 
-def attend_back_kernel(causal, q_ref, k_ref, v_ref, g_ref, probs_ref, *rest):
-    if causal:
-        dq_ref, dk_ref, dv_ref, sums_ref, dk_sum, dv_sum = rest
-    else:
-        dq_ref, dk_ref, dv_ref, dk_sum, dv_sum = rest
+def attend_back_pair(
+    causal, pair, q_ref, k_ref, v_ref, g_ref, probs_ref, dq_ref, dk_ref, dv_ref, sums_ref,
+    dk_sum, dv_sum,
+):
     rows = q_ref.shape[0]
+    lanes = pl.ds(pl.multiple_of(pair * LANES, LANES), LANES)
     dk_sum[...] = jnp.zeros_like(dk_sum)
     dv_sum[...] = jnp.zeros_like(dv_sum)
     near = [[], []]
@@ -158,12 +142,12 @@
     for at, depth in spans(rows, causal):
         dq = jnp.zeros((CUT, LANES), jnp.float32)
         for head in range(GROUP):
-            grad = only_head(g_ref[at : at + CUT], head, 1.0)
-            query = only_head(q_ref[at : at + CUT], head, HEAD**-0.5)
-            keys = only_head(k_ref[:depth], head, HEAD**-0.5)
+            grad = only_head(g_ref[at : at + CUT, lanes], head, 1.0)
+            query = only_head(q_ref[at : at + CUT, lanes], head, HEAD**-0.5)
+            keys = only_head(k_ref[:depth, lanes], head, HEAD**-0.5)
             low = probs_ref[head, :depth, at : at + CUT]
             probs = low.astype(jnp.float32)
-            scaled = probs * dot(v_ref[:depth], grad, NT)
+            scaled = probs * dot(v_ref[:depth, lanes], grad, NT)
             centre = jnp.sum(scaled, axis=0, keepdims=True)
             grad_scores = (scaled - probs * centre).astype(jnp.bfloat16)
             dv_sum[:depth] += dot(low, grad)
@@ -181,9 +165,9 @@
                     near[head].append((column[own : own + LANES], before))
                     if own > LANES:
                         far[head].append(jnp.sum(column[: own - LANES], axis=0, keepdims=True))
-        dq_ref[at : at + CUT] = dq.astype(jnp.bfloat16)
-    dk_ref[...] = dk_sum[...].astype(jnp.bfloat16)
-    dv_ref[...] = dv_sum[...].astype(jnp.bfloat16)
+        dq_ref[at : at + CUT, lanes] = dq.astype(jnp.bfloat16)
+    dk_ref[:, lanes] = dk_sum[...].astype(jnp.bfloat16)
+    dv_ref[:, lanes] = dv_sum[...].astype(jnp.bfloat16)
     if causal:
         lines = []
         for head in range(GROUP):
@@ -195,55 +179,6 @@
             lines.append(jnp.concatenate([line, jnp.zeros_like(line)], axis=1))
         lines.append(jnp.zeros((8 - len(lines), 2 * LANES), jnp.float32))
         sums_ref[0] = jnp.concatenate(lines, axis=0)
-
-
-def head_spec(rows):
-    return pl.BlockSpec((rows, LANES), lambda pair: (0, pair))
-
-
-def probs_spec(rows):
-    return pl.BlockSpec((GROUP, rows, rows), lambda pair: (pair, 0, 0))
-
-
-def attend_forward(query, keys, values, mask, lines, causal):
-    rows = query.shape[0]
-    return pl.pallas_call(
-        functools.partial(attend_kernel, causal),
-        grid=(HEADS // GROUP,),
-        in_specs=[head_spec(rows)] * 3
-        + [
-            pl.BlockSpec((rows, rows), lambda pair: (0, 0)),
-            pl.BlockSpec((1, 8, 2 * LANES), lambda pair: (pair, 0, 0)),
-        ],
-        out_specs=[probs_spec(rows), head_spec(rows)],
-        out_shape=[
-            jax.ShapeDtypeStruct((HEADS, rows, rows), jnp.bfloat16),
-            jax.ShapeDtypeStruct(query.shape, jnp.bfloat16),
-        ],
-        compiler_params=pltpu.CompilerParams(vmem_limit_bytes=VMEM_BYTES),
-        cost_estimate=COST,
-        name="attend",
-    )(query, keys, values, mask, lines)
-
-
-def attend_backward(query, keys, values, grad, probs, causal):
-    rows = query.shape[0]
-    out_specs = [head_spec(rows)] * 3
-    out_shape = [jax.ShapeDtypeStruct(query.shape, jnp.bfloat16)] * 3
-    if causal:
-        out_specs.append(pl.BlockSpec((1, 8, 2 * LANES), lambda pair: (pair, 0, 0)))
-        out_shape.append(jax.ShapeDtypeStruct((HEADS // GROUP, 8, 2 * LANES), jnp.float32))
-    return pl.pallas_call(
-        functools.partial(attend_back_kernel, causal),
-        grid=(HEADS // GROUP,),
-        in_specs=[head_spec(rows)] * 4 + [probs_spec(rows)],
-        out_specs=out_specs,
-        out_shape=out_shape,
-        scratch_shapes=[pltpu.VMEM((rows, LANES), jnp.float32)] * 2,
-        compiler_params=pltpu.CompilerParams(vmem_limit_bytes=VMEM_BYTES),
-        cost_estimate=COST,
-        name="attend_back",
-    )(query, keys, values, grad, probs)
 
 
 def self_mask(segment, key_valid):
@@ -370,9 +305,196 @@
             jax.ShapeDtypeStruct((FF, half), jnp.bfloat16),
         ],
         compiler_params=pltpu.CompilerParams(vmem_limit_bytes=VMEM_BYTES),
-        cost_estimate=COST,
+
         name="ffn",
     )(core[None], third, upper, cotangent, w_in, other_in, w_out, other_out)
+
+
+def scale_of(hidden):
+    return lax.rsqrt(jnp.mean(hidden * hidden, axis=-1, keepdims=True) + EPSILON)
+
+
+def norm_back(hidden, gain, grad):
+    scale = scale_of(hidden)
+    grown = grad * gain
+    inner = jnp.mean(grown * hidden, axis=-1, keepdims=True)
+    gain_grad = jnp.sum(grad * (hidden * scale), axis=0, keepdims=True)
+    return scale * grown - hidden * (scale * scale * scale * inner), gain_grad
+
+
+def fused(kernel, outs, *args):
+    space = pl.BlockSpec(memory_space=pltpu.VMEM)
+    return pl.pallas_call(
+        kernel,
+        in_specs=[space] * len(args),
+        out_specs=[space] * len(outs),
+        out_shape=[jax.ShapeDtypeStruct(shape, held_as) for shape, held_as in outs],
+        compiler_params=pltpu.CompilerParams(vmem_limit_bytes=VMEM_BYTES),
+
+        name=kernel.__name__,
+    )(*args)
+
+
+PAIRS = HEADS // GROUP
+
+
+def whole_spec(array, space=None):
+    rank = len(array.shape)
+    return pl.BlockSpec(array.shape, lambda pair: (0,) * rank, pipeline_mode=space)
+
+
+def by_pair(kernel, args, outs, scratch, by_step, name):
+    held = [jax.ShapeDtypeStruct(shape, held_as) for shape, held_as in outs]
+
+    def spec(array, once):
+        if len(array.shape) == 3 and array.shape in by_step:
+            block = (array.shape[0] // PAIRS,) + array.shape[1:]
+            return pl.BlockSpec(block, lambda pair: (pair, 0, 0))
+        if array.shape == (1,):
+            return pl.BlockSpec(memory_space=pltpu.SMEM)
+        return whole_spec(array, pl.Buffered(1) if once else None)
+
+    return pl.pallas_call(
+        kernel,
+        grid=(PAIRS,),
+        in_specs=[spec(array, True) for array in args],
+        out_specs=[spec(array, False) for array in held],
+        out_shape=held,
+        scratch_shapes=scratch,
+        compiler_params=pltpu.CompilerParams(vmem_limit_bytes=VMEM_BYTES),
+        name=name,
+    )(*args)
+
+
+def self_part(
+    tokens_ref, gain_ref, wq_ref, wk_ref, wv_ref, mask_ref, line_ref,
+    first_ref, q_ref, k_ref, v_ref, probs_ref, mixed_ref,
+):
+    pair = pl.program_id(0)
+
+    @pl.when(pair == 0)
+    def _():
+        hidden = tokens_ref[...].astype(jnp.float32)
+        first = (hidden * scale_of(hidden) * gain_ref[...]).astype(jnp.bfloat16)
+        first_ref[...] = first
+        for weight, result in ((wq_ref, q_ref), (wk_ref, k_ref), (wv_ref, v_ref)):
+            result[...] = dot(first, weight[...]).astype(jnp.bfloat16)
+
+    attend_pair(True, pair, q_ref, k_ref, v_ref, mask_ref, line_ref, probs_ref, mixed_ref)
+
+
+def cross_part(
+    tokens_ref, mixed_ref, memory_ref, gain_ref, wso_ref, wq_ref, wk_ref, wv_ref, wo_ref,
+    next_gain_ref, mask_ref,
+    middle_ref, second_ref, q_ref, k_ref, v_ref, probs_ref, crossed_ref, upper_ref, third_ref,
+):
+    pair = pl.program_id(0)
+
+    @pl.when(pair == 0)
+    def _():
+        middle = tokens_ref[...].astype(jnp.float32) + dot(mixed_ref[...], wso_ref[...])
+        middle_ref[...] = middle
+        second = (middle * scale_of(middle) * gain_ref[...]).astype(jnp.bfloat16)
+        second_ref[...] = second
+        q_ref[...] = dot(second, wq_ref[...]).astype(jnp.bfloat16)
+        k_ref[...] = dot(memory_ref[...], wk_ref[...]).astype(jnp.bfloat16)
+        v_ref[...] = dot(memory_ref[...], wv_ref[...]).astype(jnp.bfloat16)
+
+    attend_pair(False, pair, q_ref, k_ref, v_ref, mask_ref, None, probs_ref, crossed_ref)
+
+    @pl.when(pair == PAIRS - 1)
+    def _():
+        upper = middle_ref[...] + dot(crossed_ref[...], wo_ref[...])
+        upper_ref[...] = upper
+        third = upper * scale_of(upper) * next_gain_ref[...]
+        third_ref[...] = third.astype(jnp.bfloat16)
+
+
+def third_back(
+    gthird_ref, upper_ref, cot_ref, gain_ref, wo_ref, gupper_ref, branch_ref, gmix_ref, ggain_ref
+):
+    grad, ggain_ref[...] = norm_back(upper_ref[...], gain_ref[...], gthird_ref[...])
+    grad = cot_ref[...].astype(jnp.float32) + grad
+    gupper_ref[...] = grad
+    low = grad.astype(jnp.bfloat16)
+    branch_ref[...] = low
+    gmix_ref[...] = dot(low, wo_ref[...], NT).astype(jnp.bfloat16)
+
+
+def last_back(
+    gq_ref, gk_ref, gv_ref, gmk_ref, gmv_ref, tokens_ref, gmiddle_ref, gain_ref,
+    wq_ref, wk_ref, wv_ref, wmk_ref, wmv_ref,
+    gtokens_ref, gmemory_ref, ggain_ref,
+):
+    gmemory_ref[...] = dot(gmk_ref[...], wmk_ref[...], NT) + dot(gmv_ref[...], wmv_ref[...], NT)
+    gfirst = dot(gq_ref[...], wq_ref[...], NT) + dot(gk_ref[...], wk_ref[...], NT)
+    gfirst = gfirst + dot(gv_ref[...], wv_ref[...], NT)
+    hidden = tokens_ref[...].astype(jnp.float32)
+    grad, ggain_ref[...] = norm_back(hidden, gain_ref[...], gfirst)
+    gtokens_ref[...] = gmiddle_ref[...] + grad
+
+
+def put_products(core_ref, rows, pairs, sent_ref, kept_ref):
+    for k, (left, right) in enumerate(pairs):
+        grads = dot(left[...], right[...], TN)
+        if kept_ref is None:
+            sent_ref[k] = grads.astype(jnp.bfloat16)
+        else:
+            grads = grads.reshape(-1, 2, rows, D)
+            even, odd = grads[:, 0].reshape(-1, D), grads[:, 1].reshape(-1, D)
+            first = core_ref[0] == 0
+            sent_ref[k] = jnp.where(first, odd, even).astype(jnp.bfloat16)
+            kept_ref[k] = jnp.where(first, even, odd).astype(jnp.bfloat16)
+
+
+def cross_back(
+    rows, core_ref, q_ref, k_ref, v_ref, gcrossed_ref, probs_ref,
+    second_ref, memory_ref, crossed_ref, gcross_ref, middle_ref, gupper_ref, gain_ref,
+    wq_ref, wso_ref,
+    gk_ref, gv_ref, gmiddle_ref, branch_ref, gmix_ref, ggain_ref, sent_ref, *rest,
+):
+    kept_ref, (gq_ref, dk_sum, dv_sum) = rest[0] if len(rest) == 4 else None, rest[-3:]
+    pair = pl.program_id(0)
+    attend_back_pair(
+        False, pair, q_ref, k_ref, v_ref, gcrossed_ref, probs_ref, gq_ref, gk_ref, gv_ref, None,
+        dk_sum, dv_sum,
+    )
+
+    @pl.when(pair == PAIRS - 1)
+    def _():
+        pairs = [
+            (second_ref, gq_ref),
+            (memory_ref, gk_ref),
+            (memory_ref, gv_ref),
+            (crossed_ref, gcross_ref),
+        ]
+        put_products(core_ref, rows, pairs, sent_ref, kept_ref)
+        gsecond = dot(gq_ref[...], wq_ref[...], NT)
+        grad, ggain_ref[...] = norm_back(middle_ref[...], gain_ref[...], gsecond)
+        grad = gupper_ref[...] + grad
+        gmiddle_ref[...] = grad
+        low = grad.astype(jnp.bfloat16)
+        branch_ref[...] = low
+        gmix_ref[...] = dot(low, wso_ref[...], NT).astype(jnp.bfloat16)
+
+
+def self_back(
+    rows, core_ref, q_ref, k_ref, v_ref, gmixed_ref, probs_ref, first_ref, mixed_ref, gself_ref,
+    gq_ref, gk_ref, gv_ref, sums_ref, late_sent_ref, early_sent_ref, *rest,
+):
+    kept, (dk_sum, dv_sum) = rest[:2] if len(rest) == 4 else (None, None), rest[-2:]
+    pair = pl.program_id(0)
+    attend_back_pair(
+        True, pair, q_ref, k_ref, v_ref, gmixed_ref, probs_ref, gq_ref, gk_ref, gv_ref, sums_ref,
+        dk_sum, dv_sum,
+    )
+
+    @pl.when(pair == PAIRS - 1)
+    def _():
+        late = [(first_ref, gv_ref), (mixed_ref, gself_ref)]
+        early = [(first_ref, gq_ref), (first_ref, gk_ref)]
+        put_products(core_ref, rows, late, late_sent_ref, kept[0])
+        put_products(core_ref, rows, early, early_sent_ref, kept[1])
 
 
 AXES = ("wide", "narrow")
@@ -427,35 +549,25 @@
         self.cube, self.value, self.plan, self.steps = cube, value, plan, 0
 
     def send(self, *behind):
-        self.value = after(self.value, *behind)
-        self.theirs = self.cube.send_step(self.value, self.plan, self.steps)
+        sent = after(self.value, *behind) if behind else self.value
+        self.theirs = self.cube.send_step(sent, self.plan, self.steps)
+        return sent
 
     def take(self, *behind):
-        value = after(self.value, *behind) if behind else self.value
-        self.value = self.cube.place_step(value, self.theirs, self.plan, self.steps)
+        theirs = after(self.theirs, *behind) if behind else self.theirs
+        self.value = self.cube.place_step(self.value, theirs, self.plan, self.steps)
         self.steps += 1
         return self.value
 
 
 def pair_weights(cube, w_in, w_out):
-    rows = w_in.shape[0]
     core = cube.bit(0)
-    count = FF // D
-    in_rows = jnp.stack([w_in[:, k * D // 2 : (k + 1) * D // 2] for k in range(2 * count)])
-
-    def packed(whose):
-        in_half = lax.dynamic_slice_in_dim(in_rows, whose * count, count, 0)
-        return [in_half, cube.half(w_out, whose)]
-
-    mine = packed(core)
-    sent = [part.reshape(-1, D // 2) for part in packed(1 - core)]
-    other = cube.swap(jnp.concatenate(sent, axis=0), 1)
-    size = count * rows
-    theirs = [other[:size].reshape(mine[0].shape), other[size:]]
-    in_pair, out_pair = [
-        cube.place(ours, others, 0, ours.ndim - 2, True) for ours, others in zip(mine, theirs)
+    return [
+        cube.place(
+            cube.half(part, core), cube.swap(cube.half(part, 1 - core), 1), 0, 0, True
+        )
+        for part in (w_in, w_out)
     ]
-    return jnp.concatenate([in_pair[k] for k in range(count)], axis=1), out_pair
 
 
 def both_halves(cube, value):
@@ -474,23 +586,27 @@
 class Sums:
     def __init__(self, cube, plan, sent, kept):
         self.cube, self.plan, self.steps = cube, plan, 0
-        self.kept, self.theirs = kept, cube.swap(sent, 1)
+        self.shape = (kept.shape[0],) + (2,) * len(plan) + (-1, kept.shape[-1])
+        self.terms, self.theirs = [kept.reshape(self.shape)], cube.swap(sent, 1)
 
     def take(self, *behind):
-        kept = after(self.kept, *behind) if behind else self.kept
-        value = kept.astype(jnp.float32) + self.theirs.astype(jnp.float32)
+        theirs = after(self.theirs, *behind) if behind else self.theirs
         if self.steps == 0:
-            shape = (value.shape[0],) + (2,) * len(self.plan) + (-1, value.shape[-1])
-            value = value.reshape(shape)
-        self.value = value
+            theirs = theirs.reshape(self.shape)
+        self.terms.append(theirs)
+
+    def value(self):
+        return sum(term.astype(jnp.float32) for term in self.terms)
 
     def send(self, *behind):
         which = self.plan[-1 - self.steps]
         axis = 1 + sum(other > which for other in self.plan[: len(self.plan) - self.steps])
         mine = self.cube.bit(which)
-        sent = lax.dynamic_index_in_dim(self.value, 1 - mine, axis, False).astype(jnp.bfloat16)
-        sent = after(sent, *behind)
-        self.kept = lax.dynamic_index_in_dim(self.value, mine, axis, False)
+        whole = self.terms
+        self.terms = [lax.dynamic_index_in_dim(term, 1 - mine, axis, False) for term in whole]
+        sent = self.value().astype(jnp.bfloat16)
+        sent = after(sent, *behind) if behind else sent
+        self.terms = [lax.dynamic_index_in_dim(term, mine, axis, False) for term in whole]
         self.theirs = self.cube.swap(sent, 1 << which)
         self.steps += 1
         return sent
@@ -499,13 +615,24 @@
         return self.steps < len(self.plan)
 
 
-def product_sums(cube, plan, pairs):
-    grads = jnp.stack([weight_grad(left, right).astype(jnp.bfloat16) for left, right in pairs])
-    grads = grads.reshape(len(pairs), cube.count // 2, 2, -1, D)
-    core = cube.bit(0)
-    sent = lax.dynamic_index_in_dim(grads, 1 - core, 2, False)
-    kept = lax.dynamic_index_in_dim(grads, core, 2, False)
-    return Sums(cube, plan, sent, kept)
+def whole_tiles(cube):
+    return (D // cube.count) % 8 == 0
+
+
+def product_outs(cube, count):
+    if whole_tiles(cube):
+        return [((count, D // 2, D), jnp.bfloat16)] * 2
+    return [((count, D, D), jnp.bfloat16)]
+
+
+def product_sums(cube, plan, parts, *behind):
+    chips, rows = cube.count // 2, D // cube.count
+    if len(parts) == 1:
+        grads = parts[0].reshape(-1, chips, 2, rows, D)
+        core = cube.bit(0)
+        parts = [lax.dynamic_index_in_dim(grads, core ^ k, 2, False) for k in (1, 0)]
+    sent, kept = [part.reshape(-1, chips, rows, D) for part in parts]
+    return Sums(cube, plan, after(sent, *behind) if behind else sent, kept)
 
 
 def half_swap(cube, value):
@@ -552,27 +679,27 @@
     for step in range(last):
         one.take()
         two.take()
-        one.send()
-        two.send()
+        ahead = one.send(), two.send()
         if step > 0:
-            three.take()
-        three.send(one.value, two.value)
+            three.take(*ahead)
+        ahead = ahead + (three.send(*ahead),)
         if step > 1:
-            inner_half.take()
-            outer_half.take()
+            inner_half.take(*ahead)
+            outer_half.take(*ahead)
         if step > 0:
-            inner_half.send(three.value)
-            outer_half.send(three.value)
+            inner_half.send(*ahead)
+            outer_half.send(*ahead)
     one.take()
     two.take()
     first_halves = both_halves(cube, one.value)
     second_halves = both_halves(cube, two.value)
-    three.take()
-    three.send(one.value, two.value)
-    inner_half.take()
-    outer_half.take()
-    inner_half.send(three.value)
-    outer_half.send(three.value)
+    ahead = first_halves[0], second_halves[0]
+    three.take(*ahead)
+    ahead = ahead + (three.send(*ahead),)
+    inner_half.take(*ahead)
+    outer_half.take(*ahead)
+    inner_half.send(*ahead)
+    outer_half.send(*ahead)
     attn_full = whole_weights(cube, first_halves, 0, 2)
     attn_full = attn_full + whole_weights(cube, second_halves, 0, 2)
     gain_full = cube.place(
@@ -584,37 +711,39 @@
     see_cross = cross_mask(segment, enc_segments[0])
     lines = bias_lines(rel_table)
 
-    residual = tokens.astype(jnp.float32)
-    normed_first, norm_back_first = jax.vjp(rms_norm, residual, gain_full[0].astype(jnp.float32))
-    first_low = normed_first.astype(jnp.bfloat16)
-    query = project(first_low, attn_full[0]).astype(jnp.bfloat16)
-    keys = project(first_low, attn_full[1]).astype(jnp.bfloat16)
-    values = project(first_low, attn_full[2]).astype(jnp.bfloat16)
-    inner_half.take(query, keys, values)
-    outer_half.take(query, keys, values)
-    query = after(query, inner_half.value, outer_half.value)
+    tile, low, full = tokens.shape, jnp.bfloat16, jnp.float32
+    gain_one, gain_two, gain_three = [gain_full[k : k + 1].astype(full) for k in range(3)]
+    probs = (HEADS, segment.shape[0], segment.shape[0])
+    first_low, query, keys, values, self_probs, mixed_low = by_pair(
+        self_part,
+        [tokens, gain_one, *attn_full[:3], see_self, lines],
+        [(tile, low)] * 4 + [(probs, low), (tile, low)],
+        [],
+        (probs, lines.shape),
+        "self_part",
+    )
+    three.take(mixed_low)
+    cross_halves = both_halves(cube, three.value)
+    inner_half.take(mixed_low)
+    outer_half.take(mixed_low)
     inner_half.send()
     outer_half.send()
-    self_probs, mixed_low = attend_forward(query, keys, values, see_self, lines, True)
-    three.take(mixed_low)
-    attn_full = attn_full + whole_weights(cube, both_halves(cube, three.value), 0, 4)
-    middle = residual + project(mixed_low, attn_full[3])
-    normed_second, norm_back_second = jax.vjp(rms_norm, middle, gain_full[1].astype(jnp.float32))
-    second_low = normed_second.astype(jnp.bfloat16)
-    cross_query = project(second_low, attn_full[4]).astype(jnp.bfloat16)
-    memory_keys = project(memory, attn_full[5]).astype(jnp.bfloat16)
-    memory_values = project(memory, attn_full[6]).astype(jnp.bfloat16)
-    inner_half.take(cross_query)
-    outer_half.take(cross_query)
-    cross_query = after(cross_query, inner_half.value, outer_half.value)
+    attn_full = attn_full + whole_weights(cube, cross_halves, 0, 4)
+    (
+        middle, second_low, cross_query, memory_keys, memory_values, cross_probs, crossed_low,
+        upper, third_low,
+    ) = by_pair(
+        cross_part,
+        [tokens, mixed_low, memory, gain_two, *attn_full[3:], gain_three, see_cross],
+        [(tile, full)] + [(tile, low)] * 4 + [(probs, low), (tile, low), (tile, full), (tile, low)],
+        [],
+        (probs,),
+        "cross_part",
+    )
+    inner_half.take(third_low)
+    outer_half.take(third_low)
     own_in, other_in = both_halves(cube, inner_half.value)
     own_out, other_out = both_halves(cube, outer_half.value)
-    cross_probs, crossed_low = attend_forward(
-        cross_query, memory_keys, memory_values, see_cross, lines, False
-    )
-    upper = middle + project(crossed_low, attn_full[7])
-    normed_third, norm_back_third = jax.vjp(rms_norm, upper, gain_full[2].astype(jnp.float32))
-    third_low = normed_third.astype(jnp.bfloat16)
     layer_out, grad_third, grad_in, other_grad_in, grad_out, other_grad_out = ffn(
         core,
         third_low,
@@ -627,84 +756,117 @@
     )
     in_sums = Sums(cube, cube.plan_b, other_grad_in[None], grad_in[None])
     out_sums = Sums(cube, cube.plan_a, other_grad_out[None], grad_out[None])
-    grad_from_third, grad_gain_third = norm_back_third(grad_third)
-    grad_upper = cotangent.astype(jnp.float32) + grad_from_third
-    grad_cross_branch = grad_upper.astype(jnp.bfloat16)
-    grad_crossed = project_back(grad_cross_branch, attn_full[7]).astype(jnp.bfloat16)
+    grad_upper, grad_cross_branch, grad_crossed, grad_gain_third = fused(
+        third_back,
+        [(tile, full), (tile, low), (tile, low), ((1, D), full)],
+        grad_third,
+        upper,
+        cotangent,
+        gain_three,
+        attn_full[7],
+    )
     in_sums.take(grad_crossed)
     out_sums.take(grad_crossed)
     grad_crossed = after(grad_crossed, in_sums.send(), out_sums.send())
-    cross_query_low, memory_key_low, memory_value_low = attend_backward(
-        cross_query, memory_keys, memory_values, grad_crossed, cross_probs, False
-    )
+    sums_scratch = [pltpu.VMEM((tile[0], LANES), full)] * 2
+    memory_key_low, memory_value_low, grad_middle, grad_self_branch, grad_mixed, *rest = by_pair(
+        functools.partial(cross_back, rows),
+        [
+            core[None],
+            cross_query,
+            memory_keys,
+            memory_values,
+            grad_crossed,
+            cross_probs,
+            second_low,
+            memory,
+            crossed_low,
+            grad_cross_branch,
+            middle,
+            grad_upper,
+            gain_two,
+            attn_full[4],
+            attn_full[3],
+        ],
+        [(tile, low)] * 2
+        + [(tile, full), (tile, low), (tile, low), ((1, D), full)]
+        + product_outs(cube, 4),
+        [pltpu.VMEM(tile, low)] + sums_scratch,
+        (probs,),
+        "cross_back",
+    )
+    grad_gain_second = rest[0]
+    for each in (in_sums, out_sums):
+        each.take(grad_mixed)
     cross_sums = product_sums(
-        cube,
-        cube.plan_a,
+        cube, cube.plan_a, rest[1:], in_sums.terms[-1], out_sums.terms[-1]
+    )
+    started = [in_sums.send(), out_sums.send()]
+    cross_sums.take(*started)
+    grad_mixed = after(grad_mixed, *started, cross_sums.send())
+    lots = (PAIRS, 8, 2 * LANES)
+    outs = product_outs(cube, 2)
+    query_low, key_low, value_low, score_sums, *rest = by_pair(
+        functools.partial(self_back, rows),
         [
-            (second_low, cross_query_low),
-            (memory, memory_key_low),
-            (memory, memory_value_low),
-            (crossed_low, grad_cross_branch),
+            core[None],
+            query,
+            keys,
+            values,
+            grad_mixed,
+            self_probs,
+            first_low,
+            mixed_low,
+            grad_self_branch,
         ],
-    )
-    grad_from_second, grad_gain_second = norm_back_second(
-        project_back(cross_query_low, attn_full[4])
-    )
-    grad_middle = grad_upper + grad_from_second
-    grad_self_branch = grad_middle.astype(jnp.bfloat16)
-    grad_mixed = project_back(grad_self_branch, attn_full[3]).astype(jnp.bfloat16)
-    sums = [cross_sums, in_sums, out_sums]
-    for each in sums:
-        each.take(grad_mixed)
-    grad_mixed = after(grad_mixed, *[each.send() for each in sums])
-    query_low, key_low, value_low, score_sums = attend_backward(
-        query, keys, values, grad_mixed, self_probs, True
-    )
-    for each in sums[1:]:
+        [(tile, low)] * 3 + [(lots, full)] + outs[:1] * 2 + outs[1:] * 2,
+        sums_scratch,
+        (probs, lots),
+        "self_back",
+    )
+    for each in (in_sums, out_sums):
         each.take(query_low)
-    query_low, key_low, value_low = lax.optimization_barrier(
-        (query_low, key_low, value_low) + tuple(each.send() for each in sums[1:])
-    )[:3]
-    late_sums = product_sums(
-        cube, cube.plan_b, [(first_low, value_low), (mixed_low, grad_self_branch)]
-    )
-    early_sums = product_sums(cube, cube.plan_a, [(first_low, query_low), (first_low, key_low)])
-    memory_key_low, memory_value_low = lax.optimization_barrier(
-        (memory_key_low, memory_value_low, late_sums.kept, early_sums.kept)
-    )[:2]
-    grad_memory = project_back(memory_key_low, attn_full[5]) + project_back(
-        memory_value_low, attn_full[6]
-    )
+    arrived = in_sums.terms[-1], out_sums.terms[-1]
+    late_sums = product_sums(cube, cube.plan_b, rest[::2], *arrived)
+    early_sums = product_sums(cube, cube.plan_a, rest[1::2], *arrived)
+    started = [in_sums.send(), out_sums.send()]
+    cross_sums.take(*started)
+    started.append(cross_sums.send())
+    late_sums.take(*started)
+    early_sums.take(*started)
+    started.extend([late_sums.send(), early_sums.send()])
     sums = [late_sums, early_sums, cross_sums, in_sums, out_sums]
-    for each in sums:
-        each.take(grad_memory)
-    started = [each.send() for each in sums if each.going()]
-    query_low, key_low, value_low = lax.optimization_barrier(
-        (query_low, key_low, value_low, *started)
-    )[:3]
-    grad_first = (
-        project_back(query_low, attn_full[0])
-        + project_back(key_low, attn_full[1])
-        + project_back(value_low, attn_full[2])
-    )
-    grad_from_first, grad_gain_first = norm_back_first(grad_first)
-    grad_tokens = grad_middle + grad_from_first
+    query_low = after(query_low, *started)
+    grad_tokens, grad_memory, grad_gain_first = fused(
+        last_back,
+        [(tile, full), (tile, full), ((1, D), full)],
+        query_low,
+        key_low,
+        value_low,
+        memory_key_low,
+        memory_value_low,
+        tokens,
+        grad_middle,
+        gain_one,
+        *attn_full[:3],
+        *attn_full[5:7],
+    )
     table_grad = table_sums(score_sums)
-    gain_local = jnp.stack([grad_gain_first, grad_gain_second, grad_gain_third])
+    gain_local = jnp.concatenate([grad_gain_first, grad_gain_second, grad_gain_third], axis=0)
     behind = (grad_tokens,)
     while any(each.going() for each in sums):
         moving = [each for each in sums if each.going()]
         for each in moving:
             each.take(*behind)
-            each.send()
+            behind = behind + (each.send(),)
         behind = ()
     for each in sums:
         each.take(*behind)
     grad_in, grad_out = [
-        cube.place(*half_swap(cube, each.value), 0, 1, True) for each in sums[3:]
+        cube.place(*half_swap(cube, each.value()), 0, 1, True) for each in sums[3:]
     ]
     grad_attn = jnp.concatenate(
-        [each.value.reshape(-1, rows, D) for each in (early_sums, late_sums, cross_sums)], axis=0
+        [each.value().reshape(-1, rows, D) for each in (early_sums, late_sums, cross_sums)], axis=0
     )
     square_attn = grad_attn * grad_attn
     square_in = grad_in * grad_in

time: 403 us -> 363 us (0.901)
  Pallas kernels: 71.9 us -> 117 us
  waiting for transfers between devices: 95.9 us -> 51.4 us
  matrix products: 33.5 us -> 1.05 us
  local copies, waits for them, and re-layouts: 62.4 us -> 33.3 us
  other arithmetic: 71.9 us -> 86.6 us
  starting transfers between devices: 58.1 us -> 65.6 us
    pallas_call x4 -> x6, Pallas kernels: 47.5 us -> 92.4 us  [the longest x4 78.3 us: by_pair(): pl.pallas_call(kernel, grid=(PAIRS,), in_specs=[spec(array, True) for arr...]
    ppermute x60 -> x61, waiting for transfers between devices: 95.9 us -> 51.4 us  [swap(): return lax.ppermute(value, AXES, [(i, i ^ flip) for i in range(self.count)])]
    dot_general x24 -> x0, matrix products: 31.7 us -> none  [the longest x8 13.1 us: project(): return jnp.dot(left_side, right_side, preferred_element_type=jnp.float32)]
    convert_element_type x2 -> x21, other arithmetic: 1.91 us -> 30.5 us  [the longest x20 29.9 us: send(): sent = self.value().astype(jnp.bfloat16)]
    add x28 -> x5, other arithmetic: 23.1 us -> 5.92 us  [value(): return sum((term.astype(jnp.float32) for term in self.terms))]
    unnamed x191 -> x102, local copies, waits for them, and re-layouts: 24.6 us -> 7.5 us
    ppermute x60 -> x61, starting transfers between devices: 58.1 us -> 65.6 us  [swap(): return lax.ppermute(value, AXES, [(i, i ^ flip) for i in range(self.count)])]
    squeeze x12 -> x0, local copies, waits for them, and re-layouts: 6.75 us -> none  [the longest x10 6.42 us: send(): self.kept = lax.dynamic_index_in_dim(self.value, mine, axis, False)]
  transfers between devices with their start and end apart: 60 -> 61, of which waited for: 24 -> 21; matrix products, arithmetic and copies ran while one was open for 35% -> 29% of each run, Pallas kernels for 12% -> 26%
where the time goes in v3:
time: 363 us; the launch traced here: 357 us
  Pallas kernels  117 us (32%)
  other arithmetic  86.6 us (24%)
  starting transfers between devices  65.6 us (18%)
  waiting for transfers between devices  51.4 us (14%)
  local copies, waits for them, and re-layouts  33.3 us (9%)
    pallas_call x4, Pallas kernels, by_pair(): pl.pallas_call(kernel, grid=(PAIRS,), in_specs=[spec(array, True) for arr...  78.3 us
    ppermute x61, starting transfers between devices, swap(): return lax.ppermute(value, AXES, [(i, i ^ flip) for i in range(self.count)])  65.6 us
    ppermute x61, waiting for transfers between devices, swap(): return lax.ppermute(value, AXES, [(i, i ^ flip) for i in range(self.count)])  51.4 us
    select_n x42, other arithmetic, place(): jnp.where(self.bit(which) == 0, join([mine, theirs], axis), join([theirs,...  33.7 us
    convert_element_type x20, other arithmetic, send(): sent = self.value().astype(jnp.bfloat16)  29.9 us
    pallas_call x1, Pallas kernels, ffn(): pl.pallas_call(ffn_kernel, grid_spec=pltpu.PrefetchScalarGridSpec(num_sca...  24.2 us
    pallas_call x2, Pallas kernels, fused(): pl.pallas_call(kernel, in_specs=[space] * len(args), out_specs=[space] *...  14.2 us
    unnamed x102, local copies, waits for them, and re-layouts  7.5 us
  transfers between devices with their start and end apart: 61, of which 21 were waited for; matrix products, arithmetic and copies ran while one was open for 29% of the time, Pallas kernels for 26%

profile of v3, /device:TPU:0, one launch (start us, length us, event | category | flops | bytes accessed | tf_op | source)
XLA Modules:
  0.0 356.5 jit_solution(6432510372670960459)
XLA Ops:
  2.4 4.1 %collective-permute-start = (bf16[56,768]{1,0:T(8,128)(2,1)S(1)}, bf16[56,768]{1,0:T(8,128)(2,1)S(1)}, u32[]{:S(2)}, u32[]{:S(2)}) collective-permute-start(bf16[56,768]{1,0:T(8,128)(2,1)S(1)} %get-tuple-element.275), channel_id=1, source_target_pairs={{0,16},{1,17},{2,18},{3,19},{4,20},{5,21},{6,22},{7,23},{8,24},{9,... | collective-permute-start | bytes 258056 | tf_op jit(solution)/shard_map/ppermute | solution.py:520
  15.6 2.6 collective-permute-start.10
  18.2 6.3 %collective-permute-done.6 = bf16[2,48,768]{2,1,0:T(8,128)(2,1)S(1)} collective-permute-done((bf16[2,48,768]{2,1,0:T(8,128)(2,1)S(1)}, bf16[2,48,768]{2,1,0:T(8,128)(2,1)S(1)}, u32[]{:S(2)}, u32[]{:S(2)}) %collective-permute-start.6) | collective-permute-done | bytes 147488 | tf_op jit(solution)/shard_map/ppermute | solution.py:520
  26.3 3.4 collective-permute-done.10
  32.2 6.6 %collective-permute-done.7 = bf16[2,2,48,768]{3,2,1,0:T(8,128)(2,1)S(1)} collective-permute-done((bf16[2,2,48,768]{3,2,1,0:T(8,128)(2,1)S(1)}, bf16[2,2,48,768]{3,2,1,0:T(8,128)(2,1)S(1)}, u32[]{:S(2)}, u32[]{:S(2)}) %collective-permute-start.7) | collective-permute-done | bytes 294944 | tf_op jit(solution)/shard_map/ppermute | solution.py:520
  48.7 2.5 collective-permute-start.23
  64.6 2.0 maximum_select_fusion.19
  66.7 2.0 maximum_select_fusion.20
  72.3 2.8 maximum_select_fusion.2
  78.9 2.1 maximum_select_fusion.1
  84.0 14.9 %self_part.1 = (bf16[512,768]{1,0:T(8,128)(2,1)}, bf16[512,768]{1,0:T(8,128)(2,1)}, bf16[512,768]{1,0:T(8,128)(2,1)}, bf16[512,768]{1,0:T(8,128)(2,1)}, bf16[12,...) custom-call(bf16[512,768]{1,0:T(8,128)(2,1)} %tokens_ref.5, f32[1,768]{1,0:T(1,128)} %reshape.3121.gain_ref, ...), custom_call_target="tpu_custom_call" | custom-call | tf_op jit(solution)/shard_map/self_part/pallas_call | solution.py:357
  98.9 2.0 maximum_select_fusion.3
  104.3 2.5 maximum_select_fusion.10
  107.3 2.5 maximum_select_fusion.11
  118.3 3.2 maximum_select_fusion
  121.5 2.4 fusion.104
  123.9 22.0 %cross_part.1 = (f32[512,768]{1,0:T(8,128)}, bf16[512,768]{1,0:T(8,128)(2,1)}, bf16[512,768]{1,0:T(8,128)(2,1)}, bf16[512,768]{1,0:T(8,128)(2,1)}, bf16[512,768]...) custom-call(bf16[512,768]{1,0:T(8,128)(2,1)} %tokens_ref.5, ...), custom_call_target="tpu_custom_call" | custom-call | tf_op jit(solution)/shard_map/cross_part/pallas_call | solution.py:357
  145.9 2.0 maximum_select_fusion.4
  148.0 2.8 maximum_select_fusion.5
  152.5 3.4 collective-permute-done.26
  157.3 24.2 %ffn.1 = (bf16[512,768]{1,0:T(8,128)(2,1)}, f32[512,768]{1,0:T(8,128)}, bf16[768,1536]{1,0:T(8,128)(2,1)}, bf16[768,1536]{1,0:T(8,128)(2,1)}, bf16[3072,384]{1,0:T(8,128)(2,1)}, /*index=5*/bf16[3072,384]{1,0:T(8,128)(2,1)}) custom-call(s32[1]{0:T(128)} %bitcast.core_ref, bf16[512,768]{1,0:T(8,128)(2,1)} %get-tuple-element.123.third_ref, ...), custom_call_target="tpu_custom_call" | custom-call | tf_op jit(solution)/shard_map/ffn/pallas_call | solution.py:285
  182.1 4.9 %third_back.1 = (f32[512,768]{1,0:T(8,128)}, bf16[512,768]{1,0:T(8,128)(2,1)}, bf16[512,768]{1,0:T(8,128)(2,1)}, f32[1,768]{1,0:T(1,128)}) custom-call(f32[512,768]{1,0:T(8,128)} %get-tuple-element.146.gthird_ref, f32[512,768]{1,0:T(8,128)} %get-tuple-element.124.upper_ref, bf16[512,768]{1,0:T(8,128)(2,1)} %cot_ref.3, ...), custom_call_target="tpu_custom_call" | custom-call | tf_op jit(solution)/shard_map/third_back/pallas_call | solution.py:327
  187.8 1.9 collective-permute-done.28
  189.7 2.5 fusion
  194.7 23.8 %cross_back.1 = (bf16[512,768]{1,0:T(8,128)(2,1)}, bf16[512,768]{1,0:T(8,128)(2,1)}, f32[512,768]{1,0:T(8,128)}, bf16[512,768]{1,0:T(8,128)(2,1)}, bf16[512,768]...) custom-call(s32[1]{0:T(128)} %bitcast.core_ref, ...), custom_call_target="tpu_custom_call" | custom-call | tf_op jit(solution)/shard_map/cross_back/pallas_call | solution.py:357
  218.5 1.9 collective-permute-done.29
  222.0 2.0 fusion.5
  224.0 2.1 collective-permute-start.32
  230.8 17.6 %self_back.1 = (bf16[512,768]{1,0:T(8,128)(2,1)}, bf16[512,768]{1,0:T(8,128)(2,1)}, bf16[512,768]{1,0:T(8,128)(2,1)}, f32[6,8,256]{2,1,0:T(8,128)}, bf16[2,384,7...) custom-call(s32[1]{0:T(128)} %bitcast.core_ref, ...), custom_call_target="tpu_custom_call" | custom-call | tf_op jit(solution)/shard_map/self_back/pallas_call | solution.py:357
  249.7 2.1 fusion.18
  251.8 4.2 %collective-permute-start.48 = (bf16[1,2,48,1536]{3,2,1,0:T(8,128)(2,1)}, bf16[1,2,48,1536]{3,2,1,0:T(8,128)(2,1)}, u32[]{:S(2)}, u32[]{:S(2)}) collective-permute-start(bf16[1,2,48,1536]{3,2,1,0:T(8,128)(2,1)} %fusion.18), channel_id=1, source_target_pairs={{0,16},{1,17},{2,18},{3,19},{4,20},{5,21},{6,22},{7,23},{8,24},{9,... | collective-permute-start | bytes 884744 | tf_op jit(solution)/shard_map/ppermute | solution.py:520
  256.0 2.0 fusion.17
  258.0 1.8 collective-permute-start.51
  268.4 1.8 collective-permute-start.37
  274.7 9.3 %last_back.1 = (f32[512,768]{1,0:T(8,128)}, f32[512,768]{1,0:T(8,128)}, f32[1,768]{1,0:T(1,128)}) custom-call(bf16[512,768]{1,0:T(8,128)(2,1)} %get-tuple-element.184.gq_ref, bf16[512,768]{1,0:T(8,128)(2,1)} %get-tuple-element.185.gk_ref, bf16[512,768]{1,0:T(8,128)(2,1)} %get-tuple-element.186.gv_ref, bf16[512,768]{1,0:T(8,128)(2,1)} %get-tuple-element.187.gmk_ref, ...), custom_call_target="tpu_custom_call" | custom-call | tf_op jit(solution)/shard_map/last_back/pallas_call | solution.py:327
  283.9 1.9 fusion.16
  285.8 1.9 fusion.15
  287.7 2.6 collective-permute-done.45
  290.3 2.1 fusion.14
  293.7 1.8 collective-permute-start.49
  302.6 7.6 %collective-permute-done.52 = bf16[1,192,384]{2,1,0:T(8,128)(2,1)S(1)} collective-permute-done((bf16[1,192,384]{2,1,0:T(8,128)(2,1)S(1)}, bf16[1,192,384]{2,1,0:T(8,128)(2,1)S(1)}, u32[]{:S(2)}, u32[]{:S(2)}) %collective-permute-start.52) | collective-permute-done | bytes 147488 | tf_op jit(solution)/shard_map/ppermute | solution.py:520
  313.6 2.7 collective-permute-start.42
  317.9 2.0 fusion.23
  319.9 2.9 collective-permute-start.47
  327.2 1.8 collective-permute-start.44
  332.8 3.0 collective-permute-done.43
  343.5 2.1 collective-permute-done.57
  347.6 3.1 collective-permute-start.59
  (334 shorter events, 125.2 us)
Async XLA Ops:
  2.4 11.5 %collective-permute-start = (bf16[56,768]{1,0:T(8,128)(2,1)S(1)}, bf16[56,768]{1,0:T(8,128)(2,1)S(1)}, u32[]{:S(2)}, u32[]{:S(2)}) collective-permute-start(bf16[56,768]{1,0:T(8,128)(2,1)S(1)} %get-tuple-element.275), channel_id=1, source_target_pairs={{0,16},{1,17},{2,18},{3,19},{4,20},{5,21},{6,22},{7,23},{8,24},{9,... | collective-permute-start | bytes 258056 | tf_op jit(solution)/shard_map/ppermute | solution.py:520
  6.5 6.8 %collective-permute-start.5 = (bf16[48,768]{1,0:T(8,128)(2,1)S(1)}, bf16[48,768]{1,0:T(8,128)(2,1)S(1)}, u32[]{:S(2)}, u32[]{:S(2)}) collective-permute-start(bf16[48,768]{1,0:T(8,128)(2,1)S(1)} %bitcast.462), channel_id=1, source_target_pairs={{0,2},{1,3},{2,0},{3,1},{4,6},{5,7},{6,4},{7,5},{8,10},{9,11},{10,... | collective-permute-start | bytes 221192 | tf_op jit(solution)/shard_map/ppermute | solution.py:520
  13.3 11.2 %collective-permute-start.6 = (bf16[2,48,768]{2,1,0:T(8,128)(2,1)S(1)}, bf16[2,48,768]{2,1,0:T(8,128)(2,1)S(1)}, u32[]{:S(2)}, u32[]{:S(2)}) collective-permute-start(bf16[2,48,768]{2,1,0:T(8,128)(2,1)S(1)} %maximum_select_fusion.36), channel_id=1, source_target_pairs={{0,16},{1,17},{2,18},{3,19},{4,20},{5,21},{6,22},{7,23},{8,24},{9,... | collective-permute-start | bytes 442376 | tf_op jit(solution)/shard_map/ppermute | solution.py:520
  13.9 10.7 %collective-permute-start.1 = (bf16[2,56,768]{2,1,0:T(8,128)(2,1)S(1)}, bf16[2,56,768]{2,1,0:T(8,128)(2,1)S(1)}, u32[]{:S(2)}, u32[]{:S(2)}) collective-permute-start(bf16[2,56,768]{2,1,0:T(8,128)(2,1)S(1)} %maximum_select_fusion.34), channel_id=1, source_target_pairs={{0,8},{1,9},{2,10},{3,11},{4,12},{5,13},{6,14},{7,15},{8,0},{9,1},... | collective-permute-start | bytes 516104 | tf_op jit(solution)/shard_map/ppermute | solution.py:520
  15.6 14.1 %collective-permute-start.10 = (bf16[96,768]{1,0:T(8,128)(2,1)S(1)}, bf16[96,768]{1,0:T(8,128)(2,1)S(1)}, u32[]{:S(2)}, u32[]{:S(2)}) collective-permute-start(bf16[96,768]{1,0:T(8,128)(2,1)S(1)} %bitcast.431), channel_id=1, source_target_pairs={{0,16},{1,17},{2,18},{3,19},{4,20},{5,21},{6,22},{7,23},{8,24},{9,... | collective-permute-start | bytes 442376 | tf_op jit(solution)/shard_map/ppermute | solution.py:520
  24.6 14.2 %collective-permute-start.7 = (bf16[2,2,48,768]{3,2,1,0:T(8,128)(2,1)S(1)}, bf16[2,2,48,768]{3,2,1,0:T(8,128)(2,1)S(1)}, u32[]{:S(2)}, u32[]{:S(2)}) collective-permute-start(bf16[2,2,48,768]{3,2,1,0:T(8,128)(2,1)S(1)} %maximum_select_fusion.24), channel_id=1, source_target_pairs={{0,8},{1,9},{2,10},{3,11},{4,12},{5,13},{6,14},{7,15},{8,0},{9,1},... | collective-permute-start | bytes 884744 | tf_op jit(solution)/shard_map/ppermute | solution.py:520
  24.7 15.8 %collective-permute-start.2 = (bf16[2,2,56,768]{3,2,0,1:T(8,128)(2,1)S(1)}, bf16[2,2,56,768]{3,2,0,1:T(8,128)(2,1)S(1)}, u32[]{:S(2)}, u32[]{:S(2)}) collective-permute-start(bf16[2,2,56,768]{3,2,0,1:T(8,128)(2,1)S(1)} %maximum_select_fusion.22), channel_id=1, source_target_pairs={{0,4},{1,5},{2,6},{3,7},{4,0},{5,1},{6,2},{7,3},{8,12},{9,13},{10,... | collective-permute-start | bytes 1032200 | tf_op jit(solution)/shard_map/ppermute | solution.py:520
  29.7 13.2 %collective-permute-start.11 = (bf16[2,96,768]{2,1,0:T(8,128)(2,1)S(1)}, bf16[2,96,768]{2,1,0:T(8,128)(2,1)S(1)}, u32[]{:S(2)}, u32[]{:S(2)}) collective-permute-start(bf16[2,96,768]{2,1,0:T(8,128)(2,1)S(1)} %maximum_select_fusion.26), channel_id=1, source_target_pairs={{0,8},{1,9},{2,10},{3,11},{4,12},{5,13},{6,14},{7,15},{8,0},{9,1},... | collective-permute-start | bytes 884744 | tf_op jit(solution)/shard_map/ppermute | solution.py:520
  29.8 15.5 %collective-permute-start.16 = (bf16[48,1536]{1,0:T(8,128)(2,1)S(1)}, bf16[48,1536]{1,0:T(8,128)(2,1)S(1)}, u32[]{:S(2)}, u32[]{:S(2)}) collective-permute-start(bf16[48,1536]{1,0:T(8,128)(2,1)S(1)} %maximum_select_fusion.38), channel_id=1, source_target_pairs={{0,2},{1,3},{2,0},{3,1},{4,6},{5,7},{6,4},{7,5},{8,10},{9,11},{10,... | collective-permute-start | bytes 442376 | tf_op jit(solution)/shard_map/ppermute | solution.py:520
  30.4 17.5 %collective-permute-start.22 = (bf16[192,384]{1,0:T(8,128)(2,1)S(1)}, bf16[192,384]{1,0:T(8,128)(2,1)S(1)}, u32[]{:S(2)}, u32[]{:S(2)}) collective-permute-start(bf16[192,384]{1,0:T(8,128)(2,1)S(1)} %maximum_select_fusion.40), channel_id=1, source_target_pairs={{0,16},{1,17},{2,18},{3,19},{4,20},{5,21},{6,22},{7,23},{8,24},{9,... | collective-permute-start | bytes 442376 | tf_op jit(solution)/shard_map/ppermute | solution.py:520
  38.8 15.8 %collective-permute-start.8 = (bf16[2,2,2,48,768]{4,3,2,0,1:T(8,128)(2,1)S(1)}, bf16[2,2,2,48,768]{4,3,2,0,1:T(8,128)(2,1)S(1)}, u32[]{:S(2)}, u32[]{:S(2)}) collective-permute-start(bf16[2,2,2,48,768]{4,3,2,0,1:T(8,128)(2,1)S(1)} %maximum_select_fusion.15), channel_id=1, source_target_pairs={{0,4},{1,5},{2,6},{3,7},{4,0},{5,1},{6,2},{7,3},{8,12},{9,13},{10,... | collective-permute-start | bytes 1769480 | tf_op jit(solution)/shard_map/ppermute | solution.py:520
  40.7 15.2 %collective-permute-start.3 = (bf16[2,2,2,56,768]{4,3,0,2,1:T(8,128)(2,1)S(1)}, bf16[2,2,2,56,768]{4,3,0,2,1:T(8,128)(2,1)S(1)}, u32[]{:S(2)}, u32[]{:S(2)}) collective-permute-start(bf16[2,2,2,56,768]{4,3,0,2,1:T(8,128)(2,1)S(1)} %maximum_select_fusion.13), channel_id=1, source_target_pairs={{0,2},{1,3},{2,0},{3,1},{4,6},{5,7},{6,4},{7,5},{8,10},{9,11},{10,... | collective-permute-start | bytes 2064392 | tf_op jit(solution)/shard_map/ppermute | solution.py:520
  43.8 17.7 %collective-permute-start.12 = (bf16[2,2,96,768]{3,2,0,1:T(8,128)(2,1)}, bf16[2,2,96,768]{3,2,0,1:T(8,128)(2,1)S(1)}, u32[]{:S(2)}, u32[]{:S(2)}) collective-permute-start(bf16[2,2,96,768]{3,2,0,1:T(8,128)(2,1)} %maximum_select_fusion.17), channel_id=1, source_target_pairs={{0,4},{1,5},{2,6},{3,7},{4,0},{5,1},{6,2},{7,3},{8,12},{9,13},{10,... | collective-permute-start | bytes 1769480 | tf_op jit(solution)/shard_map/ppermute | solution.py:520
  46.0 18.6 %collective-permute-start.17 = (bf16[2,48,1536]{2,1,0:T(8,128)(2,1)}, bf16[2,48,1536]{2,1,0:T(8,128)(2,1)S(1)}, u32[]{:S(2)}, u32[]{:S(2)}) collective-permute-start(bf16[2,48,1536]{2,1,0:T(8,128)(2,1)} %maximum_select_fusion.28), channel_id=1, source_target_pairs={{0,16},{1,17},{2,18},{3,19},{4,20},{5,21},{6,22},{7,23},{8,24},{9,... | collective-permute-start | bytes 884744 | tf_op jit(solution)/shard_map/ppermute | solution.py:520
  48.7 18.0 %collective-permute-start.23 = (bf16[2,192,384]{2,1,0:T(8,128)(2,1)}, bf16[2,192,384]{2,1,0:T(8,128)(2,1)}, u32[]{:S(2)}, u32[]{:S(2)}) collective-permute-start(bf16[2,192,384]{2,1,0:T(8,128)(2,1)} %maximum_select_fusion.30), channel_id=1, source_target_pairs={{0,8},{1,9},{2,10},{3,11},{4,12},{5,13},{6,14},{7,15},{8,0},{9,1},... | collective-permute-start | bytes 884744 | tf_op jit(solution)/shard_map/ppermute | solution.py:520
  55.9 16.4 %collective-permute-start.9 = (bf16[16,48,768]{2,1,0:T(8,128)(2,1)}, bf16[16,48,768]{2,1,0:T(8,128)(2,1)}, u32[]{:S(2)}, u32[]{:S(2)}) collective-permute-start(bf16[16,48,768]{2,1,0:T(8,128)(2,1)} %bitcast.32), channel_id=1, source_target_pairs={{0,1},{1,0},{2,3},{3,2},{4,5},{5,4},{6,7},{7,6},{8,9},{9,8},{10,11... | collective-permute-start | bytes 3538952 | tf_op jit(solution)/shard_map/ppermute | solution.py:520
  59.2 17.5 %collective-permute-start.4 = (bf16[16,56,768]{2,0,1:T(8,128)(2,1)}, bf16[16,56,768]{2,0,1:T(8,128)(2,1)}, u32[]{:S(2)}, u32[]{:S(2)}) collective-permute-start(bf16[16,56,768]{2,0,1:T(8,128)(2,1)} %select_n.815), channel_id=1, source_target_pairs={{0,1},{1,0},{2,3},{3,2},{4,5},{5,4},{6,7},{7,6},{8,9},{9,8},{10,11... | collective-permute-start | bytes 4128776 | tf_op jit(solution)/shard_map/ppermute | solution.py:520
  64.0 34.8 %collective-permute-start.13 = (bf16[2,2,2,96,768]{4,3,0,1,2:T(8,128)(2,1)}, bf16[2,2,2,96,768]{4,3,0,1,2:T(8,128)(2,1)}, u32[]{:S(2)}, u32[]{:S(2)}) collective-permute-start(bf16[2,2,2,96,768]{4,3,0,1,2:T(8,128)(2,1)} %maximum_select_fusion.9), channel_id=1, source_target_pairs={{0,2},{1,3},{2,0},{3,1},{4,6},{5,7},{6,4},{7,5},{8,10},{9,11},{10,... | collective-permute-start | bytes 3538952 | tf_op jit(solution)/shard_map/ppermute | solution.py:520
  66.7 36.6 %collective-permute-start.18 = (bf16[2,2,48,1536]{3,2,1,0:T(8,128)(2,1)}, bf16[2,2,48,1536]{3,2,1,0:T(8,128)(2,1)}, u32[]{:S(2)}, u32[]{:S(2)}) collective-permute-start(bf16[2,2,48,1536]{3,2,1,0:T(8,128)(2,1)} %maximum_select_fusion.19), channel_id=1, source_target_pairs={{0,8},{1,9},{2,10},{3,11},{4,12},{5,13},{6,14},{7,15},{8,0},{9,1},... | collective-permute-start | bytes 1769480 | tf_op jit(solution)/shard_map/ppermute | solution.py:520
  68.7 38.6 %collective-permute-start.24 = (bf16[2,2,192,384]{3,2,1,0:T(8,128)(2,1)}, bf16[2,2,192,384]{3,2,1,0:T(8,128)(2,1)}, u32[]{:S(2)}, u32[]{:S(2)}) collective-permute-start(bf16[2,2,192,384]{3,2,1,0:T(8,128)(2,1)} %maximum_select_fusion.20), channel_id=1, source_target_pairs={{0,4},{1,5},{2,6},{3,7},{4,0},{5,1},{6,2},{7,3},{8,12},{9,13},{10,... | collective-permute-start | bytes 1769480 | tf_op jit(solution)/shard_map/ppermute | solution.py:520
  101.0 17.2 %collective-permute-start.14 = (bf16[16,96,768]{2,1,0:T(8,128)(2,1)S(1)}, bf16[16,96,768]{2,1,0:T(8,128)(2,1)}, u32[]{:S(2)}, u32[]{:S(2)}) collective-permute-start(bf16[16,96,768]{2,1,0:T(8,128)(2,1)S(1)} %bitcast.380), channel_id=1, source_target_pairs={{0,1},{1,0},{2,3},{3,2},{4,5},{5,4},{6,7},{7,6},{8,9},{9,8},{10,11... | collective-permute-start | bytes 7077896 | tf_op jit(solution)/shard_map/ppermute | solution.py:520
  106.8 39.1 %collective-permute-start.19 = (bf16[2,2,2,48,1536]{4,3,2,1,0:T(8,128)(2,1)}, bf16[2,2,2,48,1536]{4,3,2,1,0:T(8,128)(2,1)}, u32[]{:S(2)}, u32[]{:S(2)}) collective-permute-start(bf16[2,2,2,48,1536]{4,3,2,1,0:T(8,128)(2,1)} %maximum_select_fusion.10), channel_id=1, source_target_pairs={{0,4},{1,5},{2,6},{3,7},{4,0},{5,1},{6,2},{7,3},{8,12},{9,13},{10,... | collective-permute-start | bytes 3538952 | tf_op jit(solution)/shard_map/ppermute | solution.py:520
  109.8 38.2 %collective-permute-start.25 = (bf16[2,2,2,192,384]{4,3,2,1,0:T(8,128)(2,1)}, bf16[2,2,2,192,384]{4,3,2,1,0:T(8,128)(2,1)}, u32[]{:S(2)}, u32[]{:S(2)}) collective-permute-start(bf16[2,2,2,192,384]{4,3,2,1,0:T(8,128)(2,1)} %maximum_select_fusion.11), channel_id=1, source_target_pairs={{0,2},{1,3},{2,0},{3,1},{4,6},{5,7},{6,4},{7,5},{8,10},{9,11},{10,... | collective-permute-start | bytes 3538952 | tf_op jit(solution)/shard_map/ppermute | solution.py:520
  181.8 7.9 %collective-permute-start.28 = (bf16[1,3072,384]{2,1,0:T(8,128)(2,1)}, bf16[1,3072,384]{2,1,0:T(8,128)(2,1)S(1)}, u32[]{:S(2)}, u32[]{:S(2)}) collective-permute-start(bf16[1,3072,384]{2,1,0:T(8,128)(2,1)} %bitcast.484), channel_id=1, source_target_pairs={{0,1},{1,0},{2,3},{3,2},{4,5},{5,4},{6,7},{7,6},{8,9},{9,8},{10,11... | collective-permute-start | bytes 7077896 | tf_op jit(solution)/shard_map/ppermute | solution.py:520
  192.2 28.1 %collective-permute-start.29 = (bf16[1,2,2,2,48,1536]{5,4,3,2,1,0:T(8,128)(2,1)S(1)}, bf16[1,2,2,2,48,1536]{5,4,3,2,1,0:T(8,128)(2,1)S(1)}, u32[]{:S(2)}, u32[]{:S(2)}) collective-permute-start(bf16[1,2,2,2,48,1536]{5,4,3,2,1,0:T(8,128)(2,1)S(1)} %fusion), channel_id=1, source_target_pairs={{0,4},{1,5},{2,6},{3,7},{4,0},{5,1},{6,2},{7,3},{8,12},{9,13},{10,... | collective-permute-start | bytes 3538952 | tf_op jit(solution)/shard_map/ppermute | solution.py:520
  194.1 27.9 %collective-permute-start.30 = (bf16[1,2,2,2,192,384]{5,4,3,2,1,0:T(8,128)(2,1)S(1)}, bf16[1,2,2,2,192,384]{5,4,3,2,1,0:T(8,128)(2,1)S(1)}, u32[]{:S(2)}, u32[]{:S(2)}) collective-permute-start(bf16[1,2,2,2,192,384]{5,4,3,2,1,0:T(8,128)(2,1)S(1)} %fusion.1), channel_id=1, source_target_pairs={{0,2},{1,3},{2,0},{3,1},{4,6},{5,7},{6,4},{7,5},{8,10},{9,11},{10,... | collective-permute-start | bytes 3538952 | tf_op jit(solution)/shard_map/ppermute | solution.py:520
  222.0 6.5 %collective-permute-start.31 = (bf16[4,16,24,768]{3,2,1,0:T(8,128)(2,1)}, bf16[4,16,24,768]{3,2,1,0:T(8,128)(2,1)S(1)}, u32[]{:S(2)}, u32[]{:S(2)}) collective-permute-start(bf16[4,16,24,768]{3,2,1,0:T(8,128)(2,1)} %bitcast.483), channel_id=1, source_target_pairs={{0,1},{1,0},{2,3},{3,2},{4,5},{5,4},{6,7},{7,6},{8,9},{9,8},{10,11... | collective-permute-start | bytes 7077896 | tf_op jit(solution)/shard_map/ppermute | solution.py:520
  224.0 24.4 %collective-permute-start.32 = (bf16[1,2,2,48,1536]{4,3,2,1,0:T(8,128)(2,1)S(1)}, bf16[1,2,2,48,1536]{4,3,2,1,0:T(8,128)(2,1)S(1)}, u32[]{:S(2)}, u32[]{:S(2)}) collective-permute-start(bf16[1,2,2,48,1536]{4,3,2,1,0:T(8,128)(2,1)S(1)} %fusion.5), channel_id=1, source_target_pairs={{0,8},{1,9},{2,10},{3,11},{4,12},{5,13},{6,14},{7,15},{8,0},{9,1},... | collective-permute-start | bytes 1769480 | tf_op jit(solution)/shard_map/ppermute | solution.py:520
  227.8 20.6 %collective-permute-start.33 = (bf16[1,2,2,192,384]{4,3,1,2,0:T(8,128)(2,1)S(1)}, bf16[1,2,2,192,384]{4,3,1,2,0:T(8,128)(2,1)S(1)}, u32[]{:S(2)}, u32[]{:S(2)}) collective-permute-start(bf16[1,2,2,192,384]{4,3,1,2,0:T(8,128)(2,1)S(1)} %copy.227), channel_id=1, source_target_pairs={{0,4},{1,5},{2,6},{3,7},{4,0},{5,1},{6,2},{7,3},{8,12},{9,13},{10,... | collective-permute-start | bytes 1769480 | tf_op jit(solution)/shard_map/ppermute | solution.py:520
  230.2 29.5 %collective-permute-start.34 = (bf16[4,2,2,2,24,768]{5,4,0,3,2,1:T(8,128)(2,1)}, bf16[4,2,2,2,24,768]{5,4,0,3,2,1:T(8,128)(2,1)}, u32[]{:S(2)}, u32[]{:S(2)}) collective-permute-start(bf16[4,2,2,2,24,768]{5,4,0,3,2,1:T(8,128)(2,1)} %fusion.2), channel_id=1, source_target_pairs={{0,2},{1,3},{2,0},{3,1},{4,6},{5,7},{6,4},{7,5},{8,10},{9,11},{10,... | collective-permute-start | bytes 3538952 | tf_op jit(solution)/shard_map/ppermute | solution.py:520
  249.2 12.2 %collective-permute-start.35 = (bf16[2,16,24,768]{3,2,1,0:T(8,128)(2,1)}, bf16[2,16,24,768]{3,2,1,0:T(8,128)(2,1)S(1)}, u32[]{:S(2)}, u32[]{:S(2)}) collective-permute-start(bf16[2,16,24,768]{3,2,1,0:T(8,128)(2,1)} %bitcast.487), channel_id=1, source_target_pairs={{0,1},{1,0},{2,3},{3,2},{4,5},{5,4},{6,7},{7,6},{8,9},{9,8},{10,11... | collective-permute-start | bytes 3538952 | tf_op jit(solution)/shard_map/ppermute | solution.py:520
  249.2 17.3 %collective-permute-start.36 = (bf16[2,16,24,768]{3,2,1,0:T(8,128)(2,1)}, bf16[2,16,24,768]{3,2,1,0:T(8,128)(2,1)}, u32[]{:S(2)}, u32[]{:S(2)}) collective-permute-start(bf16[2,16,24,768]{3,2,1,0:T(8,128)(2,1)} %bitcast.486), channel_id=1, source_target_pairs={{0,1},{1,0},{2,3},{3,2},{4,5},{5,4},{6,7},{7,6},{8,9},{9,8},{10,11... | collective-permute-start | bytes 3538952 | tf_op jit(solution)/shard_map/ppermute | solution.py:520
  251.8 40.6 %collective-permute-start.48 = (bf16[1,2,48,1536]{3,2,1,0:T(8,128)(2,1)}, bf16[1,2,48,1536]{3,2,1,0:T(8,128)(2,1)}, u32[]{:S(2)}, u32[]{:S(2)}) collective-permute-start(bf16[1,2,48,1536]{3,2,1,0:T(8,128)(2,1)} %fusion.18), channel_id=1, source_target_pairs={{0,16},{1,17},{2,18},{3,19},{4,20},{5,21},{6,22},{7,23},{8,24},{9,... | collective-permute-start | bytes 884744 | tf_op jit(solution)/shard_map/ppermute | solution.py:520
  258.0 41.1 %collective-permute-start.51 = (bf16[1,2,192,384]{3,2,1,0:T(8,128)(2,1)}, bf16[1,2,192,384]{3,2,1,0:T(8,128)(2,1)}, u32[]{:S(2)}, u32[]{:S(2)}) collective-permute-start(bf16[1,2,192,384]{3,2,1,0:T(8,128)(2,1)} %fusion.17), channel_id=1, source_target_pairs={{0,8},{1,9},{2,10},{3,11},{4,12},{5,13},{6,14},{7,15},{8,0},{9,1},... | collective-permute-start | bytes 884744 | tf_op jit(solution)/shard_map/ppermute | solution.py:520
  262.8 21.1 %collective-permute-start.38 = (bf16[2,2,2,2,24,768]{5,4,0,3,2,1:T(8,128)(2,1)S(1)}, bf16[2,2,2,2,24,768]{5,4,0,3,2,1:T(8,128)(2,1)}, u32[]{:S(2)}, u32[]{:S(2)}) collective-permute-start(bf16[2,2,2,2,24,768]{5,4,0,3,2,1:T(8,128)(2,1)S(1)} %fusion.12), channel_id=1, source_target_pairs={{0,4},{1,5},{2,6},{3,7},{4,0},{5,1},{6,2},{7,3},{8,12},{9,13},{10,... | collective-permute-start | bytes 1769480 | tf_op jit(solution)/shard_map/ppermute | solution.py:520
  266.5 23.8 %collective-permute-start.45 = (bf16[4,2,2,24,768]{4,3,0,1,2:T(8,128)(2,1)}, bf16[4,2,2,24,768]{4,3,0,1,2:T(8,128)(2,1)}, u32[]{:S(2)}, u32[]{:S(2)}) collective-permute-start(bf16[4,2,2,24,768]{4,3,0,1,2:T(8,128)(2,1)} %copy.250), channel_id=1, source_target_pairs={{0,4},{1,5},{2,6},{3,7},{4,0},{5,1},{6,2},{7,3},{8,12},{9,13},{10,... | collective-permute-start | bytes 1769480 | tf_op jit(solution)/shard_map/ppermute | solution.py:520
  268.4 17.4 %collective-permute-start.37 = (bf16[2,2,2,2,24,768]{5,4,0,3,2,1:T(8,128)(2,1)S(1)}, bf16[2,2,2,2,24,768]{5,4,0,3,2,1:T(8,128)(2,1)}, u32[]{:S(2)}, u32[]{:S(2)}) collective-permute-start(bf16[2,2,2,2,24,768]{5,4,0,3,2,1:T(8,128)(2,1)S(1)} %fusion.13), channel_id=1, source_target_pairs={{0,2},{1,3},{2,0},{3,1},{4,6},{5,7},{6,4},{7,5},{8,10},{9,11},{10,... | collective-permute-start | bytes 1769480 | tf_op jit(solution)/shard_map/ppermute | solution.py:520
  293.7 7.5 %collective-permute-start.49 = (bf16[1,48,1536]{2,1,0:T(8,128)(2,1)S(1)}, bf16[1,48,1536]{2,1,0:T(8,128)(2,1)S(1)}, u32[]{:S(2)}, u32[]{:S(2)}) collective-permute-start(bf16[1,48,1536]{2,1,0:T(8,128)(2,1)S(1)} %fusion.21), channel_id=1, source_target_pairs={{0,2},{1,3},{2,0},{3,1},{4,6},{5,7},{6,4},{7,5},{8,10},{9,11},{10,... | collective-permute-start | bytes 442376 | tf_op jit(solution)/shard_map/ppermute | solution.py:520
  295.5 22.4 %collective-permute-start.46 = (bf16[4,2,24,768]{3,2,0,1:T(8,128)(2,1)}, bf16[4,2,24,768]{3,2,0,1:T(8,128)(2,1)S(1)}, u32[]{:S(2)}, u32[]{:S(2)}) collective-permute-start(bf16[4,2,24,768]{3,2,0,1:T(8,128)(2,1)} %fusion.14), channel_id=1, source_target_pairs={{0,8},{1,9},{2,10},{3,11},{4,12},{5,13},{6,14},{7,15},{8,0},{9,1},... | collective-permute-start | bytes 884744 | tf_op jit(solution)/shard_map/ppermute | solution.py:520
  295.9 16.5 %collective-permute-start.40 = (bf16[2,2,2,24,768]{4,3,0,2,1:T(8,128)(2,1)}, bf16[2,2,2,24,768]{4,3,0,2,1:T(8,128)(2,1)S(1)}, u32[]{:S(2)}, u32[]{:S(2)}) collective-permute-start(bf16[2,2,2,24,768]{4,3,0,2,1:T(8,128)(2,1)} %fusion.16), channel_id=1, source_target_pairs={{0,8},{1,9},{2,10},{3,11},{4,12},{5,13},{6,14},{7,15},{8,0},{9,1},... | collective-permute-start | bytes 884744 | tf_op jit(solution)/shard_map/ppermute | solution.py:520
  297.6 18.7 %collective-permute-start.39 = (bf16[2,2,2,24,768]{4,3,0,2,1:T(8,128)(2,1)}, bf16[2,2,2,24,768]{4,3,0,2,1:T(8,128)(2,1)S(1)}, u32[]{:S(2)}, u32[]{:S(2)}) collective-permute-start(bf16[2,2,2,24,768]{4,3,0,2,1:T(8,128)(2,1)} %fusion.15), channel_id=1, source_target_pairs={{0,4},{1,5},{2,6},{3,7},{4,0},{5,1},{6,2},{7,3},{8,12},{9,13},{10,... | collective-permute-start | bytes 884744 | tf_op jit(solution)/shard_map/ppermute | solution.py:520
  300.3 10.0 %collective-permute-start.52 = (bf16[1,192,384]{2,1,0:T(8,128)(2,1)S(1)}, bf16[1,192,384]{2,1,0:T(8,128)(2,1)S(1)}, u32[]{:S(2)}, u32[]{:S(2)}) collective-permute-start(bf16[1,192,384]{2,1,0:T(8,128)(2,1)S(1)} %fusion.19), channel_id=1, source_target_pairs={{0,16},{1,17},{2,18},{3,19},{4,20},{5,21},{6,22},{7,23},{8,24},{9,... | collective-permute-start | bytes 442376 | tf_op jit(solution)/shard_map/ppermute | solution.py:520
  302.6 21.6 %collective-permute-start.50 = (f32[24,1536]{1,0:T(8,128)S(1)}, f32[24,1536]{1,0:T(8,128)S(1)}, u32[]{:S(2)}, u32[]{:S(2)}) collective-permute-start(f32[24,1536]{1,0:T(8,128)S(1)} %get-tuple-element.265), channel_id=1, source_target_pairs={{0,1},{1,0},{2,3},{3,2},{4,5},{5,4},{6,7},{7,6},{8,9},{9,8},{10,11... | collective-permute-start | bytes 442376 | tf_op jit(solution)/shard_map/ppermute | solution.py:520
  311.6 11.3 %collective-permute-start.53 = (f32[96,384]{1,0:T(8,128)S(1)}, f32[96,384]{1,0:T(8,128)S(1)}, u32[]{:S(2)}, u32[]{:S(2)}) collective-permute-start(f32[96,384]{1,0:T(8,128)S(1)} %get-tuple-element.263), channel_id=1, source_target_pairs={{0,1},{1,0},{2,3},{3,2},{4,5},{5,4},{6,7},{7,6},{8,9},{9,8},{10,11... | collective-permute-start | bytes 442376 | tf_op jit(solution)/shard_map/ppermute | solution.py:520
  313.6 12.6 %collective-permute-start.42 = (bf16[2,2,24,768]{3,2,0,1:T(8,128)(2,1)S(1)}, bf16[2,2,24,768]{3,2,0,1:T(8,128)(2,1)S(1)}, u32[]{:S(2)}, u32[]{:S(2)}) collective-permute-start(bf16[2,2,24,768]{3,2,0,1:T(8,128)(2,1)S(1)} %fusion.26), channel_id=1, source_target_pairs={{0,16},{1,17},{2,18},{3,19},{4,20},{5,21},{6,22},{7,23},{8,24},{9,... | collective-permute-start | bytes 442376 | tf_op jit(solution)/shard_map/ppermute | solution.py:520
  317.5 11.5 %collective-permute-start.41 = (bf16[2,2,24,768]{3,2,0,1:T(8,128)(2,1)S(1)}, bf16[2,2,24,768]{3,2,0,1:T(8,128)(2,1)S(1)}, u32[]{:S(2)}, u32[]{:S(2)}) collective-permute-start(bf16[2,2,24,768]{3,2,0,1:T(8,128)(2,1)S(1)} %fusion.25), channel_id=1, source_target_pairs={{0,8},{1,9},{2,10},{3,11},{4,12},{5,13},{6,14},{7,15},{8,0},{9,1},... | collective-permute-start | bytes 442376 | tf_op jit(solution)/shard_map/ppermute | solution.py:520
  319.9 10.5 %collective-permute-start.47 = (bf16[4,24,768]{2,1,0:T(8,128)(2,1)}, bf16[4,24,768]{2,1,0:T(8,128)(2,1)}, u32[]{:S(2)}, u32[]{:S(2)}) collective-permute-start(bf16[4,24,768]{2,1,0:T(8,128)(2,1)} %fusion.23), channel_id=1, source_target_pairs={{0,16},{1,17},{2,18},{3,19},{4,20},{5,21},{6,22},{7,23},{8,24},{9,... | collective-permute-start | bytes 442376 | tf_op jit(solution)/shard_map/ppermute | solution.py:520
  346.3 6.6 %collective-permute-start.60 = (f32[40,384]{1,0:T(8,128)S(1)}, f32[40,384]{1,0:T(8,128)S(1)}, u32[]{:S(2)}, u32[]{:S(2)}) collective-permute-start(f32[40,384]{1,0:T(8,128)S(1)} %add_add_fusion.1), channel_id=1, source_target_pairs={{0,24},{1,25},{2,26},{3,27},{4,28},{5,29},{6,30},{7,31},{8,16},{9,... | collective-permute-start | bytes 184328 | tf_op jit(solution)/shard_map/ppermute | solution.py:520
  (63 other events, 393.3 us)

commit v4 on v3

--- a/solution.py
+++ b/solution.py
@@ -221,15 +221,49 @@
 CUTS = FF // (2 * BLOCK)
 
 
-def ffn_kernel(
-    core_ref, third_ref, upper_ref, cot_ref, in_ref, other_in_ref, out_ref, other_out_ref,
-    layer_ref, gthird_ref, gin_ref, other_gin_ref, gout_ref, other_gout_ref,
-    total, third_turned, out_block, gout_block,
-):
+def chip_of(chip, place, plan):
+    bits = [which for group in plan for which in group]
+    flip = sum(((place >> k) & 1) << (which - 1) for k, which in enumerate(bits))
+    return chip ^ flip
+
+
+def halves_of(core):
+    half = D // 2
+    mine = pl.ds(pl.multiple_of(core * half, half), half)
+    return mine, pl.ds(pl.multiple_of((1 - core) * half, half), half)
+
+
+def fill_weight(weight_ref, parts, at, spot_ref, plan):
+    if len(parts) == 1:
+        weight_ref[...] = parts[0][at]
+        return
+    blocks, rows = parts[0].shape[0], D // (2 * parts[0].shape[0])
+    mine, other = halves_of(spot_ref[1])
+    for place in range(2 * blocks):
+        chip = chip_of(spot_ref[0], place, plan)
+        lines = pl.ds(pl.multiple_of(chip * rows, rows), rows)
+        which, block = divmod(place, blocks)
+        weight_ref[lines, mine] = parts[which][block, at * rows : (at + 1) * rows]
+        weight_ref[lines, other] = parts[2 + which][block, at * rows : (at + 1) * rows]
+
+
+def put_divided(grads, rows, core, sent_ref, kept_ref):
+    columns = grads.shape[1]
+    grads = grads.reshape(-1, 2, rows, columns)
+    even, odd = grads[:, 0].reshape(-1, columns), grads[:, 1].reshape(-1, columns)
+    sent_ref[...] = jnp.where(core == 0, odd, even).astype(jnp.bfloat16)
+    kept_ref[...] = jnp.where(core == 0, even, odd).astype(jnp.bfloat16)
+
+
+def ffn_kernel(tiled, plan, spot_ref, third_ref, upper_ref, cot_ref, *refs):
     step = pl.program_id(0)
-    half = D // 2
-    mine = pl.ds(pl.multiple_of(core_ref[0] * half, half), half)
-    other = pl.ds(pl.multiple_of((1 - core_ref[0]) * half, half), half)
+    if tiled:
+        own_in, other_in, out_parts, refs = refs[:2], refs[2:4], refs[4:8], refs[8:]
+        layer_ref, gthird_ref, gin_ref, kept_gin_ref, gout_ref, kept_gout_ref = refs[:6]
+        total, third_turned, in_block, out_block = refs[6:]
+    else:
+        in_block, out_block, layer_ref, gthird_ref, gin_ref, gout_ref = refs[:6]
+        total, third_turned = refs[6:]
 
     @pl.when(step == 0)
     def _():
@@ -237,77 +271,97 @@
         gthird_ref[...] = jnp.zeros_like(gthird_ref)
         third_turned[...] = third_ref[...].T
 
-    out_block[:, mine] = out_ref[...]
-    out_block[:, other] = other_out_ref[...]
-
-    def block(weight_ref, grad_ref):
-        inner = dot(third_ref[...], weight_ref[...])
-        square = inner * inner
-        slope = jnp.tanh(inner * (GELU_SCALE + (GELU_SCALE * GELU_CUBE) * square))
-        half_up = 0.5 + 0.5 * slope
-        active = (inner * half_up).astype(jnp.bfloat16)
-        total[...] += dot(active, out_block[...])
-        grad_active = dot(cot_ref[...], out_block[...], NT)
-        bend = (0.5 * inner) * (1.0 - slope * slope)
-        bend = bend * (GELU_SCALE + (3.0 * GELU_SCALE * GELU_CUBE) * square)
-        grad_inner = (grad_active * (half_up + bend)).astype(jnp.bfloat16)
-        gthird_ref[...] += dot(grad_inner, weight_ref[...], NT)
-        grad_ref[...] = dot(third_turned[...], grad_inner).astype(jnp.bfloat16)
-        gout_block[...] = dot(active, cot_ref[...], TN).astype(jnp.bfloat16)
-
-    @pl.when(step < CUTS)
-    def _():
-        block(other_in_ref, other_gin_ref)
-
-    @pl.when(step >= CUTS)
-    def _():
-        block(in_ref, gin_ref)
-
-    gout_ref[...] = gout_block[:, mine]
-    other_gout_ref[...] = gout_block[:, other]
+    def fill_in(parts):
+        blocks, rows, _ = parts[0].shape
+        for place in range(2 * blocks):
+            chip = chip_of(spot_ref[0], place, plan)
+            lines = pl.ds(pl.multiple_of(chip * rows, rows), rows)
+            in_block[lines, :] = parts[place // blocks][place % blocks]
+
+    if tiled:
+        pl.when(step < CUTS)(lambda: fill_in(other_in))
+        pl.when(step >= CUTS)(lambda: fill_in(own_in))
+        mine, other = halves_of(spot_ref[1])
+        rows = out_parts[0].shape[2]
+        for place in range(4):
+            chip = (spot_ref[0] & 3) ^ place
+            lines = pl.ds(pl.multiple_of(chip * rows, rows), rows)
+            out_block[lines, mine] = out_parts[place % 2][place // 2, 0]
+            out_block[lines, other] = out_parts[2 + place % 2][place // 2, 0]
+
+    inner = dot(third_ref[...], in_block[...])
+    square = inner * inner
+    slope = jnp.tanh(inner * (GELU_SCALE + (GELU_SCALE * GELU_CUBE) * square))
+    half_up = 0.5 + 0.5 * slope
+    active = (inner * half_up).astype(jnp.bfloat16)
+    total[...] += dot(active, out_block[...])
+    grad_active = dot(cot_ref[...], out_block[...], NT)
+    bend = (0.5 * inner) * (1.0 - slope * slope)
+    bend = bend * (GELU_SCALE + (3.0 * GELU_SCALE * GELU_CUBE) * square)
+    grad_inner = (grad_active * (half_up + bend)).astype(jnp.bfloat16)
+    gthird_ref[...] += dot(grad_inner, in_block[...], NT)
+    grad_in = dot(third_turned[...], grad_inner)
+    grad_out = dot(active, cot_ref[...], TN)
+    if tiled:
+        chips = 2 * own_in[0].shape[0]
+        put_divided(grad_in, D // (2 * chips), spot_ref[1], gin_ref, kept_gin_ref)
+        put_divided(grad_out, FF // (2 * chips), spot_ref[1], gout_ref, kept_gout_ref)
+    else:
+        gin_ref[...] = grad_in.astype(jnp.bfloat16)
+        gout_ref[...] = grad_out.astype(jnp.bfloat16)
 
     @pl.when(step == 2 * CUTS - 1)
     def _():
         layer_ref[...] = total[...].astype(jnp.bfloat16)
 
 
-def ffn(core, third, upper, cotangent, w_in, other_in, w_out, other_out):
+def ffn(spot, plan, third, upper, cotangent, in_parts, out_parts):
     rows = third.shape[0]
-    half = D // 2
-
-    def place(step, core_ref):
-        return ((1 - core_ref[0]) * CUTS + step) % (2 * CUTS)
-
-    whole = pl.BlockSpec((rows, D), lambda step, core_ref: (0, 0))
-    late = pl.BlockSpec((D, BLOCK), lambda step, core_ref: (0, jnp.maximum(step - CUTS, 0)))
-    early = pl.BlockSpec((D, BLOCK), lambda step, core_ref: (0, jnp.minimum(step, CUTS - 1)))
-    lines = pl.BlockSpec((BLOCK, half), lambda step, core_ref: (place(step, core_ref), 0))
+    tiled = len(in_parts) > 1
+
+    def block(step, spot_ref):
+        return ((1 - spot_ref[1]) * CUTS + step) % (2 * CUTS)
+
+    def line(step, spot_ref):
+        flips = block(step, spot_ref) ^ (spot_ref[0] >> 2)
+        return (0, (flips >> 1) + 2 * (flips & 1), 0, 0)
+
+    whole = pl.BlockSpec((rows, D), lambda step, spot_ref: (0, 0))
+    across = lambda step, spot_ref: (0, block(step, spot_ref))
+    down = lambda step, spot_ref: (block(step, spot_ref), 0)
+    scratch = [pltpu.VMEM((rows, D), jnp.float32), pltpu.VMEM((D, rows), jnp.bfloat16)]
+    if tiled:
+        chips, lines, _ = in_parts[0].shape
+        late = lambda step, spot_ref: (0, 0, jnp.maximum(step - CUTS, 0))
+        early = lambda step, spot_ref: (0, 0, jnp.minimum(step, CUTS - 1))
+        in_specs = [pl.BlockSpec((chips, lines, BLOCK), late)] * 2
+        in_specs += [pl.BlockSpec((chips, lines, BLOCK), early)] * 2
+        out_parts = [part.reshape(2, 4, -1, D // 2) for part in out_parts]
+        in_specs += [pl.BlockSpec((2, 1) + out_parts[0].shape[2:], line)] * 4
+        out_specs = [pl.BlockSpec((D // 2, BLOCK), across)] * 2
+        out_specs += [pl.BlockSpec((BLOCK // 2, D), down)] * 2
+        shapes = [(D // 2, FF)] * 2 + [(FF // 2, D)] * 2
+        scratch += [pltpu.VMEM((D, BLOCK), jnp.bfloat16), pltpu.VMEM((BLOCK, D), jnp.bfloat16)]
+    else:
+        in_specs = [pl.BlockSpec((D, BLOCK), across), pl.BlockSpec((BLOCK, D), down)]
+        out_specs, shapes = in_specs, [(D, FF), (FF, D)]
     return pl.pallas_call(
-        ffn_kernel,
+        functools.partial(ffn_kernel, tiled, plan),
         grid_spec=pltpu.PrefetchScalarGridSpec(
             num_scalar_prefetch=1,
             grid=(2 * CUTS,),
-            in_specs=[whole, whole, whole, late, early, lines, lines],
-            out_specs=[whole, whole, late, early, lines, lines],
-            scratch_shapes=[
-                pltpu.VMEM((rows, D), jnp.float32),
-                pltpu.VMEM((D, rows), jnp.bfloat16),
-                pltpu.VMEM((BLOCK, D), jnp.bfloat16),
-                pltpu.VMEM((BLOCK, D), jnp.bfloat16),
-            ],
+            in_specs=[whole, whole, whole] + in_specs,
+            out_specs=[whole, whole] + out_specs,
+            scratch_shapes=scratch,
         ),
         out_shape=[
             jax.ShapeDtypeStruct((rows, D), jnp.bfloat16),
             jax.ShapeDtypeStruct((rows, D), jnp.float32),
-            jax.ShapeDtypeStruct((D, FF // 2), jnp.bfloat16),
-            jax.ShapeDtypeStruct((D, FF // 2), jnp.bfloat16),
-            jax.ShapeDtypeStruct((FF, half), jnp.bfloat16),
-            jax.ShapeDtypeStruct((FF, half), jnp.bfloat16),
-        ],
+        ]
+        + [jax.ShapeDtypeStruct(shape, jnp.bfloat16) for shape in shapes],
         compiler_params=pltpu.CompilerParams(vmem_limit_bytes=VMEM_BYTES),
-
         name="ffn",
-    )(core[None], third, upper, cotangent, w_in, other_in, w_out, other_out)
+    )(spot, third, upper, cotangent, *in_parts, *out_parts)
 
 
 def scale_of(hidden):
@@ -350,7 +404,7 @@
         if len(array.shape) == 3 and array.shape in by_step:
             block = (array.shape[0] // PAIRS,) + array.shape[1:]
             return pl.BlockSpec(block, lambda pair: (pair, 0, 0))
-        if array.shape == (1,):
+        if len(array.shape) == 1:
             return pl.BlockSpec(memory_space=pltpu.SMEM)
         return whole_spec(array, pl.Buffered(1) if once else None)
 
@@ -366,10 +420,10 @@
     )(*args)
 
 
-def self_part(
-    tokens_ref, gain_ref, wq_ref, wk_ref, wv_ref, mask_ref, line_ref,
-    first_ref, q_ref, k_ref, v_ref, probs_ref, mixed_ref,
-):
+def self_part(plans, spot_ref, tokens_ref, gain_ref, mask_ref, line_ref, *refs):
+    count = (len(refs) - 10) // 2
+    one, two, refs = refs[:count], refs[count : 2 * count], refs[2 * count :]
+    first_ref, q_ref, k_ref, v_ref, probs_ref, mixed_ref, wq_ref, wk_ref, wv_ref, wo_ref = refs
     pair = pl.program_id(0)
 
     @pl.when(pair == 0)
@@ -377,21 +431,28 @@
         hidden = tokens_ref[...].astype(jnp.float32)
         first = (hidden * scale_of(hidden) * gain_ref[...]).astype(jnp.bfloat16)
         first_ref[...] = first
-        for weight, result in ((wq_ref, q_ref), (wk_ref, k_ref), (wv_ref, v_ref)):
-            result[...] = dot(first, weight[...]).astype(jnp.bfloat16)
+        weights = [(wq_ref, one, 0, q_ref), (wk_ref, one, 1, k_ref), (wv_ref, two, 0, v_ref)]
+        for weight_ref, parts, at, result in weights:
+            fill_weight(weight_ref, parts, at, spot_ref, plans[parts is two])
+            result[...] = dot(first, weight_ref[...]).astype(jnp.bfloat16)
+        fill_weight(wo_ref, two, 1, spot_ref, plans[1])
 
     attend_pair(True, pair, q_ref, k_ref, v_ref, mask_ref, line_ref, probs_ref, mixed_ref)
 
 
 def cross_part(
-    tokens_ref, mixed_ref, memory_ref, gain_ref, wso_ref, wq_ref, wk_ref, wv_ref, wo_ref,
-    next_gain_ref, mask_ref,
-    middle_ref, second_ref, q_ref, k_ref, v_ref, probs_ref, crossed_ref, upper_ref, third_ref,
+    plan, spot_ref, tokens_ref, mixed_ref, memory_ref, gain_ref, wso_ref, next_gain_ref, mask_ref,
+    *refs,
 ):
+    parts, refs = refs[:-13], refs[-13:]
+    middle_ref, second_ref, q_ref, k_ref, v_ref, probs_ref, crossed_ref = refs[:7]
+    upper_ref, third_ref, wq_ref, wk_ref, wv_ref, wo_ref = refs[7:]
     pair = pl.program_id(0)
 
     @pl.when(pair == 0)
     def _():
+        for at, weight_ref in enumerate((wq_ref, wk_ref, wv_ref, wo_ref)):
+            fill_weight(weight_ref, parts, at, spot_ref, plan)
         middle = tokens_ref[...].astype(jnp.float32) + dot(mixed_ref[...], wso_ref[...])
         middle_ref[...] = middle
         second = (middle * scale_of(middle) * gain_ref[...]).astype(jnp.bfloat16)
@@ -440,11 +501,7 @@
         if kept_ref is None:
             sent_ref[k] = grads.astype(jnp.bfloat16)
         else:
-            grads = grads.reshape(-1, 2, rows, D)
-            even, odd = grads[:, 0].reshape(-1, D), grads[:, 1].reshape(-1, D)
-            first = core_ref[0] == 0
-            sent_ref[k] = jnp.where(first, odd, even).astype(jnp.bfloat16)
-            kept_ref[k] = jnp.where(first, even, odd).astype(jnp.bfloat16)
+            put_divided(grads, rows, core_ref[0], sent_ref.at[k], kept_ref.at[k])
 
 
 def cross_back(
@@ -509,9 +566,9 @@
         self.count = lax.axis_size("wide") * lax.axis_size("narrow")
         self.bits = self.count.bit_length() - 1
         self.me = lax.axis_index("wide") * lax.axis_size("narrow") + lax.axis_index("narrow")
-        high = list(range(self.bits - 1, 1, -1))
-        self.plan_a = high + [1]
-        self.plan_b = [1] + high
+        high = [[which] for which in range(self.bits - 1, 1, -1)]
+        self.plan_a = high + [[1]]
+        self.plan_b = [[1]] + high
 
     def bit(self, which):
         return (self.me >> which) & 1
@@ -519,18 +576,11 @@
     def swap(self, value, flip):
         return lax.ppermute(value, AXES, [(i, i ^ flip) for i in range(self.count)])
 
-    def place(self, mine, theirs, which, axis, joined):
-        join = jnp.concatenate if joined else jnp.stack
+    def place(self, mine, theirs, axis):
+        first = self.bit(0) == 0
         return jnp.where(
-            self.bit(which) == 0, join([mine, theirs], axis), join([theirs, mine], axis)
+            first, jnp.concatenate([mine, theirs], axis), jnp.concatenate([theirs, mine], axis)
         )
-
-    def send_step(self, value, plan, step):
-        return self.swap(value, 1 << plan[step])
-
-    def place_step(self, value, theirs, plan, step):
-        axis = sum(other > plan[step] for other in plan[:step])
-        return self.place(value, theirs, plan[step], axis, False)
 
     def half(self, value, whose):
         size = value.shape[-1] // 2
@@ -544,79 +594,82 @@
         return value
 
 
+def flips_of(group):
+    picks = range(1, 1 << len(group))
+    return [sum(((pick >> k) & 1) << which for k, which in enumerate(group)) for pick in picks]
+
+
 class Gather:
     def __init__(self, cube, value, plan):
-        self.cube, self.value, self.plan, self.steps = cube, value, plan, 0
+        self.cube, self.plan, self.steps = cube, plan, 0
+        self.held, self.parts = value[None], []
 
     def send(self, *behind):
-        sent = after(self.value, *behind) if behind else self.value
-        self.theirs = self.cube.send_step(sent, self.plan, self.steps)
+        sent = after(self.held, *behind) if behind else self.held
+        self.theirs = [self.cube.swap(sent, flip) for flip in flips_of(self.plan[self.steps])]
+        self.steps += 1
+        if self.steps == len(self.plan):
+            self.parts = [self.held, self.cube.swap(sent, 1)]
         return sent
 
     def take(self, *behind):
-        theirs = after(self.theirs, *behind) if behind else self.theirs
-        self.value = self.cube.place_step(self.value, theirs, self.plan, self.steps)
-        self.steps += 1
-        return self.value
-
-
-def pair_weights(cube, w_in, w_out):
+        theirs = [after(their, *behind) if behind else their for their in self.theirs]
+        if self.parts:
+            self.parts = [self.parts[0], *theirs, self.parts[1], self.cube.swap(theirs[0], 1)]
+        else:
+            self.held = jnp.concatenate([self.held, *theirs], axis=0)
+
+
+def pair_columns(cube, value, *behind):
     core = cube.bit(0)
-    return [
-        cube.place(
-            cube.half(part, core), cube.swap(cube.half(part, 1 - core), 1), 0, 0, True
-        )
-        for part in (w_in, w_out)
-    ]
-
-
-def both_halves(cube, value):
-    value = value.reshape((-1,) + value.shape[-2:])
-    return value, cube.swap(value, 1)
-
-
-def whole_weights(cube, parts, first, count):
-    rows = D // cube.count
-    full = cube.place(parts[0], parts[1], 0, 1, False)
-    return [
-        full[:, :, first + k * rows : first + (k + 1) * rows].reshape(D, D) for k in range(count)
-    ]
+    sent = cube.half(value, 1 - core)
+    theirs = cube.swap(after(sent, *behind) if behind else sent, 1)
+    return cube.half(value, core), theirs
 
 
 class Sums:
     def __init__(self, cube, plan, sent, kept):
         self.cube, self.plan, self.steps = cube, plan, 0
-        self.shape = (kept.shape[0],) + (2,) * len(plan) + (-1, kept.shape[-1])
-        self.terms, self.theirs = [kept.reshape(self.shape)], cube.swap(sent, 1)
+        self.bits = sorted(which for group in plan for which in group)
+        self.shape = (kept.shape[0],) + (2,) * len(self.bits) + (-1, kept.shape[-1])
+        self.terms, self.theirs = [kept.reshape(self.shape)], [cube.swap(sent, 1)]
 
     def take(self, *behind):
-        theirs = after(self.theirs, *behind) if behind else self.theirs
-        if self.steps == 0:
-            theirs = theirs.reshape(self.shape)
-        self.terms.append(theirs)
+        for their in self.theirs:
+            their = after(their, *behind) if behind else their
+            self.terms.append(their.reshape(self.shape) if self.steps == 0 else their)
 
     def value(self):
         return sum(term.astype(jnp.float32) for term in self.terms)
 
+    def pick(self, group, flip):
+        terms = self.terms
+        for which in sorted(group):
+            axis = 1 + sum(other > which for other in self.bits)
+            index = self.cube.bit(which) ^ ((flip >> which) & 1)
+            terms = [lax.dynamic_index_in_dim(term, index, axis, False) for term in terms]
+        return terms
+
     def send(self, *behind):
-        which = self.plan[-1 - self.steps]
-        axis = 1 + sum(other > which for other in self.plan[: len(self.plan) - self.steps])
-        mine = self.cube.bit(which)
-        whole = self.terms
-        self.terms = [lax.dynamic_index_in_dim(term, 1 - mine, axis, False) for term in whole]
-        sent = self.value().astype(jnp.bfloat16)
-        sent = after(sent, *behind) if behind else sent
-        self.terms = [lax.dynamic_index_in_dim(term, mine, axis, False) for term in whole]
-        self.theirs = self.cube.swap(sent, 1 << which)
+        group = self.plan[-1 - self.steps]
+        everything, sent = self.terms, []
+        for flip in flips_of(group):
+            self.terms = self.pick(group, flip)
+            part = self.value().astype(jnp.bfloat16)
+            sent.append(after(part, *behind) if behind else part)
+            self.terms = everything
+        self.terms = self.pick(group, 0)
+        self.bits = [which for which in self.bits if which not in group]
+        self.theirs = [self.cube.swap(part, flip) for part, flip in zip(sent, flips_of(group))]
         self.steps += 1
-        return sent
+        return tuple(sent)
 
     def going(self):
         return self.steps < len(self.plan)
 
 
 def whole_tiles(cube):
-    return (D // cube.count) % 8 == 0
+    return cube.bits == 5
 
 
 def product_outs(cube, count):
@@ -626,20 +679,21 @@
 
 
 def product_sums(cube, plan, parts, *behind):
-    chips, rows = cube.count // 2, D // cube.count
+    chips, count, columns = cube.count // 2, parts[0].shape[0], parts[0].shape[2]
     if len(parts) == 1:
-        grads = parts[0].reshape(-1, chips, 2, rows, D)
+        grads = parts[0].reshape(count, chips, 2, -1, columns)
         core = cube.bit(0)
         parts = [lax.dynamic_index_in_dim(grads, core ^ k, 2, False) for k in (1, 0)]
-    sent, kept = [part.reshape(-1, chips, rows, D) for part in parts]
+    sent, kept = [part.reshape(count, chips, -1, columns) for part in parts]
     return Sums(cube, plan, after(sent, *behind) if behind else sent, kept)
 
 
-def half_swap(cube, value):
-    value = value.reshape(2, -1, value.shape[-1])
-    core = cube.bit(0)
-    mine = lax.dynamic_index_in_dim(value, core, 0, False)
-    return mine, cube.swap(lax.dynamic_index_in_dim(value, 1 - core, 0, False), 1)
+def chip_order(cube, parts, plan):
+    places = jnp.concatenate(parts, axis=0)
+    chips = chip_of(cube.me >> 1, jnp.arange(places.shape[0], dtype=jnp.int32), plan)
+    moves = jnp.arange(places.shape[0], dtype=jnp.int32)[:, None] == chips[None, :]
+    moved = jnp.dot(moves.astype(places.dtype), places.reshape(places.shape[0], -1))
+    return moved.reshape(places.shape)
 
 
 def on_device(
@@ -661,101 +715,114 @@
 ):
     cube = Cube()
     core = cube.bit(0)
+    spot = jnp.stack([cube.me >> 1, core])
     rows = attn_weights.shape[1]
-    gain_rows = jnp.pad(norm_gains, ((0, 5), (0, D - norm_gains.shape[1])))
-    one = Gather(
-        cube,
-        jnp.concatenate([attn_weights[:2].reshape(-1, D), gain_rows], axis=0),
-        cube.plan_a,
-    )
-    two = Gather(cube, attn_weights[2:4].reshape(-1, D), cube.plan_b)
-    one.send()
-    two.send()
-    in_pair, out_pair = pair_weights(cube, w_in, w_out)
-    three = Gather(cube, attn_weights[4:].reshape(-1, D), cube.plan_a)
-    inner_half = Gather(cube, in_pair, cube.plan_b)
-    outer_half = Gather(cube, out_pair, cube.plan_a)
-    last = len(cube.plan_a) - 1
-    for step in range(last):
-        one.take()
-        two.take()
-        ahead = one.send(), two.send()
-        if step > 0:
-            three.take(*ahead)
-        ahead = ahead + (three.send(*ahead),)
-        if step > 1:
-            inner_half.take(*ahead)
-            outer_half.take(*ahead)
-        if step > 0:
-            inner_half.send(*ahead)
-            outer_half.send(*ahead)
-    one.take()
-    two.take()
-    first_halves = both_halves(cube, one.value)
-    second_halves = both_halves(cube, two.value)
-    ahead = first_halves[0], second_halves[0]
-    three.take(*ahead)
-    ahead = ahead + (three.send(*ahead),)
-    inner_half.take(*ahead)
-    outer_half.take(*ahead)
-    inner_half.send(*ahead)
-    outer_half.send(*ahead)
-    attn_full = whole_weights(cube, first_halves, 0, 2)
-    attn_full = attn_full + whole_weights(cube, second_halves, 0, 2)
-    gain_full = cube.place(
-        first_halves[0][:, 2 * rows :], first_halves[1][:, 2 * rows :], 0, 1, False
-    )[:, :, :3, : norm_gains.shape[1]]
-    gain_full = gain_full.transpose(2, 0, 1, 3).reshape(3, D)
+    tiled = whole_tiles(cube)
+    plans = cube.plan_a, cube.plan_b
     segment = dec_segments[0]
     see_self = self_mask(segment, dec_valid[0])
     see_cross = cross_mask(segment, enc_segments[0])
     lines = bias_lines(rel_table)
-
     tile, low, full = tokens.shape, jnp.bfloat16, jnp.float32
+    square = ((D, D), low)
+    probs = (HEADS, segment.shape[0], segment.shape[0])
+    if tiled:
+        attn_rows = attn_weights[:4].reshape(-1, D)
+        gain_rows = jnp.pad(norm_gains, ((0, 5), (0, D // 2 - rows)))
+        sent = jnp.concatenate([cube.half(attn_rows, 1 - core), gain_rows], axis=0)
+        theirs = cube.swap(sent, 1)
+        pairs = cube.place(
+            cube.half(attn_rows, core).reshape(4, rows, -1),
+            theirs[: 4 * rows].reshape(4, rows, -1),
+            1,
+        ).reshape(4 * 2 * rows, -1)
+        gain_pair = cube.place(gain_rows, theirs[4 * rows :], 0)
+        one = Gather(cube, jnp.concatenate([pairs[: 4 * rows], gain_pair], axis=0), cube.plan_a)
+        two = Gather(cube, pairs[4 * rows :], cube.plan_b)
+        ahead = one.send(), two.send()
+        cross = pair_columns(cube, attn_weights[4:], *ahead)
+        inner = pair_columns(cube, w_in, *ahead)
+        outer = pair_columns(cube, w_out, *ahead)
+        three = Gather(cube, cube.place(*cross, 1).reshape(8 * rows, -1), cube.plan_a)
+        inner = Gather(cube, cube.place(*inner, 0), cube.plan_b)
+        outer = Gather(cube, cube.place(*outer, 0), cube.plan_a)
+        last = len(cube.plan_a) - 1
+        for step in range(last):
+            one.take()
+            two.take()
+            ahead = one.send(), two.send()
+            if step > 0:
+                three.take(*ahead)
+            ahead = ahead + (three.send(*ahead),)
+            if step > 1:
+                inner.take(*ahead)
+                outer.take(*ahead)
+            if step > 0:
+                inner.send(*ahead)
+                outer.send(*ahead)
+        one.take()
+        two.take()
+        ahead = one.parts[2], two.parts[2]
+        three.take(*ahead)
+        ahead = ahead + (three.send(*ahead),)
+        inner.take(*ahead)
+        outer.take(*ahead)
+        ahead = ahead + (inner.send(*ahead), outer.send(*ahead))
+        gain_full = chip_order(cube, [part[:, 4 * rows :, :rows] for part in one.parts[:2]], plans[0])
+        gain_full = gain_full.reshape(-1, 2, 8, rows)[:, :, :3].transpose(2, 0, 1, 3)
+        gain_full = gain_full.reshape(3, D)
+        first_chunk, second_chunk = one.parts, two.parts
+        gain_full = after(gain_full, *ahead)
+    else:
+        attn_full = lax.all_gather(attn_weights, AXES, axis=1, tiled=True)
+        gain_full = lax.all_gather(norm_gains, AXES, axis=1, tiled=True)
+        first_chunk, second_chunk = [attn_full[:2]], [attn_full[2:4]]
     gain_one, gain_two, gain_three = [gain_full[k : k + 1].astype(full) for k in range(3)]
-    probs = (HEADS, segment.shape[0], segment.shape[0])
-    first_low, query, keys, values, self_probs, mixed_low = by_pair(
-        self_part,
-        [tokens, gain_one, *attn_full[:3], see_self, lines],
-        [(tile, low)] * 4 + [(probs, low), (tile, low)],
+    first_low, query, keys, values, self_probs, mixed_low, *weights = by_pair(
+        functools.partial(self_part, plans),
+        [spot, tokens, gain_one, see_self, lines, *first_chunk, *second_chunk],
+        [(tile, low)] * 4 + [(probs, low), (tile, low)] + [square] * 4,
         [],
         (probs, lines.shape),
         "self_part",
     )
-    three.take(mixed_low)
-    cross_halves = both_halves(cube, three.value)
-    inner_half.take(mixed_low)
-    outer_half.take(mixed_low)
-    inner_half.send()
-    outer_half.send()
-    attn_full = attn_full + whole_weights(cube, cross_halves, 0, 4)
+    if tiled:
+        three.take(mixed_low)
+        cross_chunk = three.parts
+        inner.take(mixed_low)
+        outer.take(mixed_low)
+        weights[3] = after(weights[3], inner.send(), outer.send())
+    else:
+        cross_chunk = [attn_full[4:]]
     (
         middle, second_low, cross_query, memory_keys, memory_values, cross_probs, crossed_low,
-        upper, third_low,
+        upper, third_low, *cross_weights,
     ) = by_pair(
-        cross_part,
-        [tokens, mixed_low, memory, gain_two, *attn_full[3:], gain_three, see_cross],
-        [(tile, full)] + [(tile, low)] * 4 + [(probs, low), (tile, low), (tile, full), (tile, low)],
+        functools.partial(cross_part, plans[0]),
+        [
+            spot, tokens, mixed_low, memory, gain_two, weights[3], gain_three, see_cross,
+            *cross_chunk,
+        ],
+        [(tile, full)] + [(tile, low)] * 4 + [(probs, low), (tile, low), (tile, full), (tile, low)]
+        + [square] * 4,
         [],
         (probs,),
         "cross_part",
     )
-    inner_half.take(third_low)
-    outer_half.take(third_low)
-    own_in, other_in = both_halves(cube, inner_half.value)
-    own_out, other_out = both_halves(cube, outer_half.value)
-    layer_out, grad_third, grad_in, other_grad_in, grad_out, other_grad_out = ffn(
-        core,
-        third_low,
-        upper,
-        cotangent,
-        own_in.reshape(D, -1),
-        other_in.reshape(D, -1),
-        own_out.reshape(FF, -1),
-        other_out.reshape(FF, -1),
-    )
-    in_sums = Sums(cube, cube.plan_b, other_grad_in[None], grad_in[None])
-    out_sums = Sums(cube, cube.plan_a, other_grad_out[None], grad_out[None])
+    attn_full = weights + cross_weights
+    if tiled:
+        inner.take(third_low)
+        outer.take(third_low)
+        in_parts, out_parts = inner.parts, outer.parts
+    else:
+        in_parts = [lax.all_gather(w_in, AXES, axis=0, tiled=True)]
+        out_parts = [lax.all_gather(w_out, AXES, axis=0, tiled=True)]
+    layer_out, grad_third, *rest = ffn(
+        spot, plans[1], third_low, upper, cotangent, in_parts, out_parts
+    )
+    half = len(rest) // 2
+    in_sums = product_sums(cube, cube.plan_b, [part[None] for part in rest[:half]])
+    out_sums = product_sums(cube, cube.plan_a, [part[None] for part in rest[half:]])
     grad_upper, grad_cross_branch, grad_crossed, grad_gain_third = fused(
         third_back,
         [(tile, full), (tile, low), (tile, low), ((1, D), full)],
@@ -767,7 +834,7 @@
     )
     in_sums.take(grad_crossed)
     out_sums.take(grad_crossed)
-    grad_crossed = after(grad_crossed, in_sums.send(), out_sums.send())
+    grad_crossed = after(grad_crossed, *in_sums.send(), *out_sums.send())
     sums_scratch = [pltpu.VMEM((tile[0], LANES), full)] * 2
     memory_key_low, memory_value_low, grad_middle, grad_self_branch, grad_mixed, *rest = by_pair(
         functools.partial(cross_back, rows),
@@ -798,12 +865,11 @@
     grad_gain_second = rest[0]
     for each in (in_sums, out_sums):
         each.take(grad_mixed)
-    cross_sums = product_sums(
-        cube, cube.plan_a, rest[1:], in_sums.terms[-1], out_sums.terms[-1]
-    )
-    started = [in_sums.send(), out_sums.send()]
+    arrived = in_sums.terms[-1], out_sums.terms[-1]
+    cross_sums = product_sums(cube, cube.plan_a, rest[1:], *arrived)
+    started = in_sums.send() + out_sums.send()
     cross_sums.take(*started)
-    grad_mixed = after(grad_mixed, *started, cross_sums.send())
+    grad_mixed = after(grad_mixed, *started, *cross_sums.send())
     lots = (PAIRS, 8, 2 * LANES)
     outs = product_outs(cube, 2)
     query_low, key_low, value_low, score_sums, *rest = by_pair(
@@ -829,13 +895,13 @@
     arrived = in_sums.terms[-1], out_sums.terms[-1]
     late_sums = product_sums(cube, cube.plan_b, rest[::2], *arrived)
     early_sums = product_sums(cube, cube.plan_a, rest[1::2], *arrived)
-    started = [in_sums.send(), out_sums.send()]
+    late_sums.take()
+    early_sums.take()
+    started = early_sums.send() + late_sums.send()
+    started = started + out_sums.send(*started) + in_sums.send(*started)
     cross_sums.take(*started)
-    started.append(cross_sums.send())
-    late_sums.take(*started)
-    early_sums.take(*started)
-    started.extend([late_sums.send(), early_sums.send()])
-    sums = [late_sums, early_sums, cross_sums, in_sums, out_sums]
+    started = started + cross_sums.send(*started)
+    sums = [early_sums, late_sums, out_sums, in_sums, cross_sums]
     query_low = after(query_low, *started)
     grad_tokens, grad_memory, grad_gain_first = fused(
         last_back,
@@ -853,31 +919,30 @@
     )
     table_grad = table_sums(score_sums)
     gain_local = jnp.concatenate([grad_gain_first, grad_gain_second, grad_gain_third], axis=0)
-    behind = (grad_tokens,)
-    while any(each.going() for each in sums):
-        moving = [each for each in sums if each.going()]
+    ahead = (grad_tokens,)
+    while sums:
+        moving, ending = [], []
+        for each in sums:
+            (moving if each.going() else ending).append(each)
         for each in moving:
-            each.take(*behind)
-            behind = behind + (each.send(),)
-        behind = ()
-    for each in sums:
-        each.take(*behind)
-    grad_in, grad_out = [
-        cube.place(*half_swap(cube, each.value()), 0, 1, True) for each in sums[3:]
-    ]
-    grad_attn = jnp.concatenate(
-        [each.value().reshape(-1, rows, D) for each in (early_sums, late_sums, cross_sums)], axis=0
-    )
-    square_attn = grad_attn * grad_attn
+            each.take(*ahead)
+            ahead = ahead + each.send()
+        for each in ending:
+            each.take(*ahead)
+        sums, ahead = moving, ()
+    grad_in, grad_out = in_sums.value()[0], out_sums.value()[0]
+    attn_sums = [each.value().reshape(-1, rows, D) for each in (early_sums, late_sums, cross_sums)]
+    grad_attn = jnp.concatenate(attn_sums, axis=0)
+    attn_squares = [value * value for value in attn_sums]
     square_in = grad_in * grad_in
     square_out = grad_out * grad_out
     row_means = jnp.concatenate(
-        [jnp.mean(square_attn, axis=2), jnp.mean(square_in, axis=1)[None]], axis=0
+        [jnp.mean(value, axis=2) for value in attn_squares] + [jnp.mean(square_in, axis=1)[None]], axis=0
     )
     new_row_main = DECAY * row_main + (1.0 - DECAY) * row_means
     new_row_out = DECAY * row_out + (1.0 - DECAY) * jnp.mean(square_out, axis=1)
     column_main = jnp.concatenate(
-        [jnp.sum(square_attn, axis=1), jnp.sum(square_out, axis=0)[None]], axis=0
+        [jnp.sum(value, axis=1) for value in attn_squares] + [jnp.sum(square_out, axis=0)[None]], axis=0
     )
     column_in = jnp.sum(square_in, axis=0)
     parts = [column_main, column_in, table_grad, gain_local]

time: 363 us -> 334 us (0.920)
  other arithmetic: 86.6 us -> 56.1 us
  local copies, waits for them, and re-layouts: 33.3 us -> 15.9 us
  waiting for transfers between devices: 51.4 us -> 68.1 us
  Pallas kernels: 117 us -> 121 us
    select_n x42 -> x5, other arithmetic: 33.7 us -> 0.12 us  [place(): jnp.where(first, jnp.concatenate([mine, theirs], axis), jnp.concatenate([...]
    ppermute x61 -> x66, waiting for transfers between devices: 51.4 us -> 68.1 us  [swap(): return lax.ppermute(value, AXES, [(i, i ^ flip) for i in range(self.count)])]
    another operation x12 -> x1, other arithmetic: 6.81 us -> 0.58 us  [on_device(): spot = jnp.stack([cube.me >> 1, core])]
    add x5 -> x0, other arithmetic: 5.92 us -> none  [value(): return sum((term.astype(jnp.float32) for term in self.terms))]
    concatenate x1 -> x19, other arithmetic: 0.01 us -> 5.92 us  [the longest x15 5.01 us: take(): self.held = jnp.concatenate([self.held, *theirs], axis=0)]
    slice x7 -> x6, local copies, waits for them, and re-layouts: 7.82 us -> 1.93 us  [the longest x1 1.13 us: on_device(): cross = pair_columns(cube, attn_weights[4:], *ahead)]
    select_n x5 -> x0, local copies, waits for them, and re-layouts: 4.83 us -> none  [place(): jnp.where(self.bit(which) == 0, join([mine, theirs], axis), join([theirs,...]
    pallas_call x4, Pallas kernels: 78.3 us -> 82.5 us  [by_pair(): pl.pallas_call(kernel, grid=(PAIRS,), in_specs=[spec(array, True) for arr...]
  transfers between devices with their start and end apart: 61 -> 66, of which waited for: 21 -> 25; matrix products, arithmetic and copies ran while one was open for 29% -> 19% of each run, Pallas kernels for 26% -> 29%
where the time goes in v4:
time: 334 us; the launch traced here: 329 us
  Pallas kernels  121 us (36%)
  waiting for transfers between devices  68.1 us (20%)
  starting transfers between devices  64.9 us (19%)
  other arithmetic  56.1 us (17%)
  local copies, waits for them, and re-layouts  15.9 us (5%)
    pallas_call x4, Pallas kernels, by_pair(): pl.pallas_call(kernel, grid=(PAIRS,), in_specs=[spec(array, True) for arr...  82.5 us
    ppermute x66, waiting for transfers between devices, swap(): return lax.ppermute(value, AXES, [(i, i ^ flip) for i in range(self.count)])  68.1 us
    ppermute x66, starting transfers between devices, swap(): return lax.ppermute(value, AXES, [(i, i ^ flip) for i in range(self.count)])  64.9 us
    convert_element_type x20, other arithmetic, send(): part = self.value().astype(jnp.bfloat16)  33.2 us
    pallas_call x1, Pallas kernels, ffn(): pl.pallas_call(functools.partial(ffn_kernel, tiled, plan), grid_spec=pltp...  24.3 us
    pallas_call x2, Pallas kernels, fused(): pl.pallas_call(kernel, in_specs=[space] * len(args), out_specs=[space] *...  14.2 us
  transfers between devices with their start and end apart: 66, of which 25 were waited for; matrix products, arithmetic and copies ran while one was open for 19% of the time, Pallas kernels for 29%

profile of v4, /device:TPU:0, one launch (start us, length us, event | category | flops | bytes accessed | tf_op | source)
XLA Modules:
  0.0 329.2 jit_solution(4771147304578859625)
XLA Ops:
  3.3 1.7 compare_select_fusion
  5.1 2.6 collective-permute-start.6
  7.7 2.7 collective-permute-start.1
  10.9 2.6 collective-permute-start.7
  13.5 1.7 collective-permute-done.1
  15.3 3.9 %collective-permute-start.2 = (bf16[2,112,384]{2,1,0:T(8,128)(2,1)S(1)}, bf16[2,112,384]{2,1,0:T(8,128)(2,1)S(1)}, u32[]{:S(2)}, u32[]{:S(2)}) collective-permute-start(bf16[2,112,384]{2,1,0:T(8,128)(2,1)S(1)} %pad_maximum_fusion.14), channel_id=1, source_target_pairs={{0,8},{1,9},{2,10},{3,11},{4,12},{5,13},{6,14},{7,15},{8,0},{9,1},... | collective-permute-start | bytes 516104 | tf_op jit(solution)/shard_map/ppermute | solution.py:577
  19.1 3.4 %collective-permute-start.11 = (bf16[1,192,384]{2,1,0:T(8,128)(2,1)S(1)}, bf16[1,192,384]{2,1,0:T(8,128)(2,1)S(1)}, u32[]{:S(2)}, u32[]{:S(2)}) collective-permute-start(bf16[1,192,384]{2,1,0:T(8,128)(2,1)S(1)} %bitcast.297), channel_id=1, source_target_pairs={{0,16},{1,17},{2,18},{3,19},{4,20},{5,21},{6,22},{7,23},{8,24},{9,... | collective-permute-start | bytes 442376 | tf_op jit(solution)/shard_map/ppermute | solution.py:577
  22.7 5.6 %collective-permute-done.2 = bf16[2,112,384]{2,1,0:T(8,128)(2,1)S(1)} collective-permute-done((bf16[2,112,384]{2,1,0:T(8,128)(2,1)S(1)}, bf16[2,112,384]{2,1,0:T(8,128)(2,1)S(1)}, u32[]{:S(2)}, u32[]{:S(2)}) %collective-permute-start.2) | collective-permute-done | bytes 172064 | tf_op jit(solution)/shard_map/ppermute | solution.py:577
  31.1 3.8 %collective-permute-start.18 = (bf16[1,192,384]{2,1,0:T(8,128)(2,1)S(1)}, bf16[1,192,384]{2,1,0:T(8,128)(2,1)S(1)}, u32[]{:S(2)}, u32[]{:S(2)}) collective-permute-start(bf16[1,192,384]{2,1,0:T(8,128)(2,1)S(1)} %maximum_select_fusion.3), channel_id=1, source_target_pairs={{0,16},{1,17},{2,18},{3,19},{4,20},{5,21},{6,22},{7,23},{8,24},{9,... | collective-permute-start | bytes 442376 | tf_op jit(solution)/shard_map/ppermute | solution.py:577
  36.4 2.0 collective-permute-done.3
  40.0 4.0 %collective-permute-done.12 = bf16[2,192,384]{2,1,0:T(8,128)(2,1)S(1)} collective-permute-done((bf16[2,192,384]{2,1,0:T(8,128)(2,1)S(1)}, bf16[2,192,384]{2,1,0:T(8,128)(2,1)S(1)}, u32[]{:S(2)}, u32[]{:S(2)}) %collective-permute-start.12) | collective-permute-done | bytes 294944 | tf_op jit(solution)/shard_map/ppermute | solution.py:577
  47.8 7.0 %collective-permute-done.21.refs_5_ = bf16[8,96,384]{2,1,0:T(8,128)(2,1)} collective-permute-done((bf16[8,96,384]{2,1,0:T(8,128)(2,1)S(1)}, bf16[8,96,384]{2,1,0:T(8,128)(2,1)}, u32[]{:S(2)}, u32[]{:S(2)}) %collective-permute-start.21) | collective-permute-done | bytes 589856 | tf_op jit(solution)/shard_map/ppermute | solution.py:577
  54.7 11.4 %collective-permute-done.13 = bf16[4,192,384]{2,1,0:T(8,128)(2,1)S(1)} collective-permute-done((bf16[4,192,384]{2,1,0:T(8,128)(2,1)S(1)}, bf16[4,192,384]{2,1,0:T(8,128)(2,1)S(1)}, u32[]{:S(2)}, u32[]{:S(2)}) %collective-permute-start.13) | collective-permute-done | bytes 589856 | tf_op jit(solution)/shard_map/ppermute | solution.py:577
  68.9 1.7 collective-permute-start.24
  73.9 17.8 %self_part.1 = (bf16[512,768]{1,0:T(8,128)(2,1)}, bf16[512,768]{1,0:T(8,128)(2,1)}, bf16[512,768]{1,0:T(8,128)(2,1)}, bf16[512,768]{1,0:T(8,128)(2,1)}, bf16[12,...) custom-call(s32[2]{0:T(128)} %pad_add_fusion.spot_ref, ...), custom_call_target="tpu_custom_call" | custom-call | tf_op jit(solution)/shard_map/self_part/pallas_call | solution.py:411
  98.1 23.3 %cross_part.1 = (f32[512,768]{1,0:T(8,128)}, bf16[512,768]{1,0:T(8,128)(2,1)}, bf16[512,768]{1,0:T(8,128)(2,1)}, bf16[512,768]{1,0:T(8,128)(2,1)}, bf16[512,768]...) custom-call(s32[2]{0:T(128)} %pad_add_fusion.spot_ref, ...), custom_call_target="tpu_custom_call" | custom-call | tf_op jit(solution)/shard_map/cross_part/pallas_call | solution.py:411
  121.6 3.0 collective-permute-done.31
  124.6 2.8 collective-permute-done.33
  128.5 24.3 %ffn.1 = (bf16[512,768]{1,0:T(8,128)(2,1)}, f32[512,768]{1,0:T(8,128)}, bf16[384,3072]{1,0:T(8,128)(2,1)}, bf16[384,3072]{1,0:T(8,128)(2,1)}, bf16[1536,768]{1,0:T(8,128)(2,1)}, /*index=5*/bf16[1536,768]{1,0:T(8,128)(2,1)}) custom-call(s32[2]{0:T(128)} %pad_add_fusion.spot_ref, bf16[512,768]{1,0:T(8,128)(2,1)} %get-tuple-element.158.third_ref, ...), custom_call_target="tpu_custom_call" | custom-call | tf_op jit(solution)/shard_map/ffn/pallas_call | solution.py:348
  153.4 4.9 %third_back.1 = (f32[512,768]{1,0:T(8,128)}, bf16[512,768]{1,0:T(8,128)(2,1)}, bf16[512,768]{1,0:T(8,128)(2,1)}, f32[1,768]{1,0:T(1,128)}) custom-call(f32[512,768]{1,0:T(8,128)} %get-tuple-element.169.gthird_ref, f32[512,768]{1,0:T(8,128)} %get-tuple-element.159.upper_ref, bf16[512,768]{1,0:T(8,128)(2,1)} %cot_ref.3, ...), custom_call_target="tpu_custom_call" | custom-call | tf_op jit(solution)/shard_map/third_back/pallas_call | solution.py:381
  162.4 1.8 fusion
  164.2 1.8 collective-permute-start.36
  167.9 23.9 %cross_back.1 = (bf16[512,768]{1,0:T(8,128)(2,1)}, bf16[512,768]{1,0:T(8,128)(2,1)}, f32[512,768]{1,0:T(8,128)}, bf16[512,768]{1,0:T(8,128)(2,1)}, bf16[512,768]...) custom-call(s32[1]{0:T(128)} %bitcast.1.core_ref, ...), custom_call_target="tpu_custom_call" | custom-call | tf_op jit(solution)/shard_map/cross_back/pallas_call | solution.py:411
  192.3 3.1 collective-permute-done.37
  195.5 2.0 fusion.5
  200.3 2.6 fusion.2
  202.9 17.5 %self_back.1 = (bf16[512,768]{1,0:T(8,128)(2,1)}, bf16[512,768]{1,0:T(8,128)(2,1)}, bf16[512,768]{1,0:T(8,128)(2,1)}, f32[6,8,256]{2,1,0:T(8,128)}, bf16[2,384,7...) custom-call(s32[1]{0:T(128)} %bitcast.1.core_ref, ...), custom_call_target="tpu_custom_call" | custom-call | tf_op jit(solution)/shard_map/self_back/pallas_call | solution.py:411
  229.7 2.0 fusion.18
  236.9 2.1 fusion.17
  239.0 11.1 %collective-permute-done.43 = bf16[4,2,2,2,24,768]{5,4,0,3,2,1:T(8,128)(2,1)} collective-permute-done((bf16[4,2,2,2,24,768]{5,4,0,3,2,1:T(8,128)(2,1)}, bf16[4,2,2,2,24,768]{5,4,0,3,2,1:T(8,128)(2,1)}, u32[]{:S(2)}, u32[]{:S(2)}) %collective-permute-start.43) | collective-permute-done | bytes 1179680 | tf_op jit(solution)/shard_map/ppermute | solution.py:577
  250.1 1.6 fusion.3
  253.0 3.5 %collective-permute-start.54 = (bf16[1,2,24,3072]{3,2,1,0:T(8,128)(2,1)}, bf16[1,2,24,3072]{3,2,1,0:T(8,128)(2,1)}, u32[]{:S(2)}, u32[]{:S(2)}) collective-permute-start(bf16[1,2,24,3072]{3,2,1,0:T(8,128)(2,1)} %fusion.17), channel_id=1, source_target_pairs={{0,16},{1,17},{2,18},{3,19},{4,20},{5,21},{6,22},{7,23},{8,24},{9,... | collective-permute-start | bytes 884744 | tf_op jit(solution)/shard_map/ppermute | solution.py:577
  257.8 9.3 %last_back.1 = (f32[512,768]{1,0:T(8,128)}, f32[512,768]{1,0:T(8,128)}, f32[1,768]{1,0:T(1,128)}) custom-call(bf16[512,768]{1,0:T(8,128)(2,1)} %get-tuple-element.210.gq_ref, bf16[512,768]{1,0:T(8,128)(2,1)} %get-tuple-element.211.gk_ref, bf16[512,768]{1,0:T(8,128)(2,1)} %get-tuple-element.212.gv_ref, bf16[512,768]{1,0:T(8,128)(2,1)} %get-tuple-element.213.gmk_ref, ...), custom_call_target="tpu_custom_call" | custom-call | tf_op jit(solution)/shard_map/last_back/pallas_call | solution.py:381
  267.0 2.1 fusion.16
  272.0 1.9 fusion.26
  273.8 2.0 fusion.25
  276.6 2.0 fusion.14
  281.9 1.9 fusion.28
  284.6 1.8 fusion.27
  286.4 2.9 collective-permute-start.50
  290.1 1.9 fusion.23
  292.0 2.7 multiply_reduce_fusion
  294.7 2.1 multiply_reduce_fusion.2
  299.1 3.0 collective-permute-start.47
  305.9 1.7 collective-permute-done.51
  311.4 1.8 collective-permute-start.62
  313.1 2.0 collective-permute-start.60
  320.1 3.8 %collective-permute-start.64 = (f32[40,384]{1,0:T(8,128)S(1)}, f32[40,384]{1,0:T(8,128)S(1)}, u32[]{:S(2)}, u32[]{:S(2)}) collective-permute-start(f32[40,384]{1,0:T(8,128)S(1)} %add_add_fusion.1), channel_id=1, source_target_pairs={{0,16},{1,17},{2,18},{3,19},{4,20},{5,21},{6,22},{7,23},{8,24},{9,... | collective-permute-start | bytes 184328 | tf_op jit(solution)/shard_map/ppermute | solution.py:577
  (283 shorter events, 81.4 us)
Async XLA Ops:
  10.3 8.8 %collective-permute-start.10 = (bf16[4,24,384]{2,1,0:T(8,128)(2,1)S(1)}, bf16[4,24,384]{2,1,0:T(8,128)(2,1)S(1)}, u32[]{:S(2)}, u32[]{:S(2)}) collective-permute-start(bf16[4,24,384]{2,1,0:T(8,128)(2,1)S(1)} %get-tuple-element.131), channel_id=1, source_target_pairs={{0,1},{1,0},{2,3},{3,2},{4,5},{5,4},{6,7},{7,6},{8,9},{9,8},{10,11... | collective-permute-start | bytes 221192 | tf_op jit(solution)/shard_map/ppermute | solution.py:577
  10.8 20.1 %collective-permute-start.17 = (bf16[96,384]{1,0:T(8,128)(2,1)S(1)}, bf16[96,384]{1,0:T(8,128)(2,1)S(1)}, u32[]{:S(2)}, u32[]{:S(2)}) collective-permute-start(bf16[96,384]{1,0:T(8,128)(2,1)S(1)} %get-tuple-element.145), channel_id=1, source_target_pairs={{0,1},{1,0},{2,3},{3,2},{4,5},{5,4},{6,7},{7,6},{8,9},{9,8},{10,11... | collective-permute-start | bytes 221192 | tf_op jit(solution)/shard_map/ppermute | solution.py:577
  10.9 11.7 %collective-permute-start.7 = (bf16[2,96,384]{2,1,0:T(8,128)(2,1)S(1)}, bf16[2,96,384]{2,1,0:T(8,128)(2,1)S(1)}, u32[]{:S(2)}, u32[]{:S(2)}) collective-permute-start(bf16[2,96,384]{2,1,0:T(8,128)(2,1)S(1)} %pad_maximum_fusion.15), channel_id=1, source_target_pairs={{0,16},{1,17},{2,18},{3,19},{4,20},{5,21},{6,22},{7,23},{8,24},{9,... | collective-permute-start | bytes 442376 | tf_op jit(solution)/shard_map/ppermute | solution.py:577
  15.3 13.1 %collective-permute-start.2 = (bf16[2,112,384]{2,1,0:T(8,128)(2,1)S(1)}, bf16[2,112,384]{2,1,0:T(8,128)(2,1)S(1)}, u32[]{:S(2)}, u32[]{:S(2)}) collective-permute-start(bf16[2,112,384]{2,1,0:T(8,128)(2,1)S(1)} %pad_maximum_fusion.14), channel_id=1, source_target_pairs={{0,8},{1,9},{2,10},{3,11},{4,12},{5,13},{6,14},{7,15},{8,0},{9,1},... | collective-permute-start | bytes 516104 | tf_op jit(solution)/shard_map/ppermute | solution.py:577
  19.1 10.8 %collective-permute-start.11 = (bf16[1,192,384]{2,1,0:T(8,128)(2,1)S(1)}, bf16[1,192,384]{2,1,0:T(8,128)(2,1)S(1)}, u32[]{:S(2)}, u32[]{:S(2)}) collective-permute-start(bf16[1,192,384]{2,1,0:T(8,128)(2,1)S(1)} %bitcast.297), channel_id=1, source_target_pairs={{0,16},{1,17},{2,18},{3,19},{4,20},{5,21},{6,22},{7,23},{8,24},{9,... | collective-permute-start | bytes 442376 | tf_op jit(solution)/shard_map/ppermute | solution.py:577
  22.6 13.6 %collective-permute-start.8 = (bf16[4,96,384]{2,1,0:T(8,128)(2,1)S(1)}, bf16[4,96,384]{2,1,0:T(8,128)(2,1)S(1)}, u32[]{:S(2)}, u32[]{:S(2)}) collective-permute-start(bf16[4,96,384]{2,1,0:T(8,128)(2,1)S(1)} %pad_maximum_fusion.10), channel_id=1, source_target_pairs={{0,8},{1,9},{2,10},{3,11},{4,12},{5,13},{6,14},{7,15},{8,0},{9,1},... | collective-permute-start | bytes 884744 | tf_op jit(solution)/shard_map/ppermute | solution.py:577
  28.4 10.0 %collective-permute-start.3 = (bf16[4,112,384]{2,1,0:T(8,128)(2,1)S(1)}, bf16[4,112,384]{2,1,0:T(8,128)(2,1)S(1)}, u32[]{:S(2)}, u32[]{:S(2)}) collective-permute-start(bf16[4,112,384]{2,1,0:T(8,128)(2,1)S(1)} %pad_maximum_fusion.9), channel_id=1, source_target_pairs={{0,4},{1,5},{2,6},{3,7},{4,0},{5,1},{6,2},{7,3},{8,12},{9,13},{10,... | collective-permute-start | bytes 1032200 | tf_op jit(solution)/shard_map/ppermute | solution.py:577
  30.0 14.1 %collective-permute-start.12 = (bf16[2,192,384]{2,1,0:T(8,128)(2,1)S(1)}, bf16[2,192,384]{2,1,0:T(8,128)(2,1)S(1)}, u32[]{:S(2)}, u32[]{:S(2)}) collective-permute-start(bf16[2,192,384]{2,1,0:T(8,128)(2,1)S(1)} %pad_maximum_fusion.11), channel_id=1, source_target_pairs={{0,8},{1,9},{2,10},{3,11},{4,12},{5,13},{6,14},{7,15},{8,0},{9,1},... | collective-permute-start | bytes 884744 | tf_op jit(solution)/shard_map/ppermute | solution.py:577
  31.0 13.3 %collective-permute-start.15 = (bf16[1,48,1536]{2,1,0:T(8,128)(2,1)S(1)}, bf16[1,48,1536]{2,1,0:T(8,128)(2,1)S(1)}, u32[]{:S(2)}, u32[]{:S(2)}) collective-permute-start(bf16[1,48,1536]{2,1,0:T(8,128)(2,1)S(1)} %maximum_select_fusion.2), channel_id=1, source_target_pairs={{0,2},{1,3},{2,0},{3,1},{4,6},{5,7},{6,4},{7,5},{8,10},{9,11},{10,... | collective-permute-start | bytes 442376 | tf_op jit(solution)/shard_map/ppermute | solution.py:577
  31.1 15.1 %collective-permute-start.18 = (bf16[1,192,384]{2,1,0:T(8,128)(2,1)S(1)}, bf16[1,192,384]{2,1,0:T(8,128)(2,1)S(1)}, u32[]{:S(2)}, u32[]{:S(2)}) collective-permute-start(bf16[1,192,384]{2,1,0:T(8,128)(2,1)S(1)} %maximum_select_fusion.3), channel_id=1, source_target_pairs={{0,16},{1,17},{2,18},{3,19},{4,20},{5,21},{6,22},{7,23},{8,24},{9,... | collective-permute-start | bytes 442376 | tf_op jit(solution)/shard_map/ppermute | solution.py:577
  36.3 9.9 %collective-permute-start.9 = (bf16[8,96,384]{2,1,0:T(8,128)(2,1)S(1)}, bf16[8,96,384]{2,1,0:T(8,128)(2,1)S(1)}, u32[]{:S(2)}, u32[]{:S(2)}) collective-permute-start(bf16[8,96,384]{2,1,0:T(8,128)(2,1)S(1)} %pad_maximum_fusion.4.refs_4_), channel_id=1, source_target_pairs={{0,1},{1,0},{2,3},{3,2},{4,5},{5,4},{6,7},{7,6},{8,9},{9,8},{10,11... | collective-permute-start | bytes 1769480 | tf_op jit(solution)/shard_map/ppermute | solution.py:577
  38.4 16.3 %collective-permute-start.21 = (bf16[8,96,384]{2,1,0:T(8,128)(2,1)S(1)}, bf16[8,96,384]{2,1,0:T(8,128)(2,1)}, u32[]{:S(2)}, u32[]{:S(2)}) collective-permute-start(bf16[8,96,384]{2,1,0:T(8,128)(2,1)S(1)} %pad_maximum_fusion.4.refs_4_), channel_id=1, source_target_pairs={{0,4},{1,5},{2,6},{3,7},{4,0},{5,1},{6,2},{7,3},{8,12},{9,13},{10,... | collective-permute-start | bytes 1769480 | tf_op jit(solution)/shard_map/ppermute | solution.py:577
  44.1 22.1 %collective-permute-start.5 = (bf16[8,112,384]{2,1,0:T(8,128)(2,1)S(1)}, bf16[8,112,384]{2,1,0:T(8,128)(2,1)}, u32[]{:S(2)}, u32[]{:S(2)}) collective-permute-start(bf16[8,112,384]{2,1,0:T(8,128)(2,1)S(1)} %pad_maximum_fusion.3.refs_0_), channel_id=1, source_target_pairs={{0,1},{1,0},{2,3},{3,2},{4,5},{5,4},{6,7},{7,6},{8,9},{9,8},{10,11... | collective-permute-start | bytes 2064392 | tf_op jit(solution)/shard_map/ppermute | solution.py:577
  44.3 21.8 %collective-permute-start.13 = (bf16[4,192,384]{2,1,0:T(8,128)(2,1)S(1)}, bf16[4,192,384]{2,1,0:T(8,128)(2,1)S(1)}, u32[]{:S(2)}, u32[]{:S(2)}) collective-permute-start(bf16[4,192,384]{2,1,0:T(8,128)(2,1)S(1)} %pad_maximum_fusion.5), channel_id=1, source_target_pairs={{0,4},{1,5},{2,6},{3,7},{4,0},{5,1},{6,2},{7,3},{8,12},{9,13},{10,... | collective-permute-start | bytes 1769480 | tf_op jit(solution)/shard_map/ppermute | solution.py:577
  46.2 21.3 %collective-permute-start.4 = (bf16[8,112,384]{2,1,0:T(8,128)(2,1)S(1)}, bf16[8,112,384]{2,1,0:T(8,128)(2,1)}, u32[]{:S(2)}, u32[]{:S(2)}) collective-permute-start(bf16[8,112,384]{2,1,0:T(8,128)(2,1)S(1)} %pad_maximum_fusion.3.refs_0_), channel_id=1, source_target_pairs={{0,2},{1,3},{2,0},{3,1},{4,6},{5,7},{6,4},{7,5},{8,10},{9,11},{10,... | collective-permute-start | bytes 2064392 | tf_op jit(solution)/shard_map/ppermute | solution.py:577
  46.2 20.2 %collective-permute-start.16 = (bf16[2,48,1536]{2,1,0:T(8,128)(2,1)S(1)}, bf16[2,48,1536]{2,1,0:T(8,128)(2,1)S(1)}, u32[]{:S(2)}, u32[]{:S(2)}) collective-permute-start(bf16[2,48,1536]{2,1,0:T(8,128)(2,1)S(1)} %pad_maximum_fusion.12), channel_id=1, source_target_pairs={{0,16},{1,17},{2,18},{3,19},{4,20},{5,21},{6,22},{7,23},{8,24},{9,... | collective-permute-start | bytes 884744 | tf_op jit(solution)/shard_map/ppermute | solution.py:577
  54.7 12.8 %collective-permute-start.19 = (bf16[2,192,384]{2,1,0:T(8,128)(2,1)S(1)}, bf16[2,192,384]{2,1,0:T(8,128)(2,1)S(1)}, u32[]{:S(2)}, u32[]{:S(2)}) collective-permute-start(bf16[2,192,384]{2,1,0:T(8,128)(2,1)S(1)} %pad_maximum_fusion.13), channel_id=1, source_target_pairs={{0,8},{1,9},{2,10},{3,11},{4,12},{5,13},{6,14},{7,15},{8,0},{9,1},... | collective-permute-start | bytes 884744 | tf_op jit(solution)/shard_map/ppermute | solution.py:577
  66.2 7.7 %collective-permute-start.22 = (bf16[8,96,384]{2,1,0:T(8,128)(2,1)}, bf16[8,96,384]{2,1,0:T(8,128)(2,1)}, u32[]{:S(2)}, u32[]{:S(2)}) collective-permute-start(bf16[8,96,384]{2,1,0:T(8,128)(2,1)} %collective-permute-done.21.refs_5_), channel_id=1, source_target_pairs={{0,1},{1,0},{2,3},{3,2},{4,5},{5,4},{6,7},{7,6},{8,9},{9,8},{10,11... | collective-permute-start | bytes 1769480 | tf_op jit(solution)/shard_map/ppermute | solution.py:577
  66.3 28.6 %collective-permute-start.25 = (bf16[8,192,384]{2,1,0:T(8,128)(2,1)S(1)}, bf16[8,192,384]{2,1,0:T(8,128)(2,1)}, u32[]{:S(2)}, u32[]{:S(2)}) collective-permute-start(bf16[8,192,384]{2,1,0:T(8,128)(2,1)S(1)} %pad_maximum_fusion.refs_0_), channel_id=1, source_target_pairs={{0,2},{1,3},{2,0},{3,1},{4,6},{5,7},{6,4},{7,5},{8,10},{9,11},{10,... | collective-permute-start | bytes 3538952 | tf_op jit(solution)/shard_map/ppermute | solution.py:577
  68.9 22.8 %collective-permute-start.23 = (bf16[4,48,1536]{2,1,0:T(8,128)(2,1)}, bf16[4,48,1536]{2,1,0:T(8,128)(2,1)}, u32[]{:S(2)}, u32[]{:S(2)}) collective-permute-start(bf16[4,48,1536]{2,1,0:T(8,128)(2,1)} %pad_maximum_fusion.6), channel_id=1, source_target_pairs={{0,8},{1,9},{2,10},{3,11},{4,12},{5,13},{6,14},{7,15},{8,0},{9,1},... | collective-permute-start | bytes 1769480 | tf_op jit(solution)/shard_map/ppermute | solution.py:577
  68.9 22.8 %collective-permute-start.24 = (bf16[4,192,384]{2,1,0:T(8,128)(2,1)}, bf16[4,192,384]{2,1,0:T(8,128)(2,1)}, u32[]{:S(2)}, u32[]{:S(2)}) collective-permute-start(bf16[4,192,384]{2,1,0:T(8,128)(2,1)} %pad_maximum_fusion.7), channel_id=1, source_target_pairs={{0,4},{1,5},{2,6},{3,7},{4,0},{5,1},{6,2},{7,3},{8,12},{9,13},{10,... | collective-permute-start | bytes 1769480 | tf_op jit(solution)/shard_map/ppermute | solution.py:577
  73.9 22.9 %collective-permute-start.26 = (bf16[8,192,384]{2,1,0:T(8,128)(2,1)S(1)}, bf16[8,192,384]{2,1,0:T(8,128)(2,1)S(1)}, u32[]{:S(2)}, u32[]{:S(2)}) collective-permute-start(bf16[8,192,384]{2,1,0:T(8,128)(2,1)S(1)} %pad_maximum_fusion.refs_0_), channel_id=1, source_target_pairs={{0,1},{1,0},{2,3},{3,2},{4,5},{5,4},{6,7},{7,6},{8,9},{9,8},{10,11... | collective-permute-start | bytes 3538952 | tf_op jit(solution)/shard_map/ppermute | solution.py:577
  92.9 28.4 %collective-permute-start.28 = (bf16[8,48,1536]{2,1,0:T(8,128)(2,1)S(1)}, bf16[8,48,1536]{2,1,0:T(8,128)(2,1)S(1)}, u32[]{:S(2)}, u32[]{:S(2)}) collective-permute-start(bf16[8,48,1536]{2,1,0:T(8,128)(2,1)S(1)} %pad_maximum_fusion.1.refs_0_), channel_id=1, source_target_pairs={{0,4},{1,5},{2,6},{3,7},{4,0},{5,1},{6,2},{7,3},{8,12},{9,13},{10,... | collective-permute-start | bytes 3538952 | tf_op jit(solution)/shard_map/ppermute | solution.py:577
  96.1 28.4 %collective-permute-start.31 = (bf16[8,192,384]{2,1,0:T(8,128)(2,1)S(1)}, bf16[8,192,384]{2,1,0:T(8,128)(2,1)S(1)}, u32[]{:S(2)}, u32[]{:S(2)}) collective-permute-start(bf16[8,192,384]{2,1,0:T(8,128)(2,1)S(1)} %pad_maximum_fusion.2), channel_id=1, source_target_pairs={{0,2},{1,3},{2,0},{3,1},{4,6},{5,7},{6,4},{7,5},{8,10},{9,11},{10,... | collective-permute-start | bytes 3538952 | tf_op jit(solution)/shard_map/ppermute | solution.py:577
  96.5 28.1 %collective-permute-start.29 = (bf16[8,48,1536]{2,1,0:T(8,128)(2,1)S(1)}, bf16[8,48,1536]{2,1,0:T(8,128)(2,1)}, u32[]{:S(2)}, u32[]{:S(2)}) collective-permute-start(bf16[8,48,1536]{2,1,0:T(8,128)(2,1)S(1)} %pad_maximum_fusion.1.refs_0_), channel_id=1, source_target_pairs={{0,1},{1,0},{2,3},{3,2},{4,5},{5,4},{6,7},{7,6},{8,9},{9,8},{10,11... | collective-permute-start | bytes 3538952 | tf_op jit(solution)/shard_map/ppermute | solution.py:577
  96.8 27.8 %collective-permute-start.32 = (bf16[8,192,384]{2,1,0:T(8,128)(2,1)S(1)}, bf16[8,192,384]{2,1,0:T(8,128)(2,1)S(1)}, u32[]{:S(2)}, u32[]{:S(2)}) collective-permute-start(bf16[8,192,384]{2,1,0:T(8,128)(2,1)S(1)} %pad_maximum_fusion.2), channel_id=1, source_target_pairs={{0,1},{1,0},{2,3},{3,2},{4,5},{5,4},{6,7},{7,6},{8,9},{9,8},{10,11... | collective-permute-start | bytes 3538952 | tf_op jit(solution)/shard_map/ppermute | solution.py:577
  153.0 8.0 %collective-permute-start.35 = (bf16[1,16,96,768]{3,2,1,0:T(8,128)(2,1)}, bf16[1,16,96,768]{3,2,1,0:T(8,128)(2,1)S(1)}, u32[]{:S(2)}, u32[]{:S(2)}) collective-permute-start(bf16[1,16,96,768]{3,2,1,0:T(8,128)(2,1)} %bitcast.349), channel_id=1, source_target_pairs={{0,1},{1,0},{2,3},{3,2},{4,5},{5,4},{6,7},{7,6},{8,9},{9,8},{10,11... | collective-permute-start | bytes 7077896 | tf_op jit(solution)/shard_map/ppermute | solution.py:577
  164.2 28.1 %collective-permute-start.36 = (bf16[1,2,2,2,24,3072]{5,4,3,2,1,0:T(8,128)(2,1)S(1)}, bf16[1,2,2,2,24,3072]{5,4,3,2,1,0:T(8,128)(2,1)S(1)}, u32[]{:S(2)}, u32[]{:S(2)}) collective-permute-start(bf16[1,2,2,2,24,3072]{5,4,3,2,1,0:T(8,128)(2,1)S(1)} %fusion), channel_id=1, source_target_pairs={{0,4},{1,5},{2,6},{3,7},{4,0},{5,1},{6,2},{7,3},{8,12},{9,13},{10,... | collective-permute-start | bytes 3538952 | tf_op jit(solution)/shard_map/ppermute | solution.py:577
  167.6 27.8 %collective-permute-start.37 = (bf16[1,2,2,2,96,768]{5,4,3,2,1,0:T(8,128)(2,1)S(1)}, bf16[1,2,2,2,96,768]{5,4,3,2,1,0:T(8,128)(2,1)S(1)}, u32[]{:S(2)}, u32[]{:S(2)}) collective-permute-start(bf16[1,2,2,2,96,768]{5,4,3,2,1,0:T(8,128)(2,1)S(1)} %fusion.1), channel_id=1, source_target_pairs={{0,2},{1,3},{2,0},{3,1},{4,6},{5,7},{6,4},{7,5},{8,10},{9,11},{10,... | collective-permute-start | bytes 3538952 | tf_op jit(solution)/shard_map/ppermute | solution.py:577
  197.5 22.9 %collective-permute-start.39 = (bf16[1,2,2,24,3072]{4,3,2,1,0:T(8,128)(2,1)S(1)}, bf16[1,2,2,24,3072]{4,3,2,1,0:T(8,128)(2,1)}, u32[]{:S(2)}, u32[]{:S(2)}) collective-permute-start(bf16[1,2,2,24,3072]{4,3,2,1,0:T(8,128)(2,1)S(1)} %fusion.5), channel_id=1, source_target_pairs={{0,8},{1,9},{2,10},{3,11},{4,12},{5,13},{6,14},{7,15},{8,0},{9,1},... | collective-permute-start | bytes 1769480 | tf_op jit(solution)/shard_map/ppermute | solution.py:577
  199.5 20.9 %collective-permute-start.40 = (bf16[1,2,2,96,768]{4,3,2,1,0:T(8,128)(2,1)S(1)}, bf16[1,2,2,96,768]{4,3,2,1,0:T(8,128)(2,1)}, u32[]{:S(2)}, u32[]{:S(2)}) collective-permute-start(bf16[1,2,2,96,768]{4,3,2,1,0:T(8,128)(2,1)S(1)} %fusion.4), channel_id=1, source_target_pairs={{0,4},{1,5},{2,6},{3,7},{4,0},{5,1},{6,2},{7,3},{8,12},{9,13},{10,... | collective-permute-start | bytes 1769480 | tf_op jit(solution)/shard_map/ppermute | solution.py:577
  220.4 11.2 %collective-permute-start.41 = (bf16[2,16,24,768]{3,2,1,0:T(8,128)(2,1)}, bf16[2,16,24,768]{3,2,1,0:T(8,128)(2,1)}, u32[]{:S(2)}, u32[]{:S(2)}) collective-permute-start(bf16[2,16,24,768]{3,2,1,0:T(8,128)(2,1)} %bitcast.352), channel_id=1, source_target_pairs={{0,1},{1,0},{2,3},{3,2},{4,5},{5,4},{6,7},{7,6},{8,9},{9,8},{10,11... | collective-permute-start | bytes 3538952 | tf_op jit(solution)/shard_map/ppermute | solution.py:577
  220.6 13.4 %collective-permute-start.42 = (bf16[2,16,24,768]{3,2,1,0:T(8,128)(2,1)}, bf16[2,16,24,768]{3,2,1,0:T(8,128)(2,1)}, u32[]{:S(2)}, u32[]{:S(2)}) collective-permute-start(bf16[2,16,24,768]{3,2,1,0:T(8,128)(2,1)} %bitcast.351), channel_id=1, source_target_pairs={{0,1},{1,0},{2,3},{3,2},{4,5},{5,4},{6,7},{7,6},{8,9},{9,8},{10,11... | collective-permute-start | bytes 3538952 | tf_op jit(solution)/shard_map/ppermute | solution.py:577
  221.0 29.1 %collective-permute-start.43 = (bf16[4,2,2,2,24,768]{5,4,0,3,2,1:T(8,128)(2,1)}, bf16[4,2,2,2,24,768]{5,4,0,3,2,1:T(8,128)(2,1)}, u32[]{:S(2)}, u32[]{:S(2)}) collective-permute-start(bf16[4,2,2,2,24,768]{5,4,0,3,2,1:T(8,128)(2,1)} %fusion.2), channel_id=1, source_target_pairs={{0,2},{1,3},{2,0},{3,1},{4,6},{5,7},{6,4},{7,5},{8,10},{9,11},{10,... | collective-permute-start | bytes 3538952 | tf_op jit(solution)/shard_map/ppermute | solution.py:577
  232.9 34.1 %collective-permute-start.44 = (bf16[2,2,2,2,24,768]{5,4,0,3,2,1:T(8,128)(2,1)S(1)}, bf16[2,2,2,2,24,768]{5,4,0,3,2,1:T(8,128)(2,1)S(1)}, u32[]{:S(2)}, u32[]{:S(2)}) collective-permute-start(bf16[2,2,2,2,24,768]{5,4,0,3,2,1:T(8,128)(2,1)S(1)} %fusion.12), channel_id=1, source_target_pairs={{0,2},{1,3},{2,0},{3,1},{4,6},{5,7},{6,4},{7,5},{8,10},{9,11},{10,... | collective-permute-start | bytes 1769480 | tf_op jit(solution)/shard_map/ppermute | solution.py:577
  235.6 34.3 %collective-permute-start.48 = (bf16[2,2,2,2,24,768]{5,4,0,3,2,1:T(8,128)(2,1)S(1)}, bf16[2,2,2,2,24,768]{5,4,0,3,2,1:T(8,128)(2,1)S(1)}, u32[]{:S(2)}, u32[]{:S(2)}) collective-permute-start(bf16[2,2,2,2,24,768]{5,4,0,3,2,1:T(8,128)(2,1)S(1)} %fusion.13), channel_id=1, source_target_pairs={{0,4},{1,5},{2,6},{3,7},{4,0},{5,1},{6,2},{7,3},{8,12},{9,13},{10,... | collective-permute-start | bytes 1769480 | tf_op jit(solution)/shard_map/ppermute | solution.py:577
  251.8 20.1 %collective-permute-start.53 = (bf16[1,2,96,768]{3,2,1,0:T(8,128)(2,1)}, bf16[1,2,96,768]{3,2,1,0:T(8,128)(2,1)}, u32[]{:S(2)}, u32[]{:S(2)}) collective-permute-start(bf16[1,2,96,768]{3,2,1,0:T(8,128)(2,1)} %fusion.18), channel_id=1, source_target_pairs={{0,8},{1,9},{2,10},{3,11},{4,12},{5,13},{6,14},{7,15},{8,0},{9,1},... | collective-permute-start | bytes 884744 | tf_op jit(solution)/shard_map/ppermute | solution.py:577
  253.0 20.9 %collective-permute-start.54 = (bf16[1,2,24,3072]{3,2,1,0:T(8,128)(2,1)}, bf16[1,2,24,3072]{3,2,1,0:T(8,128)(2,1)}, u32[]{:S(2)}, u32[]{:S(2)}) collective-permute-start(bf16[1,2,24,3072]{3,2,1,0:T(8,128)(2,1)} %fusion.17), channel_id=1, source_target_pairs={{0,16},{1,17},{2,18},{3,19},{4,20},{5,21},{6,22},{7,23},{8,24},{9,... | collective-permute-start | bytes 884744 | tf_op jit(solution)/shard_map/ppermute | solution.py:577
  256.4 19.4 %collective-permute-start.52 = (bf16[4,2,2,24,768]{4,3,0,1,2:T(8,128)(2,1)S(1)}, bf16[4,2,2,24,768]{4,3,0,1,2:T(8,128)(2,1)S(1)}, u32[]{:S(2)}, u32[]{:S(2)}) collective-permute-start(bf16[4,2,2,24,768]{4,3,0,1,2:T(8,128)(2,1)S(1)} %copy.88), channel_id=1, source_target_pairs={{0,4},{1,5},{2,6},{3,7},{4,0},{5,1},{6,2},{7,3},{8,12},{9,13},{10,... | collective-permute-start | bytes 1769480 | tf_op jit(solution)/shard_map/ppermute | solution.py:577
  269.1 12.8 %collective-permute-start.45 = (bf16[2,2,2,24,768]{4,3,0,2,1:T(8,128)(2,1)}, bf16[2,2,2,24,768]{4,3,0,2,1:T(8,128)(2,1)}, u32[]{:S(2)}, u32[]{:S(2)}) collective-permute-start(bf16[2,2,2,24,768]{4,3,0,2,1:T(8,128)(2,1)} %fusion.16), channel_id=1, source_target_pairs={{0,4},{1,5},{2,6},{3,7},{4,0},{5,1},{6,2},{7,3},{8,12},{9,13},{10,... | collective-permute-start | bytes 884744 | tf_op jit(solution)/shard_map/ppermute | solution.py:577
  270.8 13.8 %collective-permute-start.49 = (bf16[2,2,2,24,768]{4,3,0,2,1:T(8,128)(2,1)}, bf16[2,2,2,24,768]{4,3,0,2,1:T(8,128)(2,1)}, u32[]{:S(2)}, u32[]{:S(2)}) collective-permute-start(bf16[2,2,2,24,768]{4,3,0,2,1:T(8,128)(2,1)} %fusion.15), channel_id=1, source_target_pairs={{0,8},{1,9},{2,10},{3,11},{4,12},{5,13},{6,14},{7,15},{8,0},{9,1},... | collective-permute-start | bytes 884744 | tf_op jit(solution)/shard_map/ppermute | solution.py:577
  278.6 11.5 %collective-permute-start.55 = (bf16[4,2,24,768]{3,2,0,1:T(8,128)(2,1)}, bf16[4,2,24,768]{3,2,0,1:T(8,128)(2,1)}, u32[]{:S(2)}, u32[]{:S(2)}) collective-permute-start(bf16[4,2,24,768]{3,2,0,1:T(8,128)(2,1)} %fusion.14), channel_id=1, source_target_pairs={{0,8},{1,9},{2,10},{3,11},{4,12},{5,13},{6,14},{7,15},{8,0},{9,1},... | collective-permute-start | bytes 884744 | tf_op jit(solution)/shard_map/ppermute | solution.py:577
  280.8 11.2 %collective-permute-start.57 = (bf16[1,24,3072]{2,1,0:T(8,128)(2,1)}, bf16[1,24,3072]{2,1,0:T(8,128)(2,1)S(1)}, u32[]{:S(2)}, u32[]{:S(2)}) collective-permute-start(bf16[1,24,3072]{2,1,0:T(8,128)(2,1)} %fusion.25), channel_id=1, source_target_pairs={{0,2},{1,3},{2,0},{3,1},{4,6},{5,7},{6,4},{7,5},{8,10},{9,11},{10,... | collective-permute-start | bytes 442376 | tf_op jit(solution)/shard_map/ppermute | solution.py:577
  281.9 12.8 %collective-permute-start.58 = (bf16[1,96,768]{2,1,0:T(8,128)(2,1)}, bf16[1,96,768]{2,1,0:T(8,128)(2,1)S(1)}, u32[]{:S(2)}, u32[]{:S(2)}) collective-permute-start(bf16[1,96,768]{2,1,0:T(8,128)(2,1)} %fusion.26), channel_id=1, source_target_pairs={{0,16},{1,17},{2,18},{3,19},{4,20},{5,21},{6,22},{7,23},{8,24},{9,... | collective-permute-start | bytes 442376 | tf_op jit(solution)/shard_map/ppermute | solution.py:577
  283.8 14.3 %collective-permute-start.46 = (bf16[2,2,24,768]{3,2,0,1:T(8,128)(2,1)}, bf16[2,2,24,768]{3,2,0,1:T(8,128)(2,1)}, u32[]{:S(2)}, u32[]{:S(2)}) collective-permute-start(bf16[2,2,24,768]{3,2,0,1:T(8,128)(2,1)} %fusion.28), channel_id=1, source_target_pairs={{0,8},{1,9},{2,10},{3,11},{4,12},{5,13},{6,14},{7,15},{8,0},{9,1},... | collective-permute-start | bytes 442376 | tf_op jit(solution)/shard_map/ppermute | solution.py:577
  286.4 15.7 %collective-permute-start.50 = (bf16[2,2,24,768]{3,2,0,1:T(8,128)(2,1)}, bf16[2,2,24,768]{3,2,0,1:T(8,128)(2,1)}, u32[]{:S(2)}, u32[]{:S(2)}) collective-permute-start(bf16[2,2,24,768]{3,2,0,1:T(8,128)(2,1)} %fusion.27), channel_id=1, source_target_pairs={{0,16},{1,17},{2,18},{3,19},{4,20},{5,21},{6,22},{7,23},{8,24},{9,... | collective-permute-start | bytes 442376 | tf_op jit(solution)/shard_map/ppermute | solution.py:577
  292.0 12.4 %collective-permute-start.56 = (bf16[4,24,768]{2,1,0:T(8,128)(2,1)}, bf16[4,24,768]{2,1,0:T(8,128)(2,1)}, u32[]{:S(2)}, u32[]{:S(2)}) collective-permute-start(bf16[4,24,768]{2,1,0:T(8,128)(2,1)} %fusion.23), channel_id=1, source_target_pairs={{0,16},{1,17},{2,18},{3,19},{4,20},{5,21},{6,22},{7,23},{8,24},{9,... | collective-permute-start | bytes 442376 | tf_op jit(solution)/shard_map/ppermute | solution.py:577
  299.1 9.6 %collective-permute-start.47 = (bf16[2,24,768]{2,1,0:T(8,128)(2,1)S(1)}, bf16[2,24,768]{2,1,0:T(8,128)(2,1)S(1)}, u32[]{:S(2)}, u32[]{:S(2)}) collective-permute-start(bf16[2,24,768]{2,1,0:T(8,128)(2,1)S(1)} %fusion.31), channel_id=1, source_target_pairs={{0,16},{1,17},{2,18},{3,19},{4,20},{5,21},{6,22},{7,23},{8,24},{9,... | collective-permute-start | bytes 221192 | tf_op jit(solution)/shard_map/ppermute | solution.py:577
  (57 other events, 425.1 us)

commit v5 on v4

--- a/solution.py
+++ b/solution.py
@@ -3,6 +3,7 @@
 
 import jax
 import jax.numpy as jnp
+import numpy as np
 from jax import lax
 from jax.experimental import pallas as pl
 from jax.experimental.pallas import tpu as pltpu
@@ -207,14 +208,6 @@
     return jnp.pad(lines, ((0, 0), (0, 8 - GROUP), (0, 0)))
 
 
-def table_sums(sums):
-    near = sums[:, :GROUP].reshape(HEADS, 2 * LANES)
-    far = jnp.sum(sums[:, GROUP : 2 * GROUP], axis=-1).reshape(HEADS)
-    places = bucket_table(jnp.arange(2 * LANES, dtype=jnp.int32), jnp.float32)
-    grad = jnp.einsum("nb,hn->bh", places, near, precision=lax.Precision.HIGHEST)
-    return grad.at[BUCKETS - 1].add(far)
-
-
 GELU_SCALE = math.sqrt(2.0 / math.pi)
 GELU_CUBE = 0.044715
 BLOCK = 768
@@ -247,15 +240,19 @@
         weight_ref[lines, other] = parts[2 + which][block, at * rows : (at + 1) * rows]
 
 
-def put_divided(grads, rows, core, sent_ref, kept_ref):
-    columns = grads.shape[1]
-    grads = grads.reshape(-1, 2, rows, columns)
-    even, odd = grads[:, 0].reshape(-1, columns), grads[:, 1].reshape(-1, columns)
-    sent_ref[...] = jnp.where(core == 0, odd, even).astype(jnp.bfloat16)
-    kept_ref[...] = jnp.where(core == 0, even, odd).astype(jnp.bfloat16)
-
-
-def ffn_kernel(tiled, plan, spot_ref, third_ref, upper_ref, cot_ref, *refs):
+def sums_order(plan):
+    bits = [which for group in plan for which in group]
+    count = 1 << len(bits)
+    return [sum(((k >> at) & 1) << (which - 1) for at, which in enumerate(bits)) for k in range(count)]
+
+
+def divided(grads, rows, core):
+    grads = grads.reshape(-1, 2, rows, grads.shape[1])
+    even, odd = grads[:, 0], grads[:, 1]
+    return jnp.where(core == 0, odd, even), jnp.where(core == 0, even, odd)
+
+
+def ffn_kernel(tiled, plans, spot_ref, third_ref, upper_ref, cot_ref, *refs):
     step = pl.program_id(0)
     if tiled:
         own_in, other_in, out_parts, refs = refs[:2], refs[2:4], refs[4:8], refs[8:]
@@ -274,7 +271,7 @@
     def fill_in(parts):
         blocks, rows, _ = parts[0].shape
         for place in range(2 * blocks):
-            chip = chip_of(spot_ref[0], place, plan)
+            chip = chip_of(spot_ref[0], place, plans[1])
             lines = pl.ds(pl.multiple_of(chip * rows, rows), rows)
             in_block[lines, :] = parts[place // blocks][place % blocks]
 
@@ -304,8 +301,16 @@
     grad_out = dot(active, cot_ref[...], TN)
     if tiled:
         chips = 2 * own_in[0].shape[0]
-        put_divided(grad_in, D // (2 * chips), spot_ref[1], gin_ref, kept_gin_ref)
-        put_divided(grad_out, FF // (2 * chips), spot_ref[1], gout_ref, kept_gout_ref)
+        order = sums_order(plans[1])
+        parts = divided(grad_in, D // (2 * chips), spot_ref[1])
+        for part, result in zip(parts, (gin_ref, kept_gin_ref)):
+            part = jnp.concatenate([part[chip] for chip in order], axis=0)
+            result[...] = part.astype(jnp.bfloat16)
+        parts = divided(grad_out, FF // (2 * chips), spot_ref[1])
+        for part, result in zip(parts, (gout_ref, kept_gout_ref)):
+            for place in range(4):
+                chip = (place >> 1) | ((place & 1) << 1)
+                result[place, 0] = part[chip].astype(jnp.bfloat16)
     else:
         gin_ref[...] = grad_in.astype(jnp.bfloat16)
         gout_ref[...] = grad_out.astype(jnp.bfloat16)
@@ -315,7 +320,7 @@
         layer_ref[...] = total[...].astype(jnp.bfloat16)
 
 
-def ffn(spot, plan, third, upper, cotangent, in_parts, out_parts):
+def ffn(spot, plans, third, upper, cotangent, in_parts, out_parts):
     rows = third.shape[0]
     tiled = len(in_parts) > 1
 
@@ -339,14 +344,15 @@
         out_parts = [part.reshape(2, 4, -1, D // 2) for part in out_parts]
         in_specs += [pl.BlockSpec((2, 1) + out_parts[0].shape[2:], line)] * 4
         out_specs = [pl.BlockSpec((D // 2, BLOCK), across)] * 2
-        out_specs += [pl.BlockSpec((BLOCK // 2, D), down)] * 2
-        shapes = [(D // 2, FF)] * 2 + [(FF // 2, D)] * 2
+        own = lambda step, spot_ref: (0, (b := block(step, spot_ref)) // 2 + 2 * (b % 2), 0, 0)
+        out_specs += [pl.BlockSpec((4, 1, FF // (4 * chips), D), own)] * 2
+        shapes = [(D // 2, FF)] * 2 + [(4, 4, FF // (4 * chips), D)] * 2
         scratch += [pltpu.VMEM((D, BLOCK), jnp.bfloat16), pltpu.VMEM((BLOCK, D), jnp.bfloat16)]
     else:
         in_specs = [pl.BlockSpec((D, BLOCK), across), pl.BlockSpec((BLOCK, D), down)]
         out_specs, shapes = in_specs, [(D, FF), (FF, D)]
     return pl.pallas_call(
-        functools.partial(ffn_kernel, tiled, plan),
+        functools.partial(ffn_kernel, tiled, plans),
         grid_spec=pltpu.PrefetchScalarGridSpec(
             num_scalar_prefetch=1,
             grid=(2 * CUTS,),
@@ -485,27 +491,45 @@
 def last_back(
     gq_ref, gk_ref, gv_ref, gmk_ref, gmv_ref, tokens_ref, gmiddle_ref, gain_ref,
     wq_ref, wk_ref, wv_ref, wmk_ref, wmv_ref,
-    gtokens_ref, gmemory_ref, ggain_ref,
+    sums_ref, places_ref, ggain_two_ref, ggain_three_ref, gtokens_ref, gmemory_ref, extra_ref,
 ):
+    near = sums_ref[:, :GROUP].reshape(HEADS, 2 * LANES)
+    far = jnp.sum(sums_ref[:, GROUP : 2 * GROUP].reshape(HEADS, 2 * LANES), axis=1, keepdims=True)
+    high = near.astype(jnp.bfloat16)
+    left = near - high.astype(jnp.float32)
+    middle = left.astype(jnp.bfloat16)
+    least = (left - middle.astype(jnp.float32)).astype(jnp.bfloat16)
+    places = places_ref[...]
+    lane = lax.broadcasted_iota(jnp.int32, (HEADS, BUCKETS * HEADS), 1)
+    head = lax.broadcasted_iota(jnp.int32, (HEADS, BUCKETS * HEADS), 0)
+    table = dot(high, places) + dot(middle, places) + dot(least, places)
+    table = table + jnp.where(lane // HEADS == BUCKETS - 1, far, 0.0)
+    table = jnp.sum(jnp.where(lane % HEADS == head, table, 0.0), axis=0, keepdims=True)
+    table = jnp.concatenate([table, jnp.zeros((1, D - table.shape[1]), jnp.float32)], axis=1)
     gmemory_ref[...] = dot(gmk_ref[...], wmk_ref[...], NT) + dot(gmv_ref[...], wmv_ref[...], NT)
     gfirst = dot(gq_ref[...], wq_ref[...], NT) + dot(gk_ref[...], wk_ref[...], NT)
     gfirst = gfirst + dot(gv_ref[...], wv_ref[...], NT)
     hidden = tokens_ref[...].astype(jnp.float32)
-    grad, ggain_ref[...] = norm_back(hidden, gain_ref[...], gfirst)
+    grad, ggain = norm_back(hidden, gain_ref[...], gfirst)
     gtokens_ref[...] = gmiddle_ref[...] + grad
-
-
-def put_products(core_ref, rows, pairs, sent_ref, kept_ref):
-    for k, (left, right) in enumerate(pairs):
-        grads = dot(left[...], right[...], TN)
-        if kept_ref is None:
-            sent_ref[k] = grads.astype(jnp.bfloat16)
-        else:
-            put_divided(grads, rows, core_ref[0], sent_ref.at[k], kept_ref.at[k])
+    lines = [ggain, ggain_two_ref[...], ggain_three_ref[...], table] + zero_rows(4)
+    extra_ref[...] = jnp.concatenate(lines, axis=0)
+
+
+def put_products(core_ref, rows, plan, pairs, sent_ref, kept_ref):
+    if kept_ref is None:
+        for k, (left, right) in enumerate(pairs):
+            sent_ref[k] = dot(left[...], right[...], TN).astype(jnp.bfloat16)
+        return
+    parts = [divided(dot(left[...], right[...], TN), rows, core_ref[0]) for left, right in pairs]
+    for which, result in enumerate((sent_ref, kept_ref)):
+        for place, chip in enumerate(sums_order(plan)):
+            lines = jnp.concatenate([part[which][chip] for part in parts], axis=0)
+            result[place] = lines.astype(jnp.bfloat16)
 
 
 def cross_back(
-    rows, core_ref, q_ref, k_ref, v_ref, gcrossed_ref, probs_ref,
+    rows, plans, core_ref, q_ref, k_ref, v_ref, gcrossed_ref, probs_ref,
     second_ref, memory_ref, crossed_ref, gcross_ref, middle_ref, gupper_ref, gain_ref,
     wq_ref, wso_ref,
     gk_ref, gv_ref, gmiddle_ref, branch_ref, gmix_ref, ggain_ref, sent_ref, *rest,
@@ -525,7 +549,7 @@
             (memory_ref, gv_ref),
             (crossed_ref, gcross_ref),
         ]
-        put_products(core_ref, rows, pairs, sent_ref, kept_ref)
+        put_products(core_ref, rows, plans[0], pairs, sent_ref, kept_ref)
         gsecond = dot(gq_ref[...], wq_ref[...], NT)
         grad, ggain_ref[...] = norm_back(middle_ref[...], gain_ref[...], gsecond)
         grad = gupper_ref[...] + grad
@@ -536,7 +560,7 @@
 
 
 def self_back(
-    rows, core_ref, q_ref, k_ref, v_ref, gmixed_ref, probs_ref, first_ref, mixed_ref, gself_ref,
+    rows, plans, core_ref, q_ref, k_ref, v_ref, gmixed_ref, probs_ref, first_ref, mixed_ref, gself_ref,
     gq_ref, gk_ref, gv_ref, sums_ref, late_sent_ref, early_sent_ref, *rest,
 ):
     kept, (dk_sum, dv_sum) = rest[:2] if len(rest) == 4 else (None, None), rest[-2:]
@@ -550,8 +574,89 @@
     def _():
         late = [(first_ref, gv_ref), (mixed_ref, gself_ref)]
         early = [(first_ref, gq_ref), (first_ref, gk_ref)]
-        put_products(core_ref, rows, late, late_sent_ref, kept[0])
-        put_products(core_ref, rows, early, early_sent_ref, kept[1])
+        put_products(core_ref, rows, plans[1], late, late_sent_ref, kept[0])
+        put_products(core_ref, rows, plans[0], early, early_sent_ref, kept[1])
+
+
+def term_specs(chains):
+    specs = []
+    for terms in chains:
+        for term, at in terms:
+
+            def place(step, spot_ref, at=at):
+                bits = [((spot_ref[0] >> (which - 1)) & 1) * weight for which, _, weight in at]
+                return (sum(bits, step), 0, 0)
+
+            specs.append(pl.BlockSpec((1,) + term.shape[1:], place))
+    return specs
+
+
+def row_sums(squares):
+    ones = jnp.ones((8, squares.shape[1]), jnp.bfloat16)
+    high = squares.astype(jnp.bfloat16)
+    left = (squares - high.astype(jnp.float32)).astype(jnp.bfloat16)
+    return (dot(ones, high, NT) + dot(ones, left, NT))[:1]
+
+
+def finish(terms, value_ref, rows_ref):
+    count, rows, columns = value_ref.shape
+    value = sum(term[0].astype(jnp.float32) for term in terms).reshape(count, rows, columns)
+    value_ref[...] = value
+    lines = []
+    for k in range(count):
+        squares = value[k] * value[k]
+        rows_ref[k : k + 1] = row_sums(squares) * (1.0 / columns)
+        lines.append(jnp.sum(squares, axis=0, keepdims=True))
+    return lines
+
+
+def zero_rows(count):
+    return [jnp.zeros((1, D), jnp.float32)] * count
+
+
+def ffn_last(counts, spot_ref, *refs):
+    ins, outs, refs = refs[: counts[0]], refs[counts[0] : sum(counts)], refs[sum(counts) :]
+    in_ref, in_rows_ref, out_ref, out_rows_ref, columns_ref = refs
+    (wide,) = finish(ins, in_ref, in_rows_ref)
+    lines = finish(outs, out_ref, out_rows_ref)
+    lines = lines + [wide[:, at : at + D] for at in range(0, FF, D)]
+    columns_ref[...] = jnp.concatenate(lines + zero_rows(8 - len(lines)), axis=0)
+
+
+def cross_last(counts, spot_ref, *refs):
+    value_ref, rows_ref, columns_ref = refs[counts[0] :]
+    lines = finish(refs[: counts[0]], value_ref, rows_ref)
+    columns_ref[...] = jnp.concatenate(lines + zero_rows(8 - len(lines)), axis=0)
+
+
+def self_last(counts, spot_ref, *refs):
+    one, two, refs = refs[: counts[0]], refs[counts[0] : sum(counts)], refs[sum(counts) :]
+    cross_ref, ffn_ref, extra_ref, early_ref, early_rows_ref, late_ref, late_rows_ref, all_ref = refs
+    lines = finish(one, early_ref, early_rows_ref) + finish(two, late_ref, late_rows_ref)
+    all_ref[:8] = jnp.concatenate(lines + [cross_ref[:4]], axis=0)
+    all_ref[8:16] = ffn_ref[...]
+    all_ref[16:] = extra_ref[...]
+
+
+def last_terms(kernel, spot, chains, shapes, extras, lines):
+    asked = [chain.terms for chain in chains]
+    outs = []
+    for shape in shapes:
+        outs += [shape, shape[:2]]
+    outs.append((lines, D))
+    whole = lambda shape: pl.BlockSpec(shape, lambda step, _: (0,) * len(shape))
+    return pl.pallas_call(
+        functools.partial(kernel, [len(terms) for terms in asked]),
+        grid_spec=pltpu.PrefetchScalarGridSpec(
+            num_scalar_prefetch=1,
+            grid=(1,),
+            in_specs=term_specs(asked) + [whole(extra.shape) for extra in extras],
+            out_specs=[whole(shape) for shape in outs],
+        ),
+        out_shape=[jax.ShapeDtypeStruct(shape, jnp.float32) for shape in outs],
+        compiler_params=pltpu.CompilerParams(vmem_limit_bytes=VMEM_BYTES),
+        name=kernel.__name__,
+    )(spot, *[term for terms in asked for term, _ in terms], *extras)
 
 
 AXES = ("wide", "narrow")
@@ -629,43 +734,37 @@
 
 class Sums:
     def __init__(self, cube, plan, sent, kept):
-        self.cube, self.plan, self.steps = cube, plan, 0
-        self.bits = sorted(which for group in plan for which in group)
-        self.shape = (kept.shape[0],) + (2,) * len(self.bits) + (-1, kept.shape[-1])
-        self.terms, self.theirs = [kept.reshape(self.shape)], [cube.swap(sent, 1)]
+        self.cube, self.bits = cube, [which for group in reversed(plan) for which in group]
+        self.blocks, self.theirs = cube.count // 2, cube.swap(sent, 1)
+        self.terms = [(kept, [])]
 
     def take(self, *behind):
-        for their in self.theirs:
-            their = after(their, *behind) if behind else their
-            self.terms.append(their.reshape(self.shape) if self.steps == 0 else their)
-
-    def value(self):
-        return sum(term.astype(jnp.float32) for term in self.terms)
-
-    def pick(self, group, flip):
-        terms = self.terms
-        for which in sorted(group):
-            axis = 1 + sum(other > which for other in self.bits)
-            index = self.cube.bit(which) ^ ((flip >> which) & 1)
-            terms = [lax.dynamic_index_in_dim(term, index, axis, False) for term in terms]
-        return terms
-
-    def send(self, *behind):
-        group = self.plan[-1 - self.steps]
-        everything, sent = self.terms, []
-        for flip in flips_of(group):
-            self.terms = self.pick(group, flip)
-            part = self.value().astype(jnp.bfloat16)
-            sent.append(after(part, *behind) if behind else part)
-            self.terms = everything
-        self.terms = self.pick(group, 0)
-        self.bits = [which for which in self.bits if which not in group]
-        self.theirs = [self.cube.swap(part, flip) for part, flip in zip(sent, flips_of(group))]
-        self.steps += 1
-        return tuple(sent)
+        self.terms.append((after(self.theirs, *behind) if behind else self.theirs, []))
+
+    def begin(self, at):
+        bits = [(self.cube.bit(which) ^ flip) * weight for which, flip, weight in at]
+        return sum(bits, jnp.int32(0))
+
+    def send(self):
+        which = self.bits.pop(0)
+        self.blocks //= 2
+        parts = [
+            lax.dynamic_slice_in_dim(
+                term, self.begin(at + [(which, 1, self.blocks)]), self.blocks, 0
+            ).astype(jnp.float32)
+            for term, at in self.terms
+        ]
+        sent = sum(parts).astype(jnp.bfloat16)
+        self.terms = [(term, at + [(which, 0, self.blocks)]) for term, at in self.terms]
+        self.theirs = self.cube.swap(sent, 1 << which)
+        return sent
 
     def going(self):
-        return self.steps < len(self.plan)
+        return len(self.bits) > 0
+
+
+def send_all(chains):
+    return tuple([chain.send() for chain in chains])
 
 
 def whole_tiles(cube):
@@ -674,17 +773,20 @@
 
 def product_outs(cube, count):
     if whole_tiles(cube):
-        return [((count, D // 2, D), jnp.bfloat16)] * 2
+        return [((cube.count // 2, count * (D // cube.count), D), jnp.bfloat16)] * 2
     return [((count, D, D), jnp.bfloat16)]
 
 
 def product_sums(cube, plan, parts, *behind):
-    chips, count, columns = cube.count // 2, parts[0].shape[0], parts[0].shape[2]
+    chips = cube.count // 2
     if len(parts) == 1:
-        grads = parts[0].reshape(count, chips, 2, -1, columns)
+        count, _, columns = parts[0].shape
+        grads = parts[0].reshape(count, chips, 2, -1, columns).transpose(2, 1, 0, 3, 4)
+        grads = grads.reshape(2, chips, -1, columns)
+        grads = jnp.take(grads, np.array(sums_order(plan)), axis=1)
         core = cube.bit(0)
-        parts = [lax.dynamic_index_in_dim(grads, core ^ k, 2, False) for k in (1, 0)]
-    sent, kept = [part.reshape(count, chips, -1, columns) for part in parts]
+        parts = [lax.dynamic_index_in_dim(grads, core ^ k, 0, False) for k in (1, 0)]
+    sent, kept = [part.reshape(chips, -1, part.shape[-1]) for part in parts]
     return Sums(cube, plan, after(sent, *behind) if behind else sent, kept)
 
 
@@ -723,6 +825,10 @@
     see_self = self_mask(segment, dec_valid[0])
     see_cross = cross_mask(segment, enc_segments[0])
     lines = bias_lines(rel_table)
+    distances = np.arange(2 * LANES)[:, None]
+    places = (distances >= np.array(thresholds())[None, :]).sum(axis=1, keepdims=True)
+    places = np.repeat(places == np.arange(BUCKETS)[None, :], HEADS, axis=1)
+    places = jnp.asarray(places.astype(np.float32), jnp.bfloat16)
     tile, low, full = tokens.shape, jnp.bfloat16, jnp.float32
     square = ((D, D), low)
     probs = (HEADS, segment.shape[0], segment.shape[0])
@@ -818,11 +924,12 @@
         in_parts = [lax.all_gather(w_in, AXES, axis=0, tiled=True)]
         out_parts = [lax.all_gather(w_out, AXES, axis=0, tiled=True)]
     layer_out, grad_third, *rest = ffn(
-        spot, plans[1], third_low, upper, cotangent, in_parts, out_parts
+        spot, plans, third_low, upper, cotangent, in_parts, out_parts
     )
     half = len(rest) // 2
-    in_sums = product_sums(cube, cube.plan_b, [part[None] for part in rest[:half]])
-    out_sums = product_sums(cube, cube.plan_a, [part[None] for part in rest[half:]])
+    parts = rest if tiled else [part[None] for part in rest]
+    in_sums = product_sums(cube, cube.plan_b, parts[:half])
+    out_sums = product_sums(cube, cube.plan_a, parts[half:])
     grad_upper, grad_cross_branch, grad_crossed, grad_gain_third = fused(
         third_back,
         [(tile, full), (tile, low), (tile, low), ((1, D), full)],
@@ -834,10 +941,10 @@
     )
     in_sums.take(grad_crossed)
     out_sums.take(grad_crossed)
-    grad_crossed = after(grad_crossed, *in_sums.send(), *out_sums.send())
+    grad_crossed = after(grad_crossed, *send_all((in_sums, out_sums)))
     sums_scratch = [pltpu.VMEM((tile[0], LANES), full)] * 2
     memory_key_low, memory_value_low, grad_middle, grad_self_branch, grad_mixed, *rest = by_pair(
-        functools.partial(cross_back, rows),
+        functools.partial(cross_back, rows, plans),
         [
             core[None],
             cross_query,
@@ -865,15 +972,15 @@
     grad_gain_second = rest[0]
     for each in (in_sums, out_sums):
         each.take(grad_mixed)
-    arrived = in_sums.terms[-1], out_sums.terms[-1]
+    arrived = in_sums.terms[-1][0], out_sums.terms[-1][0]
     cross_sums = product_sums(cube, cube.plan_a, rest[1:], *arrived)
-    started = in_sums.send() + out_sums.send()
+    started = send_all((in_sums, out_sums))
     cross_sums.take(*started)
-    grad_mixed = after(grad_mixed, *started, *cross_sums.send())
+    grad_mixed = after(grad_mixed, *started, *send_all((cross_sums,)))
     lots = (PAIRS, 8, 2 * LANES)
     outs = product_outs(cube, 2)
     query_low, key_low, value_low, score_sums, *rest = by_pair(
-        functools.partial(self_back, rows),
+        functools.partial(self_back, rows, plans),
         [
             core[None],
             query,
@@ -892,20 +999,18 @@
     )
     for each in (in_sums, out_sums):
         each.take(query_low)
-    arrived = in_sums.terms[-1], out_sums.terms[-1]
+    arrived = in_sums.terms[-1][0], out_sums.terms[-1][0]
     late_sums = product_sums(cube, cube.plan_b, rest[::2], *arrived)
     early_sums = product_sums(cube, cube.plan_a, rest[1::2], *arrived)
-    late_sums.take()
-    early_sums.take()
-    started = early_sums.send() + late_sums.send()
-    started = started + out_sums.send(*started) + in_sums.send(*started)
-    cross_sums.take(*started)
-    started = started + cross_sums.send(*started)
-    sums = [early_sums, late_sums, out_sums, in_sums, cross_sums]
+    cross_sums.take(query_low)
+    started = send_all((out_sums, in_sums, cross_sums))
+    late_sums.take(*started)
+    early_sums.take(*started)
+    started = started + send_all((early_sums, late_sums))
     query_low = after(query_low, *started)
-    grad_tokens, grad_memory, grad_gain_first = fused(
+    grad_tokens, grad_memory, extra = fused(
         last_back,
-        [(tile, full), (tile, full), ((1, D), full)],
+        [(tile, full), (tile, full), ((8, D), full)],
         query_low,
         key_low,
         value_low,
@@ -916,52 +1021,56 @@
         gain_one,
         *attn_full[:3],
         *attn_full[5:7],
-    )
-    table_grad = table_sums(score_sums)
-    gain_local = jnp.concatenate([grad_gain_first, grad_gain_second, grad_gain_third], axis=0)
-    ahead = (grad_tokens,)
-    while sums:
-        moving, ending = [], []
-        for each in sums:
-            (moving if each.going() else ending).append(each)
-        for each in moving:
-            each.take(*ahead)
-            ahead = ahead + each.send()
-        for each in ending:
-            each.take(*ahead)
-        sums, ahead = moving, ()
-    grad_in, grad_out = in_sums.value()[0], out_sums.value()[0]
-    attn_sums = [each.value().reshape(-1, rows, D) for each in (early_sums, late_sums, cross_sums)]
-    grad_attn = jnp.concatenate(attn_sums, axis=0)
-    attn_squares = [value * value for value in attn_sums]
-    square_in = grad_in * grad_in
-    square_out = grad_out * grad_out
-    row_means = jnp.concatenate(
-        [jnp.mean(value, axis=2) for value in attn_squares] + [jnp.mean(square_in, axis=1)[None]], axis=0
-    )
+        score_sums,
+        places,
+        grad_gain_second,
+        grad_gain_third,
+    )
+
+    def move(chains, *behind):
+        for each in chains:
+            each.take(*behind)
+        return send_all(chains)
+
+    started = move((early_sums, late_sums, out_sums, in_sums), grad_tokens)
+    move((cross_sums,), *started)
+    started = move((early_sums, late_sums))
+    while in_sums.going():
+        move((out_sums, in_sums))
+    while cross_sums.going():
+        started = started + move((cross_sums,), *started)
+    for each in (out_sums, in_sums):
+        each.take(*started)
+    grad_in, in_rows, grad_out, out_rows, ffn_columns = last_terms(
+        ffn_last, spot, [in_sums, out_sums], [(1, rows, FF), (1, FF // cube.count, D)], [], 8
+    )
+    while early_sums.going():
+        move((early_sums, late_sums), ffn_columns)
+    cross_sums.take()
+    cross_grads, cross_rows, cross_columns = last_terms(
+        cross_last, spot, [cross_sums], [(4, rows, D)], [], 8
+    )
+    early_sums.take(cross_columns)
+    late_sums.take(cross_columns)
+    early_grads, early_rows, late_grads, late_rows, columns = last_terms(
+        self_last,
+        spot,
+        [early_sums, late_sums],
+        [(2, rows, D)] * 2,
+        [cross_columns, ffn_columns, extra],
+        24,
+    )
+    grad_attn = jnp.concatenate([early_grads, late_grads, cross_grads], axis=0)
+    grad_in, grad_out = grad_in[0], grad_out[0]
+    row_means = jnp.concatenate([early_rows, late_rows, cross_rows, in_rows], axis=0)
     new_row_main = DECAY * row_main + (1.0 - DECAY) * row_means
-    new_row_out = DECAY * row_out + (1.0 - DECAY) * jnp.mean(square_out, axis=1)
-    column_main = jnp.concatenate(
-        [jnp.sum(value, axis=1) for value in attn_squares] + [jnp.sum(square_out, axis=0)[None]], axis=0
-    )
-    column_in = jnp.sum(square_in, axis=0)
-    parts = [column_main, column_in, table_grad, gain_local]
-    sizes = [part.size for part in parts]
-    width = D // 2
-    lines = -(-sum(sizes) // (8 * width)) * 8
-    flat = jnp.concatenate([part.reshape(-1, width) for part in parts], axis=0)
-    flat = cube.total(jnp.pad(flat, ((0, lines - flat.shape[0]), (0, 0))))
-    sums, at = [], 0
-    for part, size in zip(parts, sizes):
-        sums.append(flat[at : at + size // width].reshape(part.shape))
-        at += size // width
-    column_main, column_in, grad_table, gain_sums = sums
-    grad_gains = lax.dynamic_slice_in_dim(
-        gain_sums, cube.me * norm_gains.shape[1], norm_gains.shape[1], 1
-    )
-    col_means = jnp.concatenate([column_main[:8] / D, column_main[8:] / FF], axis=0)
+    new_row_out = DECAY * row_out + (1.0 - DECAY) * out_rows[0]
+    columns = cube.total(columns)
+    col_means = jnp.concatenate([columns[:8] / D, columns[8:9] / FF], axis=0)
     new_col_main = DECAY * col_main + (1.0 - DECAY) * col_means
-    new_col_in = DECAY * col_in + (1.0 - DECAY) * (column_in / D)
+    new_col_in = DECAY * col_in + (1.0 - DECAY) * (columns[9 : 9 + FF // D].reshape(FF) / D)
+    grad_gains = lax.dynamic_slice_in_dim(columns[16:19], cube.me * rows, rows, 1)
+    grad_table = columns[19, : BUCKETS * HEADS].reshape(BUCKETS, HEADS)
     return (
         layer_out,
         grad_tokens,

time: 334 us -> 326 us (0.976)
  other arithmetic: 56.1 us -> 45.4 us
  Pallas kernels: 121 us -> 131 us
  local copies, waits for them, and re-layouts: 15.9 us -> 10.6 us
    reduce_sum x6 -> x0, other arithmetic: 9.47 us -> none  [the longest x3 3.76 us: on_device(): jnp.mean(value, axis=2)]
    pallas_call x1 -> x4, Pallas kernels: 24.3 us -> 33.8 us  [the longest x1 24.5 us: ffn(): pl.pallas_call(functools.partial(ffn_kernel, tiled, plans), grid_spec=plt...]
    reshape x7 -> x0, local copies, waits for them, and re-layouts: 3.54 us -> none  [the longest x4 2.82 us: on_device(): flat = jnp.concatenate([part.reshape(-1, width) for part in parts], axis=0)]
  transfers between devices with their start and end apart: 66 -> 66, of which waited for: 25 -> 25; matrix products, arithmetic and copies ran while one was open for 19% -> 14% of each run, Pallas kernels for 29% -> 32%
where the time goes in v5:
time: 326 us; the launch traced here: 321 us
  Pallas kernels  131 us (40%)
  waiting for transfers between devices  66.8 us (20%)
  starting transfers between devices  65.4 us (20%)
  other arithmetic  45.4 us (14%)
  local copies, waits for them, and re-layouts  10.6 us (3%)
    pallas_call x4, Pallas kernels, by_pair(): pl.pallas_call(kernel, grid=(PAIRS,), in_specs=[spec(array, True) for arr...  82.6 us
    ppermute x66, waiting for transfers between devices, swap(): return lax.ppermute(value, AXES, [(i, i ^ flip) for i in range(self.count)])  66.8 us
    ppermute x66, starting transfers between devices, swap(): return lax.ppermute(value, AXES, [(i, i ^ flip) for i in range(self.count)])  65.4 us
    convert_element_type x20, other arithmetic, send(): sent = sum(parts).astype(jnp.bfloat16)  31.5 us
    pallas_call x1, Pallas kernels, ffn(): pl.pallas_call(functools.partial(ffn_kernel, tiled, plans), grid_spec=plt...  24.5 us
    pallas_call x2, Pallas kernels, fused(): pl.pallas_call(kernel, in_specs=[space] * len(args), out_specs=[space] *...  14.4 us
    pallas_call x3, Pallas kernels, last_terms(): pl.pallas_call(functools.partial(kernel, [len(terms) for terms in asked])...  9.29 us
  transfers between devices with their start and end apart: 66, of which 25 were waited for; matrix products, arithmetic and copies ran while one was open for 14% of the time, Pallas kernels for 32%

profile of v5, /device:TPU:0, one launch (start us, length us, event | category | flops | bytes accessed | tf_op | source)
XLA Modules:
  0.0 321.2 jit_solution(16162886728650896314)
XLA Ops:
  3.3 1.7 compare_select_fusion
  5.1 2.6 collective-permute-start.6
  7.7 2.7 collective-permute-start.1
  10.9 2.6 collective-permute-start.7
  13.5 1.7 collective-permute-done.1
  15.2 3.9 %collective-permute-start.2 = (bf16[2,112,384]{2,1,0:T(8,128)(2,1)S(1)}, bf16[2,112,384]{2,1,0:T(8,128)(2,1)S(1)}, u32[]{:S(2)}, u32[]{:S(2)}) collective-permute-start(bf16[2,112,384]{2,1,0:T(8,128)(2,1)S(1)} %pad_maximum_fusion.14), channel_id=1, source_target_pairs={{0,8},{1,9},{2,10},{3,11},{4,12},{5,13},{6,14},{7,15},{8,0},{9,1},... | collective-permute-start | bytes 516104 | tf_op jit(solution)/shard_map/ppermute | solution.py:682
  19.1 3.4 %collective-permute-start.11 = (bf16[1,192,384]{2,1,0:T(8,128)(2,1)S(1)}, bf16[1,192,384]{2,1,0:T(8,128)(2,1)S(1)}, u32[]{:S(2)}, u32[]{:S(2)}) collective-permute-start(bf16[1,192,384]{2,1,0:T(8,128)(2,1)S(1)} %bitcast.54), channel_id=1, source_target_pairs={{0,16},{1,17},{2,18},{3,19},{4,20},{5,21},{6,22},{7,23},{8,24},{9,... | collective-permute-start | bytes 442376 | tf_op jit(solution)/shard_map/ppermute | solution.py:682
  22.7 5.6 %collective-permute-done.2 = bf16[2,112,384]{2,1,0:T(8,128)(2,1)S(1)} collective-permute-done((bf16[2,112,384]{2,1,0:T(8,128)(2,1)S(1)}, bf16[2,112,384]{2,1,0:T(8,128)(2,1)S(1)}, u32[]{:S(2)}, u32[]{:S(2)}) %collective-permute-start.2) | collective-permute-done | bytes 172064 | tf_op jit(solution)/shard_map/ppermute | solution.py:682
  31.1 3.8 %collective-permute-start.18 = (bf16[1,192,384]{2,1,0:T(8,128)(2,1)S(1)}, bf16[1,192,384]{2,1,0:T(8,128)(2,1)S(1)}, u32[]{:S(2)}, u32[]{:S(2)}) collective-permute-start(bf16[1,192,384]{2,1,0:T(8,128)(2,1)S(1)} %maximum_select_fusion.3), channel_id=1, source_target_pairs={{0,16},{1,17},{2,18},{3,19},{4,20},{5,21},{6,22},{7,23},{8,24},{9,... | collective-permute-start | bytes 442376 | tf_op jit(solution)/shard_map/ppermute | solution.py:682
  36.4 2.0 collective-permute-done.3
  40.0 4.0 %collective-permute-done.12 = bf16[2,192,384]{2,1,0:T(8,128)(2,1)S(1)} collective-permute-done((bf16[2,192,384]{2,1,0:T(8,128)(2,1)S(1)}, bf16[2,192,384]{2,1,0:T(8,128)(2,1)S(1)}, u32[]{:S(2)}, u32[]{:S(2)}) %collective-permute-start.12) | collective-permute-done | bytes 294944 | tf_op jit(solution)/shard_map/ppermute | solution.py:682
  44.3 1.6 collective-permute-start.13
  47.7 7.0 %collective-permute-done.21.refs_5_ = bf16[8,96,384]{2,1,0:T(8,128)(2,1)} collective-permute-done((bf16[8,96,384]{2,1,0:T(8,128)(2,1)S(1)}, bf16[8,96,384]{2,1,0:T(8,128)(2,1)}, u32[]{:S(2)}, u32[]{:S(2)}) %collective-permute-start.21) | collective-permute-done | bytes 589856 | tf_op jit(solution)/shard_map/ppermute | solution.py:682
  54.7 11.4 %collective-permute-done.13 = bf16[4,192,384]{2,1,0:T(8,128)(2,1)S(1)} collective-permute-done((bf16[4,192,384]{2,1,0:T(8,128)(2,1)S(1)}, bf16[4,192,384]{2,1,0:T(8,128)(2,1)S(1)}, u32[]{:S(2)}, u32[]{:S(2)}) %collective-permute-start.13) | collective-permute-done | bytes 589856 | tf_op jit(solution)/shard_map/ppermute | solution.py:682
  68.8 1.7 collective-permute-start.24
  73.9 17.6 %self_part.1 = (bf16[512,768]{1,0:T(8,128)(2,1)}, bf16[512,768]{1,0:T(8,128)(2,1)}, bf16[512,768]{1,0:T(8,128)(2,1)}, bf16[512,768]{1,0:T(8,128)(2,1)}, bf16[12,...) custom-call(s32[2]{0:T(128)} %pad_add_fusion.spot_ref, ...), custom_call_target="tpu_custom_call" | custom-call | tf_op jit(solution)/shard_map/self_part/pallas_call | solution.py:417
  93.1 1.8 collective-permute-done.25.refs_1_
  98.1 23.3 %cross_part.1 = (f32[512,768]{1,0:T(8,128)}, bf16[512,768]{1,0:T(8,128)(2,1)}, bf16[512,768]{1,0:T(8,128)(2,1)}, bf16[512,768]{1,0:T(8,128)(2,1)}, bf16[512,768]...) custom-call(s32[2]{0:T(128)} %pad_add_fusion.spot_ref, ...), custom_call_target="tpu_custom_call" | custom-call | tf_op jit(solution)/shard_map/cross_part/pallas_call | solution.py:417
  121.6 2.9 collective-permute-done.31
  124.6 2.8 collective-permute-done.33
  128.4 24.5 %ffn.1 = (bf16[512,768]{1,0:T(8,128)(2,1)}, f32[512,768]{1,0:T(8,128)}, bf16[384,3072]{1,0:T(8,128)(2,1)}, bf16[384,3072]{1,0:T(8,128)(2,1)}, bf16[4,4,96,768]{3...) custom-call(s32[2]{0:T(128)} %pad_add_fusion.spot_ref, bf16[512,768]{1,0:T(8,128)(2,1)} %get-tuple-element.159.third_ref, ...), custom_call_target="tpu_custom_call" | custom-call | tf_op jit(solution)/shard_map/ffn/pallas_call | solution.py:354
  153.5 5.0 %third_back.1 = (f32[512,768]{1,0:T(8,128)}, bf16[512,768]{1,0:T(8,128)(2,1)}, bf16[512,768]{1,0:T(8,128)(2,1)}, f32[1,768]{1,0:T(1,128)}) custom-call(f32[512,768]{1,0:T(8,128)} %get-tuple-element.170.gthird_ref, f32[512,768]{1,0:T(8,128)} %get-tuple-element.160.upper_ref, bf16[512,768]{1,0:T(8,128)(2,1)} %cot_ref.3, ...), custom_call_target="tpu_custom_call" | custom-call | tf_op jit(solution)/shard_map/third_back/pallas_call | solution.py:387
  161.2 1.8 add_convert_fusion.2
  163.0 1.8 collective-permute-start.36
  166.8 24.0 %cross_back.1 = (bf16[512,768]{1,0:T(8,128)(2,1)}, bf16[512,768]{1,0:T(8,128)(2,1)}, f32[512,768]{1,0:T(8,128)}, bf16[512,768]{1,0:T(8,128)(2,1)}, bf16[512,768]...) custom-call(s32[1]{0:T(128)} %bitcast.1.core_ref, ...), custom_call_target="tpu_custom_call" | custom-call | tf_op jit(solution)/shard_map/cross_back/pallas_call | solution.py:417
  191.1 3.2 collective-permute-done.37.refs_8_
  196.3 1.8 add_convert_fusion.7
  199.2 2.6 add_convert_fusion
  202.6 17.7 %self_back.1 = (bf16[512,768]{1,0:T(8,128)(2,1)}, bf16[512,768]{1,0:T(8,128)(2,1)}, bf16[512,768]{1,0:T(8,128)(2,1)}, f32[6,8,256]{2,1,0:T(8,128)}, bf16[16,48,7...) custom-call(s32[1]{0:T(128)} %bitcast.1.core_ref, ...), custom_call_target="tpu_custom_call" | custom-call | tf_op jit(solution)/shard_map/self_back/pallas_call | solution.py:417
  222.5 2.1 add_convert_fusion.12
  225.7 2.0 add_convert_fusion.11
  227.8 3.5 %collective-permute-start.47 = (bf16[2,24,3072]{2,1,0:T(8,128)(2,1)}, bf16[2,24,3072]{2,1,0:T(8,128)(2,1)}, u32[]{:S(2)}, u32[]{:S(2)}) collective-permute-start(bf16[2,24,3072]{2,1,0:T(8,128)(2,1)} %add_convert_fusion.11), channel_id=1, source_target_pairs={{0,16},{1,17},{2,18},{3,19},{4,20},{5,21},{6,22},{7,23},{8,24},{9,... | collective-permute-start | bytes 884744 | tf_op jit(solution)/shard_map/ppermute | solution.py:682
  231.2 2.3 add_convert_fusion.5
  235.8 2.0 add_convert_fusion.3
  239.8 9.4 %last_back.1 = (f32[512,768]{1,0:T(8,128)}, f32[512,768]{1,0:T(8,128)}, f32[8,768]{1,0:T(8,128)}) custom-call(bf16[512,768]{1,0:T(8,128)(2,1)} %get-tuple-element.210.gq_ref, bf16[512,768]{1,0:T(8,128)(2,1)} %get-tuple-element.211.gk_ref, bf16[512,768]{1,0:T(8,128)(2,1)} %get-tuple-element.212.gv_ref, bf16[512,768]{1,0:T(8,128)(2,1)} %get-tuple-element.213.gmk_ref, ...), custom_call_target="tpu_custom_call" | custom-call | tf_op jit(solution)/shard_map/last_back/pallas_call | solution.py:387
  251.9 2.5 collective-permute-done.49.refs_8_
  259.3 7.7 %collective-permute-done.51.refs_3_ = bf16[4,96,768]{2,1,0:T(8,128)(2,1)S(1)} collective-permute-done((bf16[4,96,768]{2,1,0:T(8,128)(2,1)}, bf16[4,96,768]{2,1,0:T(8,128)(2,1)S(1)}, u32[]{:S(2)}, u32[]{:S(2)}) %collective-permute-start.51) | collective-permute-done | bytes 589856 | tf_op jit(solution)/shard_map/ppermute | solution.py:682
  270.3 2.4 collective-permute-start.54
  277.2 2.8 collective-permute-done.53.refs_4_
  280.0 1.8 add_convert_fusion.13
  283.6 3.4 %ffn_last.1 = (f32[1,24,3072]{2,1,0:T(8,128)}, f32[1,24]{1,0:T(1,128)}, f32[1,96,768]{2,1,0:T(8,128)}, f32[1,96]{1,0:T(1,128)}, f32[8,768]{1,0:T(8,128)}) custom-call(s32[2]{0:T(128)} %pad_add_fusion.spot_ref, bf16[16,24,3072]{2,1,0:T(8,128)(2,1)} %bitcast.46, bf16[16,24,3072]{2,1,0:T(8,128)(2,1)} %copy-done.5, bf16[8,24,3072]{2,1,0:T(8,128)(2,1)} %copy-done.12, ...), custom_call_target="tpu_custom_call" | custom-call | tf_op jit(solution)/shard_map/ffn_last/pallas_call | solution.py:648
  288.1 2.6 collective-permute-start.55
  294.0 2.9 cross_last.1
  297.5 3.0 self_last.1
  303.0 1.7 collective-permute-start.62
  310.0 1.8 collective-permute-start.65
  311.8 2.7 collective-permute-start.64
  314.5 1.8 pad_maximum_fusion.8
  (277 shorter events, 74.5 us)
Async XLA Ops:
  10.3 8.8 %collective-permute-start.10 = (bf16[4,24,384]{2,1,0:T(8,128)(2,1)S(1)}, bf16[4,24,384]{2,1,0:T(8,128)(2,1)S(1)}, u32[]{:S(2)}, u32[]{:S(2)}) collective-permute-start(bf16[4,24,384]{2,1,0:T(8,128)(2,1)S(1)} %get-tuple-element.132), channel_id=1, source_target_pairs={{0,1},{1,0},{2,3},{3,2},{4,5},{5,4},{6,7},{7,6},{8,9},{9,8},{10,11... | collective-permute-start | bytes 221192 | tf_op jit(solution)/shard_map/ppermute | solution.py:682
  10.8 20.1 %collective-permute-start.17 = (bf16[96,384]{1,0:T(8,128)(2,1)S(1)}, bf16[96,384]{1,0:T(8,128)(2,1)S(1)}, u32[]{:S(2)}, u32[]{:S(2)}) collective-permute-start(bf16[96,384]{1,0:T(8,128)(2,1)S(1)} %get-tuple-element.146), channel_id=1, source_target_pairs={{0,1},{1,0},{2,3},{3,2},{4,5},{5,4},{6,7},{7,6},{8,9},{9,8},{10,11... | collective-permute-start | bytes 221192 | tf_op jit(solution)/shard_map/ppermute | solution.py:682
  10.9 11.7 %collective-permute-start.7 = (bf16[2,96,384]{2,1,0:T(8,128)(2,1)S(1)}, bf16[2,96,384]{2,1,0:T(8,128)(2,1)S(1)}, u32[]{:S(2)}, u32[]{:S(2)}) collective-permute-start(bf16[2,96,384]{2,1,0:T(8,128)(2,1)S(1)} %pad_maximum_fusion.15), channel_id=1, source_target_pairs={{0,16},{1,17},{2,18},{3,19},{4,20},{5,21},{6,22},{7,23},{8,24},{9,... | collective-permute-start | bytes 442376 | tf_op jit(solution)/shard_map/ppermute | solution.py:682
  15.2 13.1 %collective-permute-start.2 = (bf16[2,112,384]{2,1,0:T(8,128)(2,1)S(1)}, bf16[2,112,384]{2,1,0:T(8,128)(2,1)S(1)}, u32[]{:S(2)}, u32[]{:S(2)}) collective-permute-start(bf16[2,112,384]{2,1,0:T(8,128)(2,1)S(1)} %pad_maximum_fusion.14), channel_id=1, source_target_pairs={{0,8},{1,9},{2,10},{3,11},{4,12},{5,13},{6,14},{7,15},{8,0},{9,1},... | collective-permute-start | bytes 516104 | tf_op jit(solution)/shard_map/ppermute | solution.py:682
  19.1 10.8 %collective-permute-start.11 = (bf16[1,192,384]{2,1,0:T(8,128)(2,1)S(1)}, bf16[1,192,384]{2,1,0:T(8,128)(2,1)S(1)}, u32[]{:S(2)}, u32[]{:S(2)}) collective-permute-start(bf16[1,192,384]{2,1,0:T(8,128)(2,1)S(1)} %bitcast.54), channel_id=1, source_target_pairs={{0,16},{1,17},{2,18},{3,19},{4,20},{5,21},{6,22},{7,23},{8,24},{9,... | collective-permute-start | bytes 442376 | tf_op jit(solution)/shard_map/ppermute | solution.py:682
  22.6 13.6 %collective-permute-start.8 = (bf16[4,96,384]{2,1,0:T(8,128)(2,1)S(1)}, bf16[4,96,384]{2,1,0:T(8,128)(2,1)S(1)}, u32[]{:S(2)}, u32[]{:S(2)}) collective-permute-start(bf16[4,96,384]{2,1,0:T(8,128)(2,1)S(1)} %pad_maximum_fusion.10), channel_id=1, source_target_pairs={{0,8},{1,9},{2,10},{3,11},{4,12},{5,13},{6,14},{7,15},{8,0},{9,1},... | collective-permute-start | bytes 884744 | tf_op jit(solution)/shard_map/ppermute | solution.py:682
  28.4 10.0 %collective-permute-start.3 = (bf16[4,112,384]{2,1,0:T(8,128)(2,1)S(1)}, bf16[4,112,384]{2,1,0:T(8,128)(2,1)S(1)}, u32[]{:S(2)}, u32[]{:S(2)}) collective-permute-start(bf16[4,112,384]{2,1,0:T(8,128)(2,1)S(1)} %pad_maximum_fusion.9), channel_id=1, source_target_pairs={{0,4},{1,5},{2,6},{3,7},{4,0},{5,1},{6,2},{7,3},{8,12},{9,13},{10,... | collective-permute-start | bytes 1032200 | tf_op jit(solution)/shard_map/ppermute | solution.py:682
  30.0 14.1 %collective-permute-start.12 = (bf16[2,192,384]{2,1,0:T(8,128)(2,1)S(1)}, bf16[2,192,384]{2,1,0:T(8,128)(2,1)S(1)}, u32[]{:S(2)}, u32[]{:S(2)}) collective-permute-start(bf16[2,192,384]{2,1,0:T(8,128)(2,1)S(1)} %pad_maximum_fusion.11), channel_id=1, source_target_pairs={{0,8},{1,9},{2,10},{3,11},{4,12},{5,13},{6,14},{7,15},{8,0},{9,1},... | collective-permute-start | bytes 884744 | tf_op jit(solution)/shard_map/ppermute | solution.py:682
  31.0 13.3 %collective-permute-start.15 = (bf16[1,48,1536]{2,1,0:T(8,128)(2,1)S(1)}, bf16[1,48,1536]{2,1,0:T(8,128)(2,1)S(1)}, u32[]{:S(2)}, u32[]{:S(2)}) collective-permute-start(bf16[1,48,1536]{2,1,0:T(8,128)(2,1)S(1)} %maximum_select_fusion.2), channel_id=1, source_target_pairs={{0,2},{1,3},{2,0},{3,1},{4,6},{5,7},{6,4},{7,5},{8,10},{9,11},{10,... | collective-permute-start | bytes 442376 | tf_op jit(solution)/shard_map/ppermute | solution.py:682
  31.1 15.1 %collective-permute-start.18 = (bf16[1,192,384]{2,1,0:T(8,128)(2,1)S(1)}, bf16[1,192,384]{2,1,0:T(8,128)(2,1)S(1)}, u32[]{:S(2)}, u32[]{:S(2)}) collective-permute-start(bf16[1,192,384]{2,1,0:T(8,128)(2,1)S(1)} %maximum_select_fusion.3), channel_id=1, source_target_pairs={{0,16},{1,17},{2,18},{3,19},{4,20},{5,21},{6,22},{7,23},{8,24},{9,... | collective-permute-start | bytes 442376 | tf_op jit(solution)/shard_map/ppermute | solution.py:682
  36.3 9.9 %collective-permute-start.9 = (bf16[8,96,384]{2,1,0:T(8,128)(2,1)S(1)}, bf16[8,96,384]{2,1,0:T(8,128)(2,1)S(1)}, u32[]{:S(2)}, u32[]{:S(2)}) collective-permute-start(bf16[8,96,384]{2,1,0:T(8,128)(2,1)S(1)} %pad_maximum_fusion.4.refs_4_), channel_id=1, source_target_pairs={{0,1},{1,0},{2,3},{3,2},{4,5},{5,4},{6,7},{7,6},{8,9},{9,8},{10,11... | collective-permute-start | bytes 1769480 | tf_op jit(solution)/shard_map/ppermute | solution.py:682
  38.4 16.3 %collective-permute-start.21 = (bf16[8,96,384]{2,1,0:T(8,128)(2,1)S(1)}, bf16[8,96,384]{2,1,0:T(8,128)(2,1)}, u32[]{:S(2)}, u32[]{:S(2)}) collective-permute-start(bf16[8,96,384]{2,1,0:T(8,128)(2,1)S(1)} %pad_maximum_fusion.4.refs_4_), channel_id=1, source_target_pairs={{0,4},{1,5},{2,6},{3,7},{4,0},{5,1},{6,2},{7,3},{8,12},{9,13},{10,... | collective-permute-start | bytes 1769480 | tf_op jit(solution)/shard_map/ppermute | solution.py:682
  44.1 22.1 %collective-permute-start.5 = (bf16[8,112,384]{2,1,0:T(8,128)(2,1)S(1)}, bf16[8,112,384]{2,1,0:T(8,128)(2,1)}, u32[]{:S(2)}, u32[]{:S(2)}) collective-permute-start(bf16[8,112,384]{2,1,0:T(8,128)(2,1)S(1)} %pad_maximum_fusion.3.refs_0_), channel_id=1, source_target_pairs={{0,1},{1,0},{2,3},{3,2},{4,5},{5,4},{6,7},{7,6},{8,9},{9,8},{10,11... | collective-permute-start | bytes 2064392 | tf_op jit(solution)/shard_map/ppermute | solution.py:682
  44.3 21.8 %collective-permute-start.13 = (bf16[4,192,384]{2,1,0:T(8,128)(2,1)S(1)}, bf16[4,192,384]{2,1,0:T(8,128)(2,1)S(1)}, u32[]{:S(2)}, u32[]{:S(2)}) collective-permute-start(bf16[4,192,384]{2,1,0:T(8,128)(2,1)S(1)} %pad_maximum_fusion.5), channel_id=1, source_target_pairs={{0,4},{1,5},{2,6},{3,7},{4,0},{5,1},{6,2},{7,3},{8,12},{9,13},{10,... | collective-permute-start | bytes 1769480 | tf_op jit(solution)/shard_map/ppermute | solution.py:682
  46.2 21.3 %collective-permute-start.4 = (bf16[8,112,384]{2,1,0:T(8,128)(2,1)S(1)}, bf16[8,112,384]{2,1,0:T(8,128)(2,1)}, u32[]{:S(2)}, u32[]{:S(2)}) collective-permute-start(bf16[8,112,384]{2,1,0:T(8,128)(2,1)S(1)} %pad_maximum_fusion.3.refs_0_), channel_id=1, source_target_pairs={{0,2},{1,3},{2,0},{3,1},{4,6},{5,7},{6,4},{7,5},{8,10},{9,11},{10,... | collective-permute-start | bytes 2064392 | tf_op jit(solution)/shard_map/ppermute | solution.py:682
  46.2 20.2 %collective-permute-start.16 = (bf16[2,48,1536]{2,1,0:T(8,128)(2,1)S(1)}, bf16[2,48,1536]{2,1,0:T(8,128)(2,1)S(1)}, u32[]{:S(2)}, u32[]{:S(2)}) collective-permute-start(bf16[2,48,1536]{2,1,0:T(8,128)(2,1)S(1)} %pad_maximum_fusion.12), channel_id=1, source_target_pairs={{0,16},{1,17},{2,18},{3,19},{4,20},{5,21},{6,22},{7,23},{8,24},{9,... | collective-permute-start | bytes 884744 | tf_op jit(solution)/shard_map/ppermute | solution.py:682
  54.7 12.7 %collective-permute-start.19 = (bf16[2,192,384]{2,1,0:T(8,128)(2,1)S(1)}, bf16[2,192,384]{2,1,0:T(8,128)(2,1)S(1)}, u32[]{:S(2)}, u32[]{:S(2)}) collective-permute-start(bf16[2,192,384]{2,1,0:T(8,128)(2,1)S(1)} %pad_maximum_fusion.13), channel_id=1, source_target_pairs={{0,8},{1,9},{2,10},{3,11},{4,12},{5,13},{6,14},{7,15},{8,0},{9,1},... | collective-permute-start | bytes 884744 | tf_op jit(solution)/shard_map/ppermute | solution.py:682
  66.1 7.7 %collective-permute-start.22 = (bf16[8,96,384]{2,1,0:T(8,128)(2,1)}, bf16[8,96,384]{2,1,0:T(8,128)(2,1)}, u32[]{:S(2)}, u32[]{:S(2)}) collective-permute-start(bf16[8,96,384]{2,1,0:T(8,128)(2,1)} %collective-permute-done.21.refs_5_), channel_id=1, source_target_pairs={{0,1},{1,0},{2,3},{3,2},{4,5},{5,4},{6,7},{7,6},{8,9},{9,8},{10,11... | collective-permute-start | bytes 1769480 | tf_op jit(solution)/shard_map/ppermute | solution.py:682
  66.3 28.5 %collective-permute-start.25 = (bf16[8,192,384]{2,1,0:T(8,128)(2,1)S(1)}, bf16[8,192,384]{2,1,0:T(8,128)(2,1)}, u32[]{:S(2)}, u32[]{:S(2)}) collective-permute-start(bf16[8,192,384]{2,1,0:T(8,128)(2,1)S(1)} %pad_maximum_fusion.refs_0_), channel_id=1, source_target_pairs={{0,2},{1,3},{2,0},{3,1},{4,6},{5,7},{6,4},{7,5},{8,10},{9,11},{10,... | collective-permute-start | bytes 3538952 | tf_op jit(solution)/shard_map/ppermute | solution.py:682
  68.8 22.7 %collective-permute-start.23 = (bf16[4,48,1536]{2,1,0:T(8,128)(2,1)}, bf16[4,48,1536]{2,1,0:T(8,128)(2,1)}, u32[]{:S(2)}, u32[]{:S(2)}) collective-permute-start(bf16[4,48,1536]{2,1,0:T(8,128)(2,1)} %pad_maximum_fusion.6), channel_id=1, source_target_pairs={{0,8},{1,9},{2,10},{3,11},{4,12},{5,13},{6,14},{7,15},{8,0},{9,1},... | collective-permute-start | bytes 1769480 | tf_op jit(solution)/shard_map/ppermute | solution.py:682
  68.8 22.7 %collective-permute-start.24 = (bf16[4,192,384]{2,1,0:T(8,128)(2,1)}, bf16[4,192,384]{2,1,0:T(8,128)(2,1)}, u32[]{:S(2)}, u32[]{:S(2)}) collective-permute-start(bf16[4,192,384]{2,1,0:T(8,128)(2,1)} %pad_maximum_fusion.7), channel_id=1, source_target_pairs={{0,4},{1,5},{2,6},{3,7},{4,0},{5,1},{6,2},{7,3},{8,12},{9,13},{10,... | collective-permute-start | bytes 1769480 | tf_op jit(solution)/shard_map/ppermute | solution.py:682
  73.9 22.9 %collective-permute-start.26 = (bf16[8,192,384]{2,1,0:T(8,128)(2,1)S(1)}, bf16[8,192,384]{2,1,0:T(8,128)(2,1)S(1)}, u32[]{:S(2)}, u32[]{:S(2)}) collective-permute-start(bf16[8,192,384]{2,1,0:T(8,128)(2,1)S(1)} %pad_maximum_fusion.refs_0_), channel_id=1, source_target_pairs={{0,1},{1,0},{2,3},{3,2},{4,5},{5,4},{6,7},{7,6},{8,9},{9,8},{10,11... | collective-permute-start | bytes 3538952 | tf_op jit(solution)/shard_map/ppermute | solution.py:682
  92.8 28.7 %collective-permute-start.28 = (bf16[8,48,1536]{2,1,0:T(8,128)(2,1)S(1)}, bf16[8,48,1536]{2,1,0:T(8,128)(2,1)S(1)}, u32[]{:S(2)}, u32[]{:S(2)}) collective-permute-start(bf16[8,48,1536]{2,1,0:T(8,128)(2,1)S(1)} %pad_maximum_fusion.1.refs_0_), channel_id=1, source_target_pairs={{0,4},{1,5},{2,6},{3,7},{4,0},{5,1},{6,2},{7,3},{8,12},{9,13},{10,... | collective-permute-start | bytes 3538952 | tf_op jit(solution)/shard_map/ppermute | solution.py:682
  96.1 28.4 %collective-permute-start.31 = (bf16[8,192,384]{2,1,0:T(8,128)(2,1)S(1)}, bf16[8,192,384]{2,1,0:T(8,128)(2,1)S(1)}, u32[]{:S(2)}, u32[]{:S(2)}) collective-permute-start(bf16[8,192,384]{2,1,0:T(8,128)(2,1)S(1)} %pad_maximum_fusion.2), channel_id=1, source_target_pairs={{0,2},{1,3},{2,0},{3,1},{4,6},{5,7},{6,4},{7,5},{8,10},{9,11},{10,... | collective-permute-start | bytes 3538952 | tf_op jit(solution)/shard_map/ppermute | solution.py:682
  96.5 28.1 %collective-permute-start.29 = (bf16[8,48,1536]{2,1,0:T(8,128)(2,1)S(1)}, bf16[8,48,1536]{2,1,0:T(8,128)(2,1)}, u32[]{:S(2)}, u32[]{:S(2)}) collective-permute-start(bf16[8,48,1536]{2,1,0:T(8,128)(2,1)S(1)} %pad_maximum_fusion.1.refs_0_), channel_id=1, source_target_pairs={{0,1},{1,0},{2,3},{3,2},{4,5},{5,4},{6,7},{7,6},{8,9},{9,8},{10,11... | collective-permute-start | bytes 3538952 | tf_op jit(solution)/shard_map/ppermute | solution.py:682
  96.8 27.8 %collective-permute-start.32 = (bf16[8,192,384]{2,1,0:T(8,128)(2,1)S(1)}, bf16[8,192,384]{2,1,0:T(8,128)(2,1)S(1)}, u32[]{:S(2)}, u32[]{:S(2)}) collective-permute-start(bf16[8,192,384]{2,1,0:T(8,128)(2,1)S(1)} %pad_maximum_fusion.2), channel_id=1, source_target_pairs={{0,1},{1,0},{2,3},{3,2},{4,5},{5,4},{6,7},{7,6},{8,9},{9,8},{10,11... | collective-permute-start | bytes 3538952 | tf_op jit(solution)/shard_map/ppermute | solution.py:682
  153.1 8.1 %collective-permute-start.35 = (bf16[16,96,768]{2,1,0:T(8,128)(2,1)}, bf16[16,96,768]{2,1,0:T(8,128)(2,1)}, u32[]{:S(2)}, u32[]{:S(2)}) collective-permute-start(bf16[16,96,768]{2,1,0:T(8,128)(2,1)} %bitcast.74), channel_id=1, source_target_pairs={{0,1},{1,0},{2,3},{3,2},{4,5},{5,4},{6,7},{7,6},{8,9},{9,8},{10,11... | collective-permute-start | bytes 7077896 | tf_op jit(solution)/shard_map/ppermute | solution.py:682
  163.0 28.1 %collective-permute-start.36 = (bf16[8,24,3072]{2,1,0:T(8,128)(2,1)S(1)}, bf16[8,24,3072]{2,1,0:T(8,128)(2,1)S(1)}, u32[]{:S(2)}, u32[]{:S(2)}) collective-permute-start(bf16[8,24,3072]{2,1,0:T(8,128)(2,1)S(1)} %add_convert_fusion.2), channel_id=1, source_target_pairs={{0,4},{1,5},{2,6},{3,7},{4,0},{5,1},{6,2},{7,3},{8,12},{9,13},{10,... | collective-permute-start | bytes 3538952 | tf_op jit(solution)/shard_map/ppermute | solution.py:682
  166.4 27.9 %collective-permute-start.37 = (bf16[8,96,768]{2,1,0:T(8,128)(2,1)S(1)}, bf16[8,96,768]{2,1,0:T(8,128)(2,1)}, u32[]{:S(2)}, u32[]{:S(2)}) collective-permute-start(bf16[8,96,768]{2,1,0:T(8,128)(2,1)S(1)} %add_convert_fusion.1), channel_id=1, source_target_pairs={{0,2},{1,3},{2,0},{3,1},{4,6},{5,7},{6,4},{7,5},{8,10},{9,11},{10,... | collective-permute-start | bytes 3538952 | tf_op jit(solution)/shard_map/ppermute | solution.py:682
  195.8 24.5 %collective-permute-start.39 = (bf16[4,96,768]{2,1,0:T(8,128)(2,1)S(1)}, bf16[4,96,768]{2,1,0:T(8,128)(2,1)S(1)}, u32[]{:S(2)}, u32[]{:S(2)}) collective-permute-start(bf16[4,96,768]{2,1,0:T(8,128)(2,1)S(1)} %add_convert_fusion.6), channel_id=1, source_target_pairs={{0,4},{1,5},{2,6},{3,7},{4,0},{5,1},{6,2},{7,3},{8,12},{9,13},{10,... | collective-permute-start | bytes 1769480 | tf_op jit(solution)/shard_map/ppermute | solution.py:682
  198.0 22.3 %collective-permute-start.40 = (bf16[4,24,3072]{2,1,0:T(8,128)(2,1)S(1)}, bf16[4,24,3072]{2,1,0:T(8,128)(2,1)S(1)}, u32[]{:S(2)}, u32[]{:S(2)}) collective-permute-start(bf16[4,24,3072]{2,1,0:T(8,128)(2,1)S(1)} %add_convert_fusion.7), channel_id=1, source_target_pairs={{0,8},{1,9},{2,10},{3,11},{4,12},{5,13},{6,14},{7,15},{8,0},{9,1},... | collective-permute-start | bytes 1769480 | tf_op jit(solution)/shard_map/ppermute | solution.py:682
  201.8 29.4 %collective-permute-start.41 = (bf16[8,96,768]{2,1,0:T(8,128)(2,1)}, bf16[8,96,768]{2,1,0:T(8,128)(2,1)}, u32[]{:S(2)}, u32[]{:S(2)}) collective-permute-start(bf16[8,96,768]{2,1,0:T(8,128)(2,1)} %add_convert_fusion), channel_id=1, source_target_pairs={{0,2},{1,3},{2,0},{3,1},{4,6},{5,7},{6,4},{7,5},{8,10},{9,11},{10,... | collective-permute-start | bytes 3538952 | tf_op jit(solution)/shard_map/ppermute | solution.py:682
  221.9 11.5 %collective-permute-start.42 = (bf16[16,48,768]{2,1,0:T(8,128)(2,1)}, bf16[16,48,768]{2,1,0:T(8,128)(2,1)S(1)}, u32[]{:S(2)}, u32[]{:S(2)}) collective-permute-start(bf16[16,48,768]{2,1,0:T(8,128)(2,1)} %get-tuple-element.204), channel_id=1, source_target_pairs={{0,1},{1,0},{2,3},{3,2},{4,5},{5,4},{6,7},{7,6},{8,9},{9,8},{10,11... | collective-permute-start | bytes 3538952 | tf_op jit(solution)/shard_map/ppermute | solution.py:682
  222.0 12.5 %collective-permute-start.43 = (bf16[16,48,768]{2,1,0:T(8,128)(2,1)}, bf16[16,48,768]{2,1,0:T(8,128)(2,1)}, u32[]{:S(2)}, u32[]{:S(2)}) collective-permute-start(bf16[16,48,768]{2,1,0:T(8,128)(2,1)} %get-tuple-element.208), channel_id=1, source_target_pairs={{0,1},{1,0},{2,3},{3,2},{4,5},{5,4},{6,7},{7,6},{8,9},{9,8},{10,11... | collective-permute-start | bytes 3538952 | tf_op jit(solution)/shard_map/ppermute | solution.py:682
  224.6 24.6 %collective-permute-start.52 = (bf16[2,96,768]{2,1,0:T(8,128)(2,1)}, bf16[2,96,768]{2,1,0:T(8,128)(2,1)}, u32[]{:S(2)}, u32[]{:S(2)}) collective-permute-start(bf16[2,96,768]{2,1,0:T(8,128)(2,1)} %add_convert_fusion.12), channel_id=1, source_target_pairs={{0,8},{1,9},{2,10},{3,11},{4,12},{5,13},{6,14},{7,15},{8,0},{9,1},... | collective-permute-start | bytes 884744 | tf_op jit(solution)/shard_map/ppermute | solution.py:682
  227.8 22.8 %collective-permute-start.47 = (bf16[2,24,3072]{2,1,0:T(8,128)(2,1)}, bf16[2,24,3072]{2,1,0:T(8,128)(2,1)}, u32[]{:S(2)}, u32[]{:S(2)}) collective-permute-start(bf16[2,24,3072]{2,1,0:T(8,128)(2,1)} %add_convert_fusion.11), channel_id=1, source_target_pairs={{0,16},{1,17},{2,18},{3,19},{4,20},{5,21},{6,22},{7,23},{8,24},{9,... | collective-permute-start | bytes 884744 | tf_op jit(solution)/shard_map/ppermute | solution.py:682
  234.5 17.4 %collective-permute-start.44 = (bf16[8,48,768]{2,1,0:T(8,128)(2,1)}, bf16[8,48,768]{2,1,0:T(8,128)(2,1)}, u32[]{:S(2)}, u32[]{:S(2)}) collective-permute-start(bf16[8,48,768]{2,1,0:T(8,128)(2,1)} %add_convert_fusion.4), channel_id=1, source_target_pairs={{0,2},{1,3},{2,0},{3,1},{4,6},{5,7},{6,4},{7,5},{8,10},{9,11},{10,... | collective-permute-start | bytes 1769480 | tf_op jit(solution)/shard_map/ppermute | solution.py:682
  237.8 16.6 %collective-permute-start.49 = (bf16[8,48,768]{2,1,0:T(8,128)(2,1)}, bf16[8,48,768]{2,1,0:T(8,128)(2,1)}, u32[]{:S(2)}, u32[]{:S(2)}) collective-permute-start(bf16[8,48,768]{2,1,0:T(8,128)(2,1)} %add_convert_fusion.3), channel_id=1, source_target_pairs={{0,4},{1,5},{2,6},{3,7},{4,0},{5,1},{6,2},{7,3},{8,12},{9,13},{10,... | collective-permute-start | bytes 1769480 | tf_op jit(solution)/shard_map/ppermute | solution.py:682
  238.9 28.1 %collective-permute-start.51 = (bf16[4,96,768]{2,1,0:T(8,128)(2,1)}, bf16[4,96,768]{2,1,0:T(8,128)(2,1)S(1)}, u32[]{:S(2)}, u32[]{:S(2)}) collective-permute-start(bf16[4,96,768]{2,1,0:T(8,128)(2,1)} %add_convert_fusion.5), channel_id=1, source_target_pairs={{0,4},{1,5},{2,6},{3,7},{4,0},{5,1},{6,2},{7,3},{8,12},{9,13},{10,... | collective-permute-start | bytes 1769480 | tf_op jit(solution)/shard_map/ppermute | solution.py:682
  255.6 17.1 %collective-permute-start.45 = (bf16[4,48,768]{2,1,0:T(8,128)(2,1)S(1)}, bf16[4,48,768]{2,1,0:T(8,128)(2,1)S(1)}, u32[]{:S(2)}, u32[]{:S(2)}) collective-permute-start(bf16[4,48,768]{2,1,0:T(8,128)(2,1)S(1)} %add_convert_fusion.10), channel_id=1, source_target_pairs={{0,4},{1,5},{2,6},{3,7},{4,0},{5,1},{6,2},{7,3},{8,12},{9,13},{10,... | collective-permute-start | bytes 884744 | tf_op jit(solution)/shard_map/ppermute | solution.py:682
  257.9 16.7 %collective-permute-start.50 = (bf16[4,48,768]{2,1,0:T(8,128)(2,1)S(1)}, bf16[4,48,768]{2,1,0:T(8,128)(2,1)S(1)}, u32[]{:S(2)}, u32[]{:S(2)}) collective-permute-start(bf16[4,48,768]{2,1,0:T(8,128)(2,1)S(1)} %add_convert_fusion.9), channel_id=1, source_target_pairs={{0,8},{1,9},{2,10},{3,11},{4,12},{5,13},{6,14},{7,15},{8,0},{9,1},... | collective-permute-start | bytes 884744 | tf_op jit(solution)/shard_map/ppermute | solution.py:682
  268.3 11.7 %collective-permute-start.53 = (bf16[2,96,768]{2,1,0:T(8,128)(2,1)S(1)}, bf16[2,96,768]{2,1,0:T(8,128)(2,1)S(1)}, u32[]{:S(2)}, u32[]{:S(2)}) collective-permute-start(bf16[2,96,768]{2,1,0:T(8,128)(2,1)S(1)} %add_convert_fusion.8), channel_id=1, source_target_pairs={{0,8},{1,9},{2,10},{3,11},{4,12},{5,13},{6,14},{7,15},{8,0},{9,1},... | collective-permute-start | bytes 884744 | tf_op jit(solution)/shard_map/ppermute | solution.py:682
  269.3 13.0 %collective-permute-start.48 = (bf16[1,24,3072]{2,1,0:T(8,128)(2,1)S(1)}, bf16[1,24,3072]{2,1,0:T(8,128)(2,1)S(1)}, u32[]{:S(2)}, u32[]{:S(2)}) collective-permute-start(bf16[1,24,3072]{2,1,0:T(8,128)(2,1)S(1)} %add_convert_fusion.16), channel_id=1, source_target_pairs={{0,2},{1,3},{2,0},{3,1},{4,6},{5,7},{6,4},{7,5},{8,10},{9,11},{10,... | collective-permute-start | bytes 442376 | tf_op jit(solution)/shard_map/ppermute | solution.py:682
  270.3 12.0 %collective-permute-start.54 = (bf16[1,96,768]{2,1,0:T(8,128)(2,1)S(1)}, bf16[1,96,768]{2,1,0:T(8,128)(2,1)S(1)}, u32[]{:S(2)}, u32[]{:S(2)}) collective-permute-start(bf16[1,96,768]{2,1,0:T(8,128)(2,1)S(1)} %add_convert_fusion.14), channel_id=1, source_target_pairs={{0,16},{1,17},{2,18},{3,19},{4,20},{5,21},{6,22},{7,23},{8,24},{9,... | collective-permute-start | bytes 442376 | tf_op jit(solution)/shard_map/ppermute | solution.py:682
  273.8 13.2 %collective-permute-start.46 = (bf16[2,48,768]{2,1,0:T(8,128)(2,1)S(1)}, bf16[2,48,768]{2,1,0:T(8,128)(2,1)S(1)}, u32[]{:S(2)}, u32[]{:S(2)}) collective-permute-start(bf16[2,48,768]{2,1,0:T(8,128)(2,1)S(1)} %add_convert_fusion.17), channel_id=1, source_target_pairs={{0,8},{1,9},{2,10},{3,11},{4,12},{5,13},{6,14},{7,15},{8,0},{9,1},... | collective-permute-start | bytes 442376 | tf_op jit(solution)/shard_map/ppermute | solution.py:682
  275.9 14.7 %collective-permute-start.57 = (bf16[2,48,768]{2,1,0:T(8,128)(2,1)S(1)}, bf16[2,48,768]{2,1,0:T(8,128)(2,1)S(1)}, u32[]{:S(2)}, u32[]{:S(2)}) collective-permute-start(bf16[2,48,768]{2,1,0:T(8,128)(2,1)S(1)} %add_convert_fusion.15), channel_id=1, source_target_pairs={{0,16},{1,17},{2,18},{3,19},{4,20},{5,21},{6,22},{7,23},{8,24},{9,... | collective-permute-start | bytes 442376 | tf_op jit(solution)/shard_map/ppermute | solution.py:682
  281.9 11.4 %collective-permute-start.56 = (bf16[1,96,768]{2,1,0:T(8,128)(2,1)}, bf16[1,96,768]{2,1,0:T(8,128)(2,1)S(1)}, u32[]{:S(2)}, u32[]{:S(2)}) collective-permute-start(bf16[1,96,768]{2,1,0:T(8,128)(2,1)} %add_convert_fusion.13), channel_id=1, source_target_pairs={{0,16},{1,17},{2,18},{3,19},{4,20},{5,21},{6,22},{7,23},{8,24},{9,... | collective-permute-start | bytes 442376 | tf_op jit(solution)/shard_map/ppermute | solution.py:682
  288.1 8.8 %collective-permute-start.55 = (bf16[1,48,768]{2,1,0:T(8,128)(2,1)S(1)}, bf16[1,48,768]{2,1,0:T(8,128)(2,1)S(1)}, u32[]{:S(2)}, u32[]{:S(2)}) collective-permute-start(bf16[1,48,768]{2,1,0:T(8,128)(2,1)S(1)} %add_convert_fusion.19), channel_id=1, source_target_pairs={{0,16},{1,17},{2,18},{3,19},{4,20},{5,21},{6,22},{7,23},{8,24},{9,... | collective-permute-start | bytes 221192 | tf_op jit(solution)/shard_map/ppermute | solution.py:682
  (67 other events, 517.6 us)

commit v6 on v5

--- a/solution.py
+++ b/solution.py
@@ -403,8 +403,44 @@
     return pl.BlockSpec(array.shape, lambda pair: (0,) * rank, pipeline_mode=space)
 
 
-def by_pair(kernel, args, outs, scratch, by_step, name):
+def by_pair(kernel, args, outs, scratch, by_step, name, late=(), early=()):
     held = [jax.ShapeDtypeStruct(shape, held_as) for shape, held_as in outs]
+    beside = pl.BlockSpec(memory_space=pl.ANY)
+    buffers = [args[k] for k in late] + [held[k] for k in early]
+    count = len(args) + len(held) + len(scratch)
+
+    def body(*refs):
+        pair = pl.program_id(0)
+        refs, places, arrived = list(refs[:count]), refs[count:-1], refs[-1]
+        wanted = list(late) + [len(args) + k for k in early]
+        copies = []
+        for k, (at, place) in enumerate(zip(wanted, places)):
+            ends = (refs[at], place) if k < len(late) else (place, refs[at])
+            copies.append(pltpu.make_async_copy(*ends, arrived.at[k]))
+            refs[at] = place
+        loads, stores = copies[: len(late)], copies[len(late) :]
+
+        @pl.when(pair == 0)
+        def _():
+            for copy in loads:
+                copy.start()
+
+        @pl.when(pair == PAIRS - 1)
+        def _():
+            for copy in loads:
+                copy.wait()
+
+        kernel(*refs)
+
+        @pl.when(pair == 0)
+        def _():
+            for copy in stores:
+                copy.start()
+
+        @pl.when(pair == PAIRS - 1)
+        def _():
+            for copy in stores:
+                copy.wait()
 
     def spec(array, once):
         if len(array.shape) == 3 and array.shape in by_step:
@@ -414,11 +450,18 @@
             return pl.BlockSpec(memory_space=pltpu.SMEM)
         return whole_spec(array, pl.Buffered(1) if once else None)
 
+    in_specs = [beside if k in late else spec(array, True) for k, array in enumerate(args)]
+    out_specs = [beside if k in early else spec(array, False) for k, array in enumerate(held)]
+    if not buffers:
+        body = kernel
+    else:
+        scratch = scratch + [pltpu.VMEM(array.shape, array.dtype) for array in buffers]
+        scratch.append(pltpu.SemaphoreType.DMA((len(buffers),)))
     return pl.pallas_call(
-        kernel,
+        body,
         grid=(PAIRS,),
-        in_specs=[spec(array, True) for array in args],
-        out_specs=[spec(array, False) for array in held],
+        in_specs=in_specs,
+        out_specs=out_specs,
         out_shape=held,
         scratch_shapes=scratch,
         compiler_params=pltpu.CompilerParams(vmem_limit_bytes=VMEM_BYTES),
@@ -674,6 +717,9 @@
         high = [[which] for which in range(self.bits - 1, 1, -1)]
         self.plan_a = high + [[1]]
         self.plan_b = [[1]] + high
+        self.plan_d = high[:1] + high[2:] + high[1:2] + [[1]]
+        self.plan_e = [[1]] + high[:1] + high[2:] + high[1:2]
+        self.plan_c = high[:1] + [[1]] + high[2:] + high[1:2]
 
     def bit(self, which):
         return (self.me >> which) & 1
@@ -844,7 +890,7 @@
         ).reshape(4 * 2 * rows, -1)
         gain_pair = cube.place(gain_rows, theirs[4 * rows :], 0)
         one = Gather(cube, jnp.concatenate([pairs[: 4 * rows], gain_pair], axis=0), cube.plan_a)
-        two = Gather(cube, pairs[4 * rows :], cube.plan_b)
+        two = Gather(cube, pairs[4 * rows :], cube.plan_c)
         ahead = one.send(), two.send()
         cross = pair_columns(cube, attn_weights[4:], *ahead)
         inner = pair_columns(cube, w_in, *ahead)
@@ -885,12 +931,13 @@
         first_chunk, second_chunk = [attn_full[:2]], [attn_full[2:4]]
     gain_one, gain_two, gain_three = [gain_full[k : k + 1].astype(full) for k in range(3)]
     first_low, query, keys, values, self_probs, mixed_low, *weights = by_pair(
-        functools.partial(self_part, plans),
+        functools.partial(self_part, (cube.plan_a, cube.plan_c)),
         [spot, tokens, gain_one, see_self, lines, *first_chunk, *second_chunk],
         [(tile, low)] * 4 + [(probs, low), (tile, low)] + [square] * 4,
         [],
         (probs, lines.shape),
         "self_part",
+        early=(0, 1, 2, 3, 6, 7, 8, 9),
     )
     if tiled:
         three.take(mixed_low)
@@ -914,6 +961,7 @@
         [],
         (probs,),
         "cross_part",
+        early=(0, 1, 2, 3, 4, 9, 10, 11, 12),
     )
     attn_full = weights + cross_weights
     if tiled:
@@ -940,8 +988,9 @@
         attn_full[7],
     )
     in_sums.take(grad_crossed)
-    out_sums.take(grad_crossed)
-    grad_crossed = after(grad_crossed, *send_all((in_sums, out_sums)))
+    started = send_all((in_sums,))
+    out_sums.take(*started)
+    grad_crossed = after(grad_crossed, *started, *send_all((out_sums,)))
     sums_scratch = [pltpu.VMEM((tile[0], LANES), full)] * 2
     memory_key_low, memory_value_low, grad_middle, grad_self_branch, grad_mixed, *rest = by_pair(
         functools.partial(cross_back, rows, plans),
@@ -968,6 +1017,7 @@
         [pltpu.VMEM(tile, low)] + sums_scratch,
         (probs,),
         "cross_back",
+        late=(6, 7, 8, 9, 10, 11, 13, 14),
     )
     grad_gain_second = rest[0]
     for each in (in_sums, out_sums):
@@ -980,7 +1030,7 @@
     lots = (PAIRS, 8, 2 * LANES)
     outs = product_outs(cube, 2)
     query_low, key_low, value_low, score_sums, *rest = by_pair(
-        functools.partial(self_back, rows, plans),
+        functools.partial(self_back, rows, (cube.plan_d, cube.plan_c)),
         [
             core[None],
             query,
@@ -996,12 +1046,13 @@
         sums_scratch,
         (probs, lots),
         "self_back",
+        late=(6, 7, 8),
     )
     for each in (in_sums, out_sums):
         each.take(query_low)
     arrived = in_sums.terms[-1][0], out_sums.terms[-1][0]
-    late_sums = product_sums(cube, cube.plan_b, rest[::2], *arrived)
-    early_sums = product_sums(cube, cube.plan_a, rest[1::2], *arrived)
+    late_sums = product_sums(cube, cube.plan_c, rest[::2], *arrived)
+    early_sums = product_sums(cube, cube.plan_d, rest[1::2], *arrived)
     cross_sums.take(query_low)
     started = send_all((out_sums, in_sums, cross_sums))
     late_sums.take(*started)

time: 326 us -> 318 us (0.975)
  waiting for transfers between devices: 66.8 us -> 49.6 us
  starting transfers between devices: 65.4 us -> 71.4 us
  Pallas kernels: 131 us -> 127 us
  local copies, waits for them, and re-layouts: 10.6 us -> 14.1 us
    ppermute x66, waiting for transfers between devices: 66.8 us -> 49.6 us  [swap(): return lax.ppermute(value, AXES, [(i, i ^ flip) for i in range(self.count)])]
    ppermute x66, starting transfers between devices: 65.4 us -> 71.4 us  [swap(): return lax.ppermute(value, AXES, [(i, i ^ flip) for i in range(self.count)])]
    unnamed x99, local copies, waits for them, and re-layouts: 6.1 us -> 9.66 us
    pallas_call x4, Pallas kernels: 82.6 us -> 79.1 us  [by_pair(): pl.pallas_call(body, grid=(PAIRS,), in_specs=in_specs, out_specs=out_spec...]
  transfers between devices with their start and end apart: 66 -> 66, of which waited for: 25 -> 22; matrix products, arithmetic and copies ran while one was open for 14% -> 15% of each run, Pallas kernels for 32% -> 32%
where the time goes in v6:
time: 318 us; the launch traced here: 313 us
  Pallas kernels  127 us (40%)
  starting transfers between devices  71.4 us (22%)
  waiting for transfers between devices  49.6 us (16%)
  other arithmetic  48.4 us (15%)
  local copies, waits for them, and re-layouts  14.1 us (4%)
    pallas_call x4, Pallas kernels, by_pair(): pl.pallas_call(body, grid=(PAIRS,), in_specs=in_specs, out_specs=out_spec...  79.1 us
    ppermute x66, starting transfers between devices, swap(): return lax.ppermute(value, AXES, [(i, i ^ flip) for i in range(self.count)])  71.4 us
    ppermute x66, waiting for transfers between devices, swap(): return lax.ppermute(value, AXES, [(i, i ^ flip) for i in range(self.count)])  49.6 us
    convert_element_type x20, other arithmetic, send(): sent = sum(parts).astype(jnp.bfloat16)  34.5 us
    pallas_call x1, Pallas kernels, ffn(): pl.pallas_call(functools.partial(ffn_kernel, tiled, plans), grid_spec=plt...  24.4 us
    pallas_call x2, Pallas kernels, fused(): pl.pallas_call(kernel, in_specs=[space] * len(args), out_specs=[space] *...  14.5 us
    unnamed x99, local copies, waits for them, and re-layouts  9.66 us
    pallas_call x3, Pallas kernels, last_terms(): pl.pallas_call(functools.partial(kernel, [len(terms) for terms in asked])...  9.3 us
  transfers between devices with their start and end apart: 66, of which 22 were waited for; matrix products, arithmetic and copies ran while one was open for 15% of the time, Pallas kernels for 32%

profile of v6, /device:TPU:0, one launch (start us, length us, event | category | flops | bytes accessed | tf_op | source)
XLA Modules:
  0.0 313.1 jit_solution(7663715598856739876)
XLA Ops:
  3.3 1.7 compare_select_fusion
  5.1 3.7 %collective-permute-start.6 = (bf16[1,96,384]{2,1,0:T(8,128)(2,1)S(1)}, bf16[1,96,384]{2,1,0:T(8,128)(2,1)S(1)}, u32[]{:S(2)}, u32[]{:S(2)}) collective-permute-start(bf16[1,96,384]{2,1,0:T(8,128)(2,1)S(1)} %bitcast.61), channel_id=1, source_target_pairs={{0,16},{1,17},{2,18},{3,19},{4,20},{5,21},{6,22},{7,23},{8,24},{9,... | collective-permute-start | bytes 221192 | tf_op jit(solution)/shard_map/ppermute | solution.py:728
  9.6 3.8 %collective-permute-done.6 = bf16[1,96,384]{2,1,0:T(8,128)(2,1)S(1)} collective-permute-done((bf16[1,96,384]{2,1,0:T(8,128)(2,1)S(1)}, bf16[1,96,384]{2,1,0:T(8,128)(2,1)S(1)}, u32[]{:S(2)}, u32[]{:S(2)}) %collective-permute-start.6) | collective-permute-done | bytes 73760 | tf_op jit(solution)/shard_map/ppermute | solution.py:728
  13.5 3.7 %collective-permute-start.7 = (bf16[2,96,384]{2,1,0:T(8,128)(2,1)S(1)}, bf16[2,96,384]{2,1,0:T(8,128)(2,1)S(1)}, u32[]{:S(2)}, u32[]{:S(2)}) collective-permute-start(bf16[2,96,384]{2,1,0:T(8,128)(2,1)S(1)} %pad_maximum_fusion.15), channel_id=1, source_target_pairs={{0,2},{1,3},{2,0},{3,1},{4,6},{5,7},{6,4},{7,5},{8,10},{9,11},{10,... | collective-permute-start | bytes 442376 | tf_op jit(solution)/shard_map/ppermute | solution.py:728
  17.8 3.4 %collective-permute-start.11 = (bf16[1,192,384]{2,1,0:T(8,128)(2,1)S(1)}, bf16[1,192,384]{2,1,0:T(8,128)(2,1)S(1)}, u32[]{:S(2)}, u32[]{:S(2)}) collective-permute-start(bf16[1,192,384]{2,1,0:T(8,128)(2,1)S(1)} %bitcast.54), channel_id=1, source_target_pairs={{0,16},{1,17},{2,18},{3,19},{4,20},{5,21},{6,22},{7,23},{8,24},{9,... | collective-permute-start | bytes 442376 | tf_op jit(solution)/shard_map/ppermute | solution.py:728
  22.9 3.5 %collective-permute-done.2 = bf16[2,112,384]{2,1,0:T(8,128)(2,1)S(1)} collective-permute-done((bf16[2,112,384]{2,1,0:T(8,128)(2,1)S(1)}, bf16[2,112,384]{2,1,0:T(8,128)(2,1)S(1)}, u32[]{:S(2)}, u32[]{:S(2)}) %collective-permute-start.2) | collective-permute-done | bytes 172064 | tf_op jit(solution)/shard_map/ppermute | solution.py:728
  30.6 2.3 collective-permute-start.18
  33.1 4.1 %collective-permute-done.3 = bf16[4,112,384]{2,1,0:T(8,128)(2,1)S(1)} collective-permute-done((bf16[4,112,384]{2,1,0:T(8,128)(2,1)S(1)}, bf16[4,112,384]{2,1,0:T(8,128)(2,1)S(1)}, u32[]{:S(2)}, u32[]{:S(2)}) %collective-permute-start.3) | collective-permute-done | bytes 344096 | tf_op jit(solution)/shard_map/ppermute | solution.py:728
  37.6 1.8 collective-permute-done.12
  39.5 1.6 collective-permute-start.13
  42.9 1.8 collective-permute-start.16
  44.7 13.3 %collective-permute-done.21.refs_10_ = bf16[8,96,384]{2,1,0:T(8,128)(2,1)} collective-permute-done((bf16[8,96,384]{2,1,0:T(8,128)(2,1)S(1)}, bf16[8,96,384]{2,1,0:T(8,128)(2,1)}, u32[]{:S(2)}, u32[]{:S(2)}) %collective-permute-start.21) | collective-permute-done | bytes 589856 | tf_op jit(solution)/shard_map/ppermute | solution.py:728
  60.7 4.4 %collective-permute-done.19 = bf16[2,192,384]{2,1,0:T(8,128)(2,1)S(1)} collective-permute-done((bf16[2,192,384]{2,1,0:T(8,128)(2,1)S(1)}, bf16[2,192,384]{2,1,0:T(8,128)(2,1)S(1)}, u32[]{:S(2)}, u32[]{:S(2)}) %collective-permute-start.19) | collective-permute-done | bytes 294944 | tf_op jit(solution)/shard_map/ppermute | solution.py:728
  71.7 17.5 %self_part.1 = (bf16[512,768]{1,0:T(8,128)(2,1)}, bf16[512,768]{1,0:T(8,128)(2,1)}, bf16[512,768]{1,0:T(8,128)(2,1)}, bf16[512,768]{1,0:T(8,128)(2,1)}, bf16[12,...) custom-call(s32[2]{0:T(128)} %pad_add_fusion.refs_0_.spot_ref, ...), custom_call_target="tpu_custom_call" | custom-call | tf_op jit(solution)/shard_map/self_part/pallas_call | solution.py:460
  95.0 22.7 %cross_part.1 = (f32[512,768]{1,0:T(8,128)}, bf16[512,768]{1,0:T(8,128)(2,1)}, bf16[512,768]{1,0:T(8,128)(2,1)}, bf16[512,768]{1,0:T(8,128)(2,1)}, bf16[512,768]...) custom-call(s32[2]{0:T(128)} %pad_add_fusion.refs_0_.spot_ref, ...), custom_call_target="tpu_custom_call" | custom-call | tf_op jit(solution)/shard_map/cross_part/pallas_call | solution.py:460
  118.8 1.8 collective-permute-done.31
  121.6 1.9 collective-permute-done.33
  124.5 24.4 %ffn.1 = (bf16[512,768]{1,0:T(8,128)(2,1)}, f32[512,768]{1,0:T(8,128)}, bf16[384,3072]{1,0:T(8,128)(2,1)}, bf16[384,3072]{1,0:T(8,128)(2,1)}, bf16[4,4,96,768]{3...) custom-call(s32[2]{0:T(128)} %pad_add_fusion.refs_0_.spot_ref, bf16[512,768]{1,0:T(8,128)(2,1)} %get-tuple-element.159.third_ref, ...), custom_call_target="tpu_custom_call" | custom-call | tf_op jit(solution)/shard_map/ffn/pallas_call | solution.py:354
  149.6 4.9 %third_back.1 = (f32[512,768]{1,0:T(8,128)}, bf16[512,768]{1,0:T(8,128)(2,1)}, bf16[512,768]{1,0:T(8,128)(2,1)}, f32[1,768]{1,0:T(1,128)}) custom-call(f32[512,768]{1,0:T(8,128)} %get-tuple-element.170.gthird_ref, f32[512,768]{1,0:T(8,128)} %get-tuple-element.160.upper_ref, bf16[512,768]{1,0:T(8,128)(2,1)} %cot_ref.3, ...), custom_call_target="tpu_custom_call" | custom-call | tf_op jit(solution)/shard_map/third_back/pallas_call | solution.py:387
  156.8 1.8 add_convert_fusion.2
  163.3 21.9 %cross_back.1 = (bf16[512,768]{1,0:T(8,128)(2,1)}, bf16[512,768]{1,0:T(8,128)(2,1)}, f32[512,768]{1,0:T(8,128)}, bf16[512,768]{1,0:T(8,128)(2,1)}, bf16[512,768]...) custom-call(s32[1]{0:T(128)} %bitcast.1.refs_0_, ...), custom_call_target="tpu_custom_call" | custom-call | tf_op jit(solution)/shard_map/cross_back/pallas_call | solution.py:460
  186.7 3.0 collective-permute-done.37.refs_8_
  191.8 1.6 add_convert_fusion.7
  194.6 2.6 add_convert_fusion
  198.7 17.1 %self_back.1 = (bf16[512,768]{1,0:T(8,128)(2,1)}, bf16[512,768]{1,0:T(8,128)(2,1)}, bf16[512,768]{1,0:T(8,128)(2,1)}, f32[6,8,256]{2,1,0:T(8,128)}, bf16[16,48,7...) custom-call(s32[1]{0:T(128)} %bitcast.1.refs_0_, ...), custom_call_target="tpu_custom_call" | custom-call | tf_op jit(solution)/shard_map/self_back/pallas_call | solution.py:460
  218.0 2.1 add_convert_fusion.12
  221.2 2.0 add_convert_fusion.11
  223.3 2.8 collective-permute-start.47
  226.1 2.3 add_convert_fusion.5
  230.2 2.1 add_convert_fusion.3
  234.4 9.6 %last_back.1 = (f32[512,768]{1,0:T(8,128)}, f32[512,768]{1,0:T(8,128)}, f32[8,768]{1,0:T(8,128)}) custom-call(bf16[512,768]{1,0:T(8,128)(2,1)} %get-tuple-element.210.gq_ref, bf16[512,768]{1,0:T(8,128)(2,1)} %get-tuple-element.211.gk_ref, bf16[512,768]{1,0:T(8,128)(2,1)} %get-tuple-element.212.gv_ref, bf16[512,768]{1,0:T(8,128)(2,1)} %get-tuple-element.213.gmk_ref, ...), custom_call_target="tpu_custom_call" | custom-call | tf_op jit(solution)/shard_map/last_back/pallas_call | solution.py:387
  243.9 2.0 add_convert_fusion.14
  245.9 1.9 add_convert_fusion.16
  248.7 1.9 add_convert_fusion.10
  251.4 2.0 add_convert_fusion.9
  255.6 1.9 add_convert_fusion.8
  257.5 2.0 collective-permute-start.53
  260.3 2.6 collective-permute-start.54
  268.2 1.9 add_convert_fusion.13
  270.1 3.3 %collective-permute-start.56 = (bf16[1,96,768]{2,1,0:T(8,128)(2,1)}, bf16[1,96,768]{2,1,0:T(8,128)(2,1)S(1)}, u32[]{:S(2)}, u32[]{:S(2)}) collective-permute-start(bf16[1,96,768]{2,1,0:T(8,128)(2,1)} %add_convert_fusion.13), channel_id=1, source_target_pairs={{0,16},{1,17},{2,18},{3,19},{4,20},{5,21},{6,22},{7,23},{8,24},{9,... | collective-permute-start | bytes 442376 | tf_op jit(solution)/shard_map/ppermute | solution.py:728
  274.7 3.4 %ffn_last.1 = (f32[1,24,3072]{2,1,0:T(8,128)}, f32[1,24]{1,0:T(1,128)}, f32[1,96,768]{2,1,0:T(8,128)}, f32[1,96]{1,0:T(1,128)}, f32[8,768]{1,0:T(8,128)}) custom-call(s32[2]{0:T(128)} %pad_add_fusion.refs_0_.spot_ref, bf16[16,24,3072]{2,1,0:T(8,128)(2,1)} %bitcast.46, bf16[16,24,3072]{2,1,0:T(8,128)(2,1)} %copy-done.5, bf16[8,24,3072]{2,1,0:T(8,128)(2,1)} %copy-done.12, ...), custom_call_target="tpu_custom_call" | custom-call | tf_op jit(solution)/shard_map/ffn_last/pallas_call | solution.py:691
  281.0 3.0 collective-permute-start.58
  284.6 2.9 cross_last.1
  288.2 3.0 self_last.1
  293.6 1.6 collective-permute-start.62
  300.6 3.7 %collective-permute-start.65 = (f32[24,768]{1,0:T(8,128)S(1)}, f32[24,768]{1,0:T(8,128)S(1)}, u32[]{:S(2)}, u32[]{:S(2)}) collective-permute-start(f32[24,768]{1,0:T(8,128)S(1)} %add_add_fusion.1), channel_id=1, source_target_pairs={{0,24},{1,25},{2,26},{3,27},{4,28},{5,29},{6,30},{7,31},{8,16},{9,... | collective-permute-start | bytes 221192 | tf_op jit(solution)/shard_map/ppermute | solution.py:728
  305.0 1.8 pad_maximum_fusion.8
  307.4 1.6 collective-permute-done.63
  (277 shorter events, 79.6 us)
Async XLA Ops:
  5.1 8.4 %collective-permute-start.6 = (bf16[1,96,384]{2,1,0:T(8,128)(2,1)S(1)}, bf16[1,96,384]{2,1,0:T(8,128)(2,1)S(1)}, u32[]{:S(2)}, u32[]{:S(2)}) collective-permute-start(bf16[1,96,384]{2,1,0:T(8,128)(2,1)S(1)} %bitcast.61), channel_id=1, source_target_pairs={{0,16},{1,17},{2,18},{3,19},{4,20},{5,21},{6,22},{7,23},{8,24},{9,... | collective-permute-start | bytes 221192 | tf_op jit(solution)/shard_map/ppermute | solution.py:728
  8.8 8.4 %collective-permute-start.1 = (bf16[1,112,384]{2,1,0:T(8,128)(2,1)S(1)}, bf16[1,112,384]{2,1,0:T(8,128)(2,1)S(1)}, u32[]{:S(2)}, u32[]{:S(2)}) collective-permute-start(bf16[1,112,384]{2,1,0:T(8,128)(2,1)S(1)} %maximum_bitcast_fusion), channel_id=1, source_target_pairs={{0,16},{1,17},{2,18},{3,19},{4,20},{5,21},{6,22},{7,23},{8,24},{9,... | collective-permute-start | bytes 258056 | tf_op jit(solution)/shard_map/ppermute | solution.py:728
  8.9 8.9 %collective-permute-start.10 = (bf16[4,24,384]{2,1,0:T(8,128)(2,1)S(1)}, bf16[4,24,384]{2,1,0:T(8,128)(2,1)S(1)}, u32[]{:S(2)}, u32[]{:S(2)}) collective-permute-start(bf16[4,24,384]{2,1,0:T(8,128)(2,1)S(1)} %get-tuple-element.132), channel_id=1, source_target_pairs={{0,1},{1,0},{2,3},{3,2},{4,5},{5,4},{6,7},{7,6},{8,9},{9,8},{10,11... | collective-permute-start | bytes 221192 | tf_op jit(solution)/shard_map/ppermute | solution.py:728
  9.5 19.6 %collective-permute-start.17 = (bf16[96,384]{1,0:T(8,128)(2,1)S(1)}, bf16[96,384]{1,0:T(8,128)(2,1)S(1)}, u32[]{:S(2)}, u32[]{:S(2)}) collective-permute-start(bf16[96,384]{1,0:T(8,128)(2,1)S(1)} %get-tuple-element.146), channel_id=1, source_target_pairs={{0,1},{1,0},{2,3},{3,2},{4,5},{5,4},{6,7},{7,6},{8,9},{9,8},{10,11... | collective-permute-start | bytes 221192 | tf_op jit(solution)/shard_map/ppermute | solution.py:728
  17.2 9.1 %collective-permute-start.2 = (bf16[2,112,384]{2,1,0:T(8,128)(2,1)S(1)}, bf16[2,112,384]{2,1,0:T(8,128)(2,1)S(1)}, u32[]{:S(2)}, u32[]{:S(2)}) collective-permute-start(bf16[2,112,384]{2,1,0:T(8,128)(2,1)S(1)} %pad_maximum_fusion.14), channel_id=1, source_target_pairs={{0,8},{1,9},{2,10},{3,11},{4,12},{5,13},{6,14},{7,15},{8,0},{9,1},... | collective-permute-start | bytes 516104 | tf_op jit(solution)/shard_map/ppermute | solution.py:728
  17.8 10.0 %collective-permute-start.11 = (bf16[1,192,384]{2,1,0:T(8,128)(2,1)S(1)}, bf16[1,192,384]{2,1,0:T(8,128)(2,1)S(1)}, u32[]{:S(2)}, u32[]{:S(2)}) collective-permute-start(bf16[1,192,384]{2,1,0:T(8,128)(2,1)S(1)} %bitcast.54), channel_id=1, source_target_pairs={{0,16},{1,17},{2,18},{3,19},{4,20},{5,21},{6,22},{7,23},{8,24},{9,... | collective-permute-start | bytes 442376 | tf_op jit(solution)/shard_map/ppermute | solution.py:728
  21.3 11.6 %collective-permute-start.8 = (bf16[4,96,384]{2,1,0:T(8,128)(2,1)S(1)}, bf16[4,96,384]{2,1,0:T(8,128)(2,1)S(1)}, u32[]{:S(2)}, u32[]{:S(2)}) collective-permute-start(bf16[4,96,384]{2,1,0:T(8,128)(2,1)S(1)} %pad_maximum_fusion.10), channel_id=1, source_target_pairs={{0,4},{1,5},{2,6},{3,7},{4,0},{5,1},{6,2},{7,3},{8,12},{9,13},{10,... | collective-permute-start | bytes 884744 | tf_op jit(solution)/shard_map/ppermute | solution.py:728
  26.4 10.7 %collective-permute-start.3 = (bf16[4,112,384]{2,1,0:T(8,128)(2,1)S(1)}, bf16[4,112,384]{2,1,0:T(8,128)(2,1)S(1)}, u32[]{:S(2)}, u32[]{:S(2)}) collective-permute-start(bf16[4,112,384]{2,1,0:T(8,128)(2,1)S(1)} %pad_maximum_fusion.9), channel_id=1, source_target_pairs={{0,4},{1,5},{2,6},{3,7},{4,0},{5,1},{6,2},{7,3},{8,12},{9,13},{10,... | collective-permute-start | bytes 1032200 | tf_op jit(solution)/shard_map/ppermute | solution.py:728
  27.9 11.5 %collective-permute-start.12 = (bf16[2,192,384]{2,1,0:T(8,128)(2,1)S(1)}, bf16[2,192,384]{2,1,0:T(8,128)(2,1)S(1)}, u32[]{:S(2)}, u32[]{:S(2)}) collective-permute-start(bf16[2,192,384]{2,1,0:T(8,128)(2,1)S(1)} %pad_maximum_fusion.11), channel_id=1, source_target_pairs={{0,8},{1,9},{2,10},{3,11},{4,12},{5,13},{6,14},{7,15},{8,0},{9,1},... | collective-permute-start | bytes 884744 | tf_op jit(solution)/shard_map/ppermute | solution.py:728
  29.1 10.4 %collective-permute-start.15 = (bf16[1,48,1536]{2,1,0:T(8,128)(2,1)S(1)}, bf16[1,48,1536]{2,1,0:T(8,128)(2,1)S(1)}, u32[]{:S(2)}, u32[]{:S(2)}) collective-permute-start(bf16[1,48,1536]{2,1,0:T(8,128)(2,1)S(1)} %maximum_select_fusion.2), channel_id=1, source_target_pairs={{0,2},{1,3},{2,0},{3,1},{4,6},{5,7},{6,4},{7,5},{8,10},{9,11},{10,... | collective-permute-start | bytes 442376 | tf_op jit(solution)/shard_map/ppermute | solution.py:728
  30.6 10.7 %collective-permute-start.18 = (bf16[1,192,384]{2,1,0:T(8,128)(2,1)S(1)}, bf16[1,192,384]{2,1,0:T(8,128)(2,1)S(1)}, u32[]{:S(2)}, u32[]{:S(2)}) collective-permute-start(bf16[1,192,384]{2,1,0:T(8,128)(2,1)S(1)} %maximum_select_fusion.3), channel_id=1, source_target_pairs={{0,16},{1,17},{2,18},{3,19},{4,20},{5,21},{6,22},{7,23},{8,24},{9,... | collective-permute-start | bytes 442376 | tf_op jit(solution)/shard_map/ppermute | solution.py:728
  33.0 9.8 %collective-permute-start.9 = (bf16[8,96,384]{2,1,0:T(8,128)(2,1)S(1)}, bf16[8,96,384]{2,1,0:T(8,128)(2,1)S(1)}, u32[]{:S(2)}, u32[]{:S(2)}) collective-permute-start(bf16[8,96,384]{2,1,0:T(8,128)(2,1)S(1)} %pad_maximum_fusion.4.refs_9_), channel_id=1, source_target_pairs={{0,1},{1,0},{2,3},{3,2},{4,5},{5,4},{6,7},{7,6},{8,9},{9,8},{10,11... | collective-permute-start | bytes 1769480 | tf_op jit(solution)/shard_map/ppermute | solution.py:728
  37.2 20.8 %collective-permute-start.21 = (bf16[8,96,384]{2,1,0:T(8,128)(2,1)S(1)}, bf16[8,96,384]{2,1,0:T(8,128)(2,1)}, u32[]{:S(2)}, u32[]{:S(2)}) collective-permute-start(bf16[8,96,384]{2,1,0:T(8,128)(2,1)S(1)} %pad_maximum_fusion.4.refs_9_), channel_id=1, source_target_pairs={{0,8},{1,9},{2,10},{3,11},{4,12},{5,13},{6,14},{7,15},{8,0},{9,1},... | collective-permute-start | bytes 1769480 | tf_op jit(solution)/shard_map/ppermute | solution.py:728
  39.4 18.6 %collective-permute-start.5 = (bf16[8,112,384]{2,1,0:T(8,128)(2,1)S(1)}, bf16[8,112,384]{2,1,0:T(8,128)(2,1)}, u32[]{:S(2)}, u32[]{:S(2)}) collective-permute-start(bf16[8,112,384]{2,1,0:T(8,128)(2,1)S(1)} %pad_maximum_fusion.3.refs_5_), channel_id=1, source_target_pairs={{0,1},{1,0},{2,3},{3,2},{4,5},{5,4},{6,7},{7,6},{8,9},{9,8},{10,11... | collective-permute-start | bytes 2064392 | tf_op jit(solution)/shard_map/ppermute | solution.py:728
  39.5 18.5 %collective-permute-start.13 = (bf16[4,192,384]{2,1,0:T(8,128)(2,1)S(1)}, bf16[4,192,384]{2,1,0:T(8,128)(2,1)S(1)}, u32[]{:S(2)}, u32[]{:S(2)}) collective-permute-start(bf16[4,192,384]{2,1,0:T(8,128)(2,1)S(1)} %pad_maximum_fusion.5), channel_id=1, source_target_pairs={{0,4},{1,5},{2,6},{3,7},{4,0},{5,1},{6,2},{7,3},{8,12},{9,13},{10,... | collective-permute-start | bytes 1769480 | tf_op jit(solution)/shard_map/ppermute | solution.py:728
  41.3 23.8 %collective-permute-start.4 = (bf16[8,112,384]{2,1,0:T(8,128)(2,1)S(1)}, bf16[8,112,384]{2,1,0:T(8,128)(2,1)}, u32[]{:S(2)}, u32[]{:S(2)}) collective-permute-start(bf16[8,112,384]{2,1,0:T(8,128)(2,1)S(1)} %pad_maximum_fusion.3.refs_5_), channel_id=1, source_target_pairs={{0,2},{1,3},{2,0},{3,1},{4,6},{5,7},{6,4},{7,5},{8,10},{9,11},{10,... | collective-permute-start | bytes 2064392 | tf_op jit(solution)/shard_map/ppermute | solution.py:728
  42.9 16.9 %collective-permute-start.16 = (bf16[2,48,1536]{2,1,0:T(8,128)(2,1)S(1)}, bf16[2,48,1536]{2,1,0:T(8,128)(2,1)S(1)}, u32[]{:S(2)}, u32[]{:S(2)}) collective-permute-start(bf16[2,48,1536]{2,1,0:T(8,128)(2,1)S(1)} %pad_maximum_fusion.12), channel_id=1, source_target_pairs={{0,16},{1,17},{2,18},{3,19},{4,20},{5,21},{6,22},{7,23},{8,24},{9,... | collective-permute-start | bytes 884744 | tf_op jit(solution)/shard_map/ppermute | solution.py:728
  58.0 13.7 %collective-permute-start.22 = (bf16[8,96,384]{2,1,0:T(8,128)(2,1)}, bf16[8,96,384]{2,1,0:T(8,128)(2,1)}, u32[]{:S(2)}, u32[]{:S(2)}) collective-permute-start(bf16[8,96,384]{2,1,0:T(8,128)(2,1)} %collective-permute-done.21.refs_10_), channel_id=1, source_target_pairs={{0,1},{1,0},{2,3},{3,2},{4,5},{5,4},{6,7},{7,6},{8,9},{9,8},{10,11... | collective-permute-start | bytes 1769480 | tf_op jit(solution)/shard_map/ppermute | solution.py:728
  58.2 32.8 %collective-permute-start.25 = (bf16[8,192,384]{2,1,0:T(8,128)(2,1)S(1)}, bf16[8,192,384]{2,1,0:T(8,128)(2,1)}, u32[]{:S(2)}, u32[]{:S(2)}) collective-permute-start(bf16[8,192,384]{2,1,0:T(8,128)(2,1)S(1)} %pad_maximum_fusion.refs_8_), channel_id=1, source_target_pairs={{0,2},{1,3},{2,0},{3,1},{4,6},{5,7},{6,4},{7,5},{8,10},{9,11},{10,... | collective-permute-start | bytes 3538952 | tf_op jit(solution)/shard_map/ppermute | solution.py:728
  66.0 23.1 %collective-permute-start.23 = (bf16[4,48,1536]{2,1,0:T(8,128)(2,1)}, bf16[4,48,1536]{2,1,0:T(8,128)(2,1)}, u32[]{:S(2)}, u32[]{:S(2)}) collective-permute-start(bf16[4,48,1536]{2,1,0:T(8,128)(2,1)} %pad_maximum_fusion.6), channel_id=1, source_target_pairs={{0,8},{1,9},{2,10},{3,11},{4,12},{5,13},{6,14},{7,15},{8,0},{9,1},... | collective-permute-start | bytes 1769480 | tf_op jit(solution)/shard_map/ppermute | solution.py:728
  66.9 22.3 %collective-permute-start.24 = (bf16[4,192,384]{2,1,0:T(8,128)(2,1)}, bf16[4,192,384]{2,1,0:T(8,128)(2,1)}, u32[]{:S(2)}, u32[]{:S(2)}) collective-permute-start(bf16[4,192,384]{2,1,0:T(8,128)(2,1)} %pad_maximum_fusion.7), channel_id=1, source_target_pairs={{0,4},{1,5},{2,6},{3,7},{4,0},{5,1},{6,2},{7,3},{8,12},{9,13},{10,... | collective-permute-start | bytes 1769480 | tf_op jit(solution)/shard_map/ppermute | solution.py:728
  71.6 22.4 %collective-permute-start.26 = (bf16[8,192,384]{2,1,0:T(8,128)(2,1)S(1)}, bf16[8,192,384]{2,1,0:T(8,128)(2,1)S(1)}, u32[]{:S(2)}, u32[]{:S(2)}) collective-permute-start(bf16[8,192,384]{2,1,0:T(8,128)(2,1)S(1)} %pad_maximum_fusion.refs_8_), channel_id=1, source_target_pairs={{0,1},{1,0},{2,3},{3,2},{4,5},{5,4},{6,7},{7,6},{8,9},{9,8},{10,11... | collective-permute-start | bytes 3538952 | tf_op jit(solution)/shard_map/ppermute | solution.py:728
  90.4 28.4 %collective-permute-start.28 = (bf16[8,48,1536]{2,1,0:T(8,128)(2,1)S(1)}, bf16[8,48,1536]{2,1,0:T(8,128)(2,1)S(1)}, u32[]{:S(2)}, u32[]{:S(2)}) collective-permute-start(bf16[8,48,1536]{2,1,0:T(8,128)(2,1)S(1)} %pad_maximum_fusion.1.refs_0_), channel_id=1, source_target_pairs={{0,4},{1,5},{2,6},{3,7},{4,0},{5,1},{6,2},{7,3},{8,12},{9,13},{10,... | collective-permute-start | bytes 3538952 | tf_op jit(solution)/shard_map/ppermute | solution.py:728
  92.4 28.3 %collective-permute-start.31 = (bf16[8,192,384]{2,1,0:T(8,128)(2,1)S(1)}, bf16[8,192,384]{2,1,0:T(8,128)(2,1)S(1)}, u32[]{:S(2)}, u32[]{:S(2)}) collective-permute-start(bf16[8,192,384]{2,1,0:T(8,128)(2,1)S(1)} %pad_maximum_fusion.2), channel_id=1, source_target_pairs={{0,2},{1,3},{2,0},{3,1},{4,6},{5,7},{6,4},{7,5},{8,10},{9,11},{10,... | collective-permute-start | bytes 3538952 | tf_op jit(solution)/shard_map/ppermute | solution.py:728
  93.9 26.7 %collective-permute-start.29 = (bf16[8,48,1536]{2,1,0:T(8,128)(2,1)S(1)}, bf16[8,48,1536]{2,1,0:T(8,128)(2,1)S(1)}, u32[]{:S(2)}, u32[]{:S(2)}) collective-permute-start(bf16[8,48,1536]{2,1,0:T(8,128)(2,1)S(1)} %pad_maximum_fusion.1.refs_0_), channel_id=1, source_target_pairs={{0,1},{1,0},{2,3},{3,2},{4,5},{5,4},{6,7},{7,6},{8,9},{9,8},{10,11... | collective-permute-start | bytes 3538952 | tf_op jit(solution)/shard_map/ppermute | solution.py:728
  94.0 26.7 %collective-permute-start.32 = (bf16[8,192,384]{2,1,0:T(8,128)(2,1)S(1)}, bf16[8,192,384]{2,1,0:T(8,128)(2,1)S(1)}, u32[]{:S(2)}, u32[]{:S(2)}) collective-permute-start(bf16[8,192,384]{2,1,0:T(8,128)(2,1)S(1)} %pad_maximum_fusion.2), channel_id=1, source_target_pairs={{0,1},{1,0},{2,3},{3,2},{4,5},{5,4},{6,7},{7,6},{8,9},{9,8},{10,11... | collective-permute-start | bytes 3538952 | tf_op jit(solution)/shard_map/ppermute | solution.py:728
  149.2 11.0 %collective-permute-start.35 = (bf16[16,96,768]{2,1,0:T(8,128)(2,1)}, bf16[16,96,768]{2,1,0:T(8,128)(2,1)}, u32[]{:S(2)}, u32[]{:S(2)}) collective-permute-start(bf16[16,96,768]{2,1,0:T(8,128)(2,1)} %bitcast.74), channel_id=1, source_target_pairs={{0,1},{1,0},{2,3},{3,2},{4,5},{5,4},{6,7},{7,6},{8,9},{9,8},{10,11... | collective-permute-start | bytes 7077896 | tf_op jit(solution)/shard_map/ppermute | solution.py:728
  158.7 28.1 %collective-permute-start.36 = (bf16[8,24,3072]{2,1,0:T(8,128)(2,1)S(1)}, bf16[8,24,3072]{2,1,0:T(8,128)(2,1)S(1)}, u32[]{:S(2)}, u32[]{:S(2)}) collective-permute-start(bf16[8,24,3072]{2,1,0:T(8,128)(2,1)S(1)} %add_convert_fusion.2), channel_id=1, source_target_pairs={{0,4},{1,5},{2,6},{3,7},{4,0},{5,1},{6,2},{7,3},{8,12},{9,13},{10,... | collective-permute-start | bytes 3538952 | tf_op jit(solution)/shard_map/ppermute | solution.py:728
  161.8 27.9 %collective-permute-start.37 = (bf16[8,96,768]{2,1,0:T(8,128)(2,1)S(1)}, bf16[8,96,768]{2,1,0:T(8,128)(2,1)}, u32[]{:S(2)}, u32[]{:S(2)}) collective-permute-start(bf16[8,96,768]{2,1,0:T(8,128)(2,1)S(1)} %add_convert_fusion.1), channel_id=1, source_target_pairs={{0,2},{1,3},{2,0},{3,1},{4,6},{5,7},{6,4},{7,5},{8,10},{9,11},{10,... | collective-permute-start | bytes 3538952 | tf_op jit(solution)/shard_map/ppermute | solution.py:728
  191.2 24.6 %collective-permute-start.39 = (bf16[4,96,768]{2,1,0:T(8,128)(2,1)S(1)}, bf16[4,96,768]{2,1,0:T(8,128)(2,1)S(1)}, u32[]{:S(2)}, u32[]{:S(2)}) collective-permute-start(bf16[4,96,768]{2,1,0:T(8,128)(2,1)S(1)} %add_convert_fusion.6), channel_id=1, source_target_pairs={{0,4},{1,5},{2,6},{3,7},{4,0},{5,1},{6,2},{7,3},{8,12},{9,13},{10,... | collective-permute-start | bytes 1769480 | tf_op jit(solution)/shard_map/ppermute | solution.py:728
  193.4 22.4 %collective-permute-start.40 = (bf16[4,24,3072]{2,1,0:T(8,128)(2,1)S(1)}, bf16[4,24,3072]{2,1,0:T(8,128)(2,1)S(1)}, u32[]{:S(2)}, u32[]{:S(2)}) collective-permute-start(bf16[4,24,3072]{2,1,0:T(8,128)(2,1)S(1)} %add_convert_fusion.7), channel_id=1, source_target_pairs={{0,8},{1,9},{2,10},{3,11},{4,12},{5,13},{6,14},{7,15},{8,0},{9,1},... | collective-permute-start | bytes 1769480 | tf_op jit(solution)/shard_map/ppermute | solution.py:728
  197.2 28.8 %collective-permute-start.41 = (bf16[8,96,768]{2,1,0:T(8,128)(2,1)}, bf16[8,96,768]{2,1,0:T(8,128)(2,1)}, u32[]{:S(2)}, u32[]{:S(2)}) collective-permute-start(bf16[8,96,768]{2,1,0:T(8,128)(2,1)} %add_convert_fusion), channel_id=1, source_target_pairs={{0,2},{1,3},{2,0},{3,1},{4,6},{5,7},{6,4},{7,5},{8,10},{9,11},{10,... | collective-permute-start | bytes 3538952 | tf_op jit(solution)/shard_map/ppermute | solution.py:728
  217.5 10.9 %collective-permute-start.42 = (bf16[16,48,768]{2,1,0:T(8,128)(2,1)}, bf16[16,48,768]{2,1,0:T(8,128)(2,1)S(1)}, u32[]{:S(2)}, u32[]{:S(2)}) collective-permute-start(bf16[16,48,768]{2,1,0:T(8,128)(2,1)} %get-tuple-element.204), channel_id=1, source_target_pairs={{0,1},{1,0},{2,3},{3,2},{4,5},{5,4},{6,7},{7,6},{8,9},{9,8},{10,11... | collective-permute-start | bytes 3538952 | tf_op jit(solution)/shard_map/ppermute | solution.py:728
  217.5 11.8 %collective-permute-start.43 = (bf16[16,48,768]{2,1,0:T(8,128)(2,1)}, bf16[16,48,768]{2,1,0:T(8,128)(2,1)}, u32[]{:S(2)}, u32[]{:S(2)}) collective-permute-start(bf16[16,48,768]{2,1,0:T(8,128)(2,1)} %get-tuple-element.208), channel_id=1, source_target_pairs={{0,1},{1,0},{2,3},{3,2},{4,5},{5,4},{6,7},{7,6},{8,9},{9,8},{10,11... | collective-permute-start | bytes 3538952 | tf_op jit(solution)/shard_map/ppermute | solution.py:728
  220.1 23.8 %collective-permute-start.52 = (bf16[2,96,768]{2,1,0:T(8,128)(2,1)}, bf16[2,96,768]{2,1,0:T(8,128)(2,1)}, u32[]{:S(2)}, u32[]{:S(2)}) collective-permute-start(bf16[2,96,768]{2,1,0:T(8,128)(2,1)} %add_convert_fusion.12), channel_id=1, source_target_pairs={{0,8},{1,9},{2,10},{3,11},{4,12},{5,13},{6,14},{7,15},{8,0},{9,1},... | collective-permute-start | bytes 884744 | tf_op jit(solution)/shard_map/ppermute | solution.py:728
  223.3 22.6 %collective-permute-start.47 = (bf16[2,24,3072]{2,1,0:T(8,128)(2,1)}, bf16[2,24,3072]{2,1,0:T(8,128)(2,1)}, u32[]{:S(2)}, u32[]{:S(2)}) collective-permute-start(bf16[2,24,3072]{2,1,0:T(8,128)(2,1)} %add_convert_fusion.11), channel_id=1, source_target_pairs={{0,16},{1,17},{2,18},{3,19},{4,20},{5,21},{6,22},{7,23},{8,24},{9,... | collective-permute-start | bytes 884744 | tf_op jit(solution)/shard_map/ppermute | solution.py:728
  229.3 18.6 %collective-permute-start.44 = (bf16[8,48,768]{2,1,0:T(8,128)(2,1)}, bf16[8,48,768]{2,1,0:T(8,128)(2,1)}, u32[]{:S(2)}, u32[]{:S(2)}) collective-permute-start(bf16[8,48,768]{2,1,0:T(8,128)(2,1)} %add_convert_fusion.4), channel_id=1, source_target_pairs={{0,2},{1,3},{2,0},{3,1},{4,6},{5,7},{6,4},{7,5},{8,10},{9,11},{10,... | collective-permute-start | bytes 1769480 | tf_op jit(solution)/shard_map/ppermute | solution.py:728
  232.3 16.4 %collective-permute-start.49 = (bf16[8,48,768]{2,1,0:T(8,128)(2,1)}, bf16[8,48,768]{2,1,0:T(8,128)(2,1)}, u32[]{:S(2)}, u32[]{:S(2)}) collective-permute-start(bf16[8,48,768]{2,1,0:T(8,128)(2,1)} %add_convert_fusion.3), channel_id=1, source_target_pairs={{0,8},{1,9},{2,10},{3,11},{4,12},{5,13},{6,14},{7,15},{8,0},{9,1},... | collective-permute-start | bytes 1769480 | tf_op jit(solution)/shard_map/ppermute | solution.py:728
  233.4 21.4 %collective-permute-start.51 = (bf16[4,96,768]{2,1,0:T(8,128)(2,1)}, bf16[4,96,768]{2,1,0:T(8,128)(2,1)S(1)}, u32[]{:S(2)}, u32[]{:S(2)}) collective-permute-start(bf16[4,96,768]{2,1,0:T(8,128)(2,1)} %add_convert_fusion.5), channel_id=1, source_target_pairs={{0,4},{1,5},{2,6},{3,7},{4,0},{5,1},{6,2},{7,3},{8,12},{9,13},{10,... | collective-permute-start | bytes 1769480 | tf_op jit(solution)/shard_map/ppermute | solution.py:728
  250.6 12.3 %collective-permute-start.45 = (bf16[4,48,768]{2,1,0:T(8,128)(2,1)}, bf16[4,48,768]{2,1,0:T(8,128)(2,1)}, u32[]{:S(2)}, u32[]{:S(2)}) collective-permute-start(bf16[4,48,768]{2,1,0:T(8,128)(2,1)} %add_convert_fusion.10), channel_id=1, source_target_pairs={{0,8},{1,9},{2,10},{3,11},{4,12},{5,13},{6,14},{7,15},{8,0},{9,1},... | collective-permute-start | bytes 884744 | tf_op jit(solution)/shard_map/ppermute | solution.py:728
  253.3 11.8 %collective-permute-start.50 = (bf16[4,48,768]{2,1,0:T(8,128)(2,1)}, bf16[4,48,768]{2,1,0:T(8,128)(2,1)}, u32[]{:S(2)}, u32[]{:S(2)}) collective-permute-start(bf16[4,48,768]{2,1,0:T(8,128)(2,1)} %add_convert_fusion.9), channel_id=1, source_target_pairs={{0,4},{1,5},{2,6},{3,7},{4,0},{5,1},{6,2},{7,3},{8,12},{9,13},{10,... | collective-permute-start | bytes 884744 | tf_op jit(solution)/shard_map/ppermute | solution.py:728
  257.5 10.6 %collective-permute-start.53 = (bf16[2,96,768]{2,1,0:T(8,128)(2,1)}, bf16[2,96,768]{2,1,0:T(8,128)(2,1)}, u32[]{:S(2)}, u32[]{:S(2)}) collective-permute-start(bf16[2,96,768]{2,1,0:T(8,128)(2,1)} %add_convert_fusion.8), channel_id=1, source_target_pairs={{0,8},{1,9},{2,10},{3,11},{4,12},{5,13},{6,14},{7,15},{8,0},{9,1},... | collective-permute-start | bytes 884744 | tf_op jit(solution)/shard_map/ppermute | solution.py:728
  259.6 13.8 %collective-permute-start.48 = (bf16[1,24,3072]{2,1,0:T(8,128)(2,1)}, bf16[1,24,3072]{2,1,0:T(8,128)(2,1)S(1)}, u32[]{:S(2)}, u32[]{:S(2)}) collective-permute-start(bf16[1,24,3072]{2,1,0:T(8,128)(2,1)} %add_convert_fusion.16), channel_id=1, source_target_pairs={{0,2},{1,3},{2,0},{3,1},{4,6},{5,7},{6,4},{7,5},{8,10},{9,11},{10,... | collective-permute-start | bytes 442376 | tf_op jit(solution)/shard_map/ppermute | solution.py:728
  260.3 13.1 %collective-permute-start.54 = (bf16[1,96,768]{2,1,0:T(8,128)(2,1)}, bf16[1,96,768]{2,1,0:T(8,128)(2,1)S(1)}, u32[]{:S(2)}, u32[]{:S(2)}) collective-permute-start(bf16[1,96,768]{2,1,0:T(8,128)(2,1)} %add_convert_fusion.14), channel_id=1, source_target_pairs={{0,16},{1,17},{2,18},{3,19},{4,20},{5,21},{6,22},{7,23},{8,24},{9,... | collective-permute-start | bytes 442376 | tf_op jit(solution)/shard_map/ppermute | solution.py:728
  264.1 14.0 %collective-permute-start.46 = (bf16[2,48,768]{2,1,0:T(8,128)(2,1)S(1)}, bf16[2,48,768]{2,1,0:T(8,128)(2,1)S(1)}, u32[]{:S(2)}, u32[]{:S(2)}) collective-permute-start(bf16[2,48,768]{2,1,0:T(8,128)(2,1)S(1)} %add_convert_fusion.17), channel_id=1, source_target_pairs={{0,4},{1,5},{2,6},{3,7},{4,0},{5,1},{6,2},{7,3},{8,12},{9,13},{10,... | collective-permute-start | bytes 442376 | tf_op jit(solution)/shard_map/ppermute | solution.py:728
  266.4 12.9 %collective-permute-start.57 = (bf16[2,48,768]{2,1,0:T(8,128)(2,1)S(1)}, bf16[2,48,768]{2,1,0:T(8,128)(2,1)S(1)}, u32[]{:S(2)}, u32[]{:S(2)}) collective-permute-start(bf16[2,48,768]{2,1,0:T(8,128)(2,1)S(1)} %add_convert_fusion.15), channel_id=1, source_target_pairs={{0,2},{1,3},{2,0},{3,1},{4,6},{5,7},{6,4},{7,5},{8,10},{9,11},{10,... | collective-permute-start | bytes 442376 | tf_op jit(solution)/shard_map/ppermute | solution.py:728
  270.1 13.9 %collective-permute-start.56 = (bf16[1,96,768]{2,1,0:T(8,128)(2,1)}, bf16[1,96,768]{2,1,0:T(8,128)(2,1)S(1)}, u32[]{:S(2)}, u32[]{:S(2)}) collective-permute-start(bf16[1,96,768]{2,1,0:T(8,128)(2,1)} %add_convert_fusion.13), channel_id=1, source_target_pairs={{0,16},{1,17},{2,18},{3,19},{4,20},{5,21},{6,22},{7,23},{8,24},{9,... | collective-permute-start | bytes 442376 | tf_op jit(solution)/shard_map/ppermute | solution.py:728
  279.2 8.3 %collective-permute-start.55 = (bf16[1,48,768]{2,1,0:T(8,128)(2,1)S(1)}, bf16[1,48,768]{2,1,0:T(8,128)(2,1)S(1)}, u32[]{:S(2)}, u32[]{:S(2)}) collective-permute-start(bf16[1,48,768]{2,1,0:T(8,128)(2,1)S(1)} %add_convert_fusion.19), channel_id=1, source_target_pairs={{0,16},{1,17},{2,18},{3,19},{4,20},{5,21},{6,22},{7,23},{8,24},{9,... | collective-permute-start | bytes 221192 | tf_op jit(solution)/shard_map/ppermute | solution.py:728
  (67 other events, 487.4 us)

commit v7 on v6

--- a/solution.py
+++ b/solution.py
@@ -53,7 +53,7 @@
 LANES = 128
 GROUP = LANES // HEAD
 CUT = 256
-VMEM_BYTES = 56 * 1024 * 1024
+VMEM_BYTES = 60 * 1024 * 1024
 
 NT = (((1,), (1,)), ((), ()))
 TN = (((0,), (0,)), ((), ()))

time: 318 us -> 315 us (level)
  local copies, waits for them, and re-layouts: 14.1 us -> 9.26 us
  starting transfers between devices: 71.4 us -> 67.5 us
  other arithmetic: 48.4 us -> 51.9 us
    unnamed x99 -> x87, local copies, waits for them, and re-layouts: 9.66 us -> 4.77 us
    ppermute x66, starting transfers between devices: 71.4 us -> 67.5 us  [swap(): return lax.ppermute(value, AXES, [(i, i ^ flip) for i in range(self.count)])]
    convert_element_type x20, other arithmetic: 34.5 us -> 38.1 us  [send(): sent = sum(parts).astype(jnp.bfloat16)]
  transfers between devices with their start and end apart: 66 -> 66, of which waited for: 22 -> 22; matrix products, arithmetic and copies ran while one was open for 15% -> 17% of each run, Pallas kernels for 32% -> 32%
where the time goes in v7:
time: 315 us; the launch traced here: 311 us
  Pallas kernels  127 us (40%)
  starting transfers between devices  67.5 us (21%)
  waiting for transfers between devices  52.4 us (17%)
  other arithmetic  51.9 us (16%)
  local copies, waits for them, and re-layouts  9.26 us (3%)
    pallas_call x4, Pallas kernels, by_pair(): pl.pallas_call(body, grid=(PAIRS,), in_specs=in_specs, out_specs=out_spec...  79.3 us
    ppermute x66, starting transfers between devices, swap(): return lax.ppermute(value, AXES, [(i, i ^ flip) for i in range(self.count)])  67.5 us
    ppermute x66, waiting for transfers between devices, swap(): return lax.ppermute(value, AXES, [(i, i ^ flip) for i in range(self.count)])  52.4 us
    convert_element_type x20, other arithmetic, send(): sent = sum(parts).astype(jnp.bfloat16)  38.1 us
    pallas_call x1, Pallas kernels, ffn(): pl.pallas_call(functools.partial(ffn_kernel, tiled, plans), grid_spec=plt...  24.5 us
    pallas_call x2, Pallas kernels, fused(): pl.pallas_call(kernel, in_specs=[space] * len(args), out_specs=[space] *...  14.4 us
    pallas_call x3, Pallas kernels, last_terms(): pl.pallas_call(functools.partial(kernel, [len(terms) for terms in asked])...  9.29 us
  transfers between devices with their start and end apart: 66, of which 22 were waited for; matrix products, arithmetic and copies ran while one was open for 17% of the time, Pallas kernels for 32%

profile of v7, /device:TPU:0, one launch (start us, length us, event | category | flops | bytes accessed | tf_op | source)
XLA Modules:
  0.0 310.7 jit_solution(15392879137469683650)
XLA Ops:
  5.1 3.7 %collective-permute-start.6 = (bf16[1,96,384]{2,1,0:T(8,128)(2,1)S(1)}, bf16[1,96,384]{2,1,0:T(8,128)(2,1)S(1)}, u32[]{:S(2)}, u32[]{:S(2)}) collective-permute-start(bf16[1,96,384]{2,1,0:T(8,128)(2,1)S(1)} %bitcast.59), channel_id=1, source_target_pairs={{0,16},{1,17},{2,18},{3,19},{4,20},{5,21},{6,22},{7,23},{8,24},{9,... | collective-permute-start | bytes 221192 | tf_op jit(solution)/shard_map/ppermute | solution.py:728
  9.6 3.8 %collective-permute-done.6 = bf16[1,96,384]{2,1,0:T(8,128)(2,1)S(1)} collective-permute-done((bf16[1,96,384]{2,1,0:T(8,128)(2,1)S(1)}, bf16[1,96,384]{2,1,0:T(8,128)(2,1)S(1)}, u32[]{:S(2)}, u32[]{:S(2)}) %collective-permute-start.6) | collective-permute-done | bytes 73760 | tf_op jit(solution)/shard_map/ppermute | solution.py:728
  13.5 3.7 %collective-permute-start.7 = (bf16[2,96,384]{2,1,0:T(8,128)(2,1)S(1)}, bf16[2,96,384]{2,1,0:T(8,128)(2,1)S(1)}, u32[]{:S(2)}, u32[]{:S(2)}) collective-permute-start(bf16[2,96,384]{2,1,0:T(8,128)(2,1)S(1)} %pad_maximum_fusion.15), channel_id=1, source_target_pairs={{0,2},{1,3},{2,0},{3,1},{4,6},{5,7},{6,4},{7,5},{8,10},{9,11},{10,... | collective-permute-start | bytes 442376 | tf_op jit(solution)/shard_map/ppermute | solution.py:728
  17.8 3.4 %collective-permute-start.11 = (bf16[1,192,384]{2,1,0:T(8,128)(2,1)S(1)}, bf16[1,192,384]{2,1,0:T(8,128)(2,1)S(1)}, u32[]{:S(2)}, u32[]{:S(2)}) collective-permute-start(bf16[1,192,384]{2,1,0:T(8,128)(2,1)S(1)} %bitcast.54), channel_id=1, source_target_pairs={{0,16},{1,17},{2,18},{3,19},{4,20},{5,21},{6,22},{7,23},{8,24},{9,... | collective-permute-start | bytes 442376 | tf_op jit(solution)/shard_map/ppermute | solution.py:728
  22.9 3.5 %collective-permute-done.2 = bf16[2,112,384]{2,1,0:T(8,128)(2,1)S(1)} collective-permute-done((bf16[2,112,384]{2,1,0:T(8,128)(2,1)S(1)}, bf16[2,112,384]{2,1,0:T(8,128)(2,1)S(1)}, u32[]{:S(2)}, u32[]{:S(2)}) %collective-permute-start.2) | collective-permute-done | bytes 172064 | tf_op jit(solution)/shard_map/ppermute | solution.py:728
  30.6 2.3 collective-permute-start.18
  33.1 4.1 %collective-permute-done.3 = bf16[4,112,384]{2,1,0:T(8,128)(2,1)S(1)} collective-permute-done((bf16[4,112,384]{2,1,0:T(8,128)(2,1)S(1)}, bf16[4,112,384]{2,1,0:T(8,128)(2,1)S(1)}, u32[]{:S(2)}, u32[]{:S(2)}) %collective-permute-start.3) | collective-permute-done | bytes 344096 | tf_op jit(solution)/shard_map/ppermute | solution.py:728
  37.5 1.8 collective-permute-done.12
  44.7 13.3 %collective-permute-done.21.refs_10_ = bf16[8,96,384]{2,1,0:T(8,128)(2,1)} collective-permute-done((bf16[8,96,384]{2,1,0:T(8,128)(2,1)S(1)}, bf16[8,96,384]{2,1,0:T(8,128)(2,1)}, u32[]{:S(2)}, u32[]{:S(2)}) %collective-permute-start.21) | collective-permute-done | bytes 589856 | tf_op jit(solution)/shard_map/ppermute | solution.py:728
  60.6 4.5 %collective-permute-done.19 = bf16[2,192,384]{2,1,0:T(8,128)(2,1)S(1)} collective-permute-done((bf16[2,192,384]{2,1,0:T(8,128)(2,1)S(1)}, bf16[2,192,384]{2,1,0:T(8,128)(2,1)S(1)}, u32[]{:S(2)}, u32[]{:S(2)}) %collective-permute-start.19) | collective-permute-done | bytes 294944 | tf_op jit(solution)/shard_map/ppermute | solution.py:728
  71.7 17.6 %self_part.1 = (bf16[512,768]{1,0:T(8,128)(2,1)}, bf16[512,768]{1,0:T(8,128)(2,1)}, bf16[512,768]{1,0:T(8,128)(2,1)}, bf16[512,768]{1,0:T(8,128)(2,1)}, bf16[12,...) custom-call(s32[2]{0:T(128)} %pad_add_fusion.refs_0_.spot_ref, ...), custom_call_target="tpu_custom_call" | custom-call | tf_op jit(solution)/shard_map/self_part/pallas_call | solution.py:460
  94.7 22.7 %cross_part.1 = (f32[512,768]{1,0:T(8,128)}, bf16[512,768]{1,0:T(8,128)(2,1)}, bf16[512,768]{1,0:T(8,128)(2,1)}, bf16[512,768]{1,0:T(8,128)(2,1)}, bf16[512,768]...) custom-call(s32[2]{0:T(128)} %pad_add_fusion.refs_0_.spot_ref, ...), custom_call_target="tpu_custom_call" | custom-call | tf_op jit(solution)/shard_map/cross_part/pallas_call | solution.py:460
  119.1 1.9 collective-permute-done.31
  122.3 1.9 collective-permute-done.33
  124.2 24.5 %ffn.1 = (bf16[512,768]{1,0:T(8,128)(2,1)}, f32[512,768]{1,0:T(8,128)}, bf16[384,3072]{1,0:T(8,128)(2,1)}, bf16[384,3072]{1,0:T(8,128)(2,1)}, bf16[4,4,96,768]{3...) custom-call(s32[2]{0:T(128)} %pad_add_fusion.refs_0_.spot_ref, bf16[512,768]{1,0:T(8,128)(2,1)} %get-tuple-element.159.third_ref, ...), custom_call_target="tpu_custom_call" | custom-call | tf_op jit(solution)/shard_map/ffn/pallas_call | solution.py:354
  149.2 5.0 %third_back.1 = (f32[512,768]{1,0:T(8,128)}, bf16[512,768]{1,0:T(8,128)(2,1)}, bf16[512,768]{1,0:T(8,128)(2,1)}, f32[1,768]{1,0:T(1,128)}) custom-call(f32[512,768]{1,0:T(8,128)} %get-tuple-element.170.gthird_ref, f32[512,768]{1,0:T(8,128)} %get-tuple-element.160.upper_ref, bf16[512,768]{1,0:T(8,128)(2,1)} %cot_ref.3, ...), custom_call_target="tpu_custom_call" | custom-call | tf_op jit(solution)/shard_map/third_back/pallas_call | solution.py:387
  154.2 2.8 add_convert_fusion.2
  161.7 21.9 %cross_back.1 = (bf16[512,768]{1,0:T(8,128)(2,1)}, bf16[512,768]{1,0:T(8,128)(2,1)}, f32[512,768]{1,0:T(8,128)}, bf16[512,768]{1,0:T(8,128)(2,1)}, bf16[512,768]...) custom-call(s32[1]{0:T(128)} %bitcast.1.refs_0_, ...), custom_call_target="tpu_custom_call" | custom-call | tf_op jit(solution)/shard_map/cross_back/pallas_call | solution.py:460
  185.3 2.6 collective-permute-done.37.refs_8_
  189.0 2.3 add_convert_fusion.6
  191.8 2.5 add_convert_fusion.7
  195.5 2.6 add_convert_fusion
  199.6 17.0 %self_back.1 = (bf16[512,768]{1,0:T(8,128)(2,1)}, bf16[512,768]{1,0:T(8,128)(2,1)}, bf16[512,768]{1,0:T(8,128)(2,1)}, f32[6,8,256]{2,1,0:T(8,128)}, bf16[16,48,7...) custom-call(s32[1]{0:T(128)} %bitcast.1.refs_0_, ...), custom_call_target="tpu_custom_call" | custom-call | tf_op jit(solution)/shard_map/self_back/pallas_call | solution.py:460
  218.0 2.1 add_convert_fusion.12
  221.0 2.0 add_convert_fusion.11
  223.0 2.9 collective-permute-start.47
  225.9 2.3 add_convert_fusion.5
  230.1 2.0 add_convert_fusion.3
  234.2 9.4 %last_back.1 = (f32[512,768]{1,0:T(8,128)}, f32[512,768]{1,0:T(8,128)}, f32[8,768]{1,0:T(8,128)}) custom-call(bf16[512,768]{1,0:T(8,128)(2,1)} %get-tuple-element.210.gq_ref, bf16[512,768]{1,0:T(8,128)(2,1)} %get-tuple-element.211.gk_ref, bf16[512,768]{1,0:T(8,128)(2,1)} %get-tuple-element.212.gv_ref, bf16[512,768]{1,0:T(8,128)(2,1)} %get-tuple-element.213.gmk_ref, ...), custom_call_target="tpu_custom_call" | custom-call | tf_op jit(solution)/shard_map/last_back/pallas_call | solution.py:387
  243.6 2.0 add_convert_fusion.14
  245.6 2.0 add_convert_fusion.16
  247.6 1.8 collective-permute-done.49.refs_8_
  249.4 1.9 add_convert_fusion.10
  251.3 2.0 add_convert_fusion.9
  254.8 2.0 add_convert_fusion.8
  256.8 2.0 collective-permute-start.53
  262.1 3.1 %collective-permute-start.46 = (bf16[2,48,768]{2,1,0:T(8,128)(2,1)S(1)}, bf16[2,48,768]{2,1,0:T(8,128)(2,1)S(1)}, u32[]{:S(2)}, u32[]{:S(2)}) collective-permute-start(bf16[2,48,768]{2,1,0:T(8,128)(2,1)S(1)} %add_convert_fusion.17), channel_id=1, source_target_pairs={{0,4},{1,5},{2,6},{3,7},{4,0},{5,1},{6,2},{7,3},{8,12},{9,13},{10,... | collective-permute-start | bytes 442376 | tf_op jit(solution)/shard_map/ppermute | solution.py:728
  265.2 1.9 add_convert_fusion.15
  268.5 1.9 add_convert_fusion.13
  270.4 3.4 %ffn_last.1 = (f32[1,24,3072]{2,1,0:T(8,128)}, f32[1,24]{1,0:T(1,128)}, f32[1,96,768]{2,1,0:T(8,128)}, f32[1,96]{1,0:T(1,128)}, f32[8,768]{1,0:T(8,128)}) custom-call(s32[2]{0:T(128)} %pad_add_fusion.refs_0_.spot_ref, bf16[16,24,3072]{2,1,0:T(8,128)(2,1)} %bitcast.46, bf16[16,24,3072]{2,1,0:T(8,128)(2,1)} %collective-permute-done.34.refs_1_, ...), custom_call_target="tpu_custom_call" | custom-call | tf_op jit(solution)/shard_map/ffn_last/pallas_call | solution.py:691
  274.9 3.0 collective-permute-start.55
  280.3 2.9 cross_last.1
  285.6 3.0 self_last.1
  291.0 2.1 collective-permute-start.62
  298.5 2.0 collective-permute-start.65
  300.5 2.4 collective-permute-start.64
  302.9 1.8 pad_maximum_fusion.8
  305.6 2.0 collective-permute-done.64
  (265 shorter events, 75.6 us)
Async XLA Ops:
  5.1 8.4 %collective-permute-start.6 = (bf16[1,96,384]{2,1,0:T(8,128)(2,1)S(1)}, bf16[1,96,384]{2,1,0:T(8,128)(2,1)S(1)}, u32[]{:S(2)}, u32[]{:S(2)}) collective-permute-start(bf16[1,96,384]{2,1,0:T(8,128)(2,1)S(1)} %bitcast.59), channel_id=1, source_target_pairs={{0,16},{1,17},{2,18},{3,19},{4,20},{5,21},{6,22},{7,23},{8,24},{9,... | collective-permute-start | bytes 221192 | tf_op jit(solution)/shard_map/ppermute | solution.py:728
  8.8 8.4 %collective-permute-start.1 = (bf16[1,112,384]{2,1,0:T(8,128)(2,1)S(1)}, bf16[1,112,384]{2,1,0:T(8,128)(2,1)S(1)}, u32[]{:S(2)}, u32[]{:S(2)}) collective-permute-start(bf16[1,112,384]{2,1,0:T(8,128)(2,1)S(1)} %maximum_bitcast_fusion), channel_id=1, source_target_pairs={{0,16},{1,17},{2,18},{3,19},{4,20},{5,21},{6,22},{7,23},{8,24},{9,... | collective-permute-start | bytes 258056 | tf_op jit(solution)/shard_map/ppermute | solution.py:728
  8.9 8.9 %collective-permute-start.10 = (bf16[4,24,384]{2,1,0:T(8,128)(2,1)S(1)}, bf16[4,24,384]{2,1,0:T(8,128)(2,1)S(1)}, u32[]{:S(2)}, u32[]{:S(2)}) collective-permute-start(bf16[4,24,384]{2,1,0:T(8,128)(2,1)S(1)} %get-tuple-element.132), channel_id=1, source_target_pairs={{0,1},{1,0},{2,3},{3,2},{4,5},{5,4},{6,7},{7,6},{8,9},{9,8},{10,11... | collective-permute-start | bytes 221192 | tf_op jit(solution)/shard_map/ppermute | solution.py:728
  9.4 19.6 %collective-permute-start.17 = (bf16[96,384]{1,0:T(8,128)(2,1)S(1)}, bf16[96,384]{1,0:T(8,128)(2,1)S(1)}, u32[]{:S(2)}, u32[]{:S(2)}) collective-permute-start(bf16[96,384]{1,0:T(8,128)(2,1)S(1)} %get-tuple-element.146), channel_id=1, source_target_pairs={{0,1},{1,0},{2,3},{3,2},{4,5},{5,4},{6,7},{7,6},{8,9},{9,8},{10,11... | collective-permute-start | bytes 221192 | tf_op jit(solution)/shard_map/ppermute | solution.py:728
  17.2 9.1 %collective-permute-start.2 = (bf16[2,112,384]{2,1,0:T(8,128)(2,1)S(1)}, bf16[2,112,384]{2,1,0:T(8,128)(2,1)S(1)}, u32[]{:S(2)}, u32[]{:S(2)}) collective-permute-start(bf16[2,112,384]{2,1,0:T(8,128)(2,1)S(1)} %pad_maximum_fusion.14), channel_id=1, source_target_pairs={{0,8},{1,9},{2,10},{3,11},{4,12},{5,13},{6,14},{7,15},{8,0},{9,1},... | collective-permute-start | bytes 516104 | tf_op jit(solution)/shard_map/ppermute | solution.py:728
  17.8 10.0 %collective-permute-start.11 = (bf16[1,192,384]{2,1,0:T(8,128)(2,1)S(1)}, bf16[1,192,384]{2,1,0:T(8,128)(2,1)S(1)}, u32[]{:S(2)}, u32[]{:S(2)}) collective-permute-start(bf16[1,192,384]{2,1,0:T(8,128)(2,1)S(1)} %bitcast.54), channel_id=1, source_target_pairs={{0,16},{1,17},{2,18},{3,19},{4,20},{5,21},{6,22},{7,23},{8,24},{9,... | collective-permute-start | bytes 442376 | tf_op jit(solution)/shard_map/ppermute | solution.py:728
  21.3 11.6 %collective-permute-start.8 = (bf16[4,96,384]{2,1,0:T(8,128)(2,1)S(1)}, bf16[4,96,384]{2,1,0:T(8,128)(2,1)S(1)}, u32[]{:S(2)}, u32[]{:S(2)}) collective-permute-start(bf16[4,96,384]{2,1,0:T(8,128)(2,1)S(1)} %pad_maximum_fusion.10), channel_id=1, source_target_pairs={{0,4},{1,5},{2,6},{3,7},{4,0},{5,1},{6,2},{7,3},{8,12},{9,13},{10,... | collective-permute-start | bytes 884744 | tf_op jit(solution)/shard_map/ppermute | solution.py:728
  26.4 10.7 %collective-permute-start.3 = (bf16[4,112,384]{2,1,0:T(8,128)(2,1)S(1)}, bf16[4,112,384]{2,1,0:T(8,128)(2,1)S(1)}, u32[]{:S(2)}, u32[]{:S(2)}) collective-permute-start(bf16[4,112,384]{2,1,0:T(8,128)(2,1)S(1)} %pad_maximum_fusion.9), channel_id=1, source_target_pairs={{0,4},{1,5},{2,6},{3,7},{4,0},{5,1},{6,2},{7,3},{8,12},{9,13},{10,... | collective-permute-start | bytes 1032200 | tf_op jit(solution)/shard_map/ppermute | solution.py:728
  27.9 11.5 %collective-permute-start.12 = (bf16[2,192,384]{2,1,0:T(8,128)(2,1)S(1)}, bf16[2,192,384]{2,1,0:T(8,128)(2,1)S(1)}, u32[]{:S(2)}, u32[]{:S(2)}) collective-permute-start(bf16[2,192,384]{2,1,0:T(8,128)(2,1)S(1)} %pad_maximum_fusion.11), channel_id=1, source_target_pairs={{0,8},{1,9},{2,10},{3,11},{4,12},{5,13},{6,14},{7,15},{8,0},{9,1},... | collective-permute-start | bytes 884744 | tf_op jit(solution)/shard_map/ppermute | solution.py:728
  29.0 10.4 %collective-permute-start.15 = (bf16[1,48,1536]{2,1,0:T(8,128)(2,1)S(1)}, bf16[1,48,1536]{2,1,0:T(8,128)(2,1)S(1)}, u32[]{:S(2)}, u32[]{:S(2)}) collective-permute-start(bf16[1,48,1536]{2,1,0:T(8,128)(2,1)S(1)} %maximum_select_fusion.2), channel_id=1, source_target_pairs={{0,2},{1,3},{2,0},{3,1},{4,6},{5,7},{6,4},{7,5},{8,10},{9,11},{10,... | collective-permute-start | bytes 442376 | tf_op jit(solution)/shard_map/ppermute | solution.py:728
  30.6 10.7 %collective-permute-start.18 = (bf16[1,192,384]{2,1,0:T(8,128)(2,1)S(1)}, bf16[1,192,384]{2,1,0:T(8,128)(2,1)S(1)}, u32[]{:S(2)}, u32[]{:S(2)}) collective-permute-start(bf16[1,192,384]{2,1,0:T(8,128)(2,1)S(1)} %maximum_select_fusion.3), channel_id=1, source_target_pairs={{0,16},{1,17},{2,18},{3,19},{4,20},{5,21},{6,22},{7,23},{8,24},{9,... | collective-permute-start | bytes 442376 | tf_op jit(solution)/shard_map/ppermute | solution.py:728
  33.0 9.8 %collective-permute-start.9 = (bf16[8,96,384]{2,1,0:T(8,128)(2,1)S(1)}, bf16[8,96,384]{2,1,0:T(8,128)(2,1)S(1)}, u32[]{:S(2)}, u32[]{:S(2)}) collective-permute-start(bf16[8,96,384]{2,1,0:T(8,128)(2,1)S(1)} %pad_maximum_fusion.4.refs_9_), channel_id=1, source_target_pairs={{0,1},{1,0},{2,3},{3,2},{4,5},{5,4},{6,7},{7,6},{8,9},{9,8},{10,11... | collective-permute-start | bytes 1769480 | tf_op jit(solution)/shard_map/ppermute | solution.py:728
  37.1 20.8 %collective-permute-start.21 = (bf16[8,96,384]{2,1,0:T(8,128)(2,1)S(1)}, bf16[8,96,384]{2,1,0:T(8,128)(2,1)}, u32[]{:S(2)}, u32[]{:S(2)}) collective-permute-start(bf16[8,96,384]{2,1,0:T(8,128)(2,1)S(1)} %pad_maximum_fusion.4.refs_9_), channel_id=1, source_target_pairs={{0,8},{1,9},{2,10},{3,11},{4,12},{5,13},{6,14},{7,15},{8,0},{9,1},... | collective-permute-start | bytes 1769480 | tf_op jit(solution)/shard_map/ppermute | solution.py:728
  39.4 18.6 %collective-permute-start.5 = (bf16[8,112,384]{2,1,0:T(8,128)(2,1)S(1)}, bf16[8,112,384]{2,1,0:T(8,128)(2,1)}, u32[]{:S(2)}, u32[]{:S(2)}) collective-permute-start(bf16[8,112,384]{2,1,0:T(8,128)(2,1)S(1)} %pad_maximum_fusion.3.refs_5_), channel_id=1, source_target_pairs={{0,1},{1,0},{2,3},{3,2},{4,5},{5,4},{6,7},{7,6},{8,9},{9,8},{10,11... | collective-permute-start | bytes 2064392 | tf_op jit(solution)/shard_map/ppermute | solution.py:728
  39.5 18.5 %collective-permute-start.13 = (bf16[4,192,384]{2,1,0:T(8,128)(2,1)S(1)}, bf16[4,192,384]{2,1,0:T(8,128)(2,1)S(1)}, u32[]{:S(2)}, u32[]{:S(2)}) collective-permute-start(bf16[4,192,384]{2,1,0:T(8,128)(2,1)S(1)} %pad_maximum_fusion.5), channel_id=1, source_target_pairs={{0,4},{1,5},{2,6},{3,7},{4,0},{5,1},{6,2},{7,3},{8,12},{9,13},{10,... | collective-permute-start | bytes 1769480 | tf_op jit(solution)/shard_map/ppermute | solution.py:728
  41.3 23.8 %collective-permute-start.4 = (bf16[8,112,384]{2,1,0:T(8,128)(2,1)S(1)}, bf16[8,112,384]{2,1,0:T(8,128)(2,1)}, u32[]{:S(2)}, u32[]{:S(2)}) collective-permute-start(bf16[8,112,384]{2,1,0:T(8,128)(2,1)S(1)} %pad_maximum_fusion.3.refs_5_), channel_id=1, source_target_pairs={{0,2},{1,3},{2,0},{3,1},{4,6},{5,7},{6,4},{7,5},{8,10},{9,11},{10,... | collective-permute-start | bytes 2064392 | tf_op jit(solution)/shard_map/ppermute | solution.py:728
  42.8 16.9 %collective-permute-start.16 = (bf16[2,48,1536]{2,1,0:T(8,128)(2,1)S(1)}, bf16[2,48,1536]{2,1,0:T(8,128)(2,1)S(1)}, u32[]{:S(2)}, u32[]{:S(2)}) collective-permute-start(bf16[2,48,1536]{2,1,0:T(8,128)(2,1)S(1)} %pad_maximum_fusion.12), channel_id=1, source_target_pairs={{0,16},{1,17},{2,18},{3,19},{4,20},{5,21},{6,22},{7,23},{8,24},{9,... | collective-permute-start | bytes 884744 | tf_op jit(solution)/shard_map/ppermute | solution.py:728
  57.9 13.7 %collective-permute-start.22 = (bf16[8,96,384]{2,1,0:T(8,128)(2,1)}, bf16[8,96,384]{2,1,0:T(8,128)(2,1)}, u32[]{:S(2)}, u32[]{:S(2)}) collective-permute-start(bf16[8,96,384]{2,1,0:T(8,128)(2,1)} %collective-permute-done.21.refs_10_), channel_id=1, source_target_pairs={{0,1},{1,0},{2,3},{3,2},{4,5},{5,4},{6,7},{7,6},{8,9},{9,8},{10,11... | collective-permute-start | bytes 1769480 | tf_op jit(solution)/shard_map/ppermute | solution.py:728
  58.2 33.0 %collective-permute-start.25 = (bf16[8,192,384]{2,1,0:T(8,128)(2,1)S(1)}, bf16[8,192,384]{2,1,0:T(8,128)(2,1)}, u32[]{:S(2)}, u32[]{:S(2)}) collective-permute-start(bf16[8,192,384]{2,1,0:T(8,128)(2,1)S(1)} %pad_maximum_fusion.refs_8_), channel_id=1, source_target_pairs={{0,2},{1,3},{2,0},{3,1},{4,6},{5,7},{6,4},{7,5},{8,10},{9,11},{10,... | collective-permute-start | bytes 3538952 | tf_op jit(solution)/shard_map/ppermute | solution.py:728
  66.0 23.3 %collective-permute-start.23 = (bf16[4,48,1536]{2,1,0:T(8,128)(2,1)}, bf16[4,48,1536]{2,1,0:T(8,128)(2,1)}, u32[]{:S(2)}, u32[]{:S(2)}) collective-permute-start(bf16[4,48,1536]{2,1,0:T(8,128)(2,1)} %pad_maximum_fusion.6), channel_id=1, source_target_pairs={{0,8},{1,9},{2,10},{3,11},{4,12},{5,13},{6,14},{7,15},{8,0},{9,1},... | collective-permute-start | bytes 1769480 | tf_op jit(solution)/shard_map/ppermute | solution.py:728
  66.9 22.4 %collective-permute-start.24 = (bf16[4,192,384]{2,1,0:T(8,128)(2,1)}, bf16[4,192,384]{2,1,0:T(8,128)(2,1)}, u32[]{:S(2)}, u32[]{:S(2)}) collective-permute-start(bf16[4,192,384]{2,1,0:T(8,128)(2,1)} %pad_maximum_fusion.7), channel_id=1, source_target_pairs={{0,4},{1,5},{2,6},{3,7},{4,0},{5,1},{6,2},{7,3},{8,12},{9,13},{10,... | collective-permute-start | bytes 1769480 | tf_op jit(solution)/shard_map/ppermute | solution.py:728
  71.7 22.6 %collective-permute-start.26 = (bf16[8,192,384]{2,1,0:T(8,128)(2,1)S(1)}, bf16[8,192,384]{2,1,0:T(8,128)(2,1)}, u32[]{:S(2)}, u32[]{:S(2)}) collective-permute-start(bf16[8,192,384]{2,1,0:T(8,128)(2,1)S(1)} %pad_maximum_fusion.refs_8_), channel_id=1, source_target_pairs={{0,1},{1,0},{2,3},{3,2},{4,5},{5,4},{6,7},{7,6},{8,9},{9,8},{10,11... | collective-permute-start | bytes 3538952 | tf_op jit(solution)/shard_map/ppermute | solution.py:728
  90.6 28.5 %collective-permute-start.28 = (bf16[8,48,1536]{2,1,0:T(8,128)(2,1)S(1)}, bf16[8,48,1536]{2,1,0:T(8,128)(2,1)}, u32[]{:S(2)}, u32[]{:S(2)}) collective-permute-start(bf16[8,48,1536]{2,1,0:T(8,128)(2,1)S(1)} %pad_maximum_fusion.1.refs_0_), channel_id=1, source_target_pairs={{0,4},{1,5},{2,6},{3,7},{4,0},{5,1},{6,2},{7,3},{8,12},{9,13},{10,... | collective-permute-start | bytes 3538952 | tf_op jit(solution)/shard_map/ppermute | solution.py:728
  92.6 28.4 %collective-permute-start.31 = (bf16[8,192,384]{2,1,0:T(8,128)(2,1)S(1)}, bf16[8,192,384]{2,1,0:T(8,128)(2,1)}, u32[]{:S(2)}, u32[]{:S(2)}) collective-permute-start(bf16[8,192,384]{2,1,0:T(8,128)(2,1)S(1)} %pad_maximum_fusion.2), channel_id=1, source_target_pairs={{0,2},{1,3},{2,0},{3,1},{4,6},{5,7},{6,4},{7,5},{8,10},{9,11},{10,... | collective-permute-start | bytes 3538952 | tf_op jit(solution)/shard_map/ppermute | solution.py:728
  94.2 26.8 %collective-permute-start.29 = (bf16[8,48,1536]{2,1,0:T(8,128)(2,1)S(1)}, bf16[8,48,1536]{2,1,0:T(8,128)(2,1)}, u32[]{:S(2)}, u32[]{:S(2)}) collective-permute-start(bf16[8,48,1536]{2,1,0:T(8,128)(2,1)S(1)} %pad_maximum_fusion.1.refs_0_), channel_id=1, source_target_pairs={{0,1},{1,0},{2,3},{3,2},{4,5},{5,4},{6,7},{7,6},{8,9},{9,8},{10,11... | collective-permute-start | bytes 3538952 | tf_op jit(solution)/shard_map/ppermute | solution.py:728
  94.2 26.8 %collective-permute-start.32 = (bf16[8,192,384]{2,1,0:T(8,128)(2,1)S(1)}, bf16[8,192,384]{2,1,0:T(8,128)(2,1)S(1)}, u32[]{:S(2)}, u32[]{:S(2)}) collective-permute-start(bf16[8,192,384]{2,1,0:T(8,128)(2,1)S(1)} %pad_maximum_fusion.2), channel_id=1, source_target_pairs={{0,1},{1,0},{2,3},{3,2},{4,5},{5,4},{6,7},{7,6},{8,9},{9,8},{10,11... | collective-permute-start | bytes 3538952 | tf_op jit(solution)/shard_map/ppermute | solution.py:728
  148.9 9.7 %collective-permute-start.35 = (bf16[16,96,768]{2,1,0:T(8,128)(2,1)}, bf16[16,96,768]{2,1,0:T(8,128)(2,1)}, u32[]{:S(2)}, u32[]{:S(2)}) collective-permute-start(bf16[16,96,768]{2,1,0:T(8,128)(2,1)} %bitcast.72), channel_id=1, source_target_pairs={{0,1},{1,0},{2,3},{3,2},{4,5},{5,4},{6,7},{7,6},{8,9},{9,8},{10,11... | collective-permute-start | bytes 7077896 | tf_op jit(solution)/shard_map/ppermute | solution.py:728
  157.1 28.2 %collective-permute-start.36 = (bf16[8,24,3072]{2,1,0:T(8,128)(2,1)}, bf16[8,24,3072]{2,1,0:T(8,128)(2,1)S(1)}, u32[]{:S(2)}, u32[]{:S(2)}) collective-permute-start(bf16[8,24,3072]{2,1,0:T(8,128)(2,1)} %add_convert_fusion.2), channel_id=1, source_target_pairs={{0,4},{1,5},{2,6},{3,7},{4,0},{5,1},{6,2},{7,3},{8,12},{9,13},{10,... | collective-permute-start | bytes 3538952 | tf_op jit(solution)/shard_map/ppermute | solution.py:728
  160.2 27.8 %collective-permute-start.37 = (bf16[8,96,768]{2,1,0:T(8,128)(2,1)S(1)}, bf16[8,96,768]{2,1,0:T(8,128)(2,1)S(1)}, u32[]{:S(2)}, u32[]{:S(2)}) collective-permute-start(bf16[8,96,768]{2,1,0:T(8,128)(2,1)S(1)} %add_convert_fusion.1), channel_id=1, source_target_pairs={{0,2},{1,3},{2,0},{3,1},{4,6},{5,7},{6,4},{7,5},{8,10},{9,11},{10,... | collective-permute-start | bytes 3538952 | tf_op jit(solution)/shard_map/ppermute | solution.py:728
  191.3 25.4 %collective-permute-start.39 = (bf16[4,96,768]{2,1,0:T(8,128)(2,1)}, bf16[4,96,768]{2,1,0:T(8,128)(2,1)}, u32[]{:S(2)}, u32[]{:S(2)}) collective-permute-start(bf16[4,96,768]{2,1,0:T(8,128)(2,1)} %add_convert_fusion.6), channel_id=1, source_target_pairs={{0,4},{1,5},{2,6},{3,7},{4,0},{5,1},{6,2},{7,3},{8,12},{9,13},{10,... | collective-permute-start | bytes 1769480 | tf_op jit(solution)/shard_map/ppermute | solution.py:728
  194.3 22.3 %collective-permute-start.40 = (bf16[4,24,3072]{2,1,0:T(8,128)(2,1)}, bf16[4,24,3072]{2,1,0:T(8,128)(2,1)S(1)}, u32[]{:S(2)}, u32[]{:S(2)}) collective-permute-start(bf16[4,24,3072]{2,1,0:T(8,128)(2,1)} %add_convert_fusion.7), channel_id=1, source_target_pairs={{0,8},{1,9},{2,10},{3,11},{4,12},{5,13},{6,14},{7,15},{8,0},{9,1},... | collective-permute-start | bytes 1769480 | tf_op jit(solution)/shard_map/ppermute | solution.py:728
  198.1 27.8 %collective-permute-start.41 = (bf16[8,96,768]{2,1,0:T(8,128)(2,1)}, bf16[8,96,768]{2,1,0:T(8,128)(2,1)}, u32[]{:S(2)}, u32[]{:S(2)}) collective-permute-start(bf16[8,96,768]{2,1,0:T(8,128)(2,1)} %add_convert_fusion), channel_id=1, source_target_pairs={{0,2},{1,3},{2,0},{3,1},{4,6},{5,7},{6,4},{7,5},{8,10},{9,11},{10,... | collective-permute-start | bytes 3538952 | tf_op jit(solution)/shard_map/ppermute | solution.py:728
  217.5 10.7 %collective-permute-start.42 = (bf16[16,48,768]{2,1,0:T(8,128)(2,1)}, bf16[16,48,768]{2,1,0:T(8,128)(2,1)S(1)}, u32[]{:S(2)}, u32[]{:S(2)}) collective-permute-start(bf16[16,48,768]{2,1,0:T(8,128)(2,1)} %get-tuple-element.204), channel_id=1, source_target_pairs={{0,1},{1,0},{2,3},{3,2},{4,5},{5,4},{6,7},{7,6},{8,9},{9,8},{10,11... | collective-permute-start | bytes 3538952 | tf_op jit(solution)/shard_map/ppermute | solution.py:728
  217.5 11.7 %collective-permute-start.43 = (bf16[16,48,768]{2,1,0:T(8,128)(2,1)}, bf16[16,48,768]{2,1,0:T(8,128)(2,1)}, u32[]{:S(2)}, u32[]{:S(2)}) collective-permute-start(bf16[16,48,768]{2,1,0:T(8,128)(2,1)} %get-tuple-element.208), channel_id=1, source_target_pairs={{0,1},{1,0},{2,3},{3,2},{4,5},{5,4},{6,7},{7,6},{8,9},{9,8},{10,11... | collective-permute-start | bytes 3538952 | tf_op jit(solution)/shard_map/ppermute | solution.py:728
  220.2 23.5 %collective-permute-start.52 = (bf16[2,96,768]{2,1,0:T(8,128)(2,1)}, bf16[2,96,768]{2,1,0:T(8,128)(2,1)}, u32[]{:S(2)}, u32[]{:S(2)}) collective-permute-start(bf16[2,96,768]{2,1,0:T(8,128)(2,1)} %add_convert_fusion.12), channel_id=1, source_target_pairs={{0,8},{1,9},{2,10},{3,11},{4,12},{5,13},{6,14},{7,15},{8,0},{9,1},... | collective-permute-start | bytes 884744 | tf_op jit(solution)/shard_map/ppermute | solution.py:728
  223.0 22.6 %collective-permute-start.47 = (bf16[2,24,3072]{2,1,0:T(8,128)(2,1)}, bf16[2,24,3072]{2,1,0:T(8,128)(2,1)}, u32[]{:S(2)}, u32[]{:S(2)}) collective-permute-start(bf16[2,24,3072]{2,1,0:T(8,128)(2,1)} %add_convert_fusion.11), channel_id=1, source_target_pairs={{0,16},{1,17},{2,18},{3,19},{4,20},{5,21},{6,22},{7,23},{8,24},{9,... | collective-permute-start | bytes 884744 | tf_op jit(solution)/shard_map/ppermute | solution.py:728
  229.2 18.4 %collective-permute-start.44 = (bf16[8,48,768]{2,1,0:T(8,128)(2,1)}, bf16[8,48,768]{2,1,0:T(8,128)(2,1)}, u32[]{:S(2)}, u32[]{:S(2)}) collective-permute-start(bf16[8,48,768]{2,1,0:T(8,128)(2,1)} %add_convert_fusion.4), channel_id=1, source_target_pairs={{0,2},{1,3},{2,0},{3,1},{4,6},{5,7},{6,4},{7,5},{8,10},{9,11},{10,... | collective-permute-start | bytes 1769480 | tf_op jit(solution)/shard_map/ppermute | solution.py:728
  232.1 17.3 %collective-permute-start.49 = (bf16[8,48,768]{2,1,0:T(8,128)(2,1)}, bf16[8,48,768]{2,1,0:T(8,128)(2,1)}, u32[]{:S(2)}, u32[]{:S(2)}) collective-permute-start(bf16[8,48,768]{2,1,0:T(8,128)(2,1)} %add_convert_fusion.3), channel_id=1, source_target_pairs={{0,8},{1,9},{2,10},{3,11},{4,12},{5,13},{6,14},{7,15},{8,0},{9,1},... | collective-permute-start | bytes 1769480 | tf_op jit(solution)/shard_map/ppermute | solution.py:728
  232.9 21.9 %collective-permute-start.51 = (bf16[4,96,768]{2,1,0:T(8,128)(2,1)}, bf16[4,96,768]{2,1,0:T(8,128)(2,1)}, u32[]{:S(2)}, u32[]{:S(2)}) collective-permute-start(bf16[4,96,768]{2,1,0:T(8,128)(2,1)} %add_convert_fusion.5), channel_id=1, source_target_pairs={{0,4},{1,5},{2,6},{3,7},{4,0},{5,1},{6,2},{7,3},{8,12},{9,13},{10,... | collective-permute-start | bytes 1769480 | tf_op jit(solution)/shard_map/ppermute | solution.py:728
  251.3 9.7 %collective-permute-start.45 = (bf16[4,48,768]{2,1,0:T(8,128)(2,1)}, bf16[4,48,768]{2,1,0:T(8,128)(2,1)}, u32[]{:S(2)}, u32[]{:S(2)}) collective-permute-start(bf16[4,48,768]{2,1,0:T(8,128)(2,1)} %add_convert_fusion.10), channel_id=1, source_target_pairs={{0,8},{1,9},{2,10},{3,11},{4,12},{5,13},{6,14},{7,15},{8,0},{9,1},... | collective-permute-start | bytes 884744 | tf_op jit(solution)/shard_map/ppermute | solution.py:728
  253.2 12.0 %collective-permute-start.50 = (bf16[4,48,768]{2,1,0:T(8,128)(2,1)}, bf16[4,48,768]{2,1,0:T(8,128)(2,1)}, u32[]{:S(2)}, u32[]{:S(2)}) collective-permute-start(bf16[4,48,768]{2,1,0:T(8,128)(2,1)} %add_convert_fusion.9), channel_id=1, source_target_pairs={{0,4},{1,5},{2,6},{3,7},{4,0},{5,1},{6,2},{7,3},{8,12},{9,13},{10,... | collective-permute-start | bytes 884744 | tf_op jit(solution)/shard_map/ppermute | solution.py:728
  256.8 11.8 %collective-permute-start.53 = (bf16[2,96,768]{2,1,0:T(8,128)(2,1)}, bf16[2,96,768]{2,1,0:T(8,128)(2,1)}, u32[]{:S(2)}, u32[]{:S(2)}) collective-permute-start(bf16[2,96,768]{2,1,0:T(8,128)(2,1)} %add_convert_fusion.8), channel_id=1, source_target_pairs={{0,8},{1,9},{2,10},{3,11},{4,12},{5,13},{6,14},{7,15},{8,0},{9,1},... | collective-permute-start | bytes 884744 | tf_op jit(solution)/shard_map/ppermute | solution.py:728
  258.8 11.6 %collective-permute-start.48 = (bf16[1,24,3072]{2,1,0:T(8,128)(2,1)}, bf16[1,24,3072]{2,1,0:T(8,128)(2,1)}, u32[]{:S(2)}, u32[]{:S(2)}) collective-permute-start(bf16[1,24,3072]{2,1,0:T(8,128)(2,1)} %add_convert_fusion.16), channel_id=1, source_target_pairs={{0,2},{1,3},{2,0},{3,1},{4,6},{5,7},{6,4},{7,5},{8,10},{9,11},{10,... | collective-permute-start | bytes 442376 | tf_op jit(solution)/shard_map/ppermute | solution.py:728
  259.6 10.8 %collective-permute-start.54 = (bf16[1,96,768]{2,1,0:T(8,128)(2,1)}, bf16[1,96,768]{2,1,0:T(8,128)(2,1)}, u32[]{:S(2)}, u32[]{:S(2)}) collective-permute-start(bf16[1,96,768]{2,1,0:T(8,128)(2,1)} %add_convert_fusion.14), channel_id=1, source_target_pairs={{0,16},{1,17},{2,18},{3,19},{4,20},{5,21},{6,22},{7,23},{8,24},{9,... | collective-permute-start | bytes 442376 | tf_op jit(solution)/shard_map/ppermute | solution.py:728
  262.1 11.7 %collective-permute-start.46 = (bf16[2,48,768]{2,1,0:T(8,128)(2,1)S(1)}, bf16[2,48,768]{2,1,0:T(8,128)(2,1)S(1)}, u32[]{:S(2)}, u32[]{:S(2)}) collective-permute-start(bf16[2,48,768]{2,1,0:T(8,128)(2,1)S(1)} %add_convert_fusion.17), channel_id=1, source_target_pairs={{0,4},{1,5},{2,6},{3,7},{4,0},{5,1},{6,2},{7,3},{8,12},{9,13},{10,... | collective-permute-start | bytes 442376 | tf_op jit(solution)/shard_map/ppermute | solution.py:728
  267.0 10.8 %collective-permute-start.57 = (bf16[2,48,768]{2,1,0:T(8,128)(2,1)}, bf16[2,48,768]{2,1,0:T(8,128)(2,1)S(1)}, u32[]{:S(2)}, u32[]{:S(2)}) collective-permute-start(bf16[2,48,768]{2,1,0:T(8,128)(2,1)} %add_convert_fusion.15), channel_id=1, source_target_pairs={{0,2},{1,3},{2,0},{3,1},{4,6},{5,7},{6,4},{7,5},{8,10},{9,11},{10,... | collective-permute-start | bytes 442376 | tf_op jit(solution)/shard_map/ppermute | solution.py:728
  270.4 9.3 %collective-permute-start.56 = (bf16[1,96,768]{2,1,0:T(8,128)(2,1)}, bf16[1,96,768]{2,1,0:T(8,128)(2,1)S(1)}, u32[]{:S(2)}, u32[]{:S(2)}) collective-permute-start(bf16[1,96,768]{2,1,0:T(8,128)(2,1)} %add_convert_fusion.13), channel_id=1, source_target_pairs={{0,16},{1,17},{2,18},{3,19},{4,20},{5,21},{6,22},{7,23},{8,24},{9,... | collective-permute-start | bytes 442376 | tf_op jit(solution)/shard_map/ppermute | solution.py:728
  274.9 8.3 %collective-permute-start.55 = (bf16[1,48,768]{2,1,0:T(8,128)(2,1)S(1)}, bf16[1,48,768]{2,1,0:T(8,128)(2,1)S(1)}, u32[]{:S(2)}, u32[]{:S(2)}) collective-permute-start(bf16[1,48,768]{2,1,0:T(8,128)(2,1)S(1)} %add_convert_fusion.19), channel_id=1, source_target_pairs={{0,16},{1,17},{2,18},{3,19},{4,20},{5,21},{6,22},{7,23},{8,24},{9,... | collective-permute-start | bytes 221192 | tf_op jit(solution)/shard_map/ppermute | solution.py:728
  (61 other events, 533.0 us)

commit v8 on v7

--- a/solution.py
+++ b/solution.py
@@ -53,7 +53,7 @@
 LANES = 128
 GROUP = LANES // HEAD
 CUT = 256
-VMEM_BYTES = 60 * 1024 * 1024
+VMEM_BYTES = 62 * 1024 * 1024
 
 NT = (((1,), (1,)), ((), ()))
 TN = (((0,), (0,)), ((), ()))

time: 315 us -> 320 us (1.016)
  starting transfers between devices: 67.5 us -> 73.2 us
    ppermute x66, starting transfers between devices: 67.5 us -> 73.2 us  [swap(): return lax.ppermute(value, AXES, [(i, i ^ flip) for i in range(self.count)])]
where the time goes in v8:
time: 320 us; the launch traced here: 315 us
  Pallas kernels  127 us (40%)
  starting transfers between devices  73.2 us (23%)
  other arithmetic  53.3 us (17%)
  waiting for transfers between devices  51.5 us (16%)
  local copies, waits for them, and re-layouts  6.96 us (2%)
    pallas_call x4, Pallas kernels, by_pair(): pl.pallas_call(body, grid=(PAIRS,), in_specs=in_specs, out_specs=out_spec...  79.2 us
    ppermute x66, starting transfers between devices, swap(): return lax.ppermute(value, AXES, [(i, i ^ flip) for i in range(self.count)])  73.2 us
    ppermute x66, waiting for transfers between devices, swap(): return lax.ppermute(value, AXES, [(i, i ^ flip) for i in range(self.count)])  51.5 us
    convert_element_type x20, other arithmetic, send(): sent = sum(parts).astype(jnp.bfloat16)  37 us
    pallas_call x1, Pallas kernels, ffn(): pl.pallas_call(functools.partial(ffn_kernel, tiled, plans), grid_spec=plt...  24.5 us
    pallas_call x2, Pallas kernels, fused(): pl.pallas_call(kernel, in_specs=[space] * len(args), out_specs=[space] *...  14.3 us
    pallas_call x3, Pallas kernels, last_terms(): pl.pallas_call(functools.partial(kernel, [len(terms) for terms in asked])...  9.3 us
    concatenate x15, other arithmetic, take(): self.held = jnp.concatenate([self.held, *theirs], axis=0)  7.23 us
  transfers between devices with their start and end apart: 66, of which 22 were waited for; matrix products, arithmetic and copies ran while one was open for 17% of the time, Pallas kernels for 32%

profile of v8, /device:TPU:0, one launch (start us, length us, event | category | flops | bytes accessed | tf_op | source)
XLA Modules:
  0.0 314.9 jit_solution(3274041403747341331)
XLA Ops:
  5.1 3.7 %collective-permute-start.6 = (bf16[1,96,384]{2,1,0:T(8,128)(2,1)S(1)}, bf16[1,96,384]{2,1,0:T(8,128)(2,1)S(1)}, u32[]{:S(2)}, u32[]{:S(2)}) collective-permute-start(bf16[1,96,384]{2,1,0:T(8,128)(2,1)S(1)} %bitcast.58), channel_id=1, source_target_pairs={{0,16},{1,17},{2,18},{3,19},{4,20},{5,21},{6,22},{7,23},{8,24},{9,... | collective-permute-start | bytes 221192 | tf_op jit(solution)/shard_map/ppermute | solution.py:728
  9.6 3.8 %collective-permute-done.6 = bf16[1,96,384]{2,1,0:T(8,128)(2,1)S(1)} collective-permute-done((bf16[1,96,384]{2,1,0:T(8,128)(2,1)S(1)}, bf16[1,96,384]{2,1,0:T(8,128)(2,1)S(1)}, u32[]{:S(2)}, u32[]{:S(2)}) %collective-permute-start.6) | collective-permute-done | bytes 73760 | tf_op jit(solution)/shard_map/ppermute | solution.py:728
  13.5 3.7 %collective-permute-start.7 = (bf16[2,96,384]{2,1,0:T(8,128)(2,1)S(1)}, bf16[2,96,384]{2,1,0:T(8,128)(2,1)S(1)}, u32[]{:S(2)}, u32[]{:S(2)}) collective-permute-start(bf16[2,96,384]{2,1,0:T(8,128)(2,1)S(1)} %pad_maximum_fusion.15), channel_id=1, source_target_pairs={{0,2},{1,3},{2,0},{3,1},{4,6},{5,7},{6,4},{7,5},{8,10},{9,11},{10,... | collective-permute-start | bytes 442376 | tf_op jit(solution)/shard_map/ppermute | solution.py:728
  17.8 3.4 %collective-permute-start.11 = (bf16[1,192,384]{2,1,0:T(8,128)(2,1)S(1)}, bf16[1,192,384]{2,1,0:T(8,128)(2,1)S(1)}, u32[]{:S(2)}, u32[]{:S(2)}) collective-permute-start(bf16[1,192,384]{2,1,0:T(8,128)(2,1)S(1)} %bitcast.53), channel_id=1, source_target_pairs={{0,16},{1,17},{2,18},{3,19},{4,20},{5,21},{6,22},{7,23},{8,24},{9,... | collective-permute-start | bytes 442376 | tf_op jit(solution)/shard_map/ppermute | solution.py:728
  22.9 3.5 %collective-permute-done.2 = bf16[2,112,384]{2,1,0:T(8,128)(2,1)S(1)} collective-permute-done((bf16[2,112,384]{2,1,0:T(8,128)(2,1)S(1)}, bf16[2,112,384]{2,1,0:T(8,128)(2,1)S(1)}, u32[]{:S(2)}, u32[]{:S(2)}) %collective-permute-start.2) | collective-permute-done | bytes 172064 | tf_op jit(solution)/shard_map/ppermute | solution.py:728
  30.6 2.3 collective-permute-start.18
  33.1 4.1 %collective-permute-done.3 = bf16[4,112,384]{2,1,0:T(8,128)(2,1)S(1)} collective-permute-done((bf16[4,112,384]{2,1,0:T(8,128)(2,1)S(1)}, bf16[4,112,384]{2,1,0:T(8,128)(2,1)S(1)}, u32[]{:S(2)}, u32[]{:S(2)}) %collective-permute-start.3) | collective-permute-done | bytes 344096 | tf_op jit(solution)/shard_map/ppermute | solution.py:728
  37.5 1.8 collective-permute-done.12
  43.4 1.8 collective-permute-start.16
  45.3 12.4 %collective-permute-done.21.refs_10_ = bf16[8,96,384]{2,1,0:T(8,128)(2,1)} collective-permute-done((bf16[8,96,384]{2,1,0:T(8,128)(2,1)S(1)}, bf16[8,96,384]{2,1,0:T(8,128)(2,1)}, u32[]{:S(2)}, u32[]{:S(2)}) %collective-permute-start.21) | collective-permute-done | bytes 589856 | tf_op jit(solution)/shard_map/ppermute | solution.py:728
  57.9 1.8 collective-permute-start.25
  60.6 4.4 %collective-permute-done.19 = bf16[2,192,384]{2,1,0:T(8,128)(2,1)S(1)} collective-permute-done((bf16[2,192,384]{2,1,0:T(8,128)(2,1)S(1)}, bf16[2,192,384]{2,1,0:T(8,128)(2,1)S(1)}, u32[]{:S(2)}, u32[]{:S(2)}) %collective-permute-start.19) | collective-permute-done | bytes 294944 | tf_op jit(solution)/shard_map/ppermute | solution.py:728
  72.1 17.4 %self_part.1 = (bf16[512,768]{1,0:T(8,128)(2,1)}, bf16[512,768]{1,0:T(8,128)(2,1)}, bf16[512,768]{1,0:T(8,128)(2,1)}, bf16[512,768]{1,0:T(8,128)(2,1)}, bf16[12,...) custom-call(s32[2]{0:T(128)} %pad_add_fusion.refs_0_.spot_ref, ...), custom_call_target="tpu_custom_call" | custom-call | tf_op jit(solution)/shard_map/self_part/pallas_call | solution.py:460
  89.6 2.4 pad_maximum_fusion.1.refs_0_
  92.7 2.2 pad_maximum_fusion.2
  96.9 22.8 %cross_part.1 = (f32[512,768]{1,0:T(8,128)}, bf16[512,768]{1,0:T(8,128)(2,1)}, bf16[512,768]{1,0:T(8,128)(2,1)}, bf16[512,768]{1,0:T(8,128)(2,1)}, bf16[512,768]...) custom-call(s32[2]{0:T(128)} %pad_add_fusion.refs_0_.spot_ref, ...), custom_call_target="tpu_custom_call" | custom-call | tf_op jit(solution)/shard_map/cross_part/pallas_call | solution.py:460
  120.6 2.8 collective-permute-done.31
  123.8 2.8 collective-permute-done.33
  126.6 24.5 %ffn.1 = (bf16[512,768]{1,0:T(8,128)(2,1)}, f32[512,768]{1,0:T(8,128)}, bf16[384,3072]{1,0:T(8,128)(2,1)}, bf16[384,3072]{1,0:T(8,128)(2,1)}, bf16[4,4,96,768]{3...) custom-call(s32[2]{0:T(128)} %pad_add_fusion.refs_0_.spot_ref, bf16[512,768]{1,0:T(8,128)(2,1)} %get-tuple-element.159.third_ref, ...), custom_call_target="tpu_custom_call" | custom-call | tf_op jit(solution)/shard_map/ffn/pallas_call | solution.py:354
  151.6 4.9 %third_back.1 = (f32[512,768]{1,0:T(8,128)}, bf16[512,768]{1,0:T(8,128)(2,1)}, bf16[512,768]{1,0:T(8,128)(2,1)}, f32[1,768]{1,0:T(1,128)}) custom-call(f32[512,768]{1,0:T(8,128)} %get-tuple-element.170.gthird_ref, f32[512,768]{1,0:T(8,128)} %get-tuple-element.160.upper_ref, bf16[512,768]{1,0:T(8,128)(2,1)} %cot_ref.3, ...), custom_call_target="tpu_custom_call" | custom-call | tf_op jit(solution)/shard_map/third_back/pallas_call | solution.py:387
  156.6 3.2 %add_convert_fusion.2 = bf16[8,24,3072]{2,1,0:T(8,128)(2,1)} fusion(bf16[16,24,3072]{2,1,0:T(8,128)(2,1)} %collective-permute-done.34.refs_1_, s32[]{:T(128)S(6)} %select_n.242, bf16[16,24,3072]{2,1,0:T(8,128)(2,1)} %bitcast.43), kind=kLoop, calls=%fused_computation.2 | loop fusion | flops 2359296 | bytes 3538948 | tf_op jit(solution)/shard_map/convert_element_type | solution.py:803
  161.3 2.6 add_convert_fusion.1
  165.4 21.9 %cross_back.1 = (bf16[512,768]{1,0:T(8,128)(2,1)}, bf16[512,768]{1,0:T(8,128)(2,1)}, f32[512,768]{1,0:T(8,128)}, bf16[512,768]{1,0:T(8,128)(2,1)}, bf16[512,768]...) custom-call(s32[1]{0:T(128)} %bitcast.1.refs_0_, ...), custom_call_target="tpu_custom_call" | custom-call | tf_op jit(solution)/shard_map/cross_back/pallas_call | solution.py:460
  188.0 4.0 %collective-permute-done.37.refs_8_ = bf16[8,96,768]{2,1,0:T(8,128)(2,1)} collective-permute-done((bf16[8,96,768]{2,1,0:T(8,128)(2,1)}, bf16[8,96,768]{2,1,0:T(8,128)(2,1)}, u32[]{:S(2)}, u32[]{:S(2)}) %collective-permute-start.37) | collective-permute-done | bytes 1179680 | tf_op jit(solution)/shard_map/ppermute | solution.py:728
  192.0 2.5 add_convert_fusion.6
  195.0 2.5 add_convert_fusion.7
  202.0 17.1 %self_back.1 = (bf16[512,768]{1,0:T(8,128)(2,1)}, bf16[512,768]{1,0:T(8,128)(2,1)}, bf16[512,768]{1,0:T(8,128)(2,1)}, f32[6,8,256]{2,1,0:T(8,128)}, bf16[16,48,7...) custom-call(s32[1]{0:T(128)} %bitcast.1.refs_0_, ...), custom_call_target="tpu_custom_call" | custom-call | tf_op jit(solution)/shard_map/self_back/pallas_call | solution.py:460
  219.6 2.1 add_convert_fusion.12
  222.6 2.0 add_convert_fusion.11
  224.6 3.0 collective-permute-start.47
  228.5 2.4 add_convert_fusion.5
  236.7 9.4 %last_back.1 = (f32[512,768]{1,0:T(8,128)}, f32[512,768]{1,0:T(8,128)}, f32[8,768]{1,0:T(8,128)}) custom-call(bf16[512,768]{1,0:T(8,128)(2,1)} %get-tuple-element.210.gq_ref, bf16[512,768]{1,0:T(8,128)(2,1)} %get-tuple-element.211.gk_ref, bf16[512,768]{1,0:T(8,128)(2,1)} %get-tuple-element.212.gv_ref, bf16[512,768]{1,0:T(8,128)(2,1)} %get-tuple-element.213.gmk_ref, ...), custom_call_target="tpu_custom_call" | custom-call | tf_op jit(solution)/shard_map/last_back/pallas_call | solution.py:387
  246.1 2.0 add_convert_fusion.14
  248.1 2.0 add_convert_fusion.16
  257.0 2.1 collective-permute-start.53
  260.4 2.9 collective-permute-start.54
  265.1 4.1 %collective-permute-start.46 = (bf16[2,48,768]{2,1,0:T(8,128)(2,1)}, bf16[2,48,768]{2,1,0:T(8,128)(2,1)S(1)}, u32[]{:S(2)}, u32[]{:S(2)}) collective-permute-start(bf16[2,48,768]{2,1,0:T(8,128)(2,1)} %add_convert_fusion.17), channel_id=1, source_target_pairs={{0,4},{1,5},{2,6},{3,7},{4,0},{5,1},{6,2},{7,3},{8,12},{9,13},{10,... | collective-permute-start | bytes 442376 | tf_op jit(solution)/shard_map/ppermute | solution.py:728
  269.2 1.9 add_convert_fusion.15
  272.6 2.0 add_convert_fusion.13
  276.1 3.4 %ffn_last.1 = (f32[1,24,3072]{2,1,0:T(8,128)}, f32[1,24]{1,0:T(1,128)}, f32[1,96,768]{2,1,0:T(8,128)}, f32[1,96]{1,0:T(1,128)}, f32[8,768]{1,0:T(8,128)}) custom-call(s32[2]{0:T(128)} %pad_add_fusion.refs_0_.spot_ref, bf16[16,24,3072]{2,1,0:T(8,128)(2,1)} %bitcast.47, bf16[16,24,3072]{2,1,0:T(8,128)(2,1)} %collective-permute-done.34.refs_1_, ...), custom_call_target="tpu_custom_call" | custom-call | tf_op jit(solution)/shard_map/ffn_last/pallas_call | solution.py:691
  280.6 2.1 collective-permute-start.55
  285.2 2.9 cross_last.1
  290.5 3.0 self_last.1
  296.0 2.3 collective-permute-start.62
  303.0 2.4 collective-permute-start.65
  305.4 2.1 collective-permute-start.64
  307.5 1.8 pad_maximum_fusion.8
  309.8 2.1 collective-permute-done.63
  (277 shorter events, 75.0 us)
Async XLA Ops:
  5.1 8.4 %collective-permute-start.6 = (bf16[1,96,384]{2,1,0:T(8,128)(2,1)S(1)}, bf16[1,96,384]{2,1,0:T(8,128)(2,1)S(1)}, u32[]{:S(2)}, u32[]{:S(2)}) collective-permute-start(bf16[1,96,384]{2,1,0:T(8,128)(2,1)S(1)} %bitcast.58), channel_id=1, source_target_pairs={{0,16},{1,17},{2,18},{3,19},{4,20},{5,21},{6,22},{7,23},{8,24},{9,... | collective-permute-start | bytes 221192 | tf_op jit(solution)/shard_map/ppermute | solution.py:728
  8.8 8.4 %collective-permute-start.1 = (bf16[1,112,384]{2,1,0:T(8,128)(2,1)S(1)}, bf16[1,112,384]{2,1,0:T(8,128)(2,1)S(1)}, u32[]{:S(2)}, u32[]{:S(2)}) collective-permute-start(bf16[1,112,384]{2,1,0:T(8,128)(2,1)S(1)} %maximum_bitcast_fusion), channel_id=1, source_target_pairs={{0,16},{1,17},{2,18},{3,19},{4,20},{5,21},{6,22},{7,23},{8,24},{9,... | collective-permute-start | bytes 258056 | tf_op jit(solution)/shard_map/ppermute | solution.py:728
  8.9 8.9 %collective-permute-start.10 = (bf16[4,24,384]{2,1,0:T(8,128)(2,1)S(1)}, bf16[4,24,384]{2,1,0:T(8,128)(2,1)S(1)}, u32[]{:S(2)}, u32[]{:S(2)}) collective-permute-start(bf16[4,24,384]{2,1,0:T(8,128)(2,1)S(1)} %get-tuple-element.132), channel_id=1, source_target_pairs={{0,1},{1,0},{2,3},{3,2},{4,5},{5,4},{6,7},{7,6},{8,9},{9,8},{10,11... | collective-permute-start | bytes 221192 | tf_op jit(solution)/shard_map/ppermute | solution.py:728
  9.1 8.0 %collective-permute-start.14 = (bf16[24,1536]{1,0:T(8,128)(2,1)S(1)}, bf16[24,1536]{1,0:T(8,128)(2,1)S(1)}, u32[]{:S(2)}, u32[]{:S(2)}) collective-permute-start(bf16[24,1536]{1,0:T(8,128)(2,1)S(1)} %get-tuple-element.140), channel_id=1, source_target_pairs={{0,1},{1,0},{2,3},{3,2},{4,5},{5,4},{6,7},{7,6},{8,9},{9,8},{10,11... | collective-permute-start | bytes 221192 | tf_op jit(solution)/shard_map/ppermute | solution.py:728
  9.4 19.6 %collective-permute-start.17 = (bf16[96,384]{1,0:T(8,128)(2,1)S(1)}, bf16[96,384]{1,0:T(8,128)(2,1)S(1)}, u32[]{:S(2)}, u32[]{:S(2)}) collective-permute-start(bf16[96,384]{1,0:T(8,128)(2,1)S(1)} %get-tuple-element.146), channel_id=1, source_target_pairs={{0,1},{1,0},{2,3},{3,2},{4,5},{5,4},{6,7},{7,6},{8,9},{9,8},{10,11... | collective-permute-start | bytes 221192 | tf_op jit(solution)/shard_map/ppermute | solution.py:728
  17.2 9.1 %collective-permute-start.2 = (bf16[2,112,384]{2,1,0:T(8,128)(2,1)S(1)}, bf16[2,112,384]{2,1,0:T(8,128)(2,1)S(1)}, u32[]{:S(2)}, u32[]{:S(2)}) collective-permute-start(bf16[2,112,384]{2,1,0:T(8,128)(2,1)S(1)} %pad_maximum_fusion.14), channel_id=1, source_target_pairs={{0,8},{1,9},{2,10},{3,11},{4,12},{5,13},{6,14},{7,15},{8,0},{9,1},... | collective-permute-start | bytes 516104 | tf_op jit(solution)/shard_map/ppermute | solution.py:728
  17.8 10.0 %collective-permute-start.11 = (bf16[1,192,384]{2,1,0:T(8,128)(2,1)S(1)}, bf16[1,192,384]{2,1,0:T(8,128)(2,1)S(1)}, u32[]{:S(2)}, u32[]{:S(2)}) collective-permute-start(bf16[1,192,384]{2,1,0:T(8,128)(2,1)S(1)} %bitcast.53), channel_id=1, source_target_pairs={{0,16},{1,17},{2,18},{3,19},{4,20},{5,21},{6,22},{7,23},{8,24},{9,... | collective-permute-start | bytes 442376 | tf_op jit(solution)/shard_map/ppermute | solution.py:728
  21.3 11.6 %collective-permute-start.8 = (bf16[4,96,384]{2,1,0:T(8,128)(2,1)S(1)}, bf16[4,96,384]{2,1,0:T(8,128)(2,1)S(1)}, u32[]{:S(2)}, u32[]{:S(2)}) collective-permute-start(bf16[4,96,384]{2,1,0:T(8,128)(2,1)S(1)} %pad_maximum_fusion.10), channel_id=1, source_target_pairs={{0,4},{1,5},{2,6},{3,7},{4,0},{5,1},{6,2},{7,3},{8,12},{9,13},{10,... | collective-permute-start | bytes 884744 | tf_op jit(solution)/shard_map/ppermute | solution.py:728
  26.4 10.7 %collective-permute-start.3 = (bf16[4,112,384]{2,1,0:T(8,128)(2,1)S(1)}, bf16[4,112,384]{2,1,0:T(8,128)(2,1)S(1)}, u32[]{:S(2)}, u32[]{:S(2)}) collective-permute-start(bf16[4,112,384]{2,1,0:T(8,128)(2,1)S(1)} %pad_maximum_fusion.9), channel_id=1, source_target_pairs={{0,4},{1,5},{2,6},{3,7},{4,0},{5,1},{6,2},{7,3},{8,12},{9,13},{10,... | collective-permute-start | bytes 1032200 | tf_op jit(solution)/shard_map/ppermute | solution.py:728
  27.9 11.5 %collective-permute-start.12 = (bf16[2,192,384]{2,1,0:T(8,128)(2,1)S(1)}, bf16[2,192,384]{2,1,0:T(8,128)(2,1)S(1)}, u32[]{:S(2)}, u32[]{:S(2)}) collective-permute-start(bf16[2,192,384]{2,1,0:T(8,128)(2,1)S(1)} %pad_maximum_fusion.11), channel_id=1, source_target_pairs={{0,8},{1,9},{2,10},{3,11},{4,12},{5,13},{6,14},{7,15},{8,0},{9,1},... | collective-permute-start | bytes 884744 | tf_op jit(solution)/shard_map/ppermute | solution.py:728
  29.0 10.4 %collective-permute-start.15 = (bf16[1,48,1536]{2,1,0:T(8,128)(2,1)S(1)}, bf16[1,48,1536]{2,1,0:T(8,128)(2,1)S(1)}, u32[]{:S(2)}, u32[]{:S(2)}) collective-permute-start(bf16[1,48,1536]{2,1,0:T(8,128)(2,1)S(1)} %maximum_select_fusion.2), channel_id=1, source_target_pairs={{0,2},{1,3},{2,0},{3,1},{4,6},{5,7},{6,4},{7,5},{8,10},{9,11},{10,... | collective-permute-start | bytes 442376 | tf_op jit(solution)/shard_map/ppermute | solution.py:728
  30.6 11.3 %collective-permute-start.18 = (bf16[1,192,384]{2,1,0:T(8,128)(2,1)S(1)}, bf16[1,192,384]{2,1,0:T(8,128)(2,1)S(1)}, u32[]{:S(2)}, u32[]{:S(2)}) collective-permute-start(bf16[1,192,384]{2,1,0:T(8,128)(2,1)S(1)} %maximum_select_fusion.3), channel_id=1, source_target_pairs={{0,16},{1,17},{2,18},{3,19},{4,20},{5,21},{6,22},{7,23},{8,24},{9,... | collective-permute-start | bytes 442376 | tf_op jit(solution)/shard_map/ppermute | solution.py:728
  33.0 10.4 %collective-permute-start.9 = (bf16[8,96,384]{2,1,0:T(8,128)(2,1)S(1)}, bf16[8,96,384]{2,1,0:T(8,128)(2,1)S(1)}, u32[]{:S(2)}, u32[]{:S(2)}) collective-permute-start(bf16[8,96,384]{2,1,0:T(8,128)(2,1)S(1)} %pad_maximum_fusion.4.refs_9_), channel_id=1, source_target_pairs={{0,1},{1,0},{2,3},{3,2},{4,5},{5,4},{6,7},{7,6},{8,9},{9,8},{10,11... | collective-permute-start | bytes 1769480 | tf_op jit(solution)/shard_map/ppermute | solution.py:728
  37.1 20.5 %collective-permute-start.21 = (bf16[8,96,384]{2,1,0:T(8,128)(2,1)S(1)}, bf16[8,96,384]{2,1,0:T(8,128)(2,1)}, u32[]{:S(2)}, u32[]{:S(2)}) collective-permute-start(bf16[8,96,384]{2,1,0:T(8,128)(2,1)S(1)} %pad_maximum_fusion.4.refs_9_), channel_id=1, source_target_pairs={{0,8},{1,9},{2,10},{3,11},{4,12},{5,13},{6,14},{7,15},{8,0},{9,1},... | collective-permute-start | bytes 1769480 | tf_op jit(solution)/shard_map/ppermute | solution.py:728
  39.4 18.3 %collective-permute-start.5 = (bf16[8,112,384]{2,1,0:T(8,128)(2,1)S(1)}, bf16[8,112,384]{2,1,0:T(8,128)(2,1)}, u32[]{:S(2)}, u32[]{:S(2)}) collective-permute-start(bf16[8,112,384]{2,1,0:T(8,128)(2,1)S(1)} %pad_maximum_fusion.3.refs_5_), channel_id=1, source_target_pairs={{0,1},{1,0},{2,3},{3,2},{4,5},{5,4},{6,7},{7,6},{8,9},{9,8},{10,11... | collective-permute-start | bytes 2064392 | tf_op jit(solution)/shard_map/ppermute | solution.py:728
  39.5 18.2 %collective-permute-start.13 = (bf16[4,192,384]{2,1,0:T(8,128)(2,1)S(1)}, bf16[4,192,384]{2,1,0:T(8,128)(2,1)S(1)}, u32[]{:S(2)}, u32[]{:S(2)}) collective-permute-start(bf16[4,192,384]{2,1,0:T(8,128)(2,1)S(1)} %pad_maximum_fusion.5), channel_id=1, source_target_pairs={{0,4},{1,5},{2,6},{3,7},{4,0},{5,1},{6,2},{7,3},{8,12},{9,13},{10,... | collective-permute-start | bytes 1769480 | tf_op jit(solution)/shard_map/ppermute | solution.py:728
  41.9 23.2 %collective-permute-start.4 = (bf16[8,112,384]{2,1,0:T(8,128)(2,1)S(1)}, bf16[8,112,384]{2,1,0:T(8,128)(2,1)S(1)}, u32[]{:S(2)}, u32[]{:S(2)}) collective-permute-start(bf16[8,112,384]{2,1,0:T(8,128)(2,1)S(1)} %pad_maximum_fusion.3.refs_5_), channel_id=1, source_target_pairs={{0,2},{1,3},{2,0},{3,1},{4,6},{5,7},{6,4},{7,5},{8,10},{9,11},{10,... | collective-permute-start | bytes 2064392 | tf_op jit(solution)/shard_map/ppermute | solution.py:728
  43.4 16.3 %collective-permute-start.16 = (bf16[2,48,1536]{2,1,0:T(8,128)(2,1)S(1)}, bf16[2,48,1536]{2,1,0:T(8,128)(2,1)S(1)}, u32[]{:S(2)}, u32[]{:S(2)}) collective-permute-start(bf16[2,48,1536]{2,1,0:T(8,128)(2,1)S(1)} %pad_maximum_fusion.12), channel_id=1, source_target_pairs={{0,16},{1,17},{2,18},{3,19},{4,20},{5,21},{6,22},{7,23},{8,24},{9,... | collective-permute-start | bytes 884744 | tf_op jit(solution)/shard_map/ppermute | solution.py:728
  57.6 13.5 %collective-permute-start.22 = (bf16[8,96,384]{2,1,0:T(8,128)(2,1)}, bf16[8,96,384]{2,1,0:T(8,128)(2,1)}, u32[]{:S(2)}, u32[]{:S(2)}) collective-permute-start(bf16[8,96,384]{2,1,0:T(8,128)(2,1)} %collective-permute-done.21.refs_10_), channel_id=1, source_target_pairs={{0,1},{1,0},{2,3},{3,2},{4,5},{5,4},{6,7},{7,6},{8,9},{9,8},{10,11... | collective-permute-start | bytes 1769480 | tf_op jit(solution)/shard_map/ppermute | solution.py:728
  57.9 34.6 %collective-permute-start.25 = (bf16[8,192,384]{2,1,0:T(8,128)(2,1)S(1)}, bf16[8,192,384]{2,1,0:T(8,128)(2,1)}, u32[]{:S(2)}, u32[]{:S(2)}) collective-permute-start(bf16[8,192,384]{2,1,0:T(8,128)(2,1)S(1)} %pad_maximum_fusion.refs_8_), channel_id=1, source_target_pairs={{0,2},{1,3},{2,0},{3,1},{4,6},{5,7},{6,4},{7,5},{8,10},{9,11},{10,... | collective-permute-start | bytes 3538952 | tf_op jit(solution)/shard_map/ppermute | solution.py:728
  66.2 23.3 %collective-permute-start.23 = (bf16[4,48,1536]{2,1,0:T(8,128)(2,1)}, bf16[4,48,1536]{2,1,0:T(8,128)(2,1)}, u32[]{:S(2)}, u32[]{:S(2)}) collective-permute-start(bf16[4,48,1536]{2,1,0:T(8,128)(2,1)} %pad_maximum_fusion.6), channel_id=1, source_target_pairs={{0,8},{1,9},{2,10},{3,11},{4,12},{5,13},{6,14},{7,15},{8,0},{9,1},... | collective-permute-start | bytes 1769480 | tf_op jit(solution)/shard_map/ppermute | solution.py:728
  67.1 22.5 %collective-permute-start.24 = (bf16[4,192,384]{2,1,0:T(8,128)(2,1)}, bf16[4,192,384]{2,1,0:T(8,128)(2,1)}, u32[]{:S(2)}, u32[]{:S(2)}) collective-permute-start(bf16[4,192,384]{2,1,0:T(8,128)(2,1)} %pad_maximum_fusion.7), channel_id=1, source_target_pairs={{0,4},{1,5},{2,6},{3,7},{4,0},{5,1},{6,2},{7,3},{8,12},{9,13},{10,... | collective-permute-start | bytes 1769480 | tf_op jit(solution)/shard_map/ppermute | solution.py:728
  71.2 25.3 %collective-permute-start.26 = (bf16[8,192,384]{2,1,0:T(8,128)(2,1)S(1)}, bf16[8,192,384]{2,1,0:T(8,128)(2,1)}, u32[]{:S(2)}, u32[]{:S(2)}) collective-permute-start(bf16[8,192,384]{2,1,0:T(8,128)(2,1)S(1)} %pad_maximum_fusion.refs_8_), channel_id=1, source_target_pairs={{0,1},{1,0},{2,3},{3,2},{4,5},{5,4},{6,7},{7,6},{8,9},{9,8},{10,11... | collective-permute-start | bytes 3538952 | tf_op jit(solution)/shard_map/ppermute | solution.py:728
  91.9 28.7 %collective-permute-start.28 = (bf16[8,48,1536]{2,1,0:T(8,128)(2,1)}, bf16[8,48,1536]{2,1,0:T(8,128)(2,1)}, u32[]{:S(2)}, u32[]{:S(2)}) collective-permute-start(bf16[8,48,1536]{2,1,0:T(8,128)(2,1)} %pad_maximum_fusion.1.refs_0_), channel_id=1, source_target_pairs={{0,4},{1,5},{2,6},{3,7},{4,0},{5,1},{6,2},{7,3},{8,12},{9,13},{10,... | collective-permute-start | bytes 3538952 | tf_op jit(solution)/shard_map/ppermute | solution.py:728
  94.9 28.5 %collective-permute-start.31 = (bf16[8,192,384]{2,1,0:T(8,128)(2,1)}, bf16[8,192,384]{2,1,0:T(8,128)(2,1)}, u32[]{:S(2)}, u32[]{:S(2)}) collective-permute-start(bf16[8,192,384]{2,1,0:T(8,128)(2,1)} %pad_maximum_fusion.2), channel_id=1, source_target_pairs={{0,2},{1,3},{2,0},{3,1},{4,6},{5,7},{6,4},{7,5},{8,10},{9,11},{10,... | collective-permute-start | bytes 3538952 | tf_op jit(solution)/shard_map/ppermute | solution.py:728
  96.4 27.0 %collective-permute-start.29 = (bf16[8,48,1536]{2,1,0:T(8,128)(2,1)}, bf16[8,48,1536]{2,1,0:T(8,128)(2,1)}, u32[]{:S(2)}, u32[]{:S(2)}) collective-permute-start(bf16[8,48,1536]{2,1,0:T(8,128)(2,1)} %pad_maximum_fusion.1.refs_0_), channel_id=1, source_target_pairs={{0,1},{1,0},{2,3},{3,2},{4,5},{5,4},{6,7},{7,6},{8,9},{9,8},{10,11... | collective-permute-start | bytes 3538952 | tf_op jit(solution)/shard_map/ppermute | solution.py:728
  96.4 27.0 %collective-permute-start.32 = (bf16[8,192,384]{2,1,0:T(8,128)(2,1)}, bf16[8,192,384]{2,1,0:T(8,128)(2,1)S(1)}, u32[]{:S(2)}, u32[]{:S(2)}) collective-permute-start(bf16[8,192,384]{2,1,0:T(8,128)(2,1)} %pad_maximum_fusion.2), channel_id=1, source_target_pairs={{0,1},{1,0},{2,3},{3,2},{4,5},{5,4},{6,7},{7,6},{8,9},{9,8},{10,11... | collective-permute-start | bytes 3538952 | tf_op jit(solution)/shard_map/ppermute | solution.py:728
  151.3 10.0 %collective-permute-start.35 = (bf16[16,96,768]{2,1,0:T(8,128)(2,1)}, bf16[16,96,768]{2,1,0:T(8,128)(2,1)}, u32[]{:S(2)}, u32[]{:S(2)}) collective-permute-start(bf16[16,96,768]{2,1,0:T(8,128)(2,1)} %bitcast.71), channel_id=1, source_target_pairs={{0,1},{1,0},{2,3},{3,2},{4,5},{5,4},{6,7},{7,6},{8,9},{9,8},{10,11... | collective-permute-start | bytes 7077896 | tf_op jit(solution)/shard_map/ppermute | solution.py:728
  159.8 28.2 %collective-permute-start.36 = (bf16[8,24,3072]{2,1,0:T(8,128)(2,1)}, bf16[8,24,3072]{2,1,0:T(8,128)(2,1)S(1)}, u32[]{:S(2)}, u32[]{:S(2)}) collective-permute-start(bf16[8,24,3072]{2,1,0:T(8,128)(2,1)} %add_convert_fusion.2), channel_id=1, source_target_pairs={{0,4},{1,5},{2,6},{3,7},{4,0},{5,1},{6,2},{7,3},{8,12},{9,13},{10,... | collective-permute-start | bytes 3538952 | tf_op jit(solution)/shard_map/ppermute | solution.py:728
  163.9 28.1 %collective-permute-start.37 = (bf16[8,96,768]{2,1,0:T(8,128)(2,1)}, bf16[8,96,768]{2,1,0:T(8,128)(2,1)}, u32[]{:S(2)}, u32[]{:S(2)}) collective-permute-start(bf16[8,96,768]{2,1,0:T(8,128)(2,1)} %add_convert_fusion.1), channel_id=1, source_target_pairs={{0,2},{1,3},{2,0},{3,1},{4,6},{5,7},{6,4},{7,5},{8,10},{9,11},{10,... | collective-permute-start | bytes 3538952 | tf_op jit(solution)/shard_map/ppermute | solution.py:728
  194.5 24.6 %collective-permute-start.39 = (bf16[4,96,768]{2,1,0:T(8,128)(2,1)}, bf16[4,96,768]{2,1,0:T(8,128)(2,1)}, u32[]{:S(2)}, u32[]{:S(2)}) collective-permute-start(bf16[4,96,768]{2,1,0:T(8,128)(2,1)} %add_convert_fusion.6), channel_id=1, source_target_pairs={{0,4},{1,5},{2,6},{3,7},{4,0},{5,1},{6,2},{7,3},{8,12},{9,13},{10,... | collective-permute-start | bytes 1769480 | tf_op jit(solution)/shard_map/ppermute | solution.py:728
  197.5 21.5 %collective-permute-start.40 = (bf16[4,24,3072]{2,1,0:T(8,128)(2,1)}, bf16[4,24,3072]{2,1,0:T(8,128)(2,1)S(1)}, u32[]{:S(2)}, u32[]{:S(2)}) collective-permute-start(bf16[4,24,3072]{2,1,0:T(8,128)(2,1)} %add_convert_fusion.7), channel_id=1, source_target_pairs={{0,8},{1,9},{2,10},{3,11},{4,12},{5,13},{6,14},{7,15},{8,0},{9,1},... | collective-permute-start | bytes 1769480 | tf_op jit(solution)/shard_map/ppermute | solution.py:728
  200.5 28.1 %collective-permute-start.41 = (bf16[8,96,768]{2,1,0:T(8,128)(2,1)}, bf16[8,96,768]{2,1,0:T(8,128)(2,1)}, u32[]{:S(2)}, u32[]{:S(2)}) collective-permute-start(bf16[8,96,768]{2,1,0:T(8,128)(2,1)} %add_convert_fusion), channel_id=1, source_target_pairs={{0,2},{1,3},{2,0},{3,1},{4,6},{5,7},{6,4},{7,5},{8,10},{9,11},{10,... | collective-permute-start | bytes 3538952 | tf_op jit(solution)/shard_map/ppermute | solution.py:728
  219.1 11.9 %collective-permute-start.42 = (bf16[16,48,768]{2,1,0:T(8,128)(2,1)}, bf16[16,48,768]{2,1,0:T(8,128)(2,1)S(1)}, u32[]{:S(2)}, u32[]{:S(2)}) collective-permute-start(bf16[16,48,768]{2,1,0:T(8,128)(2,1)} %get-tuple-element.204), channel_id=1, source_target_pairs={{0,1},{1,0},{2,3},{3,2},{4,5},{5,4},{6,7},{7,6},{8,9},{9,8},{10,11... | collective-permute-start | bytes 3538952 | tf_op jit(solution)/shard_map/ppermute | solution.py:728
  219.1 12.9 %collective-permute-start.43 = (bf16[16,48,768]{2,1,0:T(8,128)(2,1)}, bf16[16,48,768]{2,1,0:T(8,128)(2,1)S(1)}, u32[]{:S(2)}, u32[]{:S(2)}) collective-permute-start(bf16[16,48,768]{2,1,0:T(8,128)(2,1)} %get-tuple-element.208), channel_id=1, source_target_pairs={{0,1},{1,0},{2,3},{3,2},{4,5},{5,4},{6,7},{7,6},{8,9},{9,8},{10,11... | collective-permute-start | bytes 3538952 | tf_op jit(solution)/shard_map/ppermute | solution.py:728
  221.7 24.4 %collective-permute-start.52 = (bf16[2,96,768]{2,1,0:T(8,128)(2,1)}, bf16[2,96,768]{2,1,0:T(8,128)(2,1)}, u32[]{:S(2)}, u32[]{:S(2)}) collective-permute-start(bf16[2,96,768]{2,1,0:T(8,128)(2,1)} %add_convert_fusion.12), channel_id=1, source_target_pairs={{0,8},{1,9},{2,10},{3,11},{4,12},{5,13},{6,14},{7,15},{8,0},{9,1},... | collective-permute-start | bytes 884744 | tf_op jit(solution)/shard_map/ppermute | solution.py:728
  224.6 23.5 %collective-permute-start.47 = (bf16[2,24,3072]{2,1,0:T(8,128)(2,1)}, bf16[2,24,3072]{2,1,0:T(8,128)(2,1)}, u32[]{:S(2)}, u32[]{:S(2)}) collective-permute-start(bf16[2,24,3072]{2,1,0:T(8,128)(2,1)} %add_convert_fusion.11), channel_id=1, source_target_pairs={{0,16},{1,17},{2,18},{3,19},{4,20},{5,21},{6,22},{7,23},{8,24},{9,... | collective-permute-start | bytes 884744 | tf_op jit(solution)/shard_map/ppermute | solution.py:728
  232.0 18.0 %collective-permute-start.44 = (bf16[8,48,768]{2,1,0:T(8,128)(2,1)}, bf16[8,48,768]{2,1,0:T(8,128)(2,1)S(1)}, u32[]{:S(2)}, u32[]{:S(2)}) collective-permute-start(bf16[8,48,768]{2,1,0:T(8,128)(2,1)} %add_convert_fusion.4), channel_id=1, source_target_pairs={{0,2},{1,3},{2,0},{3,1},{4,6},{5,7},{6,4},{7,5},{8,10},{9,11},{10,... | collective-permute-start | bytes 1769480 | tf_op jit(solution)/shard_map/ppermute | solution.py:728
  234.5 16.5 %collective-permute-start.49 = (bf16[8,48,768]{2,1,0:T(8,128)(2,1)}, bf16[8,48,768]{2,1,0:T(8,128)(2,1)}, u32[]{:S(2)}, u32[]{:S(2)}) collective-permute-start(bf16[8,48,768]{2,1,0:T(8,128)(2,1)} %add_convert_fusion.3), channel_id=1, source_target_pairs={{0,8},{1,9},{2,10},{3,11},{4,12},{5,13},{6,14},{7,15},{8,0},{9,1},... | collective-permute-start | bytes 1769480 | tf_op jit(solution)/shard_map/ppermute | solution.py:728
  235.3 20.3 %collective-permute-start.51 = (bf16[4,96,768]{2,1,0:T(8,128)(2,1)}, bf16[4,96,768]{2,1,0:T(8,128)(2,1)}, u32[]{:S(2)}, u32[]{:S(2)}) collective-permute-start(bf16[4,96,768]{2,1,0:T(8,128)(2,1)} %add_convert_fusion.5), channel_id=1, source_target_pairs={{0,4},{1,5},{2,6},{3,7},{4,0},{5,1},{6,2},{7,3},{8,12},{9,13},{10,... | collective-permute-start | bytes 1769480 | tf_op jit(solution)/shard_map/ppermute | solution.py:728
  252.8 10.5 %collective-permute-start.45 = (bf16[4,48,768]{2,1,0:T(8,128)(2,1)}, bf16[4,48,768]{2,1,0:T(8,128)(2,1)S(1)}, u32[]{:S(2)}, u32[]{:S(2)}) collective-permute-start(bf16[4,48,768]{2,1,0:T(8,128)(2,1)} %add_convert_fusion.10), channel_id=1, source_target_pairs={{0,8},{1,9},{2,10},{3,11},{4,12},{5,13},{6,14},{7,15},{8,0},{9,1},... | collective-permute-start | bytes 884744 | tf_op jit(solution)/shard_map/ppermute | solution.py:728
  254.5 14.7 %collective-permute-start.50 = (bf16[4,48,768]{2,1,0:T(8,128)(2,1)S(1)}, bf16[4,48,768]{2,1,0:T(8,128)(2,1)S(1)}, u32[]{:S(2)}, u32[]{:S(2)}) collective-permute-start(bf16[4,48,768]{2,1,0:T(8,128)(2,1)S(1)} %add_convert_fusion.9), channel_id=1, source_target_pairs={{0,4},{1,5},{2,6},{3,7},{4,0},{5,1},{6,2},{7,3},{8,12},{9,13},{10,... | collective-permute-start | bytes 884744 | tf_op jit(solution)/shard_map/ppermute | solution.py:728
  257.0 15.6 %collective-permute-start.53 = (bf16[2,96,768]{2,1,0:T(8,128)(2,1)S(1)}, bf16[2,96,768]{2,1,0:T(8,128)(2,1)S(1)}, u32[]{:S(2)}, u32[]{:S(2)}) collective-permute-start(bf16[2,96,768]{2,1,0:T(8,128)(2,1)S(1)} %add_convert_fusion.8), channel_id=1, source_target_pairs={{0,8},{1,9},{2,10},{3,11},{4,12},{5,13},{6,14},{7,15},{8,0},{9,1},... | collective-permute-start | bytes 884744 | tf_op jit(solution)/shard_map/ppermute | solution.py:728
  259.1 16.4 %collective-permute-start.48 = (bf16[1,24,3072]{2,1,0:T(8,128)(2,1)}, bf16[1,24,3072]{2,1,0:T(8,128)(2,1)S(1)}, u32[]{:S(2)}, u32[]{:S(2)}) collective-permute-start(bf16[1,24,3072]{2,1,0:T(8,128)(2,1)} %add_convert_fusion.16), channel_id=1, source_target_pairs={{0,2},{1,3},{2,0},{3,1},{4,6},{5,7},{6,4},{7,5},{8,10},{9,11},{10,... | collective-permute-start | bytes 442376 | tf_op jit(solution)/shard_map/ppermute | solution.py:728
  260.4 15.7 %collective-permute-start.54 = (bf16[1,96,768]{2,1,0:T(8,128)(2,1)}, bf16[1,96,768]{2,1,0:T(8,128)(2,1)}, u32[]{:S(2)}, u32[]{:S(2)}) collective-permute-start(bf16[1,96,768]{2,1,0:T(8,128)(2,1)} %add_convert_fusion.14), channel_id=1, source_target_pairs={{0,16},{1,17},{2,18},{3,19},{4,20},{5,21},{6,22},{7,23},{8,24},{9,... | collective-permute-start | bytes 442376 | tf_op jit(solution)/shard_map/ppermute | solution.py:728
  265.1 14.5 %collective-permute-start.46 = (bf16[2,48,768]{2,1,0:T(8,128)(2,1)}, bf16[2,48,768]{2,1,0:T(8,128)(2,1)S(1)}, u32[]{:S(2)}, u32[]{:S(2)}) collective-permute-start(bf16[2,48,768]{2,1,0:T(8,128)(2,1)} %add_convert_fusion.17), channel_id=1, source_target_pairs={{0,4},{1,5},{2,6},{3,7},{4,0},{5,1},{6,2},{7,3},{8,12},{9,13},{10,... | collective-permute-start | bytes 442376 | tf_op jit(solution)/shard_map/ppermute | solution.py:728
  271.1 11.6 %collective-permute-start.57 = (bf16[2,48,768]{2,1,0:T(8,128)(2,1)}, bf16[2,48,768]{2,1,0:T(8,128)(2,1)}, u32[]{:S(2)}, u32[]{:S(2)}) collective-permute-start(bf16[2,48,768]{2,1,0:T(8,128)(2,1)} %add_convert_fusion.15), channel_id=1, source_target_pairs={{0,2},{1,3},{2,0},{3,1},{4,6},{5,7},{6,4},{7,5},{8,10},{9,11},{10,... | collective-permute-start | bytes 442376 | tf_op jit(solution)/shard_map/ppermute | solution.py:728
  274.6 10.7 %collective-permute-start.56 = (bf16[1,96,768]{2,1,0:T(8,128)(2,1)}, bf16[1,96,768]{2,1,0:T(8,128)(2,1)}, u32[]{:S(2)}, u32[]{:S(2)}) collective-permute-start(bf16[1,96,768]{2,1,0:T(8,128)(2,1)} %add_convert_fusion.13), channel_id=1, source_target_pairs={{0,16},{1,17},{2,18},{3,19},{4,20},{5,21},{6,22},{7,23},{8,24},{9,... | collective-permute-start | bytes 442376 | tf_op jit(solution)/shard_map/ppermute | solution.py:728
  (67 other events, 605.4 us)
